TPU v7x, 32 devices: a whole 2x2x4 slice. The times are simulated.
32 devices in a mesh: az: 8 (over y, x, core), rad: 4 (over z).
Axes of the slice: x: 2, y: 2, z: 4, core: 2. Of those that a mesh axis runs over, the one named last changes fastest.
Arguments:
- velocity: float32 [3, 128, 512, 128], P(None, 'rad', 'az'), may hold values from -6 to 6
- dumbbells: float32 [3, 4, 8, 4096], P(None, 'rad', 'az'), may hold values from -1.6 to 1.6
- cell_ids: int32 [2, 4, 8, 4096], P(None, 'rad', 'az'), may hold values from 0 to 2047, as said below
- brownian: float32 [3, 4, 8, 4096], P(None, 'rad', 'az'), may hold values from -5 to 5
- stencil_coef: float32 [9, 128], P(None, 'rad'), may hold values from -3 to 3
- block_inverse: float32 [128, 32], P('rad'), may hold values from -1 to 4, as said below
- azim_coef: float32 [128], P('rad'), may hold values from 1e-05 to 10
Outputs:
- velocity_next: float32 [3, 128, 512, 128], P(None, 'rad', 'az')
- dumbbells_next: float32 [3, 4, 8, 4096], P(None, 'rad', 'az')
Inputs may be any that keep to these rules, and one draw needn't show every extreme that they name: cell_ids[0] is local radius times 64 plus local azimuth within the block, below 2048; cell_ids[1] is below 128. `block_inverse`: row r holds the weights that map the stencil sums of its radial block to the derivative at r.
All inputs are finite; a program needn't handle non-finite values.
Results may differ from a plain program's by a relative error of at most 0.000064.
Values sent between devices are 32-bit elements; how exact they have to be, the bound alone decides.
No kernel may reach another device: no remote copies, remote signals or barrier semaphores. Data moves between devices by JAX's collectives and lax.ppermute only.
A program may use at most 192 MiB of HBM per device.

v0:
```python
import math

import jax
import jax.numpy as jnp
from jax import lax
from jax.sharding import PartitionSpec as P

TIME_STEP = 0.05
MAX_STRETCH = 10.0
STRESS_SCALE = 4.0
PRECISE = lax.Precision.HIGHEST


def with_halo(block, sides, width):
    for axis, dim in sides:
        count = lax.axis_size(axis)
        forward = [(i, i + 1) for i in range(count - 1)]
        backward = [(target, source) for source, target in forward]
        low = lax.ppermute(
            lax.slice_in_dim(block, block.shape[dim] - width, None, axis=dim), axis, forward
        )
        high = lax.ppermute(lax.slice_in_dim(block, 0, width, axis=dim), axis, backward)
        block = jnp.concatenate([low, block, high], axis=dim)
    return block


def radial_derivative(padded, stencil_coef, block_inverse):
    row_count = stencil_coef.shape[1]
    stencil_sum = stencil_coef[0][None, :, None, None] * padded[:, 0:row_count]
    for offset in range(1, 9):
        stencil_sum = (
            stencil_sum
            + stencil_coef[offset][None, :, None, None] * padded[:, offset : offset + row_count]
        )
    return jnp.einsum("ij,cjtz->citz", block_inverse, stencil_sum, precision=PRECISE)


def spectral_scale(row_ids, all_angles, azim_coef):
    nyquist = all_angles // 2
    wave_number = jnp.where(row_ids <= nyquist, row_ids, row_ids - nyquist).astype(jnp.float32)
    weight = jnp.where((row_ids == 0) | (row_ids == nyquist), 1.0, 2.0) / all_angles
    return weight[None, :] / (
        1.0 + azim_coef[:, None] * wave_number[None, :] * wave_number[None, :]
    )


def one_hot_rows(indices, count):
    return (lax.iota(jnp.int32, count)[:, None] == indices[None, :]).astype(jnp.float32)


def per_device(velocity, dumbbells, cell_ids, brownian, stencil_coef, block_inverse, azim_coef):
    local_angles = velocity.shape[2]
    axial_points = velocity.shape[3]
    local_radii = velocity.shape[1]
    plane_count = local_radii * local_angles
    all_angles = local_angles * lax.axis_size("az")
    first_angle = lax.axis_index("az") * local_angles
    my_angles = first_angle + lax.iota(jnp.int32, local_angles)
    spring = dumbbells[:, 0, 0, :]
    noise = brownian[:, 0, 0, :]
    count_dumb = spring.shape[1]
    block_size = min(count_dumb, 1024)
    block_count = count_dumb // block_size
    plane_blocks = cell_ids[0, 0, 0, :].reshape(block_count, block_size)
    axial_blocks = cell_ids[1, 0, 0, :].reshape(block_count, block_size)
    stretch_sq = jnp.sum(spring * spring, axis=0)
    fene_factor = 1.0 / (1.0 - stretch_sq / MAX_STRETCH)
    weighted = STRESS_SCALE * fene_factor * spring[0] * spring
    weighted_blocks = jnp.transpose(weighted.reshape(3, block_count, block_size), (1, 0, 2))

    def deposit(total, pieces):
        plane_ids, axial_ids, weight_piece = pieces
        plane_hot = one_hot_rows(plane_ids, plane_count)
        axial_hot = one_hot_rows(axial_ids, axial_points)
        left = (plane_hot[None, :, :] * weight_piece[:, None, :]).reshape(
            3 * plane_count, block_size
        )
        added = lax.dot_general(
            left,
            axial_hot,
            (((1,), (1,)), ((), ())),
            precision=PRECISE,
            preferred_element_type=jnp.float32,
        )
        return (total + added, None)

    stress_flat, _ = lax.scan(
        deposit,
        jnp.zeros((3 * plane_count, axial_points), jnp.float32),
        (plane_blocks, axial_blocks, weighted_blocks),
    )
    stress = stress_flat.reshape(velocity.shape)
    widened_velocity = with_halo(velocity, (("rad", 1),), 4)
    radial_grad = radial_derivative(widened_velocity, stencil_coef, block_inverse)
    widened_stress = with_halo(stress, (("rad", 1),), 4)
    polymer_force = radial_derivative(widened_stress, stencil_coef, block_inverse)
    grad_matrix = radial_grad.reshape(3 * plane_count, axial_points)

    def read_shear(carry, pieces):
        plane_ids, axial_ids = pieces
        plane_hot = one_hot_rows(plane_ids, plane_count)
        axial_hot = one_hot_rows(axial_ids, axial_points)
        picked = jnp.dot(
            grad_matrix, axial_hot, precision=PRECISE, preferred_element_type=jnp.float32
        )
        picked = picked.reshape(3, plane_count, block_size)
        return (carry, jnp.sum(picked * plane_hot[None, :, :], axis=1))

    _, shear_blocks = lax.scan(read_shear, jnp.zeros((), jnp.float32), (plane_blocks, axial_blocks))
    shear = jnp.transpose(shear_blocks, (1, 0, 2)).reshape(3, count_dumb)
    moved = (
        spring
        + TIME_STEP * (shear * spring[0] - 0.5 * fene_factor * spring)
        + math.sqrt(TIME_STEP) * noise
    )
    cosine_rows = lax.iota(jnp.int32, all_angles // 2 + 1)
    scale_rows = spectral_scale(cosine_rows, all_angles, azim_coef)
    slab_piece = lax.all_gather(velocity, "az", axis=2, tiled=True)
    piece_width = slab_piece.shape[2]
    out_angle = my_angles[:, None]
    in_angle = lax.iota(jnp.int32, piece_width)[None, :]
    offsets = jnp.mod(out_angle - in_angle, all_angles)
    phase = jnp.mod(cosine_rows[:, None, None] * offsets[None, :, :], all_angles).astype(
        jnp.float32
    )
    cos_table = jnp.cos(phase * (2.0 * math.pi / all_angles))
    kernel_block = jnp.einsum("rk,koi->roi", scale_rows, cos_table, precision=PRECISE)
    smooth = jnp.einsum("roi,crix->crox", kernel_block, slab_piece, precision=PRECISE)
    velocity_next = smooth + TIME_STEP * polymer_force
    return (velocity_next, moved.reshape(dumbbells.shape))


def solution(mesh):
    placed = (
        P(None, "rad", "az", None),
        P(None, "rad", "az", None),
        P(None, "rad", "az", None),
        P(None, "rad", "az", None),
        P(None, "rad"),
        P("rad", None),
        P("rad"),
    )
    return jax.shard_map(
        per_device,
        mesh=mesh,
        in_specs=placed,
        out_specs=(P(None, "rad", "az", None), P(None, "rad", "az", None)),
        check_vma=False,
    )
```

profile of v0, /device:TPU:0, one launch (start us, length us, event | category | flops | bytes accessed | tf_op | source)
XLA Modules:
  0.0 586.2 jit_solution(17376316830565741664)
XLA Ops:
  7.2 4.0 copy.16
  13.6 105.1 %while.22 = (s32[]{:T(128)}, f32[6144,128]{1,0:T(8,128)S(1)}, s32[4,1024]{1,0:T(4,128)S(1)}, f32[4,3,1024]{2,0,1:T(4,128)S(1)}, s32[4,1024]{1,0:T(4,128)S(1)}, /*index=5*/s32[]{:T(128)}, s32[]{:T(128)}) while((s32[]{:T(128)}, f32[6144,128]{1,0:T(8,128)S(1)}, s32[4,1024]{1,0:T(4,128)S(1)}, f32[4,3,1024]{2,0,1:T(4,128)S(1)}, ...), condition=%wide.region_2.3_spmd.clone, body=%wide.region_1.2_spmd.clone.sunk | while | flops 9675866112 | bytes 73486432 | solution.py:87
  14.9 10.6 %broadcast_multiply_fusion.4 = f32[3,2048,1024]{2,1,0:T(8,128)} fusion(f32[3,1024]{1,0:T(4,128)S(1)} %bitcast.86, f32[2048,1024]{1,0:T(8,128)S(1)} %fusion.92), kind=kLoop, calls=%fused_computation.10.clone.1 | loop fusion | flops 6291456 | bytes 33566720 | tf_op jit(solution)/shard_map/while/body/eval_jaxpr/mul | solution.py:75
  25.5 15.8 %convolution_add_fusion.2 = f32[6144,128]{1,0:T(8,128)S(1)} fusion(f32[6144,1024]{1,0:T(8,128)} %bitcast.80, f32[6144,128]{1,0:T(8,128)S(1)} %get-tuple-element.210, pred[]{:T(512)S(6)} %compare.8, s32[1024]{0:T(1024)S(1)} %bitcast.87), kind=kOutput, calls=%fused_computation.13.clone.1 | convolution fusion | flops 9665380352 | bytes 31461376 | tf_op jit(solution)/shard_map/while/body/eval_jaxpr/dot_general | solution.py:78
  42.6 9.5 %broadcast_multiply_fusion.4 = f32[3,2048,1024]{2,1,0:T(8,128)} fusion(f32[3,1024]{1,0:T(4,128)S(1)} %bitcast.86, f32[2048,1024]{1,0:T(8,128)S(1)} %fusion.92), kind=kLoop, calls=%fused_computation.10.clone.1 | loop fusion | flops 6291456 | bytes 33566720 | tf_op jit(solution)/shard_map/while/body/eval_jaxpr/mul | solution.py:75
  52.1 14.8 %convolution_add_fusion.2 = f32[6144,128]{1,0:T(8,128)S(1)} fusion(f32[6144,1024]{1,0:T(8,128)} %bitcast.80, f32[6144,128]{1,0:T(8,128)S(1)} %get-tuple-element.210, pred[]{:T(512)S(6)} %compare.8, s32[1024]{0:T(1024)S(1)} %bitcast.87), kind=kOutput, calls=%fused_computation.13.clone.1 | convolution fusion | flops 9665380352 | bytes 31461376 | tf_op jit(solution)/shard_map/while/body/eval_jaxpr/dot_general | solution.py:78
  68.2 9.9 %broadcast_multiply_fusion.4 = f32[3,2048,1024]{2,1,0:T(8,128)} fusion(f32[3,1024]{1,0:T(4,128)S(1)} %bitcast.86, f32[2048,1024]{1,0:T(8,128)S(1)} %fusion.92), kind=kLoop, calls=%fused_computation.10.clone.1 | loop fusion | flops 6291456 | bytes 33566720 | tf_op jit(solution)/shard_map/while/body/eval_jaxpr/mul | solution.py:75
  78.2 14.9 %convolution_add_fusion.2 = f32[6144,128]{1,0:T(8,128)S(1)} fusion(f32[6144,1024]{1,0:T(8,128)} %bitcast.80, f32[6144,128]{1,0:T(8,128)S(1)} %get-tuple-element.210, pred[]{:T(512)S(6)} %compare.8, s32[1024]{0:T(1024)S(1)} %bitcast.87), kind=kOutput, calls=%fused_computation.13.clone.1 | convolution fusion | flops 9665380352 | bytes 31461376 | tf_op jit(solution)/shard_map/while/body/eval_jaxpr/dot_general | solution.py:78
  94.4 9.5 %broadcast_multiply_fusion.4 = f32[3,2048,1024]{2,1,0:T(8,128)} fusion(f32[3,1024]{1,0:T(4,128)S(1)} %bitcast.86, f32[2048,1024]{1,0:T(8,128)S(1)} %fusion.92), kind=kLoop, calls=%fused_computation.10.clone.1 | loop fusion | flops 6291456 | bytes 33566720 | tf_op jit(solution)/shard_map/while/body/eval_jaxpr/mul | solution.py:75
  103.9 14.8 %convolution_add_fusion.2 = f32[6144,128]{1,0:T(8,128)S(1)} fusion(f32[6144,1024]{1,0:T(8,128)} %bitcast.80, f32[6144,128]{1,0:T(8,128)S(1)} %get-tuple-element.210, pred[]{:T(512)S(6)} %compare.8, s32[1024]{0:T(1024)S(1)} %bitcast.87), kind=kOutput, calls=%fused_computation.13.clone.1 | convolution fusion | flops 9665380352 | bytes 31461376 | tf_op jit(solution)/shard_map/while/body/eval_jaxpr/dot_general | solution.py:78
  119.8 5.5 collective-permute-start
  128.7 5.3 collective-permute-start.2
  135.4 122.0 %fusion.11 = f32[257,64,512]{2,1,0:T(8,128)} fusion(s32[64,512]{1,0:T(8,128)S(1)} %add_select_fusion.1), kind=kLoop, calls=%fused_computation.28 | loop fusion | flops 117899264 | bytes 33816576 | tf_op jit(solution)/shard_map/cos | solution.py:126
  257.4 52.1 %fusion.51 = f32[32,64,512,1]{2,0,1,3:T(8,128)} fusion(f32[257,64,512]{2,1,0:T(8,128)} %fusion.11, f32[257]{0:T(512)S(1)} %fusion.74, f32[32]{0:T(128)S(1)} %copy-done.31, f32[257]{0:T(512)S(1)} %select_multiply_fusion), kind=kOutput, calls=%fused_computation.92 | convolution fusion | flops 3233841152 | bytes 37881992 | tf_op jit(solution)/shard_map/rk,koi->roi/dot_general | solution.py:127
  314.6 4.4 fusion.37
  319.0 4.9 fusion.54
  327.6 210.9 %while.21 = (s32[]{:T(128)}, f32[4,3,1024]{2,1,0:T(4,128)S(1)}, s32[4,1024]{1,0:T(4,128)}, f32[6144,128]{1,0:T(8,128)}, s32[4,1024]{1,0:T(4,128)}, /*index=5*/s32[]{:T(128)}) while((s32[]{:T(128)}, f32[4,3,1024]{2,1,0:T(4,128)S(1)}, s32[4,1024]{1,0:T(4,128)}, f32[6144,128]{1,0:T(8,128)}, s32[4,1024]{1,0:T(4,128)}, /*index=5*/s32[]{:T(128)}) %tuple.74), condition=%wide.region_5.6_spmd, body=%wide.region_3.5_spmd.sunk | while | flops 9680712704 | bytes 120655944 | solution.py:109
  328.7 15.8 %convolution_bitcast_fusion.2 = f32[6144,1024]{0,1:T(8,128)} fusion(f32[6144,128]{1,0:T(8,128)} %get-tuple-element.238, s32[1024]{0:T(1024)S(1)} %bitcast.85), kind=kOutput, calls=%fused_computation.1.clone.1 | convolution fusion | flops 9663938560 | bytes 28315648 | tf_op jit(solution)/shard_map/while/body/eval_jaxpr/dot_general | solution.py:103
  344.5 24.7 %copy.52 = f32[6144,1024]{1,0:T(8,128)} copy(f32[6144,1024]{0,1:T(8,128)} %convolution_bitcast_fusion.2) | data formatting | bytes 50331648 | tf_op jit(solution)/shard_map/while/body/eval_jaxpr/dot_general | solution.py:103
  370.5 10.1 %multiply_reduce_fusion.3 = f32[3,1024]{1,0:T(4,128)S(1)} fusion(f32[3,2048,1024]{2,1,0:T(8,128)} %bitcast.81, f32[2048,1024]{1,0:T(8,128)S(1)} %fusion.90), kind=kLoop, calls=%fused_computation.clone.1 | loop fusion | flops 12579840 | bytes 33566720 | tf_op jit(solution)/shard_map/while/body/eval_jaxpr/reduce_sum | solution.py:107
  381.4 15.8 %convolution_bitcast_fusion.2 = f32[6144,1024]{0,1:T(8,128)} fusion(f32[6144,128]{1,0:T(8,128)} %get-tuple-element.238, s32[1024]{0:T(1024)S(1)} %bitcast.85), kind=kOutput, calls=%fused_computation.1.clone.1 | convolution fusion | flops 9663938560 | bytes 28315648 | tf_op jit(solution)/shard_map/while/body/eval_jaxpr/dot_general | solution.py:103
  397.2 24.7 %copy.52 = f32[6144,1024]{1,0:T(8,128)} copy(f32[6144,1024]{0,1:T(8,128)} %convolution_bitcast_fusion.2) | data formatting | bytes 50331648 | tf_op jit(solution)/shard_map/while/body/eval_jaxpr/dot_general | solution.py:103
  423.1 10.1 %multiply_reduce_fusion.3 = f32[3,1024]{1,0:T(4,128)S(1)} fusion(f32[3,2048,1024]{2,1,0:T(8,128)} %bitcast.81, f32[2048,1024]{1,0:T(8,128)S(1)} %fusion.90), kind=kLoop, calls=%fused_computation.clone.1 | loop fusion | flops 12579840 | bytes 33566720 | tf_op jit(solution)/shard_map/while/body/eval_jaxpr/reduce_sum | solution.py:107
  434.0 15.8 %convolution_bitcast_fusion.2 = f32[6144,1024]{0,1:T(8,128)} fusion(f32[6144,128]{1,0:T(8,128)} %get-tuple-element.238, s32[1024]{0:T(1024)S(1)} %bitcast.85), kind=kOutput, calls=%fused_computation.1.clone.1 | convolution fusion | flops 9663938560 | bytes 28315648 | tf_op jit(solution)/shard_map/while/body/eval_jaxpr/dot_general | solution.py:103
  449.8 24.7 %copy.52 = f32[6144,1024]{1,0:T(8,128)} copy(f32[6144,1024]{0,1:T(8,128)} %convolution_bitcast_fusion.2) | data formatting | bytes 50331648 | tf_op jit(solution)/shard_map/while/body/eval_jaxpr/dot_general | solution.py:103
  475.7 10.1 %multiply_reduce_fusion.3 = f32[3,1024]{1,0:T(4,128)S(1)} fusion(f32[3,2048,1024]{2,1,0:T(8,128)} %bitcast.81, f32[2048,1024]{1,0:T(8,128)S(1)} %fusion.90), kind=kLoop, calls=%fused_computation.clone.1 | loop fusion | flops 12579840 | bytes 33566720 | tf_op jit(solution)/shard_map/while/body/eval_jaxpr/reduce_sum | solution.py:107
  486.7 15.8 %convolution_bitcast_fusion.2 = f32[6144,1024]{0,1:T(8,128)} fusion(f32[6144,128]{1,0:T(8,128)} %get-tuple-element.238, s32[1024]{0:T(1024)S(1)} %bitcast.85), kind=kOutput, calls=%fused_computation.1.clone.1 | convolution fusion | flops 9663938560 | bytes 28315648 | tf_op jit(solution)/shard_map/while/body/eval_jaxpr/dot_general | solution.py:103
  502.5 24.7 %copy.52 = f32[6144,1024]{1,0:T(8,128)} copy(f32[6144,1024]{0,1:T(8,128)} %convolution_bitcast_fusion.2) | data formatting | bytes 50331648 | tf_op jit(solution)/shard_map/while/body/eval_jaxpr/dot_general | solution.py:103
  528.4 10.1 %multiply_reduce_fusion.3 = f32[3,1024]{1,0:T(4,128)S(1)} fusion(f32[3,2048,1024]{2,1,0:T(8,128)} %bitcast.81, f32[2048,1024]{1,0:T(8,128)S(1)} %fusion.90), kind=kLoop, calls=%fused_computation.clone.1 | loop fusion | flops 12579840 | bytes 33566720 | tf_op jit(solution)/shard_map/while/body/eval_jaxpr/reduce_sum | solution.py:107
  538.8 8.0 %fusion.20 = f32[3,32,64,128]{3,2,1,0:T(8,128)S(1)} fusion(f32[3,32,64,128]{3,2,1,0:T(8,128)S(1)} %bitcast.83, f32[3,4,64,128]{3,2,1,0:T(8,128)} %collective-permute-done.1, f32[3,4,64,128]{3,2,1,0:T(8,128)} %collective-permute-done, f32[32]{0:T(128)S(1)} %copy-done.28, f32[32]{0:T(128)S(1)} %copy-done.30, f32[32]{0:T(128)S(1)} %copy-done.16, ...), kind=kLoop, calls=%fused_computation.49 | loop fusion | flops 19660800 | bytes 7079040 | tf_op jit(solution)/shard_map/add | solution.py:32
  546.8 4.8 fusion.49
  552.4 24.6 %bitcast_add_fusion = f32[3,32,64,128]{3,2,0,1:T(8,128)S(1)} fusion(f32[3,64,128,32]{2,3,1,0:T(8,128)S(1)} %fusion.49, f32[3,32,512,128]{3,2,0,1:T(8,128)} %all-gather.2.cloned.1.call-done, f32[32,64,512,1]{2,0,1,3:T(8,128)} %fusion.51), kind=kOutput, calls=%fused_computation.86 | convolution fusion | flops 4833411072 | bytes 35651584 | tf_op jit(solution)/shard_map/roi,crix->crox/dot_general | solution.py:128
  (129 shorter events, 32.6 us)
Async XLA Ops:
  7.2 311.9 %copy-start = (f32[32,32]{1,0:T(8,128)S(1)}, f32[32,32]{1,0:T(8,128)}, u32[]{:S(2)}) copy-start(f32[32,32]{1,0:T(8,128)} %param.16) | copy-start | bytes 12292
  7.2 545.2 %all-gather.2.cloned.1.call-start = ((), (), s32[]{:S(2)}) async-start(), calls=%async_computation | async-start | bytes 28311552 | tf_op jit(solution)/shard_map/all_gather | solution.py:118
  118.8 15.2 %copy-start.6 = (s32[4,1024]{1,0:T(4,128)}, s32[4,1024]{1,0:T(4,128)S(1)}, u32[]{:S(2)}) copy-start(s32[4,1024]{1,0:T(4,128)S(1)} %get-tuple-element.246) | copy-start | bytes 49156
  118.8 15.2 %copy-start.7 = (s32[4,1024]{1,0:T(4,128)}, s32[4,1024]{1,0:T(4,128)S(1)}, u32[]{:S(2)}) copy-start(s32[4,1024]{1,0:T(4,128)S(1)} %get-tuple-element.247) | copy-start | bytes 49156
  118.8 138.6 %copy-start.1 = (f32[6144,128]{1,0:T(8,128)}, f32[6144,128]{1,0:T(8,128)S(1)}, u32[]{:S(2)}) copy-start(f32[6144,128]{1,0:T(8,128)S(1)} %get-tuple-element.56) | copy-start | bytes 9437188
  119.8 418.9 %collective-permute-start = (f32[3,4,64,128]{3,2,1,0:T(8,128)}, f32[3,4,64,128]{3,2,1,0:T(8,128)}, u32[]{:S(2)}, u32[]{:S(2)}) collective-permute-start(f32[3,4,64,128]{3,2,1,0:T(8,128)} %get-tuple-element.117), channel_id=1, source_target_pairs={{0,1},{1,2},{2,3},{4,5},{5,6},{6,7},{8,9},{9,10},{10,11},{12,13},{... | collective-permute-start | bytes 1179656 | tf_op jit(solution)/shard_map/ppermute | solution.py:19
  125.2 413.4 %collective-permute-start.1 = (f32[3,4,64,128]{3,2,1,0:T(8,128)}, f32[3,4,64,128]{3,2,1,0:T(8,128)}, u32[]{:S(2)}, u32[]{:S(2)}) collective-permute-start(f32[3,4,64,128]{3,2,1,0:T(8,128)} %get-tuple-element.118), channel_id=1, source_target_pairs={{1,0},{2,1},{3,2},{5,4},{6,5},{7,6},{9,8},{10,9},{11,10},{13,12},{... | collective-permute-start | bytes 1179656 | tf_op jit(solution)/shard_map/ppermute | solution.py:22
  128.7 181.9 %collective-permute-start.2 = (f32[3,4,64,128]{3,2,1,0:T(8,128)}, f32[3,4,64,128]{3,2,1,0:T(8,128)}, u32[]{:S(2)}, u32[]{:S(2)}) collective-permute-start(f32[3,4,64,128]{3,2,1,0:T(8,128)} %get-tuple-element.115), channel_id=1, source_target_pairs={{0,1},{1,2},{2,3},{4,5},{5,6},{6,7},{8,9},{9,10},{10,11},{12,13},{... | collective-permute-start | bytes 1179656 | tf_op jit(solution)/shard_map/ppermute | solution.py:19
  134.0 180.5 %collective-permute-start.3 = (f32[3,4,64,128]{3,2,1,0:T(8,128)}, f32[3,4,64,128]{3,2,1,0:T(8,128)S(1)}, u32[]{:S(2)}, u32[]{:S(2)}) collective-permute-start(f32[3,4,64,128]{3,2,1,0:T(8,128)} %get-tuple-element.116), channel_id=1, source_target_pairs={{1,0},{2,1},{3,2},{5,4},{6,5},{7,6},{9,8},{10,9},{11,10},{13,12},{... | collective-permute-start | bytes 1179656 | tf_op jit(solution)/shard_map/ppermute | solution.py:22
  135.4 122.0 %copy-start.31 = (f32[32]{0:T(128)S(1)}, f32[32]{0:T(128)}, u32[]{:S(2)}) copy-start(f32[32]{0:T(128)} %param.17) | copy-start | bytes 388
  310.5 4.0 copy-start.15
  310.5 4.0 copy-start.17
  310.5 4.0 copy-start.19
  310.5 4.0 copy-start.21
  310.6 4.0 copy-start.23
  310.6 4.0 copy-start.25
  310.6 4.0 copy-start.27
  310.6 4.0 copy-start.29
  327.5 211.1 %copy-start.2 = (f32[6144,128]{1,0:T(8,128)S(1)}, f32[6144,128]{1,0:T(8,128)}, u32[]{:S(2)}) copy-start(f32[6144,128]{1,0:T(8,128)} %copy-done.1) | copy-start | bytes 9437188
  327.5 211.1 %copy-start.14 = (f32[32]{0:T(128)S(1)}, f32[32]{0:T(128)}, u32[]{:S(2)}) copy-start(f32[32]{0:T(128)} %copy-done.13) | copy-start | bytes 388
  327.5 211.2 %copy-start.16 = (f32[32]{0:T(128)S(1)}, f32[32]{0:T(128)}, u32[]{:S(2)}) copy-start(f32[32]{0:T(128)} %copy-done.15) | copy-start | bytes 388
  327.5 211.2 %copy-start.18 = (f32[32]{0:T(128)S(1)}, f32[32]{0:T(128)}, u32[]{:S(2)}) copy-start(f32[32]{0:T(128)} %copy-done.17) | copy-start | bytes 388
  327.6 211.2 %copy-start.20 = (f32[32]{0:T(128)S(1)}, f32[32]{0:T(128)}, u32[]{:S(2)}) copy-start(f32[32]{0:T(128)} %copy-done.19) | copy-start | bytes 388
  327.6 211.2 %copy-start.22 = (f32[32]{0:T(128)S(1)}, f32[32]{0:T(128)}, u32[]{:S(2)}) copy-start(f32[32]{0:T(128)} %copy-done.21) | copy-start | bytes 388
  327.6 211.2 %copy-start.24 = (f32[32]{0:T(128)S(1)}, f32[32]{0:T(128)}, u32[]{:S(2)}) copy-start(f32[32]{0:T(128)} %copy-done.23) | copy-start | bytes 388
  327.6 211.2 %copy-start.26 = (f32[32]{0:T(128)S(1)}, f32[32]{0:T(128)}, u32[]{:S(2)}) copy-start(f32[32]{0:T(128)} %copy-done.25) | copy-start | bytes 388
  327.6 211.2 %copy-start.28 = (f32[32]{0:T(128)S(1)}, f32[32]{0:T(128)}, u32[]{:S(2)}) copy-start(f32[32]{0:T(128)} %copy-done.27) | copy-start | bytes 388
  327.6 211.2 %copy-start.30 = (f32[32]{0:T(128)S(1)}, f32[32]{0:T(128)}, u32[]{:S(2)}) copy-start(f32[32]{0:T(128)} %copy-done.29) | copy-start | bytes 388
  546.8 4.8 copy-start.5
  546.8 4.8 copy-start.8
  546.8 4.8 copy-start.9
  546.8 4.8 copy-start.11
  (5 other events, 13.7 us)
Sparse Core Ops, SparseCore 0:
  11.3 128.0 all-gather.1
where the time goes:
time: 595 us; the launch traced here: 586 us
  other arithmetic  226 us (38%)
  matrix products  210 us (35%)
  local copies, waits for them, and re-layouts  121 us (20%)
  between operations  15.1 us (3%)
  starting transfers between devices  13.4 us (2%)
    cos x1, other arithmetic, per_device(): cos_table = jnp.cos(phase * (2.0 * math.pi / all_angles))  122 us
    dot_general x4, local copies, waits for them, and re-layouts, read_shear(): jnp.dot(grad_matrix, axial_hot, precision=PRECISE, preferred_element_type...  98.8 us
    dot_general x4, matrix products, read_shear(): jnp.dot(grad_matrix, axial_hot, precision=PRECISE, preferred_element_type...  63.3 us
    dot_general x4, matrix products, deposit(): lax.dot_general(left, axial_hot, (((1,), (1,)), ((), ())), precision=PREC...  60.3 us
    dot_general x1, matrix products, per_device(): jnp.einsum('rk,koi->roi', scale_rows, cos_table, precision=PRECISE)  52.1 us
    reduce_sum x4, other arithmetic, read_shear(): return (carry, jnp.sum(picked * plane_hot[None, :, :], axis=1))  40.5 us
    mul x4, other arithmetic, deposit(): plane_hot[None, :, :] * weight_piece[:, None, :]  39.6 us
    dot_general x1, matrix products, per_device(): jnp.einsum('roi,crix->crox', kernel_block, slab_piece, precision=PRECISE)  24.6 us
  transfers between devices with their start and end apart: 5, of which 0 were waited for; matrix products, arithmetic and copies ran while one was open for 90% of the time, Pallas kernels for 0%

commit v1 on v0

v1 whole, which is shorter than its diff:
```python
import functools
import math

import jax
import jax.numpy as jnp
import numpy as np
from jax import lax
from jax.experimental import pallas as pl
from jax.experimental.pallas import tpu as pltpu
from jax.sharding import PartitionSpec as P

TIME_STEP = 0.05
MAX_STRETCH = 10.0
STRESS_SCALE = 4.0
PRECISE = lax.Precision.HIGHEST
HALO = 4
SUB = 8
VMEM_LIMIT = 56 * 1024 * 1024
F32 = jnp.float32
BF16 = jnp.bfloat16


def split(value):
    high = value.astype(BF16)
    return high, (value - high.astype(F32)).astype(BF16)


def dot(a, b):
    return jnp.dot(a, b, preferred_element_type=F32)


def dot3(a_high, a_low, b_high, b_low):
    return dot(a_high, b_high) + dot(a_high, b_low) + dot(a_low, b_high)


def derivative_matrix(stencil_coef, block_inverse):
    rows = stencil_coef.shape[1]
    wide = rows + 2 * HALO
    offset = lax.broadcasted_iota(jnp.int32, (rows, wide), 1) - lax.broadcasted_iota(
        jnp.int32, (rows, wide), 0
    )
    band = jnp.zeros((rows, wide), F32)
    for s in range(2 * HALO + 1):
        band = band + jnp.where(offset == s, stencil_coef[s][:, None], 0.0)
    small = jnp.dot(block_inverse, band, precision=PRECISE)
    big = jnp.repeat(jnp.repeat(small, SUB, axis=0), SUB, axis=1)
    row = lax.broadcasted_iota(jnp.int32, big.shape, 0)
    col = lax.broadcasted_iota(jnp.int32, big.shape, 1)
    return jnp.where(row % SUB == col % SUB, big, 0.0)


def widened_rows(low_ref, own_ref, high_ref, c, angles):
    parts = [ref[c, :, angles, :] for ref in (low_ref, own_ref, high_ref)]
    value = jnp.concatenate(parts, axis=0)
    return value.reshape(value.shape[0] * SUB, value.shape[2])


def deposit_kernel(ids_ref, spring_ref, stress_ref, weight_ref):
    step = pl.program_id(0)
    count = ids_ref.shape[3]
    axial = stress_ref.shape[3]

    @pl.when(step == 0)
    def _():
        q = [spring_ref[c, 0] for c in range(3)]
        stretch_sq = q[0] * q[0] + q[1] * q[1] + q[2] * q[2]
        factor = 1.0 / (1.0 - stretch_sq / MAX_STRETCH)
        here = lax.broadcasted_iota(jnp.int32, (axial, count), 0) == ids_ref[1, 0]
        for c in range(3):
            weight = STRESS_SCALE * factor * q[0] * q[c]
            high = weight.astype(BF16).astype(F32)
            weight_ref[c * axial : (c + 1) * axial, :] = jnp.where(here, high, 0.0).astype(BF16)
            weight_ref[(3 + c) * axial : (4 + c) * axial, :] = jnp.where(
                here, weight - high, 0.0
            ).astype(BF16)

    radii, angles = stress_ref.shape[1], stress_ref.shape[2]
    rows = radii * angles
    plane = lax.broadcasted_iota(jnp.int32, (rows, count), 0) + step * rows
    hot = jnp.where(plane == ids_ref[0, 0], 1.0, 0.0).astype(BF16)
    both = lax.dot_general(
        hot, weight_ref[...], (((1,), (1,)), ((), ())), preferred_element_type=F32
    )
    for c in range(3):
        total = (
            both[:, c * axial : (c + 1) * axial] + both[:, (3 + c) * axial : (4 + c) * axial]
        )
        stress_ref[c] = total.reshape(radii, angles, axial)


def deposit(ids, spring, shape):
    _, radii, angles, axial = shape
    count = ids.shape[3]
    part = max(1, min(radii, 512 // angles))
    return pl.pallas_call(
        deposit_kernel,
        grid=(radii // part,),
        in_specs=[
            pl.BlockSpec(ids.shape, lambda i: (0, 0, 0, 0)),
            pl.BlockSpec(spring.shape, lambda i: (0, 0, 0, 0)),
        ],
        out_specs=pl.BlockSpec((3, part, angles, axial), lambda i: (0, i, 0, 0)),
        out_shape=jax.ShapeDtypeStruct(shape, F32),
        scratch_shapes=[pltpu.VMEM((6 * axial, count), BF16)],
        compiler_params=pltpu.CompilerParams(vmem_limit_bytes=VMEM_LIMIT),
        cost_estimate=pl.CostEstimate(
            flops=12 * radii * angles * count * axial,
            bytes_accessed=12 * radii * angles * axial,
            transcendentals=0,
        ),
        name="deposit",
    )(ids, spring)


def move_kernel(
    matrix_ref, low_ref, own_ref, high_ref, ids_ref, spring_ref, noise_ref, moved_ref, grad_ref
):
    radii, angles, axial = own_ref.shape[1:]
    group = radii * SUB
    matrix_high, matrix_low = split(matrix_ref[...])

    def grad_step(i, carry):
        at = pl.ds(pl.multiple_of(i * SUB, SUB), SUB)
        field = jnp.concatenate(
            [widened_rows(low_ref, own_ref, high_ref, c, at) for c in range(3)], axis=1
        )
        field_high, field_low = split(field)
        grad = dot3(matrix_high, matrix_low, field_high, field_low)
        turned_high, turned_low = split(grad.T)
        cols = pl.ds(pl.multiple_of(i * group, group), group)
        grad_ref[: 3 * axial, cols] = turned_high
        grad_ref[3 * axial :, cols] = turned_low
        return carry

    lax.fori_loop(0, angles // SUB, grad_step, 0)

    count = ids_ref.shape[3]
    part = min(count, 512)

    def read_step(i, carry):
        at = pl.ds(pl.multiple_of(i * part, part), part)
        plane = ids_ref[0, 0, :, at]
        radius, angle = plane // angles, plane % angles
        column = (angle // SUB) * group + radius * SUB + angle % SUB
        row_ids = lax.broadcasted_iota(jnp.int32, (radii * angles, part), 0)
        hot = jnp.where(row_ids == column, 1.0, 0.0).astype(BF16)
        picked = dot(grad_ref[...], hot)
        here = lax.broadcasted_iota(jnp.int32, (axial, part), 0) == ids_ref[1, 0, :, at]
        q = [spring_ref[c, 0, :, at] for c in range(3)]
        stretch_sq = q[0] * q[0] + q[1] * q[1] + q[2] * q[2]
        factor = 1.0 / (1.0 - stretch_sq / MAX_STRETCH)
        for c in range(3):
            value = (
                picked[c * axial : (c + 1) * axial] + picked[(3 + c) * axial : (4 + c) * axial]
            )
            shear = jnp.sum(jnp.where(here, value, 0.0), axis=0, keepdims=True)
            moved_ref[c, 0, :, at] = (
                q[c]
                + TIME_STEP * (shear * q[0] - 0.5 * factor * q[c])
                + math.sqrt(TIME_STEP) * noise_ref[c, 0, :, at]
            )
        return carry

    lax.fori_loop(0, count // part, read_step, 0)


def move(matrix, low, velocity, high, ids, spring, noise):
    radii, angles, axial = velocity.shape[1:]
    count = ids.shape[3]
    return pl.pallas_call(
        move_kernel,
        out_shape=jax.ShapeDtypeStruct(spring.shape, F32),
        scratch_shapes=[pltpu.VMEM((6 * axial, radii * angles), BF16)],
        compiler_params=pltpu.CompilerParams(vmem_limit_bytes=VMEM_LIMIT),
        cost_estimate=pl.CostEstimate(
            flops=12 * radii * angles * count * axial,
            bytes_accessed=15 * radii * angles * axial,
            transcendentals=0,
        ),
        name="move",
    )(matrix, low, velocity, high, ids, spring, noise)


def force_kernel(matrix_ref, low_ref, own_ref, high_ref, out_ref):
    radii, angles, axial = own_ref.shape[1:]
    matrix_high, matrix_low = split(matrix_ref[...])
    for i in range(angles // SUB):
        at = pl.ds(i * SUB, SUB)
        field = jnp.concatenate(
            [widened_rows(low_ref, own_ref, high_ref, c, at) for c in range(3)], axis=1
        )
        field_high, field_low = split(field)
        force = TIME_STEP * dot3(matrix_high, matrix_low, field_high, field_low)
        for c in range(3):
            out_ref[c, :, at, :] = force[:, c * axial : (c + 1) * axial].reshape(radii, SUB, axial)


def force_term(matrix, low, stress, high):
    _, radii, angles, axial = stress.shape
    part = 2 * SUB

    def block(count):
        return pl.BlockSpec((3, count, part, axial), lambda i: (0, 0, i, 0))

    return pl.pallas_call(
        force_kernel,
        grid=(angles // part,),
        in_specs=[
            pl.BlockSpec(matrix.shape, lambda i: (0, 0)),
            block(HALO),
            block(radii),
            block(HALO),
        ],
        out_specs=block(radii),
        out_shape=jax.ShapeDtypeStruct(stress.shape, F32),
        compiler_params=pltpu.CompilerParams(vmem_limit_bytes=VMEM_LIMIT),
        cost_estimate=pl.CostEstimate(
            flops=18 * matrix.shape[0] * matrix.shape[1] * angles * axial // SUB,
            bytes_accessed=27 * radii * angles * axial,
            transcendentals=0,
        ),
        name="force",
    )(matrix, low, stress, high)


def fourier_table(all_angles):
    half = all_angles // 2
    row = np.arange(all_angles)
    wave = np.where(row <= half, row, row - half)
    phase = (wave[:, None] * row[None, :]) % all_angles
    angle = phase * (2.0 * math.pi / all_angles)
    table = np.where((row <= half)[:, None], np.cos(angle), np.sin(angle)).astype(np.float32)
    high = table.astype(BF16)
    low = (table - high.astype(np.float32)).astype(BF16)
    return high, low


def solve_kernel(coef_ref, first_ref, fh_ref, fl_ref, bh_ref, bl_ref, in_ref, out_ref):
    blocks, rows, angles, axial = in_ref.shape
    all_angles = blocks * angles
    half = all_angles // 2
    row_ids = lax.broadcasted_iota(jnp.int32, (all_angles, axial), 0)
    wave = jnp.where(row_ids <= half, row_ids, row_ids - half).astype(F32)
    weight = jnp.where((row_ids == 0) | (row_ids == half), 1.0 / all_angles, 2.0 / all_angles)
    base = first_ref[0] + pl.program_id(0) * rows
    field = jnp.concatenate(
        [in_ref[:, q].reshape(all_angles, axial) for q in range(rows)], axis=1
    )
    field_high, field_low = split(field)
    spectrum = dot3(fh_ref[...], fl_ref[...], field_high, field_low)
    scale = []
    for q in range(rows):
        coef = coef_ref[lax.rem(base + q, coef_ref.shape[0])]
        scale.append(weight / (1.0 + coef * (wave * wave)))
    spectrum_high, spectrum_low = split(spectrum * jnp.concatenate(scale, axis=1))
    result = dot3(bh_ref[...], bl_ref[...], spectrum_high, spectrum_low)
    for q in range(rows):
        out_ref[:, q] = result[:, q * axial : (q + 1) * axial].reshape(blocks, angles, axial)


def solve(coef, first, field):
    blocks, rows, angles, axial = field.shape
    all_angles = blocks * angles
    high, low = fourier_table(all_angles)
    tables = [high, low, np.ascontiguousarray(high.T), np.ascontiguousarray(low.T)]
    part = 2 if rows % 2 == 0 else 1
    table_spec = pl.BlockSpec((all_angles, all_angles), lambda i: (0, 0))
    field_spec = pl.BlockSpec((blocks, part, angles, axial), lambda i: (0, i, 0, 0))
    smem = pl.BlockSpec(memory_space=pltpu.SMEM)
    return pl.pallas_call(
        solve_kernel,
        grid=(rows // part,),
        in_specs=[smem, smem, table_spec, table_spec, table_spec, table_spec, field_spec],
        out_specs=field_spec,
        out_shape=jax.ShapeDtypeStruct(field.shape, F32),
        compiler_params=pltpu.CompilerParams(vmem_limit_bytes=VMEM_LIMIT),
        cost_estimate=pl.CostEstimate(
            flops=12 * all_angles * all_angles * rows * axial,
            bytes_accessed=8 * all_angles * rows * axial,
            transcendentals=0,
        ),
        name="solve",
    )(coef, first, *[jnp.asarray(t) for t in tables], field)


def halos(block):
    count = lax.axis_size("rad")
    forward = [(i, i + 1) for i in range(count - 1)]
    backward = [(target, source) for source, target in forward]
    radii = block.shape[1]
    low = lax.ppermute(block[:, radii - HALO :], "rad", forward)
    high = lax.ppermute(block[:, :HALO], "rad", backward)
    return low, high


def per_device(velocity, dumbbells, cell_ids, brownian, stencil_coef, block_inverse, azim_coef):
    _, radii, angles, axial = velocity.shape
    az = lax.axis_size("az")
    rows = 3 * radii // az
    pieces = velocity.reshape(az, rows, angles, axial)
    gathered = lax.all_to_all(pieces, "az", 0, 0, tiled=True)
    low, high = halos(velocity)
    stress = deposit(cell_ids, dumbbells, velocity.shape)
    stress_low, stress_high = halos(stress)
    matrix = derivative_matrix(stencil_coef, block_inverse)
    moved = move(matrix, low, velocity, high, cell_ids, dumbbells, brownian)
    first = (lax.axis_index("az") * rows).astype(jnp.int32).reshape(1)
    solved = solve(azim_coef, first, gathered)
    smooth = lax.all_to_all(solved, "az", 0, 0, tiled=True).reshape(velocity.shape)
    force = force_term(matrix, stress_low, stress, stress_high)
    return smooth + force, moved


def solution(mesh):
    placed = (
        P(None, "rad", "az", None),
        P(None, "rad", "az", None),
        P(None, "rad", "az", None),
        P(None, "rad", "az", None),
        P(None, "rad"),
        P("rad", None),
        P("rad"),
    )
    return jax.shard_map(
        per_device,
        mesh=mesh,
        in_specs=placed,
        out_specs=(P(None, "rad", "az", None), P(None, "rad", "az", None)),
        check_vma=False,
    )
```

time: 595 us -> 106 us (0.18); the launches traced: 586 us -> 106 us
  other arithmetic: 226 us -> 5.15 us
  matrix products: 210 us -> 0.23 us
  local copies, waits for them, and re-layouts: 121 us -> 6.88 us
  Pallas kernels: 0 us -> 60 us
  between operations: 15.1 us -> 0.77 us
  waiting for transfers between devices: 0.03 us -> 11.5 us
  starting transfers between devices: 13.4 us -> 21.1 us
    dot_general x12 -> x1, matrix products: 210 us -> 0.23 us  [derivative_matrix(): small = jnp.dot(block_inverse, band, precision=PRECISE)]
    cos x1 -> x0, other arithmetic: 122 us -> none  [per_device(): cos_table = jnp.cos(phase * (2.0 * math.pi / all_angles))]
    dot_general x4 -> x0, local copies, waits for them, and re-layouts: 98.8 us -> none  [read_shear(): jnp.dot(grad_matrix, axial_hot, precision=PRECISE, preferred_element_type...]
    pallas_call x0 -> x4, Pallas kernels: none -> 60 us  [the longest x1 23.1 us: move(): pl.pallas_call(move_kernel, out_shape=jax.ShapeDtypeStruct(spring.shape,...]
    reduce_sum x5 -> x0, other arithmetic: 40.7 us -> none  [the longest x4 40.5 us: read_shear(): return (carry, jnp.sum(picked * plane_hot[None, :, :], axis=1))]
    mul x6 -> x0, other arithmetic: 40.2 us -> none  [the longest x4 39.6 us: deposit(): plane_hot[None, :, :] * weight_piece[:, None, :]]
    all_to_all x0 -> x2, waiting for transfers between devices: none -> 11.5 us  [the longest x1 6.11 us: per_device(): lax.all_to_all(solved, 'az', 0, 0, tiled=True).reshape(velocity.shape)]
    all_to_all x0 -> x2, starting transfers between devices: none -> 9.77 us  [the longest x1 5.18 us: per_device(): gathered = lax.all_to_all(pieces, 'az', 0, 0, tiled=True)]
  transfers between devices with their start and end apart: 5 -> 6, of which waited for: 0 -> 2; matrix products, arithmetic and copies ran while one was open for 90% -> 5% of each run, Pallas kernels for 0% -> 57%
where the time goes in v1:
time: 106 us
  Pallas kernels  60 us (57%)
  starting transfers between devices  21.1 us (20%)
  waiting for transfers between devices  11.5 us (11%)
  local copies, waits for them, and re-layouts  6.88 us (6%)
  other arithmetic  5.15 us (5%)
    pallas_call x1, Pallas kernels, move(): pl.pallas_call(move_kernel, out_shape=jax.ShapeDtypeStruct(spring.shape,...  23.1 us
    pallas_call x1, Pallas kernels, deposit(): pl.pallas_call(deposit_kernel, grid=(radii // part,), in_specs=[pl.BlockS...  16.9 us
    pallas_call x1, Pallas kernels, solve(): pl.pallas_call(solve_kernel, grid=(rows // part,), in_specs=[smem, smem,...  13.7 us
    ppermute x2, starting transfers between devices, halos(): low = lax.ppermute(block[:, radii - HALO:], 'rad', forward)  8.8 us
    pallas_call x1, Pallas kernels, force_term(): pl.pallas_call(force_kernel, grid=(angles // part,), in_specs=[pl.BlockSp...  6.41 us
    all_to_all x1, waiting for transfers between devices, per_device(): lax.all_to_all(solved, 'az', 0, 0, tiled=True).reshape(velocity.shape)  6.11 us
    all_to_all x1, waiting for transfers between devices, per_device(): gathered = lax.all_to_all(pieces, 'az', 0, 0, tiled=True)  5.43 us
    all_to_all x1, starting transfers between devices, per_device(): gathered = lax.all_to_all(pieces, 'az', 0, 0, tiled=True)  5.18 us
  transfers between devices with their start and end apart: 6, of which 2 were waited for; matrix products, arithmetic and copies ran while one was open for 5% of the time, Pallas kernels for 57%

profile of v1, /device:TPU:0, one launch (start us, length us, event | category | flops | bytes accessed | tf_op | source)
XLA Modules:
  0.0 105.8 jit_solution(13935011356248308465)
XLA Ops:
  0.6 0.0 copy-start
  0.6 5.2 %all-to-all-start = ((f32[8,12,64,128]{3,2,1,0:T(8,128)}), f32[8,12,64,128]{3,2,1,0:T(8,128)S(1)}, u32[]{:S(2)}, u32[]{:S(2)}) async-start(f32[8,12,64,128]{3,2,1,0:T(8,128)} %bitcast.28), calls=%async_computation | async-start | bytes 6291456 | tf_op jit(solution)/shard_map/all_to_all | solution.py:301
  5.8 16.9 %deposit.1.own_ref = f32[3,32,64,128]{3,2,1,0:T(8,128)} custom-call(s32[2,1,1,4096]{3,2,1,0:T(1,128)} %ids_ref.3, f32[3,1,1,4096]{3,2,1,0:T(1,128)} %spring_ref.3), custom_call_target="tpu_custom_call" | custom-call | flops 12884901888 | bytes 3145728 | tf_op jit(solution)/shard_map/deposit/pallas_call | solution.py:95
  22.7 2.1 %fusion.71 = (f32[3,4,64,128]{3,2,1,0:T(8,128)}, f32[3,4,64,128]{3,2,1,0:T(8,128)}) fusion(f32[3,32,64,128]{3,2,1,0:T(8,128)} %deposit.1.own_ref), kind=kLoop, calls=%fused_computation.79 | loop fusion | bytes 1572864 | tf_op jit(solution)/shard_map/slice | solution.py:292
  24.8 3.5 %collective-permute-start = (f32[3,4,64,128]{3,2,1,0:T(8,128)}, f32[3,4,64,128]{3,2,1,0:T(8,128)S(1)}, u32[]{:S(2)}, u32[]{:S(2)}) collective-permute-start(f32[3,4,64,128]{3,2,1,0:T(8,128)} %get-tuple-element.5), channel_id=1, source_target_pairs={{0,1},{1,2},{2,3},{4,5},{5,6},{6,7},{8,9},{9,10},{10,11},{12,13},{... | collective-permute-start | bytes 1179656 | tf_op jit(solution)/shard_map/ppermute | solution.py:291
  28.3 1.3 %collective-permute-start.1 = (f32[3,4,64,128]{3,2,1,0:T(8,128)}, f32[3,4,64,128]{3,2,1,0:T(8,128)}, u32[]{:S(2)}, u32[]{:S(2)}) collective-permute-start(f32[3,4,64,128]{3,2,1,0:T(8,128)} %get-tuple-element.4), channel_id=1, source_target_pairs={{1,0},{2,1},{3,2},{5,4},{6,5},{7,6},{9,8},{10,9},{11,10},{13,12},{... | collective-permute-start | bytes 1179656 | tf_op jit(solution)/shard_map/ppermute | solution.py:292
  29.6 2.1 %fusion.70 = (f32[3,4,64,128]{3,2,1,0:T(8,128)}, f32[3,4,64,128]{3,2,1,0:T(8,128)}) fusion(f32[3,32,64,128]{3,2,1,0:T(8,128)} %own_ref.1), kind=kLoop, calls=%fused_computation.78 | loop fusion | bytes 1572864 | tf_op jit(solution)/shard_map/slice | solution.py:292
  31.7 5.3 %collective-permute-start.2 = (f32[3,4,64,128]{3,2,1,0:T(8,128)}, f32[3,4,64,128]{3,2,1,0:T(8,128)}, u32[]{:S(2)}, u32[]{:S(2)}) collective-permute-start(f32[3,4,64,128]{3,2,1,0:T(8,128)} %get-tuple-element.3), channel_id=1, source_target_pairs={{0,1},{1,2},{2,3},{4,5},{5,6},{6,7},{8,9},{9,10},{10,11},{12,13},{... | collective-permute-start | bytes 1179656 | tf_op jit(solution)/shard_map/ppermute | solution.py:291
  37.0 1.3 %collective-permute-start.3 = (f32[3,4,64,128]{3,2,1,0:T(8,128)}, f32[3,4,64,128]{3,2,1,0:T(8,128)}, u32[]{:S(2)}, u32[]{:S(2)}) collective-permute-start(f32[3,4,64,128]{3,2,1,0:T(8,128)} %get-tuple-element.2), channel_id=1, source_target_pairs={{1,0},{2,1},{3,2},{5,4},{6,5},{7,6},{9,8},{10,9},{11,10},{13,12},{... | collective-permute-start | bytes 1179656 | tf_op jit(solution)/shard_map/ppermute | solution.py:292
  38.3 5.4 %all-to-all-done.in_ref = f32[8,12,64,128]{3,2,1,0:T(8,128)S(1)} async-done(((f32[8,12,64,128]{3,2,1,0:T(8,128)}), f32[8,12,64,128]{3,2,1,0:T(8,128)S(1)}, u32[]{:S(2)}, u32[]{:S(2)}) %all-to-all-start) | async-done | bytes 3145760 | tf_op jit(solution)/shard_map/all_to_all | solution.py:301
  43.7 0.0 copy-start.2
  43.7 1.7 %copy-done.2 = f32[8,12,64,128]{3,2,1,0:T(8,128)} copy-done((f32[8,12,64,128]{3,2,1,0:T(8,128)}, f32[8,12,64,128]{3,2,1,0:T(8,128)S(1)}, u32[]{:S(2)}) %copy-start.2) | copy-done | bytes 3145752
  45.4 13.7 %solve.1 = f32[8,12,64,128]{3,2,1,0:T(8,128)} custom-call(f32[32]{0:T(128)} %coef_ref.1, s32[1]{0:T(128)} %bitcast.first_ref, bf16[512,512]{1,0:T(8,128)(2,1)} %constant.55.clone.fh_ref, bf16[512,512]{1,0:T(8,128)(2,1)} %constant.56.clone.fl_ref, bf16[512,512]{1,0:T(8,128)(2,1)} %constant.57.clone.bh_ref, bf16[512,512]{1,0:T(8,128)(2,1)} %constant.58.clone.bl_ref, ...), custom_call_target="tpu_custom_call" | custom-call | flops 4831838208 | bytes 6291456 | tf_op jit(solution)/shard_map/solve/pallas_call | solution.py:270
  59.1 0.0 copy-start.4
  59.1 4.6 %all-to-all-start.1 = ((f32[8,12,64,128]{3,2,1,0:T(8,128)}), f32[8,12,64,128]{3,2,1,0:T(8,128)}, u32[]{:S(2)}, u32[]{:S(2)}) async-start(f32[8,12,64,128]{3,2,1,0:T(8,128)} %solve.1), calls=%async_computation.1 | async-start | bytes 6291456 | tf_op jit(solution)/shard_map/all_to_all | solution.py:309
  63.6 0.0 copy-done.4
  63.7 0.0 copy-done
  63.7 0.2 convolution_bitcast_fusion
  64.0 0.1 copy.15
  64.1 0.2 copy.16
  64.3 0.9 fusion.matrix_ref
  65.2 0.0 collective-permute-done.low_ref
  65.2 0.0 copy-start.3
  65.2 0.0 collective-permute-done.1.high_ref
  65.2 0.7 copy-done.3
  65.9 6.4 %force.1 = f32[3,32,64,128]{3,2,1,0:T(8,128)} custom-call(f32[256,320]{1,0:T(8,128)} %fusion.matrix_ref, f32[3,4,64,128]{3,2,1,0:T(8,128)} %copy-done.3, f32[3,32,64,128]{3,2,1,0:T(8,128)} %deposit.1.own_ref, f32[3,4,64,128]{3,2,1,0:T(8,128)} %collective-permute-done.1.high_ref), custom_call_target="tpu_custom_call" | custom-call | flops 1509949440 | bytes 7077888 | tf_op jit(solution)/shard_map/force/pallas_call | solution.py:205
  72.4 0.0 collective-permute-done.2.low_ref
  72.4 0.0 collective-permute-done.3.high_ref
  72.4 23.1 %move.1 = f32[3,1,1,4096]{3,2,1,0:T(1,128)} custom-call(f32[256,320]{1,0:T(8,128)} %fusion.matrix_ref, f32[3,4,64,128]{3,2,1,0:T(8,128)} %collective-permute-done.2.low_ref, f32[3,32,64,128]{3,2,1,0:T(8,128)} %own_ref.1, f32[3,4,64,128]{3,2,1,0:T(8,128)} %collective-permute-done.3.high_ref, s32[2,1,1,4096]{3,2,1,0:T(1,128)} %ids_ref.3, ...), custom_call_target="tpu_custom_call" | custom-call | flops 12884901888 | bytes 3932160 | tf_op jit(solution)/shard_map/move/pallas_call | solution.py:170
  95.4 6.1 %all-to-all-done.1 = f32[8,12,64,128]{3,2,1,0:T(8,128)} async-done(((f32[8,12,64,128]{3,2,1,0:T(8,128)}), f32[8,12,64,128]{3,2,1,0:T(8,128)}, u32[]{:S(2)}, u32[]{:S(2)}) %all-to-all-start.1) | async-done | bytes 3145760 | tf_op jit(solution)/shard_map/all_to_all | solution.py:309
  101.5 0.0 copy-done.1
  101.5 4.2 %add.49 = f32[3,32,64,128]{3,2,1,0:T(8,128)} add(f32[3,32,64,128]{3,2,1,0:T(8,128)} %bitcast.2, f32[3,32,64,128]{3,2,1,0:T(8,128)S(1)} %copy-done.1) | non-fusion elementwise | flops 786432 | bytes 9437184 | tf_op jit(solution)/shard_map/add | solution.py:311
  (8 shorter events, 0.1 us)
Async XLA Ops:
  0.6 63.0 %copy-start = (f32[32,32]{1,0:T(8,128)S(1)}, f32[32,32]{1,0:T(8,128)}, u32[]{:S(2)}) copy-start(f32[32,32]{1,0:T(8,128)} %param.16) | copy-start | bytes 12292
  0.6 43.1 %all-to-all-start = ((f32[8,12,64,128]{3,2,1,0:T(8,128)}), f32[8,12,64,128]{3,2,1,0:T(8,128)S(1)}, u32[]{:S(2)}, u32[]{:S(2)}) async-start(f32[8,12,64,128]{3,2,1,0:T(8,128)} %bitcast.28), calls=%async_computation | async-start | bytes 6291456 | tf_op jit(solution)/shard_map/all_to_all | solution.py:301
  24.8 40.4 %collective-permute-start = (f32[3,4,64,128]{3,2,1,0:T(8,128)}, f32[3,4,64,128]{3,2,1,0:T(8,128)S(1)}, u32[]{:S(2)}, u32[]{:S(2)}) collective-permute-start(f32[3,4,64,128]{3,2,1,0:T(8,128)} %get-tuple-element.5), channel_id=1, source_target_pairs={{0,1},{1,2},{2,3},{4,5},{5,6},{6,7},{8,9},{9,10},{10,11},{12,13},{... | collective-permute-start | bytes 1179656 | tf_op jit(solution)/shard_map/ppermute | solution.py:291
  28.3 36.9 %collective-permute-start.1 = (f32[3,4,64,128]{3,2,1,0:T(8,128)}, f32[3,4,64,128]{3,2,1,0:T(8,128)}, u32[]{:S(2)}, u32[]{:S(2)}) collective-permute-start(f32[3,4,64,128]{3,2,1,0:T(8,128)} %get-tuple-element.4), channel_id=1, source_target_pairs={{1,0},{2,1},{3,2},{5,4},{6,5},{7,6},{9,8},{10,9},{11,10},{13,12},{... | collective-permute-start | bytes 1179656 | tf_op jit(solution)/shard_map/ppermute | solution.py:292
  31.7 40.7 %collective-permute-start.2 = (f32[3,4,64,128]{3,2,1,0:T(8,128)}, f32[3,4,64,128]{3,2,1,0:T(8,128)}, u32[]{:S(2)}, u32[]{:S(2)}) collective-permute-start(f32[3,4,64,128]{3,2,1,0:T(8,128)} %get-tuple-element.3), channel_id=1, source_target_pairs={{0,1},{1,2},{2,3},{4,5},{5,6},{6,7},{8,9},{9,10},{10,11},{12,13},{... | collective-permute-start | bytes 1179656 | tf_op jit(solution)/shard_map/ppermute | solution.py:291
  37.0 35.4 %collective-permute-start.3 = (f32[3,4,64,128]{3,2,1,0:T(8,128)}, f32[3,4,64,128]{3,2,1,0:T(8,128)}, u32[]{:S(2)}, u32[]{:S(2)}) collective-permute-start(f32[3,4,64,128]{3,2,1,0:T(8,128)} %get-tuple-element.2), channel_id=1, source_target_pairs={{1,0},{2,1},{3,2},{5,4},{6,5},{7,6},{9,8},{10,9},{11,10},{13,12},{... | collective-permute-start | bytes 1179656 | tf_op jit(solution)/shard_map/ppermute | solution.py:292
  43.7 1.7 %copy-start.2 = (f32[8,12,64,128]{3,2,1,0:T(8,128)}, f32[8,12,64,128]{3,2,1,0:T(8,128)S(1)}, u32[]{:S(2)}) copy-start(f32[8,12,64,128]{3,2,1,0:T(8,128)S(1)} %all-to-all-done.in_ref) | copy-start | bytes 9437188
  59.1 4.6 %copy-start.4 = (f32[9,32]{1,0:T(8,128)S(1)}, f32[9,32]{1,0:T(8,128)}, u32[]{:S(2)}) copy-start(f32[9,32]{1,0:T(8,128)} %param.15) | copy-start | bytes 3460
  59.1 42.5 %all-to-all-start.1 = ((f32[8,12,64,128]{3,2,1,0:T(8,128)}), f32[8,12,64,128]{3,2,1,0:T(8,128)}, u32[]{:S(2)}, u32[]{:S(2)}) async-start(f32[8,12,64,128]{3,2,1,0:T(8,128)} %solve.1), calls=%async_computation.1 | async-start | bytes 6291456 | tf_op jit(solution)/shard_map/all_to_all | solution.py:309
  65.2 0.8 copy-start.3
  72.4 29.2 %copy-start.1 = (f32[3,32,64,128]{3,2,1,0:T(8,128)S(1)}, f32[3,32,64,128]{3,2,1,0:T(8,128)}, u32[]{:S(2)}) copy-start(f32[3,32,64,128]{3,2,1,0:T(8,128)} %force.1) | copy-start | bytes 9437188

commit v2 on v0

v2 whole, which is shorter than its diff:
```python
import functools
import math

import jax
import jax.numpy as jnp
import numpy as np
from jax import lax
from jax.experimental import pallas as pl
from jax.experimental.pallas import tpu as pltpu
from jax.sharding import PartitionSpec as P

TIME_STEP = 0.05
MAX_STRETCH = 10.0
STRESS_SCALE = 4.0
PRECISE = lax.Precision.HIGHEST
HALO = 4
SUB = 8
VMEM_LIMIT = 56 * 1024 * 1024
F32 = jnp.float32
BF16 = jnp.bfloat16


def split(value):
    high = value.astype(BF16)
    return high, (value - high.astype(F32)).astype(BF16)


def dot(a, b):
    return jnp.dot(a, b, preferred_element_type=F32)


def dot3(stacked, b_high, b_low):
    rows = stacked.shape[0] // 2
    both = dot(stacked, b_high)
    return both[:rows] + both[rows:] + dot(stacked[:rows], b_low)

def iota(shape, dim):
    return lax.broadcasted_iota(jnp.int32, shape, dim)


def deposit_kernel(
    ids_ref, spring_ref, first_ref, last_ref, stress_ref, low_ref, high_ref, total_ref, weight_ref
):
    _, radii, angles, axial = stress_ref.shape
    count = spring_ref.shape[3]
    cells = radii * angles
    low_ref[0] = first_ref[...]
    high_ref[0] = last_ref[...]

    chunk = 64

    def clear(i, carry):
        total_ref[pl.ds(i * chunk, chunk)] = jnp.zeros((chunk, SUB, axial), F32)
        return carry

    lax.fori_loop(0, cells // chunk, clear, 0)

    q = [spring_ref[c, 0] for c in range(3)]
    stretch_sq = q[0] * q[0] + q[1] * q[1] + q[2] * q[2]
    factor = 1.0 / (1.0 - stretch_sq / MAX_STRETCH)
    for c in range(3):
        weight_ref[c : c + 1, :] = STRESS_SCALE * factor * q[0] * q[c]
    weight_ref[3:SUB, :] = jnp.zeros((SUB - 3, count), F32)

    lane = iota((SUB, axial), 1)
    batch = 4

    def block(i, carry):
        start = pl.multiple_of(i * axial, axial)
        tile = weight_ref[:, pl.ds(start, axial)]
        for g in range(axial // batch):
            cell, added = [], []
            for j in range(batch):
                at = g * batch + j
                place = ids_ref[1, 0, 0, start + at]
                turned = pltpu.roll(tile, (place + (axial - at)) & (axial - 1), axis=1)
                cell.append(ids_ref[0, 0, 0, start + at])
                added.append(jnp.where(lane == place, turned, 0.0))
            sums = []
            for j in range(batch):
                value = added[j]
                for k in range(j):
                    value = value + jnp.where(cell[k] == cell[j], added[k], 0.0)
                sums.append(value)
            old = [total_ref[cell[j]] for j in range(batch)]
            for j in range(batch):
                total_ref[cell[j]] = old[j] + sums[j]
        return carry

    lax.fori_loop(0, count // axial, block, 0)

    flat = total_ref.reshape(cells * SUB, axial)

    def unpack(r, carry):
        for i in range(angles // SUB):
            for c in range(3):
                at = (r * angles + i * SUB) * SUB + c
                stress_ref[c, r, i * SUB : (i + 1) * SUB, :] = flat[pl.ds(at, SUB, stride=SUB), :]
        return carry

    lax.fori_loop(0, radii, unpack, 0)
    low_ref[1] = stress_ref[:, :HALO]
    high_ref[1] = stress_ref[:, radii - HALO :]


def deposit(ids, spring, velocity):
    _, radii, angles, axial = velocity.shape
    count = ids.shape[3]
    edge = (2, 3, HALO, angles, axial)
    edge_block = (3, HALO, angles, axial)
    whole = pl.BlockSpec(memory_space=pltpu.VMEM)
    return pl.pallas_call(
        deposit_kernel,
        grid=(1,),
        in_specs=[
            pl.BlockSpec(memory_space=pltpu.SMEM),
            whole,
            pl.BlockSpec(edge_block, lambda i: (0, 0, 0, 0)),
            pl.BlockSpec(edge_block, lambda i: (0, radii // HALO - 1, 0, 0)),
        ],
        out_specs=[whole, whole, whole],
        out_shape=[
            jax.ShapeDtypeStruct(velocity.shape, F32),
            jax.ShapeDtypeStruct(edge, F32),
            jax.ShapeDtypeStruct(edge, F32),
        ],
        scratch_shapes=[
            pltpu.VMEM((radii * angles, SUB, axial), F32),
            pltpu.VMEM((SUB, count), F32),
        ],
        compiler_params=pltpu.CompilerParams(vmem_limit_bytes=VMEM_LIMIT),
        cost_estimate=pl.CostEstimate(
            flops=8 * radii * angles * count * axial,
            bytes_accessed=12 * radii * angles * axial,
            transcendentals=0,
        ),
        name="deposit",
    )(ids, spring, velocity, velocity)


def derivative_matrix(stencil_ref, inverse_ref):
    rows = inverse_ref.shape[1]
    wide = rows + 2 * HALO
    offset = iota((wide, rows), 0) - iota((wide, rows), 1)
    band = jnp.zeros((wide, rows), F32)
    for s in range(2 * HALO + 1):
        band = band + jnp.where(offset == s, stencil_ref[s : s + 1, :], 0.0)
    small = lax.dot_general(
        inverse_ref[...],
        band,
        (((1,), (1,)), ((), ())),
        precision=PRECISE,
        preferred_element_type=F32,
    )
    tall = jnp.where(iota((rows * SUB, rows), 0) // SUB == iota((rows * SUB, rows), 1), 1.0, 0.0)
    flat = jnp.where(iota((wide, wide * SUB), 1) // SUB == iota((wide, wide * SUB), 0), 1.0, 0.0)
    big = (rows * SUB, wide * SUB)
    same = iota(big, 0) % SUB == iota(big, 1) % SUB
    parts = []
    for part in split(small):
        spread = dot(dot(tall.astype(BF16), part).astype(BF16), flat.astype(BF16))
        parts.append(jnp.where(same, spread, 0.0).astype(BF16))
    return jnp.concatenate(parts, axis=0)


def move_kernel(
    stencil_ref,
    inverse_ref,
    low_ref,
    velocity_ref,
    stress_ref,
    high_ref,
    ids_ref,
    spring_ref,
    noise_ref,
    moved_ref,
    force_ref,
    grad_ref,
    matrix_ref,
):
    radii, angles, axial = velocity_ref.shape[1:]
    matrix_ref[...] = derivative_matrix(stencil_ref, inverse_ref)
    flat = grad_ref.reshape(radii * angles * SUB, axial)

    def derive(i, carry):
        at = pl.ds(pl.multiple_of(i * SUB, SUB), SUB)
        columns = []
        for f, own_ref in enumerate((velocity_ref, stress_ref)):
            for c in range(3):
                value = jnp.concatenate(
                    [low_ref[f, c, :, at, :], own_ref[c, :, at, :], high_ref[f, c, :, at, :]],
                    axis=0,
                )
                columns.append(value.reshape((radii + 2 * HALO) * SUB, axial))
        field_high, field_low = split(jnp.concatenate(columns, axis=1))
        result = dot3(matrix_ref[...], field_high, field_low)
        for c in range(3):
            force = TIME_STEP * result[:, (3 + c) * axial : (4 + c) * axial]
            force_ref[c, :, at, :] = force.reshape(radii, SUB, axial)
            for r in range(radii):
                place = (r * angles + i * SUB) * SUB + c
                flat[pl.ds(place, SUB, stride=SUB), :] = result[
                    r * SUB : (r + 1) * SUB, c * axial : (c + 1) * axial
                ]
        return carry

    lax.fori_loop(0, angles // SUB, derive, 0)

    lane = iota((SUB, axial), 1)

    def read(i, carry):
        start = pl.multiple_of(i * axial, axial)
        kept = [jnp.zeros((SUB, axial), F32) for _ in range(4)]
        for j in range(axial):
            tile = grad_ref[ids_ref[0, 0, 0, start + j]]
            turn = (axial + j - ids_ref[1, 0, 0, start + j]) & (axial - 1)
            kept[j % 4] = jnp.where(lane == j, pltpu.roll(tile, turn, axis=1), kept[j % 4])
        shear = (kept[0] + kept[1]) + (kept[2] + kept[3])
        at = pl.ds(start, axial)
        q = [spring_ref[c, 0, :, at] for c in range(3)]
        stretch_sq = q[0] * q[0] + q[1] * q[1] + q[2] * q[2]
        factor = 1.0 / (1.0 - stretch_sq / MAX_STRETCH)
        for c in range(3):
            moved_ref[c, 0, :, at] = (
                q[c]
                + TIME_STEP * (shear[c : c + 1] * q[0] - 0.5 * factor * q[c])
                + math.sqrt(TIME_STEP) * noise_ref[c, 0, :, at]
            )
        return carry

    lax.fori_loop(0, spring_ref.shape[3] // axial, read, 0)


def move(stencil, inverse, low, velocity, stress, high, ids, spring, noise):
    radii, angles, axial = velocity.shape[1:]
    whole = pl.BlockSpec(memory_space=pltpu.VMEM)
    return pl.pallas_call(
        move_kernel,
        in_specs=[whole] * 6 + [pl.BlockSpec(memory_space=pltpu.SMEM)] + [whole] * 2,
        out_specs=[whole, whole],
        out_shape=[
            jax.ShapeDtypeStruct(spring.shape, F32),
            jax.ShapeDtypeStruct(velocity.shape, F32),
        ],
        scratch_shapes=[
            pltpu.VMEM((radii * angles, SUB, axial), F32),
            pltpu.VMEM((2 * radii * SUB, (radii + 2 * HALO) * SUB), BF16),
        ],
        compiler_params=pltpu.CompilerParams(vmem_limit_bytes=VMEM_LIMIT),
        cost_estimate=pl.CostEstimate(
            flops=10 * radii * angles * spring.shape[3] * axial,
            bytes_accessed=40 * radii * angles * axial,
            transcendentals=0,
        ),
        name="move",
    )(stencil, inverse, low, velocity, stress, high, ids, spring, noise)


def fourier_tables(all_angles):
    half = all_angles // 2
    row = np.arange(half)
    quarter = half // 2
    waves = [
        np.where(row <= quarter, 2 * row, 2 * (row - quarter)),
        np.where(row < quarter, 2 * row + 1, 2 * (row - quarter) + 1),
    ]
    cosine = [row <= quarter, row < quarter]
    tables, squares = [], []
    for wave, even in zip(waves, cosine):
        phase = (wave[:, None] * row[None, :]) % all_angles
        angle = phase * (2.0 * math.pi / all_angles)
        table = np.where(even[:, None], np.cos(angle), np.sin(angle))
        weight = np.where((wave == 0) | (wave == half), 1.0, 2.0) / all_angles
        for value in (table, table.T * weight[None, :]):
            value = value.astype(np.float32)
            high = value.astype(BF16)
            low = (value - high.astype(np.float32)).astype(BF16)
            tables.append(np.concatenate([high, low], axis=0))
        squares.append(wave.astype(np.float32) ** 2)
    return np.stack(tables), np.stack(squares)


def solve_kernel(coef_ref, first_ref, table_ref, square_ref, in_ref, out_ref):
    blocks, rows, angles, axial = in_ref.shape
    half = blocks * angles // 2
    base = first_ref[0] + pl.program_id(0) * rows
    scale = [
        coef_ref[lax.rem(base + q, coef_ref.shape[0])] for q in range(rows)
    ]
    near = [in_ref[: blocks // 2, q].reshape(half, axial) for q in range(rows)]
    far = [in_ref[blocks // 2 :, q].reshape(half, axial) for q in range(rows)]
    results = []
    for odd in range(2):
        field = jnp.concatenate(
            [a - b if odd else a + b for a, b in zip(near, far)], axis=1
        )
        spectrum = dot3(table_ref[2 * odd], *split(field))
        square = square_ref[odd]
        damped = spectrum / (1.0 + jnp.concatenate([s * square for s in scale], axis=1))
        results.append(dot3(table_ref[2 * odd + 1], *split(damped)))
    for q in range(rows):
        even, odd = [value[:, q * axial : (q + 1) * axial] for value in results]
        out_ref[: blocks // 2, q] = (even + odd).reshape(blocks // 2, angles, axial)
        out_ref[blocks // 2 :, q] = (even - odd).reshape(blocks // 2, angles, axial)


def solve(coef, first, field):
    blocks, rows, angles, axial = field.shape
    all_angles = blocks * angles
    tables, squares = fourier_tables(all_angles)
    squares = jnp.broadcast_to(squares[:, :, None], squares.shape + (axial,))
    part = 2 if rows % 2 == 0 else 1
    field_spec = pl.BlockSpec((blocks, part, angles, axial), lambda i: (0, i, 0, 0))
    smem = pl.BlockSpec(memory_space=pltpu.SMEM)
    whole = pl.BlockSpec(memory_space=pltpu.VMEM)
    return pl.pallas_call(
        solve_kernel,
        grid=(rows // part,),
        in_specs=[smem, smem, whole, whole, field_spec],
        out_specs=field_spec,
        out_shape=jax.ShapeDtypeStruct(field.shape, F32),
        compiler_params=pltpu.CompilerParams(vmem_limit_bytes=VMEM_LIMIT),
        cost_estimate=pl.CostEstimate(
            flops=12 * all_angles * all_angles * rows * axial,
            bytes_accessed=8 * all_angles * rows * axial,
            transcendentals=0,
        ),
        name="solve",
    )(coef, first, jnp.asarray(tables), squares, field)


def add_kernel(force_ref, smooth_ref, out_ref):
    out_ref[...] = force_ref[...] + smooth_ref[...]


def add_part(force, smooth, first_row):
    rows, angles, axial = smooth.shape
    part = math.gcd(math.gcd(rows, first_row), 16)
    shifted = pl.BlockSpec((part, angles, axial), lambda i: (i + first_row // part, 0, 0))
    return pl.pallas_call(
        add_kernel,
        grid=(rows // part,),
        in_specs=[shifted, pl.BlockSpec((part, angles, axial), lambda i: (i, 0, 0))],
        out_specs=shifted,
        out_shape=jax.ShapeDtypeStruct(force.shape, F32),
        input_output_aliases={0: 0},
        compiler_params=pltpu.CompilerParams(vmem_limit_bytes=VMEM_LIMIT),
        cost_estimate=pl.CostEstimate(
            flops=rows * angles * axial,
            bytes_accessed=12 * rows * angles * axial,
            transcendentals=0,
        ),
        name="add",
    )(force, smooth)


def from_neighbours(low_edge, high_edge):
    count = lax.axis_size("rad")
    forward = [(i, i + 1) for i in range(count - 1)]
    backward = [(target, source) for source, target in forward]
    low = lax.ppermute(high_edge, "rad", forward)
    high = lax.ppermute(low_edge, "rad", backward)
    return low, high


PARTS = 2


def per_device(velocity, dumbbells, cell_ids, brownian, stencil_coef, block_inverse, azim_coef):
    _, radii, angles, axial = velocity.shape
    az = lax.axis_size("az")
    total = 3 * radii
    size = total // PARTS
    rows = size // az
    lines = velocity.reshape(total, angles, axial)
    gathered = []
    for part in range(PARTS):
        pieces = lines[part * size : (part + 1) * size].reshape(az, rows, angles, axial)
        gathered.append(lax.all_to_all(pieces, "az", 0, 0, tiled=True))
    stress, low_edge, high_edge = deposit(cell_ids, dumbbells, velocity)
    low, high = from_neighbours(low_edge, high_edge)
    moved, force = move(
        stencil_coef, block_inverse, low, velocity, stress, high, cell_ids, dumbbells, brownian
    )
    result = force.reshape(lines.shape)
    for part in range(PARTS):
        first = (lax.axis_index("az") * rows + part * size).astype(jnp.int32).reshape(1)
        solved = solve(azim_coef, first, gathered[part])
        smooth = lax.all_to_all(solved, "az", 0, 0, tiled=True)
        result = add_part(result, smooth.reshape(size, angles, axial), part * size)
    return result.reshape(velocity.shape), moved


def solution(mesh):
    placed = (
        P(None, "rad", "az", None),
        P(None, "rad", "az", None),
        P(None, "rad", "az", None),
        P(None, "rad", "az", None),
        P(None, "rad"),
        P("rad", None),
        P("rad"),
    )
    return jax.shard_map(
        per_device,
        mesh=mesh,
        in_specs=placed,
        out_specs=(P(None, "rad", "az", None), P(None, "rad", "az", None)),
        check_vma=False,
    )
```

time: 595 us -> 150 us (0.25); the launches traced: 586 us -> 149 us
  other arithmetic: 226 us -> 0 us
  matrix products: 210 us -> 0 us
  local copies, waits for them, and re-layouts: 121 us -> 7.67 us
  Pallas kernels: 0 us -> 72.8 us
  blocking collectives: 0 us -> 26 us
  waiting for transfers between devices: 0.03 us -> 24.7 us
  between operations: 15.1 us -> 0.68 us
    dot_general x12 -> x0, matrix products: 210 us -> none  [the longest x4 63.3 us: read_shear(): jnp.dot(grad_matrix, axial_hot, precision=PRECISE, preferred_element_type...]
    cos x1 -> x0, other arithmetic: 122 us -> none  [per_device(): cos_table = jnp.cos(phase * (2.0 * math.pi / all_angles))]
    dot_general x4 -> x0, local copies, waits for them, and re-layouts: 98.8 us -> none  [read_shear(): jnp.dot(grad_matrix, axial_hot, precision=PRECISE, preferred_element_type...]
    pallas_call x0 -> x6, Pallas kernels: none -> 72.8 us  [the longest x1 27.6 us: move(): pl.pallas_call(move_kernel, in_specs=[whole] * 6 + [pl.BlockSpec(memory_s...]
    reduce_sum x5 -> x0, other arithmetic: 40.7 us -> none  [the longest x4 40.5 us: read_shear(): return (carry, jnp.sum(picked * plane_hot[None, :, :], axis=1))]
    mul x6 -> x0, other arithmetic: 40.2 us -> none  [the longest x4 39.6 us: deposit(): plane_hot[None, :, :] * weight_piece[:, None, :]]
    all_to_all x0 -> x1, blocking collectives: none -> 26 us  [per_device(): gathered.append(lax.all_to_all(pieces, 'az', 0, 0, tiled=True))]
    all_to_all x0 -> x3, waiting for transfers between devices: none -> 14.8 us  [the longest x1 14.8 us: per_device(): gathered.append(lax.all_to_all(pieces, 'az', 0, 0, tiled=True))]
  transfers between devices with their start and end apart: 5 -> 5, of which waited for: 0 -> 3; matrix products, arithmetic and copies ran while one was open for 90% -> 1% of each run, Pallas kernels for 0% -> 46%
where the time goes in v2:
time: 150 us; the launch traced here: 149 us
  Pallas kernels  72.8 us (49%)
  blocking collectives  26 us (17%)
  waiting for transfers between devices  24.7 us (16%)
  starting transfers between devices  17.1 us (11%)
  local copies, waits for them, and re-layouts  7.67 us (5%)
    pallas_call x1, Pallas kernels, move(): pl.pallas_call(move_kernel, in_specs=[whole] * 6 + [pl.BlockSpec(memory_s...  27.6 us
    pallas_call x1, Pallas kernels, deposit(): pl.pallas_call(deposit_kernel, grid=(1,), in_specs=[pl.BlockSpec(memory_s...  27.1 us
    all_to_all x1, blocking collectives, per_device(): gathered.append(lax.all_to_all(pieces, 'az', 0, 0, tiled=True))  26 us
    all_to_all x1, waiting for transfers between devices, per_device(): gathered.append(lax.all_to_all(pieces, 'az', 0, 0, tiled=True))  14.8 us
    pallas_call x2, Pallas kernels, solve(): pl.pallas_call(solve_kernel, grid=(rows // part,), in_specs=[smem, smem,...  10.6 us
    all_to_all x2, starting transfers between devices, per_device(): smooth = lax.all_to_all(solved, 'az', 0, 0, tiled=True)  7.7 us
    pallas_call x2, Pallas kernels, add_part(): pl.pallas_call(add_kernel, grid=(rows // part,), in_specs=[shifted, pl.Bl...  7.5 us
    ppermute x1, waiting for transfers between devices, from_neighbours(): high = lax.ppermute(low_edge, 'rad', backward)  5.06 us
  transfers between devices with their start and end apart: 5, of which 3 were waited for; matrix products, arithmetic and copies ran while one was open for 1% of the time, Pallas kernels for 46%

profile of v2, /device:TPU:0, one launch (start us, length us, event | category | flops | bytes accessed | tf_op | source)
XLA Modules:
  0.0 149.0 jit_solution(4084960114141271553)
XLA Ops:
  0.6 3.3 %fusion = (f32[48,64,128]{2,1,0:T(8,128)}, f32[48,64,128]{2,1,0:T(8,128)S(1)}) fusion(f32[96,64,128]{2,1,0:T(8,128)} %bitcast.14), kind=kLoop, calls=%fused_computation | loop fusion | bytes 6291456 | tf_op jit(solution)/shard_map/slice | solution.py:378
  4.0 26.0 %all_to_all.20.in_ref = f32[8,6,64,128]{3,2,1,0:T(8,128)} all-to-all(f32[8,6,64,128]{3,2,1,0:T(8,128)S(1)} %bitcast.11), channel_id=1, replica_groups=mesh['az'=8,'rad'=4] {'az'}, dimensions={0} | all-to-all | bytes 3145728 | tf_op jit(solution)/shard_map/all_to_all | solution.py:379
  30.0 0.0 copy-start.3
  30.0 3.7 %all-to-all-start.2 = ((f32[8,6,64,128]{3,2,1,0:T(8,128)}), f32[8,6,64,128]{3,2,1,0:T(8,128)S(1)}, u32[]{:S(2)}, u32[]{:S(2)}) async-start(f32[8,6,64,128]{3,2,1,0:T(8,128)} %bitcast.6), calls=%async_computation.2 | async-start | bytes 3145728 | tf_op jit(solution)/shard_map/all_to_all | solution.py:379
  33.7 0.0 copy-done.3
  33.7 0.8 broadcast_in_dim.15.square_ref
  34.6 5.3 %solve.2 = f32[8,6,64,128]{3,2,1,0:T(8,128)} custom-call(f32[32]{0:T(128)} %coef_ref.3, s32[1]{0:T(128)} %bitcast.1.first_ref, bf16[4,512,256]{2,1,0:T(8,128)(2,1)} %constant.15.clone.table_ref, f32[2,256,128]{2,1,0:T(8,128)} %broadcast_in_dim.15.square_ref, f32[8,6,64,128]{3,2,1,0:T(8,128)} %all_to_all.20.in_ref), custom_call_target="tpu_custom_call" | custom-call | flops 2415919104 | bytes 3145728 | tf_op jit(solution)/shard_map/solve/pallas_call | solution.py:316
  39.9 14.8 %all-to-all-done.2.in_ref = f32[8,6,64,128]{3,2,1,0:T(8,128)S(1)} async-done(((f32[8,6,64,128]{3,2,1,0:T(8,128)}), f32[8,6,64,128]{3,2,1,0:T(8,128)S(1)}, u32[]{:S(2)}, u32[]{:S(2)}) %all-to-all-start.2) | async-done | bytes 1572896 | tf_op jit(solution)/shard_map/all_to_all | solution.py:379
  54.7 0.0 copy-start.2
  54.7 1.1 copy-done.2
  55.8 3.6 %all-to-all-start.1 = ((f32[8,6,64,128]{3,2,1,0:T(8,128)}), f32[8,6,64,128]{3,2,1,0:T(8,128)S(1)}, u32[]{:S(2)}, u32[]{:S(2)}) async-start(f32[8,6,64,128]{3,2,1,0:T(8,128)} %solve.2), calls=%async_computation.1 | async-start | bytes 3145728 | tf_op jit(solution)/shard_map/all_to_all | solution.py:389
  59.4 27.1 %deposit.1 = (f32[3,32,64,128]{3,2,1,0:T(8,128)}, f32[2,3,4,64,128]{4,3,2,1,0:T(8,128)}, f32[2,3,4,64,128]{4,3,2,1,0:T(8,128)}) custom-call(s32[2,1,1,4096]{3,2,1,0:T(1,128)} %ids_ref.3, f32[3,1,1,4096]{3,2,1,0:T(1,128)} %spring_ref.3, f32[3,32,64,128]{3,2,1,0:T(8,128)} %velocity_ref.1, f32[3,32,64,128]{3,2,1,0:T(8,128)} %velocity_ref.1), custom_call_target="tpu_custom_call" | custom-call | flops 8589934592 | bytes 3145728 | tf_op jit(solution)/shard_map/deposit/pallas_call | solution.py:112
  86.5 4.4 %collective-permute-start = (f32[2,3,4,64,128]{4,3,2,1,0:T(8,128)}, f32[2,3,4,64,128]{4,3,2,1,0:T(8,128)}, u32[]{:S(2)}, u32[]{:S(2)}) collective-permute-start(f32[2,3,4,64,128]{4,3,2,1,0:T(8,128)} %get-tuple-element.7), channel_id=1, source_target_pairs={{0,1},{1,2},{2,3},{4,5},{5,6},{6,7},{8,9},{9,10},{10,11},{12,13},{... | collective-permute-start | bytes 2359304 | tf_op jit(solution)/shard_map/ppermute | solution.py:361
  91.0 1.3 collective-permute-start.1
  92.3 5.3 %solve.3 = f32[8,6,64,128]{3,2,1,0:T(8,128)} custom-call(f32[32]{0:T(128)} %coef_ref.3, s32[1]{0:T(128)} %bitcast.5.first_ref, bf16[4,512,256]{2,1,0:T(8,128)(2,1)} %constant.15.clone.table_ref, f32[2,256,128]{2,1,0:T(8,128)} %broadcast_in_dim.15.square_ref, f32[8,6,64,128]{3,2,1,0:T(8,128)} %copy-done.2), custom_call_target="tpu_custom_call" | custom-call | flops 2415919104 | bytes 3145728 | tf_op jit(solution)/shard_map/solve/pallas_call | solution.py:316
  97.6 0.0 all-to-all-done.1
  97.6 0.0 copy-start
  97.6 1.2 copy-done
  98.8 4.1 %all-to-all-start.3 = ((f32[8,6,64,128]{3,2,1,0:T(8,128)}), f32[8,6,64,128]{3,2,1,0:T(8,128)S(1)}, u32[]{:S(2)}, u32[]{:S(2)}) async-start(f32[8,6,64,128]{3,2,1,0:T(8,128)} %solve.3), calls=%async_computation.3 | async-start | bytes 3145728 | tf_op jit(solution)/shard_map/all_to_all | solution.py:389
  102.9 4.8 %collective-permute-done.low_ref = f32[2,3,4,64,128]{4,3,2,1,0:T(8,128)} collective-permute-done((f32[2,3,4,64,128]{4,3,2,1,0:T(8,128)}, f32[2,3,4,64,128]{4,3,2,1,0:T(8,128)}, u32[]{:S(2)}, u32[]{:S(2)}) %collective-permute-start) | collective-permute-done | bytes 786464 | tf_op jit(solution)/shard_map/ppermute | solution.py:361
  107.7 5.1 %collective-permute-done.1.high_ref = f32[2,3,4,64,128]{4,3,2,1,0:T(8,128)} collective-permute-done((f32[2,3,4,64,128]{4,3,2,1,0:T(8,128)}, f32[2,3,4,64,128]{4,3,2,1,0:T(8,128)}, u32[]{:S(2)}, u32[]{:S(2)}) %collective-permute-start.1) | collective-permute-done | bytes 786464 | tf_op jit(solution)/shard_map/ppermute | solution.py:362
  112.8 27.6 %move.1 = (f32[3,1,1,4096]{3,2,1,0:T(1,128)}, f32[3,32,64,128]{3,2,1,0:T(8,128)}) custom-call(f32[9,32]{1,0:T(8,128)} %stencil_ref.1, f32[32,32]{1,0:T(8,128)} %inverse_ref.1, f32[2,3,4,64,128]{4,3,2,1,0:T(8,128)} %collective-permute-done.low_ref, f32[3,32,64,128]{3,2,1,0:T(8,128)} %velocity_ref.1, f32[3,32,64,128]{3,2,1,0:T(8,128)} %get-tuple-element.8.stress_ref, ...), custom_call_target="tpu_custom_call" | custom-call | flops 10737418240 | bytes 10485760 | tf_op jit(solution)/shard_map/move/pallas_call | solution.py:237
  140.3 3.8 %add.6.force_ref = f32[96,64,128]{2,1,0:T(8,128)} custom-call(f32[96,64,128]{2,1,0:T(8,128)} %bitcast.9, f32[48,64,128]{2,1,0:T(8,128)} %bitcast.12), custom_call_target="tpu_custom_call", output_to_operand_aliasing={{}: (0, {})} | custom-call | flops 393216 | bytes 4718592 | tf_op jit(solution)/shard_map/add/pallas_call | solution.py:340
  144.1 0.0 all-to-all-done.3
  144.1 0.0 copy-start.1
  144.1 1.2 copy-done.1
  145.3 3.8 %add.7 = f32[96,64,128]{2,1,0:T(8,128)} custom-call(f32[96,64,128]{2,1,0:T(8,128)} %add.6.force_ref, f32[48,64,128]{2,1,0:T(8,128)} %bitcast.13), custom_call_target="tpu_custom_call", output_to_operand_aliasing={{}: (0, {})} | custom-call | flops 393216 | bytes 4718592 | tf_op jit(solution)/shard_map/add/pallas_call | solution.py:340
Async XLA Ops:
  30.0 3.7 %copy-start.3 = (f32[2,256]{1,0:T(2,128)S(1)}, f32[2,256]{1,0:T(2,128)}, u32[]{:S(2)}) copy-start(f32[2,256]{1,0:T(2,128)} %constant.19) | copy-start | bytes 6148
  30.0 24.7 %all-to-all-start.2 = ((f32[8,6,64,128]{3,2,1,0:T(8,128)}), f32[8,6,64,128]{3,2,1,0:T(8,128)S(1)}, u32[]{:S(2)}, u32[]{:S(2)}) async-start(f32[8,6,64,128]{3,2,1,0:T(8,128)} %bitcast.6), calls=%async_computation.2 | async-start | bytes 3145728 | tf_op jit(solution)/shard_map/all_to_all | solution.py:379
  54.7 1.1 copy-start.2
  55.8 41.7 %all-to-all-start.1 = ((f32[8,6,64,128]{3,2,1,0:T(8,128)}), f32[8,6,64,128]{3,2,1,0:T(8,128)S(1)}, u32[]{:S(2)}, u32[]{:S(2)}) async-start(f32[8,6,64,128]{3,2,1,0:T(8,128)} %solve.2), calls=%async_computation.1 | async-start | bytes 3145728 | tf_op jit(solution)/shard_map/all_to_all | solution.py:389
  86.5 21.2 %collective-permute-start = (f32[2,3,4,64,128]{4,3,2,1,0:T(8,128)}, f32[2,3,4,64,128]{4,3,2,1,0:T(8,128)}, u32[]{:S(2)}, u32[]{:S(2)}) collective-permute-start(f32[2,3,4,64,128]{4,3,2,1,0:T(8,128)} %get-tuple-element.7), channel_id=1, source_target_pairs={{0,1},{1,2},{2,3},{4,5},{5,6},{6,7},{8,9},{9,10},{10,11},{12,13},{... | collective-permute-start | bytes 2359304 | tf_op jit(solution)/shard_map/ppermute | solution.py:361
  91.0 21.8 %collective-permute-start.1 = (f32[2,3,4,64,128]{4,3,2,1,0:T(8,128)}, f32[2,3,4,64,128]{4,3,2,1,0:T(8,128)}, u32[]{:S(2)}, u32[]{:S(2)}) collective-permute-start(f32[2,3,4,64,128]{4,3,2,1,0:T(8,128)} %get-tuple-element.9), channel_id=1, source_target_pairs={{1,0},{2,1},{3,2},{5,4},{6,5},{7,6},{9,8},{10,9},{11,10},{13,12},{... | collective-permute-start | bytes 2359304 | tf_op jit(solution)/shard_map/ppermute | solution.py:362
  97.6 1.2 copy-start
  98.8 45.3 %all-to-all-start.3 = ((f32[8,6,64,128]{3,2,1,0:T(8,128)}), f32[8,6,64,128]{3,2,1,0:T(8,128)S(1)}, u32[]{:S(2)}, u32[]{:S(2)}) async-start(f32[8,6,64,128]{3,2,1,0:T(8,128)} %solve.3), calls=%async_computation.3 | async-start | bytes 3145728 | tf_op jit(solution)/shard_map/all_to_all | solution.py:389
  144.1 1.2 copy-start.1

commit v3 on v2

--- a/solution.py
+++ b/solution.py
@@ -39,98 +39,79 @@
 
 
 def deposit_kernel(
-    ids_ref, spring_ref, first_ref, last_ref, stress_ref, low_ref, high_ref, total_ref, weight_ref
+    ids_ref, spring_ref, first_ref, last_ref, stress_ref, low_ref, high_ref, weight_ref
 ):
-    _, radii, angles, axial = stress_ref.shape
+    step = pl.program_id(0)
     count = spring_ref.shape[3]
-    cells = radii * angles
-    low_ref[0] = first_ref[...]
-    high_ref[0] = last_ref[...]
-
-    chunk = 64
-
-    def clear(i, carry):
-        total_ref[pl.ds(i * chunk, chunk)] = jnp.zeros((chunk, SUB, axial), F32)
-        return carry
-
-    lax.fori_loop(0, cells // chunk, clear, 0)
-
-    q = [spring_ref[c, 0] for c in range(3)]
-    stretch_sq = q[0] * q[0] + q[1] * q[1] + q[2] * q[2]
-    factor = 1.0 / (1.0 - stretch_sq / MAX_STRETCH)
+    axial = stress_ref.shape[3]
+
+    @pl.when(step == 0)
+    def _():
+        low_ref[0] = first_ref[...]
+        high_ref[0] = last_ref[...]
+        q = [spring_ref[c, 0] for c in range(3)]
+        stretch_sq = q[0] * q[0] + q[1] * q[1] + q[2] * q[2]
+        factor = 1.0 / (1.0 - stretch_sq / MAX_STRETCH)
+        here = iota((axial, count), 0) == ids_ref[1, 0]
+        for c in range(3):
+            weight = STRESS_SCALE * factor * q[0] * q[c]
+            high = weight.astype(BF16).astype(F32)
+            weight_ref[c * axial : (c + 1) * axial, :] = jnp.where(here, high, 0.0).astype(BF16)
+            weight_ref[(3 + c) * axial : (4 + c) * axial, :] = jnp.where(
+                here, weight - high, 0.0
+            ).astype(BF16)
+
+    radii, angles = stress_ref.shape[1], stress_ref.shape[2]
+    rows = radii * angles
+    hot = jnp.where(iota((rows, count), 0) + step * rows == ids_ref[0, 0], 1.0, 0.0).astype(BF16)
+    both = lax.dot_general(
+        hot, weight_ref[...], (((1,), (1,)), ((), ())), preferred_element_type=F32
+    )
     for c in range(3):
-        weight_ref[c : c + 1, :] = STRESS_SCALE * factor * q[0] * q[c]
-    weight_ref[3:SUB, :] = jnp.zeros((SUB - 3, count), F32)
-
-    lane = iota((SUB, axial), 1)
-    batch = 4
-
-    def block(i, carry):
-        start = pl.multiple_of(i * axial, axial)
-        tile = weight_ref[:, pl.ds(start, axial)]
-        for g in range(axial // batch):
-            cell, added = [], []
-            for j in range(batch):
-                at = g * batch + j
-                place = ids_ref[1, 0, 0, start + at]
-                turned = pltpu.roll(tile, (place + (axial - at)) & (axial - 1), axis=1)
-                cell.append(ids_ref[0, 0, 0, start + at])
-                added.append(jnp.where(lane == place, turned, 0.0))
-            sums = []
-            for j in range(batch):
-                value = added[j]
-                for k in range(j):
-                    value = value + jnp.where(cell[k] == cell[j], added[k], 0.0)
-                sums.append(value)
-            old = [total_ref[cell[j]] for j in range(batch)]
-            for j in range(batch):
-                total_ref[cell[j]] = old[j] + sums[j]
-        return carry
-
-    lax.fori_loop(0, count // axial, block, 0)
-
-    flat = total_ref.reshape(cells * SUB, axial)
-
-    def unpack(r, carry):
-        for i in range(angles // SUB):
-            for c in range(3):
-                at = (r * angles + i * SUB) * SUB + c
-                stress_ref[c, r, i * SUB : (i + 1) * SUB, :] = flat[pl.ds(at, SUB, stride=SUB), :]
-        return carry
-
-    lax.fori_loop(0, radii, unpack, 0)
-    low_ref[1] = stress_ref[:, :HALO]
-    high_ref[1] = stress_ref[:, radii - HALO :]
+        total = (
+            both[:, c * axial : (c + 1) * axial] + both[:, (3 + c) * axial : (4 + c) * axial]
+        )
+        stress_ref[c] = total.reshape(radii, angles, axial)
+
+    @pl.when(step == 0)
+    def _():
+        low_ref[1] = stress_ref[:, :HALO]
+
+    @pl.when(step == pl.num_programs(0) - 1)
+    def _():
+        high_ref[1] = stress_ref[:, radii - HALO :]
 
 
 def deposit(ids, spring, velocity):
     _, radii, angles, axial = velocity.shape
     count = ids.shape[3]
+    part = max(HALO, min(radii, 512 // angles))
     edge = (2, 3, HALO, angles, axial)
     edge_block = (3, HALO, angles, axial)
     whole = pl.BlockSpec(memory_space=pltpu.VMEM)
     return pl.pallas_call(
         deposit_kernel,
-        grid=(1,),
+        grid=(radii // part,),
         in_specs=[
-            pl.BlockSpec(memory_space=pltpu.SMEM),
+            whole,
             whole,
             pl.BlockSpec(edge_block, lambda i: (0, 0, 0, 0)),
             pl.BlockSpec(edge_block, lambda i: (0, radii // HALO - 1, 0, 0)),
         ],
-        out_specs=[whole, whole, whole],
+        out_specs=[
+            pl.BlockSpec((3, part, angles, axial), lambda i: (0, i, 0, 0)),
+            pl.BlockSpec(edge, lambda i: (0, 0, 0, 0, 0)),
+            pl.BlockSpec(edge, lambda i: (0, 0, 0, 0, 0)),
+        ],
         out_shape=[
             jax.ShapeDtypeStruct(velocity.shape, F32),
             jax.ShapeDtypeStruct(edge, F32),
             jax.ShapeDtypeStruct(edge, F32),
         ],
-        scratch_shapes=[
-            pltpu.VMEM((radii * angles, SUB, axial), F32),
-            pltpu.VMEM((SUB, count), F32),
-        ],
+        scratch_shapes=[pltpu.VMEM((6 * axial, count), BF16)],
         compiler_params=pltpu.CompilerParams(vmem_limit_bytes=VMEM_LIMIT),
         cost_estimate=pl.CostEstimate(
-            flops=8 * radii * angles * count * axial,
+            flops=12 * radii * angles * count * axial,
             bytes_accessed=12 * radii * angles * axial,
             transcendentals=0,
         ),
@@ -180,7 +161,7 @@
 ):
     radii, angles, axial = velocity_ref.shape[1:]
     matrix_ref[...] = derivative_matrix(stencil_ref, inverse_ref)
-    flat = grad_ref.reshape(radii * angles * SUB, axial)
+    group = radii * SUB
 
     def derive(i, carry):
         at = pl.ds(pl.multiple_of(i * SUB, SUB), SUB)
@@ -197,38 +178,41 @@
         for c in range(3):
             force = TIME_STEP * result[:, (3 + c) * axial : (4 + c) * axial]
             force_ref[c, :, at, :] = force.reshape(radii, SUB, axial)
-            for r in range(radii):
-                place = (r * angles + i * SUB) * SUB + c
-                flat[pl.ds(place, SUB, stride=SUB), :] = result[
-                    r * SUB : (r + 1) * SUB, c * axial : (c + 1) * axial
-                ]
+        turned_high, turned_low = split(result[:, : 3 * axial].T)
+        cols = pl.ds(pl.multiple_of(i * group, group), group)
+        grad_ref[: 3 * axial, cols] = turned_high
+        grad_ref[3 * axial :, cols] = turned_low
         return carry
 
     lax.fori_loop(0, angles // SUB, derive, 0)
 
-    lane = iota((SUB, axial), 1)
+    count = spring_ref.shape[3]
+    part = min(count, 512)
 
     def read(i, carry):
-        start = pl.multiple_of(i * axial, axial)
-        kept = [jnp.zeros((SUB, axial), F32) for _ in range(4)]
-        for j in range(axial):
-            tile = grad_ref[ids_ref[0, 0, 0, start + j]]
-            turn = (axial + j - ids_ref[1, 0, 0, start + j]) & (axial - 1)
-            kept[j % 4] = jnp.where(lane == j, pltpu.roll(tile, turn, axis=1), kept[j % 4])
-        shear = (kept[0] + kept[1]) + (kept[2] + kept[3])
-        at = pl.ds(start, axial)
+        at = pl.ds(pl.multiple_of(i * part, part), part)
+        plane = ids_ref[0, 0, :, at]
+        radius, angle = plane // angles, plane % angles
+        column = (angle // SUB) * group + radius * SUB + angle % SUB
+        hot = jnp.where(iota((radii * angles, part), 0) == column, 1.0, 0.0).astype(BF16)
+        picked = dot(grad_ref[...], hot)
+        here = iota((axial, part), 0) == ids_ref[1, 0, :, at]
         q = [spring_ref[c, 0, :, at] for c in range(3)]
         stretch_sq = q[0] * q[0] + q[1] * q[1] + q[2] * q[2]
         factor = 1.0 / (1.0 - stretch_sq / MAX_STRETCH)
         for c in range(3):
+            value = (
+                picked[c * axial : (c + 1) * axial] + picked[(3 + c) * axial : (4 + c) * axial]
+            )
+            shear = jnp.sum(jnp.where(here, value, 0.0), axis=0, keepdims=True)
             moved_ref[c, 0, :, at] = (
                 q[c]
-                + TIME_STEP * (shear[c : c + 1] * q[0] - 0.5 * factor * q[c])
+                + TIME_STEP * (shear * q[0] - 0.5 * factor * q[c])
                 + math.sqrt(TIME_STEP) * noise_ref[c, 0, :, at]
             )
         return carry
 
-    lax.fori_loop(0, spring_ref.shape[3] // axial, read, 0)
+    lax.fori_loop(0, count // part, read, 0)
 
 
 def move(stencil, inverse, low, velocity, stress, high, ids, spring, noise):
@@ -236,19 +220,19 @@
     whole = pl.BlockSpec(memory_space=pltpu.VMEM)
     return pl.pallas_call(
         move_kernel,
-        in_specs=[whole] * 6 + [pl.BlockSpec(memory_space=pltpu.SMEM)] + [whole] * 2,
+        in_specs=[whole] * 9,
         out_specs=[whole, whole],
         out_shape=[
             jax.ShapeDtypeStruct(spring.shape, F32),
             jax.ShapeDtypeStruct(velocity.shape, F32),
         ],
         scratch_shapes=[
-            pltpu.VMEM((radii * angles, SUB, axial), F32),
+            pltpu.VMEM((6 * axial, radii * angles), BF16),
             pltpu.VMEM((2 * radii * SUB, (radii + 2 * HALO) * SUB), BF16),
         ],
         compiler_params=pltpu.CompilerParams(vmem_limit_bytes=VMEM_LIMIT),
         cost_estimate=pl.CostEstimate(
-            flops=10 * radii * angles * spring.shape[3] * axial,
+            flops=14 * radii * angles * spring.shape[3] * axial,
             bytes_accessed=40 * radii * angles * axial,
             transcendentals=0,
         ),
@@ -265,28 +249,36 @@
         np.where(row < quarter, 2 * row + 1, 2 * (row - quarter) + 1),
     ]
     cosine = [row <= quarter, row < quarter]
-    tables, squares = [], []
+    tables = []
     for wave, even in zip(waves, cosine):
         phase = (wave[:, None] * row[None, :]) % all_angles
         angle = phase * (2.0 * math.pi / all_angles)
         table = np.where(even[:, None], np.cos(angle), np.sin(angle))
         weight = np.where((wave == 0) | (wave == half), 1.0, 2.0) / all_angles
         for value in (table, table.T * weight[None, :]):
-            value = value.astype(np.float32)
-            high = value.astype(BF16)
-            low = (value - high.astype(np.float32)).astype(BF16)
-            tables.append(np.concatenate([high, low], axis=0))
-        squares.append(wave.astype(np.float32) ** 2)
-    return np.stack(tables), np.stack(squares)
-
-
-def solve_kernel(coef_ref, first_ref, table_ref, square_ref, in_ref, out_ref):
+            tables.append(value.astype(np.float32))
+    return np.stack(tables)
+
+
+def solve_kernel(coef_ref, first_ref, float_ref, in_ref, out_ref, table_ref):
     blocks, rows, angles, axial = in_ref.shape
     half = blocks * angles // 2
+    quarter = half // 2
+
+    @pl.when(pl.program_id(0) == 0)
+    def _():
+        for i in range(4):
+            high, low = split(float_ref[i])
+            table_ref[i, :half] = high
+            table_ref[i, half:] = low
+
+    row = iota((half, axial), 0)
+    waves = [
+        jnp.where(row <= quarter, 2 * row, 2 * (row - quarter)),
+        jnp.where(row < quarter, 2 * row + 1, 2 * (row - quarter) + 1),
+    ]
     base = first_ref[0] + pl.program_id(0) * rows
-    scale = [
-        coef_ref[lax.rem(base + q, coef_ref.shape[0])] for q in range(rows)
-    ]
+    scale = [coef_ref[lax.rem(base + q, coef_ref.shape[0])] for q in range(rows)]
     near = [in_ref[: blocks // 2, q].reshape(half, axial) for q in range(rows)]
     far = [in_ref[blocks // 2 :, q].reshape(half, axial) for q in range(rows)]
     results = []
@@ -295,7 +287,7 @@
             [a - b if odd else a + b for a, b in zip(near, far)], axis=1
         )
         spectrum = dot3(table_ref[2 * odd], *split(field))
-        square = square_ref[odd]
+        square = (waves[odd] * waves[odd]).astype(F32)
         damped = spectrum / (1.0 + jnp.concatenate([s * square for s in scale], axis=1))
         results.append(dot3(table_ref[2 * odd + 1], *split(damped)))
     for q in range(rows):
@@ -307,8 +299,8 @@
 def solve(coef, first, field):
     blocks, rows, angles, axial = field.shape
     all_angles = blocks * angles
-    tables, squares = fourier_tables(all_angles)
-    squares = jnp.broadcast_to(squares[:, :, None], squares.shape + (axial,))
+    tables = fourier_tables(all_angles)
+    half = all_angles // 2
     part = 2 if rows % 2 == 0 else 1
     field_spec = pl.BlockSpec((blocks, part, angles, axial), lambda i: (0, i, 0, 0))
     smem = pl.BlockSpec(memory_space=pltpu.SMEM)
@@ -316,9 +308,10 @@
     return pl.pallas_call(
         solve_kernel,
         grid=(rows // part,),
-        in_specs=[smem, smem, whole, whole, field_spec],
+        in_specs=[smem, smem, whole, field_spec],
         out_specs=field_spec,
         out_shape=jax.ShapeDtypeStruct(field.shape, F32),
+        scratch_shapes=[pltpu.VMEM((4, 2 * half, half), BF16)],
         compiler_params=pltpu.CompilerParams(vmem_limit_bytes=VMEM_LIMIT),
         cost_estimate=pl.CostEstimate(
             flops=12 * all_angles * all_angles * rows * axial,
@@ -326,7 +319,7 @@
             transcendentals=0,
         ),
         name="solve",
-    )(coef, first, jnp.asarray(tables), squares, field)
+    )(coef, first, jnp.asarray(tables), field)
 
 
 def add_kernel(force_ref, smooth_ref, out_ref):
@@ -335,7 +328,7 @@
 
 def add_part(force, smooth, first_row):
     rows, angles, axial = smooth.shape
-    part = math.gcd(math.gcd(rows, first_row), 16)
+    part = math.gcd(math.gcd(rows, first_row), 8)
     shifted = pl.BlockSpec((part, angles, axial), lambda i: (i + first_row // part, 0, 0))
     return pl.pallas_call(
         add_kernel,
@@ -363,7 +356,7 @@
     return low, high
 
 
-PARTS = 2
+PARTS = 1
 
 
 def per_device(velocity, dumbbells, cell_ids, brownian, stencil_coef, block_inverse, azim_coef):

time: 150 us -> 139 us (0.927)
  waiting for transfers between devices: 24.7 us -> 58.2 us
  blocking collectives: 26 us -> 0 us
  Pallas kernels: 72.8 us -> 61.3 us
  local copies, waits for them, and re-layouts: 7.67 us -> 4.16 us
  starting transfers between devices: 17.1 us -> 13.6 us
    all_to_all x1 -> x0, blocking collectives: 26 us -> none  [per_device(): gathered.append(lax.all_to_all(pieces, 'az', 0, 0, tiled=True))]
    all_to_all x1, waiting for transfers between devices: 14.8 us -> 37.9 us  [per_device(): gathered.append(lax.all_to_all(pieces, 'az', 0, 0, tiled=True))]
    ppermute x1, waiting for transfers between devices: 4.83 us -> 16.3 us  [from_neighbours(): low = lax.ppermute(high_edge, 'rad', forward)]
    pallas_call x2, Pallas kernels: 54.7 us -> 44.3 us  [the longest x1 26.4 us: move(): pl.pallas_call(move_kernel, in_specs=[whole] * 9, out_specs=[whole, whole...]
    all_to_all x2 -> x1, starting transfers between devices: 7.7 us -> 3.65 us  [per_device(): smooth = lax.all_to_all(solved, 'az', 0, 0, tiled=True)]
    slice x1 -> x0, local copies, waits for them, and re-layouts: 3.34 us -> none  [per_device(): lines[part * size:(part + 1) * size].reshape(az, rows, angles, axial)]
    pallas_call x2 -> x1, Pallas kernels: 10.6 us -> 8.52 us  [solve(): pl.pallas_call(solve_kernel, grid=(rows // part,), in_specs=[smem, smem,...]
    pallas_call x2 -> x1, Pallas kernels: 7.5 us -> 8.44 us  [add_part(): pl.pallas_call(add_kernel, grid=(rows // part,), in_specs=[shifted, pl.Bl...]
  transfers between devices with their start and end apart: 5 -> 4, of which waited for: 3 -> 3; matrix products, arithmetic and copies ran while one was open for 1% -> 0% of each run, Pallas kernels for 46% -> 32%
where the time goes in v3:
time: 139 us; the launch traced here: 138 us
  Pallas kernels  61.3 us (44%)
  waiting for transfers between devices  58.2 us (42%)
  starting transfers between devices  13.6 us (10%)
  local copies, waits for them, and re-layouts  4.16 us (3%)
    all_to_all x1, waiting for transfers between devices, per_device(): gathered.append(lax.all_to_all(pieces, 'az', 0, 0, tiled=True))  37.9 us
    pallas_call x1, Pallas kernels, move(): pl.pallas_call(move_kernel, in_specs=[whole] * 9, out_specs=[whole, whole...  26.4 us
    pallas_call x1, Pallas kernels, deposit(): pl.pallas_call(deposit_kernel, grid=(radii // part,), in_specs=[whole, wh...  18 us
    ppermute x1, waiting for transfers between devices, from_neighbours(): low = lax.ppermute(high_edge, 'rad', forward)  16.3 us
    pallas_call x1, Pallas kernels, solve(): pl.pallas_call(solve_kernel, grid=(rows // part,), in_specs=[smem, smem,...  8.52 us
    pallas_call x1, Pallas kernels, add_part(): pl.pallas_call(add_kernel, grid=(rows // part,), in_specs=[shifted, pl.Bl...  8.44 us
    all_to_all x1, starting transfers between devices, per_device(): gathered.append(lax.all_to_all(pieces, 'az', 0, 0, tiled=True))  5.18 us
    unnamed x8, local copies, waits for them, and re-layouts  4.16 us
  transfers between devices with their start and end apart: 4, of which 3 were waited for; matrix products, arithmetic and copies ran while one was open for 0% of the time, Pallas kernels for 32%

profile of v3, /device:TPU:0, one launch (start us, length us, event | category | flops | bytes accessed | tf_op | source)
XLA Modules:
  0.0 138.0 jit_solution(15057251141779342586)
XLA Ops:
  0.6 5.2 %all-to-all-start = ((f32[8,12,64,128]{3,2,1,0:T(8,128)}), f32[8,12,64,128]{3,2,1,0:T(8,128)S(1)}, u32[]{:S(2)}, u32[]{:S(2)}) async-start(f32[8,12,64,128]{3,2,1,0:T(8,128)} %bitcast.6), calls=%async_computation | async-start | bytes 6291456 | tf_op jit(solution)/shard_map/all_to_all | solution.py:372
  5.8 37.9 %all-to-all-done.in_ref = f32[8,12,64,128]{3,2,1,0:T(8,128)S(1)} async-done(((f32[8,12,64,128]{3,2,1,0:T(8,128)}), f32[8,12,64,128]{3,2,1,0:T(8,128)S(1)}, u32[]{:S(2)}, u32[]{:S(2)}) %all-to-all-start) | async-done | bytes 3145760 | tf_op jit(solution)/shard_map/all_to_all | solution.py:372
  43.7 0.0 copy-start.1
  43.7 1.7 %copy-done.1 = f32[8,12,64,128]{3,2,1,0:T(8,128)} copy-done((f32[8,12,64,128]{3,2,1,0:T(8,128)}, f32[8,12,64,128]{3,2,1,0:T(8,128)S(1)}, u32[]{:S(2)}) %copy-start.1) | copy-done | bytes 3145752
  45.4 8.5 %solve.1 = f32[8,12,64,128]{3,2,1,0:T(8,128)} custom-call(f32[32]{0:T(128)} %coef_ref.1, s32[1]{0:T(128)} %bitcast.1.first_ref, f32[4,256,256]{2,1,0:T(8,128)} %constant.10.clone.float_ref, f32[8,12,64,128]{3,2,1,0:T(8,128)} %copy-done.1), custom_call_target="tpu_custom_call" | custom-call | flops 4831838208 | bytes 6291456 | tf_op jit(solution)/shard_map/solve/pallas_call | solution.py:308
  53.9 3.6 %all-to-all-start.1 = ((f32[8,12,64,128]{3,2,1,0:T(8,128)}), f32[8,12,64,128]{3,2,1,0:T(8,128)S(1)}, u32[]{:S(2)}, u32[]{:S(2)}) async-start(f32[8,12,64,128]{3,2,1,0:T(8,128)} %solve.1), calls=%async_computation.1 | async-start | bytes 6291456 | tf_op jit(solution)/shard_map/all_to_all | solution.py:382
  57.5 18.0 %deposit.1 = (f32[3,32,64,128]{3,2,1,0:T(8,128)}, f32[2,3,4,64,128]{4,3,2,1,0:T(8,128)}, f32[2,3,4,64,128]{4,3,2,1,0:T(8,128)}) custom-call(s32[2,1,1,4096]{3,2,1,0:T(1,128)} %ids_ref.3, f32[3,1,1,4096]{3,2,1,0:T(1,128)} %spring_ref.3, f32[3,32,64,128]{3,2,1,0:T(8,128)} %velocity_ref.1, f32[3,32,64,128]{3,2,1,0:T(8,128)} %velocity_ref.1), custom_call_target="tpu_custom_call" | custom-call | flops 12884901888 | bytes 3145728 | tf_op jit(solution)/shard_map/deposit/pallas_call | solution.py:92
  75.5 3.5 %collective-permute-start = (f32[2,3,4,64,128]{4,3,2,1,0:T(8,128)}, f32[2,3,4,64,128]{4,3,2,1,0:T(8,128)S(1)}, u32[]{:S(2)}, u32[]{:S(2)}) collective-permute-start(f32[2,3,4,64,128]{4,3,2,1,0:T(8,128)} %get-tuple-element.7), channel_id=1, source_target_pairs={{0,1},{1,2},{2,3},{4,5},{5,6},{6,7},{8,9},{9,10},{10,11},{12,13},{... | collective-permute-start | bytes 2359304 | tf_op jit(solution)/shard_map/ppermute | solution.py:354
  79.0 1.3 collective-permute-start.1
  80.3 16.3 %collective-permute-done.low_ref = f32[2,3,4,64,128]{4,3,2,1,0:T(8,128)S(1)} collective-permute-done((f32[2,3,4,64,128]{4,3,2,1,0:T(8,128)}, f32[2,3,4,64,128]{4,3,2,1,0:T(8,128)S(1)}, u32[]{:S(2)}, u32[]{:S(2)}) %collective-permute-start) | collective-permute-done | bytes 786464 | tf_op jit(solution)/shard_map/ppermute | solution.py:354
  96.6 0.0 copy-start.2
  96.6 4.1 %collective-permute-done.1.high_ref = f32[2,3,4,64,128]{4,3,2,1,0:T(8,128)S(1)} collective-permute-done((f32[2,3,4,64,128]{4,3,2,1,0:T(8,128)}, f32[2,3,4,64,128]{4,3,2,1,0:T(8,128)S(1)}, u32[]{:S(2)}, u32[]{:S(2)}) %collective-permute-start.1) | collective-permute-done | bytes 786464 | tf_op jit(solution)/shard_map/ppermute | solution.py:355
  100.6 0.0 copy-start.3
  100.6 0.0 copy-done.2
  100.7 0.9 copy-done.3
  101.5 26.4 %move.1 = (f32[3,1,1,4096]{3,2,1,0:T(1,128)}, f32[3,32,64,128]{3,2,1,0:T(8,128)}) custom-call(f32[9,32]{1,0:T(8,128)} %stencil_ref.1, f32[32,32]{1,0:T(8,128)} %inverse_ref.1, f32[2,3,4,64,128]{4,3,2,1,0:T(8,128)} %copy-done.2, f32[3,32,64,128]{3,2,1,0:T(8,128)} %velocity_ref.1, f32[3,32,64,128]{3,2,1,0:T(8,128)} %get-tuple-element.8.stress_ref, ...), custom_call_target="tpu_custom_call" | custom-call | flops 15032385536 | bytes 10485760 | tf_op jit(solution)/shard_map/move/pallas_call | solution.py:221
  127.9 0.0 all-to-all-done.1
  127.9 0.0 copy-start
  127.9 1.6 %copy-done = f32[8,12,64,128]{3,2,1,0:T(8,128)} copy-done((f32[8,12,64,128]{3,2,1,0:T(8,128)}, f32[8,12,64,128]{3,2,1,0:T(8,128)S(1)}, u32[]{:S(2)}) %copy-start) | copy-done | bytes 3145752
  129.5 8.4 %add.1 = f32[96,64,128]{2,1,0:T(8,128)} custom-call(f32[96,64,128]{2,1,0:T(8,128)} %bitcast.7, f32[96,64,128]{2,1,0:T(8,128)} %bitcast.5), custom_call_target="tpu_custom_call", output_to_operand_aliasing={{}: (0, {})} | custom-call | flops 786432 | bytes 9437184 | tf_op jit(solution)/shard_map/add/pallas_call | solution.py:333
Async XLA Ops:
  0.6 43.1 %all-to-all-start = ((f32[8,12,64,128]{3,2,1,0:T(8,128)}), f32[8,12,64,128]{3,2,1,0:T(8,128)S(1)}, u32[]{:S(2)}, u32[]{:S(2)}) async-start(f32[8,12,64,128]{3,2,1,0:T(8,128)} %bitcast.6), calls=%async_computation | async-start | bytes 6291456 | tf_op jit(solution)/shard_map/all_to_all | solution.py:372
  43.7 1.7 %copy-start.1 = (f32[8,12,64,128]{3,2,1,0:T(8,128)}, f32[8,12,64,128]{3,2,1,0:T(8,128)S(1)}, u32[]{:S(2)}) copy-start(f32[8,12,64,128]{3,2,1,0:T(8,128)S(1)} %all-to-all-done.in_ref) | copy-start | bytes 9437188
  53.9 74.0 %all-to-all-start.1 = ((f32[8,12,64,128]{3,2,1,0:T(8,128)}), f32[8,12,64,128]{3,2,1,0:T(8,128)S(1)}, u32[]{:S(2)}, u32[]{:S(2)}) async-start(f32[8,12,64,128]{3,2,1,0:T(8,128)} %solve.1), calls=%async_computation.1 | async-start | bytes 6291456 | tf_op jit(solution)/shard_map/all_to_all | solution.py:382
  75.5 21.1 %collective-permute-start = (f32[2,3,4,64,128]{4,3,2,1,0:T(8,128)}, f32[2,3,4,64,128]{4,3,2,1,0:T(8,128)S(1)}, u32[]{:S(2)}, u32[]{:S(2)}) collective-permute-start(f32[2,3,4,64,128]{4,3,2,1,0:T(8,128)} %get-tuple-element.7), channel_id=1, source_target_pairs={{0,1},{1,2},{2,3},{4,5},{5,6},{6,7},{8,9},{9,10},{10,11},{12,13},{... | collective-permute-start | bytes 2359304 | tf_op jit(solution)/shard_map/ppermute | solution.py:354
  79.0 21.6 %collective-permute-start.1 = (f32[2,3,4,64,128]{4,3,2,1,0:T(8,128)}, f32[2,3,4,64,128]{4,3,2,1,0:T(8,128)S(1)}, u32[]{:S(2)}, u32[]{:S(2)}) collective-permute-start(f32[2,3,4,64,128]{4,3,2,1,0:T(8,128)} %get-tuple-element.9), channel_id=1, source_target_pairs={{1,0},{2,1},{3,2},{5,4},{6,5},{7,6},{9,8},{10,9},{11,10},{13,12},{... | collective-permute-start | bytes 2359304 | tf_op jit(solution)/shard_map/ppermute | solution.py:355
  96.6 4.1 %copy-start.2 = (f32[2,3,4,64,128]{4,3,2,1,0:T(8,128)}, f32[2,3,4,64,128]{4,3,2,1,0:T(8,128)S(1)}, u32[]{:S(2)}) copy-start(f32[2,3,4,64,128]{4,3,2,1,0:T(8,128)S(1)} %collective-permute-done.low_ref) | copy-start | bytes 2359300
  100.6 0.9 copy-start.3
  127.9 1.6 %copy-start = (f32[8,12,64,128]{3,2,1,0:T(8,128)}, f32[8,12,64,128]{3,2,1,0:T(8,128)S(1)}, u32[]{:S(2)}) copy-start(f32[8,12,64,128]{3,2,1,0:T(8,128)S(1)} %all-to-all-done.1) | copy-start | bytes 9437188

commit v4 on v3

--- a/solution.py
+++ b/solution.py
@@ -15,7 +15,7 @@
 PRECISE = lax.Precision.HIGHEST
 HALO = 4
 SUB = 8
-VMEM_LIMIT = 56 * 1024 * 1024
+MIB = 1024 * 1024
 F32 = jnp.float32
 BF16 = jnp.bfloat16
 
@@ -109,7 +109,7 @@
             jax.ShapeDtypeStruct(edge, F32),
         ],
         scratch_shapes=[pltpu.VMEM((6 * axial, count), BF16)],
-        compiler_params=pltpu.CompilerParams(vmem_limit_bytes=VMEM_LIMIT),
+        compiler_params=pltpu.CompilerParams(vmem_limit_bytes=24 * MIB),
         cost_estimate=pl.CostEstimate(
             flops=12 * radii * angles * count * axial,
             bytes_accessed=12 * radii * angles * axial,
@@ -230,7 +230,7 @@
             pltpu.VMEM((6 * axial, radii * angles), BF16),
             pltpu.VMEM((2 * radii * SUB, (radii + 2 * HALO) * SUB), BF16),
         ],
-        compiler_params=pltpu.CompilerParams(vmem_limit_bytes=VMEM_LIMIT),
+        compiler_params=pltpu.CompilerParams(vmem_limit_bytes=28 * MIB),
         cost_estimate=pl.CostEstimate(
             flops=14 * radii * angles * spring.shape[3] * axial,
             bytes_accessed=40 * radii * angles * axial,
@@ -260,7 +260,7 @@
     return np.stack(tables)
 
 
-def solve_kernel(coef_ref, first_ref, float_ref, in_ref, out_ref, table_ref):
+def solve_kernel(coef_ref, first_ref, float_ref, after_ref, in_ref, out_ref, table_ref):
     blocks, rows, angles, axial = in_ref.shape
     half = blocks * angles // 2
     quarter = half // 2
@@ -296,7 +296,7 @@
         out_ref[blocks // 2 :, q] = (even - odd).reshape(blocks // 2, angles, axial)
 
 
-def solve(coef, first, field):
+def solve(coef, first, field, after):
     blocks, rows, angles, axial = field.shape
     all_angles = blocks * angles
     tables = fourier_tables(all_angles)
@@ -308,43 +308,18 @@
     return pl.pallas_call(
         solve_kernel,
         grid=(rows // part,),
-        in_specs=[smem, smem, whole, field_spec],
+        in_specs=[smem, smem, whole, pl.BlockSpec(memory_space=pl.ANY), field_spec],
         out_specs=field_spec,
         out_shape=jax.ShapeDtypeStruct(field.shape, F32),
         scratch_shapes=[pltpu.VMEM((4, 2 * half, half), BF16)],
-        compiler_params=pltpu.CompilerParams(vmem_limit_bytes=VMEM_LIMIT),
+        compiler_params=pltpu.CompilerParams(vmem_limit_bytes=14 * MIB),
         cost_estimate=pl.CostEstimate(
             flops=12 * all_angles * all_angles * rows * axial,
             bytes_accessed=8 * all_angles * rows * axial,
             transcendentals=0,
         ),
         name="solve",
-    )(coef, first, jnp.asarray(tables), field)
-
-
-def add_kernel(force_ref, smooth_ref, out_ref):
-    out_ref[...] = force_ref[...] + smooth_ref[...]
-
-
-def add_part(force, smooth, first_row):
-    rows, angles, axial = smooth.shape
-    part = math.gcd(math.gcd(rows, first_row), 8)
-    shifted = pl.BlockSpec((part, angles, axial), lambda i: (i + first_row // part, 0, 0))
-    return pl.pallas_call(
-        add_kernel,
-        grid=(rows // part,),
-        in_specs=[shifted, pl.BlockSpec((part, angles, axial), lambda i: (i, 0, 0))],
-        out_specs=shifted,
-        out_shape=jax.ShapeDtypeStruct(force.shape, F32),
-        input_output_aliases={0: 0},
-        compiler_params=pltpu.CompilerParams(vmem_limit_bytes=VMEM_LIMIT),
-        cost_estimate=pl.CostEstimate(
-            flops=rows * angles * axial,
-            bytes_accessed=12 * rows * angles * axial,
-            transcendentals=0,
-        ),
-        name="add",
-    )(force, smooth)
+    )(coef, first, jnp.asarray(tables), after, field)
 
 
 def from_neighbours(low_edge, high_edge):
@@ -356,32 +331,21 @@
     return low, high
 
 
-PARTS = 1
-
-
 def per_device(velocity, dumbbells, cell_ids, brownian, stencil_coef, block_inverse, azim_coef):
     _, radii, angles, axial = velocity.shape
     az = lax.axis_size("az")
-    total = 3 * radii
-    size = total // PARTS
-    rows = size // az
-    lines = velocity.reshape(total, angles, axial)
-    gathered = []
-    for part in range(PARTS):
-        pieces = lines[part * size : (part + 1) * size].reshape(az, rows, angles, axial)
-        gathered.append(lax.all_to_all(pieces, "az", 0, 0, tiled=True))
+    rows = 3 * radii // az
+    pieces = velocity.reshape(az, rows, angles, axial)
+    gathered = lax.all_to_all(pieces, "az", 0, 0, tiled=True)
     stress, low_edge, high_edge = deposit(cell_ids, dumbbells, velocity)
     low, high = from_neighbours(low_edge, high_edge)
+    first = (lax.axis_index("az") * rows).astype(jnp.int32).reshape(1)
+    solved = solve(azim_coef, first, gathered, low_edge)
+    smooth = lax.all_to_all(solved, "az", 0, 0, tiled=True).reshape(velocity.shape)
     moved, force = move(
         stencil_coef, block_inverse, low, velocity, stress, high, cell_ids, dumbbells, brownian
     )
-    result = force.reshape(lines.shape)
-    for part in range(PARTS):
-        first = (lax.axis_index("az") * rows + part * size).astype(jnp.int32).reshape(1)
-        solved = solve(azim_coef, first, gathered[part])
-        smooth = lax.all_to_all(solved, "az", 0, 0, tiled=True)
-        result = add_part(result, smooth.reshape(size, angles, axial), part * size)
-    return result.reshape(velocity.shape), moved
+    return smooth + force, moved
 
 
 def solution(mesh):

time: 139 us -> 116 us (0.83)
  waiting for transfers between devices: 58.2 us -> 36.5 us
  Pallas kernels: 61.3 us -> 45.6 us
  local copies, waits for them, and re-layouts: 4.16 us -> 11.1 us
  other arithmetic: 0 us -> 5.47 us
  starting transfers between devices: 13.6 us -> 16.1 us
    all_to_all x2, waiting for transfers between devices: 37.9 us -> 18.9 us  [the longest x1 18.9 us: per_device(): gathered = lax.all_to_all(pieces, 'az', 0, 0, tiled=True)]
    ppermute x1, waiting for transfers between devices: 16.3 us -> 1.29 us  [from_neighbours(): low = lax.ppermute(high_edge, 'rad', forward)]
    ppermute x1, waiting for transfers between devices: 4.05 us -> 16.3 us  [from_neighbours(): high = lax.ppermute(low_edge, 'rad', backward)]
    pallas_call x1 -> x0, Pallas kernels: 8.44 us -> none  [add_part(): pl.pallas_call(add_kernel, grid=(rows // part,), in_specs=[shifted, pl.Bl...]
    unnamed x8 -> x30, local copies, waits for them, and re-layouts: 4.16 us -> 11.1 us
    add x0 -> x1, other arithmetic: none -> 5.47 us  [per_device(): return (smooth + force, moved)]
    pallas_call x1, Pallas kernels: 26.4 us -> 23 us  [move(): pl.pallas_call(move_kernel, in_specs=[whole] * 9, out_specs=[whole, whole...]
    pallas_call x1, Pallas kernels: 18 us -> 15.6 us  [deposit(): pl.pallas_call(deposit_kernel, grid=(radii // part,), in_specs=[whole, wh...]
  transfers between devices with their start and end apart: 4 -> 4, of which waited for: 3 -> 3; matrix products, arithmetic and copies ran while one was open for 0% -> 0% of each run, Pallas kernels for 32% -> 33%
where the time goes in v4:
time: 116 us
  Pallas kernels  45.6 us (39%)
  waiting for transfers between devices  36.5 us (31%)
  starting transfers between devices  16.1 us (14%)
  local copies, waits for them, and re-layouts  11.1 us (10%)
  other arithmetic  5.47 us (5%)
    pallas_call x1, Pallas kernels, move(): pl.pallas_call(move_kernel, in_specs=[whole] * 9, out_specs=[whole, whole...  23 us
    all_to_all x1, waiting for transfers between devices, per_device(): gathered = lax.all_to_all(pieces, 'az', 0, 0, tiled=True)  18.9 us
    ppermute x1, waiting for transfers between devices, from_neighbours(): high = lax.ppermute(low_edge, 'rad', backward)  16.3 us
    pallas_call x1, Pallas kernels, deposit(): pl.pallas_call(deposit_kernel, grid=(radii // part,), in_specs=[whole, wh...  15.6 us
    unnamed x30, local copies, waits for them, and re-layouts  11.1 us
    pallas_call x1, Pallas kernels, solve(): pl.pallas_call(solve_kernel, grid=(rows // part,), in_specs=[smem, smem,...  7.09 us
    add x1, other arithmetic, per_device(): return (smooth + force, moved)  5.47 us
    all_to_all x1, starting transfers between devices, per_device(): gathered = lax.all_to_all(pieces, 'az', 0, 0, tiled=True)  5.45 us
  transfers between devices with their start and end apart: 4, of which 3 were waited for; matrix products, arithmetic and copies ran while one was open for 0% of the time, Pallas kernels for 33%

profile of v4, /device:TPU:0, one launch (start us, length us, event | category | flops | bytes accessed | tf_op | source)
XLA Modules:
  0.0 115.5 jit_solution(12622548760223160971)
XLA Ops:
  0.6 0.0 copy-start
  0.6 0.0 copy-start.6
  0.6 0.0 copy-start.8
  0.7 5.4 %all-to-all-start = ((f32[8,12,64,128]{3,2,1,0:T(8,128)}), f32[8,12,64,128]{3,2,1,0:T(8,128)}, u32[]{:S(2)}, u32[]{:S(2)}) async-start(f32[8,12,64,128]{3,2,1,0:T(8,128)} %bitcast.3), calls=%async_computation | async-start | bytes 6291456 | tf_op jit(solution)/shard_map/all_to_all | solution.py:339
  6.1 0.0 copy-done
  6.1 0.0 copy-done.6
  6.1 0.0 copy-done.8
  6.1 0.0 copy-start.11
  6.1 15.6 %deposit.1 = (f32[3,32,64,128]{3,2,1,0:T(8,128)S(1)}, f32[2,3,4,64,128]{4,3,2,1,0:T(8,128)S(1)}, f32[2,3,4,64,128]{4,3,2,1,0:T(8,128)S(1)}) custom-call(s32[2,1,1,4096]{3,2,1,0:T(1,128)S(1)} %copy-done.8, f32[3,1,1,4096]{3,2,1,0:T(1,128)S(1)} %copy-done.6, f32[3,32,64,128]{3,2,1,0:T(8,128)S(1)} %copy-done, f32[3,32,64,128]{3,2,1,0:T(8,128)S(1)} %copy-done), custom_call_target="tpu_custom_call" | custom-call | flops 12884901888 | bytes 3145728 | tf_op jit(solution)/shard_map/deposit/pallas_call | solution.py:92
  21.7 0.0 copy-start.3
  21.7 0.9 copy-done.3
  22.6 0.9 copy-done.4
  23.5 1.7 %copy-done.13 = f32[3,32,64,128]{3,2,1,0:T(8,128)} copy-done((f32[3,32,64,128]{3,2,1,0:T(8,128)}, f32[3,32,64,128]{3,2,1,0:T(8,128)S(1)}, u32[]{:S(2)}) %copy-start.13) | copy-done | bytes 3145752
  25.2 18.9 %all-to-all-done.in_ref = f32[8,12,64,128]{3,2,1,0:T(8,128)} async-done(((f32[8,12,64,128]{3,2,1,0:T(8,128)}), f32[8,12,64,128]{3,2,1,0:T(8,128)}, u32[]{:S(2)}, u32[]{:S(2)}) %all-to-all-start) | async-done | bytes 3145760 | tf_op jit(solution)/shard_map/all_to_all | solution.py:339
  44.1 0.0 copy-done.11
  44.1 1.1 copy-done.5
  45.2 1.2 %copy-done.12 = f32[4,256,256]{2,1,0:T(8,128)S(1)} copy-done((f32[4,256,256]{2,1,0:T(8,128)S(1)}, f32[4,256,256]{2,1,0:T(8,128)}, u32[]{:S(2)}) %copy-start.12) | copy-done | bytes 1048600
  46.5 7.1 %solve.1 = f32[8,12,64,128]{3,2,1,0:T(8,128)S(1)} custom-call(f32[32]{0:T(128)S(1)} %copy-done.11, s32[1]{0:T(128)} %bitcast.first_ref, f32[4,256,256]{2,1,0:T(8,128)S(1)} %copy-done.12, f32[2,3,4,64,128]{4,3,2,1,0:T(8,128)S(1)} %copy-done.5, f32[8,12,64,128]{3,2,1,0:T(8,128)} %all-to-all-done.in_ref), custom_call_target="tpu_custom_call" | custom-call | flops 4831838208 | bytes 6291456 | tf_op jit(solution)/shard_map/solve/pallas_call | solution.py:308
  53.6 0.0 copy-start.1
  53.6 1.7 %copy-done.1 = f32[8,12,64,128]{3,2,1,0:T(8,128)} copy-done((f32[8,12,64,128]{3,2,1,0:T(8,128)}, f32[8,12,64,128]{3,2,1,0:T(8,128)S(1)}, u32[]{:S(2)}) %copy-start.1) | copy-done | bytes 3145752
  55.2 4.6 %all-to-all-start.1 = ((f32[8,12,64,128]{3,2,1,0:T(8,128)}), f32[8,12,64,128]{3,2,1,0:T(8,128)}, u32[]{:S(2)}, u32[]{:S(2)}) async-start(f32[8,12,64,128]{3,2,1,0:T(8,128)} %copy-done.1), calls=%async_computation.1 | async-start | bytes 6291456 | tf_op jit(solution)/shard_map/all_to_all | solution.py:344
  59.8 1.3 %collective-permute-start.1 = (f32[2,3,4,64,128]{4,3,2,1,0:T(8,128)}, f32[2,3,4,64,128]{4,3,2,1,0:T(8,128)S(1)}, u32[]{:S(2)}, u32[]{:S(2)}) collective-permute-start(f32[2,3,4,64,128]{4,3,2,1,0:T(8,128)} %copy-done.4), channel_id=1, source_target_pairs={{1,0},{2,1},{3,2},{5,4},{6,5},{7,6},{9,8},{10,9},{11,10},{13,12},{... | collective-permute-start | bytes 2359304 | tf_op jit(solution)/shard_map/ppermute | solution.py:330
  61.1 4.8 %collective-permute-start = (f32[2,3,4,64,128]{4,3,2,1,0:T(8,128)}, f32[2,3,4,64,128]{4,3,2,1,0:T(8,128)S(1)}, u32[]{:S(2)}, u32[]{:S(2)}) collective-permute-start(f32[2,3,4,64,128]{4,3,2,1,0:T(8,128)} %copy-done.3), channel_id=1, source_target_pairs={{0,1},{1,2},{2,3},{4,5},{5,6},{6,7},{8,9},{9,10},{10,11},{12,13},{... | collective-permute-start | bytes 2359304 | tf_op jit(solution)/shard_map/ppermute | solution.py:329
  65.9 16.3 %collective-permute-done.1.high_ref = f32[2,3,4,64,128]{4,3,2,1,0:T(8,128)S(1)} collective-permute-done((f32[2,3,4,64,128]{4,3,2,1,0:T(8,128)}, f32[2,3,4,64,128]{4,3,2,1,0:T(8,128)S(1)}, u32[]{:S(2)}, u32[]{:S(2)}) %collective-permute-start.1) | collective-permute-done | bytes 786464 | tf_op jit(solution)/shard_map/ppermute | solution.py:330
  82.2 1.3 %collective-permute-done.low_ref = f32[2,3,4,64,128]{4,3,2,1,0:T(8,128)S(1)} collective-permute-done((f32[2,3,4,64,128]{4,3,2,1,0:T(8,128)}, f32[2,3,4,64,128]{4,3,2,1,0:T(8,128)S(1)}, u32[]{:S(2)}, u32[]{:S(2)}) %collective-permute-start) | collective-permute-done | bytes 786464 | tf_op jit(solution)/shard_map/ppermute | solution.py:329
  83.5 0.0 copy-done.7
  83.5 0.0 copy-done.9
  83.5 1.9 %copy-done.14 = f32[3,32,64,128]{3,2,1,0:T(8,128)S(1)} copy-done((f32[3,32,64,128]{3,2,1,0:T(8,128)S(1)}, f32[3,32,64,128]{3,2,1,0:T(8,128)}, u32[]{:S(2)}) %copy-start.14) | copy-done | bytes 3145752
  85.4 23.0 %move.1 = (f32[3,1,1,4096]{3,2,1,0:T(1,128)}, f32[3,32,64,128]{3,2,1,0:T(8,128)S(1)}) custom-call(f32[9,32]{1,0:T(8,128)S(1)} %copy-done.10, f32[32,32]{1,0:T(8,128)S(1)} %copy-done.9, f32[2,3,4,64,128]{4,3,2,1,0:T(8,128)S(1)} %collective-permute-done.low_ref, f32[3,32,64,128]{3,2,1,0:T(8,128)S(1)} %copy-done, f32[3,32,64,128]{3,2,1,0:T(8,128)S(1)} %copy-done.14, ...), custom_call_target="tpu_custom_call" | custom-call | flops 15032385536 | bytes 10485760 | tf_op jit(solution)/shard_map/move/pallas_call | solution.py:221
  108.4 1.7 %copy-done.2 = f32[3,32,64,128]{3,2,1,0:T(8,128)} copy-done((f32[3,32,64,128]{3,2,1,0:T(8,128)}, f32[3,32,64,128]{3,2,1,0:T(8,128)S(1)}, u32[]{:S(2)}) %copy-start.2) | copy-done | bytes 3145752
  110.1 0.0 all-to-all-done.1
  110.1 5.5 %add.3 = f32[3,32,64,128]{3,2,1,0:T(8,128)} add(f32[3,32,64,128]{3,2,1,0:T(8,128)} %bitcast.2, f32[3,32,64,128]{3,2,1,0:T(8,128)} %copy-done.2) | non-fusion elementwise | flops 786432 | bytes 9437184 | tf_op jit(solution)/shard_map/add | solution.py:348
  (10 shorter events, 0.0 us)
Async XLA Ops:
  0.6 5.5 %copy-start = (f32[3,32,64,128]{3,2,1,0:T(8,128)S(1)}, f32[3,32,64,128]{3,2,1,0:T(8,128)}, u32[]{:S(2)}) copy-start(f32[3,32,64,128]{3,2,1,0:T(8,128)} %velocity_ref.1) | copy-start | bytes 9437188
  0.6 5.5 %copy-start.6 = (f32[3,1,1,4096]{3,2,1,0:T(1,128)S(1)}, f32[3,1,1,4096]{3,2,1,0:T(1,128)}, u32[]{:S(2)}) copy-start(f32[3,1,1,4096]{3,2,1,0:T(1,128)} %spring_ref.3) | copy-start | bytes 147460
  0.6 5.5 %copy-start.8 = (s32[2,1,1,4096]{3,2,1,0:T(1,128)S(1)}, s32[2,1,1,4096]{3,2,1,0:T(1,128)}, u32[]{:S(2)}) copy-start(s32[2,1,1,4096]{3,2,1,0:T(1,128)} %ids_ref.3) | copy-start | bytes 98308
  0.7 43.4 %all-to-all-start = ((f32[8,12,64,128]{3,2,1,0:T(8,128)}), f32[8,12,64,128]{3,2,1,0:T(8,128)}, u32[]{:S(2)}, u32[]{:S(2)}) async-start(f32[8,12,64,128]{3,2,1,0:T(8,128)} %bitcast.3), calls=%async_computation | async-start | bytes 6291456 | tf_op jit(solution)/shard_map/all_to_all | solution.py:339
  6.1 38.0 %copy-start.11 = (f32[32]{0:T(128)S(1)}, f32[32]{0:T(128)}, u32[]{:S(2)}) copy-start(f32[32]{0:T(128)} %coef_ref.1) | copy-start | bytes 388
  21.7 0.9 copy-start.3
  22.6 0.9 copy-start.4
  23.5 1.7 %copy-start.13 = (f32[3,32,64,128]{3,2,1,0:T(8,128)}, f32[3,32,64,128]{3,2,1,0:T(8,128)S(1)}, u32[]{:S(2)}) copy-start(f32[3,32,64,128]{3,2,1,0:T(8,128)S(1)} %get-tuple-element.9.stress_ref) | copy-start | bytes 9437188
  44.1 1.1 copy-start.5
  45.2 1.2 %copy-start.12 = (f32[4,256,256]{2,1,0:T(8,128)S(1)}, f32[4,256,256]{2,1,0:T(8,128)}, u32[]{:S(2)}) copy-start(f32[4,256,256]{2,1,0:T(8,128)} %constant.10.clone.float_ref) | copy-start | bytes 3145732
  53.6 1.7 %copy-start.1 = (f32[8,12,64,128]{3,2,1,0:T(8,128)}, f32[8,12,64,128]{3,2,1,0:T(8,128)S(1)}, u32[]{:S(2)}) copy-start(f32[8,12,64,128]{3,2,1,0:T(8,128)S(1)} %solve.1) | copy-start | bytes 9437188
  55.2 28.3 %copy-start.7 = (f32[3,1,1,4096]{3,2,1,0:T(1,128)S(1)}, f32[3,1,1,4096]{3,2,1,0:T(1,128)}, u32[]{:S(2)}) copy-start(f32[3,1,1,4096]{3,2,1,0:T(1,128)} %noise_ref.1) | copy-start | bytes 147460
  55.2 28.3 %copy-start.9 = (f32[32,32]{1,0:T(8,128)S(1)}, f32[32,32]{1,0:T(8,128)}, u32[]{:S(2)}) copy-start(f32[32,32]{1,0:T(8,128)} %inverse_ref.1) | copy-start | bytes 12292
  55.2 28.3 %copy-start.10 = (f32[9,32]{1,0:T(8,128)S(1)}, f32[9,32]{1,0:T(8,128)}, u32[]{:S(2)}) copy-start(f32[9,32]{1,0:T(8,128)} %stencil_ref.1) | copy-start | bytes 3460
  55.2 54.8 %all-to-all-start.1 = ((f32[8,12,64,128]{3,2,1,0:T(8,128)}), f32[8,12,64,128]{3,2,1,0:T(8,128)}, u32[]{:S(2)}, u32[]{:S(2)}) async-start(f32[8,12,64,128]{3,2,1,0:T(8,128)} %copy-done.1), calls=%async_computation.1 | async-start | bytes 6291456 | tf_op jit(solution)/shard_map/all_to_all | solution.py:344
  59.8 22.4 %collective-permute-start.1 = (f32[2,3,4,64,128]{4,3,2,1,0:T(8,128)}, f32[2,3,4,64,128]{4,3,2,1,0:T(8,128)S(1)}, u32[]{:S(2)}, u32[]{:S(2)}) collective-permute-start(f32[2,3,4,64,128]{4,3,2,1,0:T(8,128)} %copy-done.4), channel_id=1, source_target_pairs={{1,0},{2,1},{3,2},{5,4},{6,5},{7,6},{9,8},{10,9},{11,10},{13,12},{... | collective-permute-start | bytes 2359304 | tf_op jit(solution)/shard_map/ppermute | solution.py:330
  61.1 22.4 %collective-permute-start = (f32[2,3,4,64,128]{4,3,2,1,0:T(8,128)}, f32[2,3,4,64,128]{4,3,2,1,0:T(8,128)S(1)}, u32[]{:S(2)}, u32[]{:S(2)}) collective-permute-start(f32[2,3,4,64,128]{4,3,2,1,0:T(8,128)} %copy-done.3), channel_id=1, source_target_pairs={{0,1},{1,2},{2,3},{4,5},{5,6},{6,7},{8,9},{9,10},{10,11},{12,13},{... | collective-permute-start | bytes 2359304 | tf_op jit(solution)/shard_map/ppermute | solution.py:329
  83.5 1.9 %copy-start.14 = (f32[3,32,64,128]{3,2,1,0:T(8,128)S(1)}, f32[3,32,64,128]{3,2,1,0:T(8,128)}, u32[]{:S(2)}) copy-start(f32[3,32,64,128]{3,2,1,0:T(8,128)} %copy-done.13) | copy-start | bytes 9437188
  108.4 1.7 %copy-start.2 = (f32[3,32,64,128]{3,2,1,0:T(8,128)}, f32[3,32,64,128]{3,2,1,0:T(8,128)S(1)}, u32[]{:S(2)}) copy-start(f32[3,32,64,128]{3,2,1,0:T(8,128)S(1)} %get-tuple-element.10) | copy-start | bytes 9437188

commit v5 on v4

--- a/solution.py
+++ b/solution.py
@@ -33,6 +33,14 @@
     rows = stacked.shape[0] // 2
     both = dot(stacked, b_high)
     return both[:rows] + both[rows:] + dot(stacked[:rows], b_low)
+
+def in_hbm(value):
+    return pltpu.with_memory_space_constraint(value, pltpu.HBM)
+
+
+def in_vmem(value):
+    return pltpu.with_memory_space_constraint(value, pltpu.VMEM)
+
 
 def iota(shape, dim):
     return lax.broadcasted_iota(jnp.int32, shape, dim)
@@ -104,9 +112,9 @@
             pl.BlockSpec(edge, lambda i: (0, 0, 0, 0, 0)),
         ],
         out_shape=[
-            jax.ShapeDtypeStruct(velocity.shape, F32),
-            jax.ShapeDtypeStruct(edge, F32),
-            jax.ShapeDtypeStruct(edge, F32),
+            pltpu.HBM(velocity.shape, F32),
+            pltpu.HBM(edge, F32),
+            pltpu.HBM(edge, F32),
         ],
         scratch_shapes=[pltpu.VMEM((6 * axial, count), BF16)],
         compiler_params=pltpu.CompilerParams(vmem_limit_bytes=24 * MIB),
@@ -116,7 +124,7 @@
             transcendentals=0,
         ),
         name="deposit",
-    )(ids, spring, velocity, velocity)
+    )(ids, spring, in_hbm(velocity), in_hbm(velocity))
 
 
 def derivative_matrix(stencil_ref, inverse_ref):
@@ -224,7 +232,7 @@
         out_specs=[whole, whole],
         out_shape=[
             jax.ShapeDtypeStruct(spring.shape, F32),
-            jax.ShapeDtypeStruct(velocity.shape, F32),
+            pltpu.VMEM(velocity.shape, F32),
         ],
         scratch_shapes=[
             pltpu.VMEM((6 * axial, radii * angles), BF16),
@@ -237,7 +245,17 @@
             transcendentals=0,
         ),
         name="move",
-    )(stencil, inverse, low, velocity, stress, high, ids, spring, noise)
+    )(
+        stencil,
+        inverse,
+        in_vmem(low),
+        in_hbm(velocity),
+        in_hbm(stress),
+        in_vmem(high),
+        ids,
+        spring,
+        noise,
+    )
 
 
 def fourier_tables(all_angles):
@@ -260,7 +278,7 @@
     return np.stack(tables)
 
 
-def solve_kernel(coef_ref, first_ref, float_ref, after_ref, in_ref, out_ref, table_ref):
+def solve_kernel(coef_ref, first_ref, float_ref, low_ref, high_ref, in_ref, out_ref, table_ref):
     blocks, rows, angles, axial = in_ref.shape
     half = blocks * angles // 2
     quarter = half // 2
@@ -296,7 +314,7 @@
         out_ref[blocks // 2 :, q] = (even - odd).reshape(blocks // 2, angles, axial)
 
 
-def solve(coef, first, field, after):
+def solve(coef, first, field, low, high):
     blocks, rows, angles, axial = field.shape
     all_angles = blocks * angles
     tables = fourier_tables(all_angles)
@@ -305,12 +323,13 @@
     field_spec = pl.BlockSpec((blocks, part, angles, axial), lambda i: (0, i, 0, 0))
     smem = pl.BlockSpec(memory_space=pltpu.SMEM)
     whole = pl.BlockSpec(memory_space=pltpu.VMEM)
+    unread = pl.BlockSpec(memory_space=pl.ANY)
     return pl.pallas_call(
         solve_kernel,
         grid=(rows // part,),
-        in_specs=[smem, smem, whole, pl.BlockSpec(memory_space=pl.ANY), field_spec],
+        in_specs=[smem, smem, whole, unread, unread, field_spec],
         out_specs=field_spec,
-        out_shape=jax.ShapeDtypeStruct(field.shape, F32),
+        out_shape=pltpu.HBM(field.shape, F32),
         scratch_shapes=[pltpu.VMEM((4, 2 * half, half), BF16)],
         compiler_params=pltpu.CompilerParams(vmem_limit_bytes=14 * MIB),
         cost_estimate=pl.CostEstimate(
@@ -319,7 +338,39 @@
             transcendentals=0,
         ),
         name="solve",
-    )(coef, first, jnp.asarray(tables), after, field)
+    )(coef, first, in_hbm(jnp.asarray(tables)), in_vmem(low), in_vmem(high), in_vmem(field))
+
+
+def join_kernel(force_ref, smooth_ref, out_ref, sum_ref, sems):
+    parts = sems.shape[0]
+    part = force_ref.shape[0] // parts
+    copies = []
+    for i in range(parts):
+        at = pl.ds(i * part, part)
+        sum_ref[at] = force_ref[at] + smooth_ref[at]
+        copies.append(pltpu.make_async_copy(sum_ref.at[at], out_ref.at[at], sems.at[i]))
+        copies[-1].start()
+    for copy in copies:
+        copy.wait()
+
+
+def join(force, smooth):
+    whole = pl.BlockSpec(memory_space=pltpu.VMEM)
+    return pl.pallas_call(
+        join_kernel,
+        in_specs=[whole, whole],
+        out_specs=pl.BlockSpec(memory_space=pl.ANY),
+        out_shape=pltpu.HBM(force.shape, F32),
+        scratch_shapes=[
+            pltpu.VMEM(force.shape, F32),
+            pltpu.SemaphoreType.DMA((math.gcd(force.shape[0], 8),)),
+        ],
+        compiler_params=pltpu.CompilerParams(vmem_limit_bytes=14 * MIB),
+        cost_estimate=pl.CostEstimate(
+            flops=force.size, bytes_accessed=12 * force.size, transcendentals=0
+        ),
+        name="join",
+    )(in_vmem(force), in_vmem(smooth))
 
 
 def from_neighbours(low_edge, high_edge):
@@ -340,12 +391,14 @@
     stress, low_edge, high_edge = deposit(cell_ids, dumbbells, velocity)
     low, high = from_neighbours(low_edge, high_edge)
     first = (lax.axis_index("az") * rows).astype(jnp.int32).reshape(1)
-    solved = solve(azim_coef, first, gathered, low_edge)
-    smooth = lax.all_to_all(solved, "az", 0, 0, tiled=True).reshape(velocity.shape)
+    solved = solve(azim_coef, first, gathered, low, high)
+    smooth = lax.all_to_all(solved, "az", 0, 0, tiled=True)
     moved, force = move(
         stencil_coef, block_inverse, low, velocity, stress, high, cell_ids, dumbbells, brownian
     )
-    return smooth + force, moved
+    lines = (3 * radii, angles, axial)
+    result = join(force.reshape(lines), smooth.reshape(lines))
+    return result.reshape(velocity.shape), moved
 
 
 def solution(mesh):

time: 116 us -> 104 us (0.90)
  Pallas kernels: 45.6 us -> 53.8 us
  local copies, waits for them, and re-layouts: 11.1 us -> 3.58 us
  waiting for transfers between devices: 36.5 us -> 30.5 us
  other arithmetic: 5.47 us -> 0 us
    all_to_all x1, waiting for transfers between devices: 18.9 us -> 0.01 us  [per_device(): gathered = lax.all_to_all(pieces, 'az', 0, 0, tiled=True)]
    ppermute x1, waiting for transfers between devices: 1.29 us -> 15.6 us  [from_neighbours(): low = lax.ppermute(high_edge, 'rad', forward)]
    ppermute x1, waiting for transfers between devices: 16.3 us -> 5.01 us  [from_neighbours(): high = lax.ppermute(low_edge, 'rad', backward)]
    all_to_all x1, waiting for transfers between devices: 0.01 us -> 9.95 us  [per_device(): smooth = lax.all_to_all(solved, 'az', 0, 0, tiled=True)]
    unnamed x30 -> x16, local copies, waits for them, and re-layouts: 11.1 us -> 3.58 us
    add x1 -> x0, other arithmetic: 5.47 us -> none  [per_device(): return (smooth + force, moved)]
    pallas_call x1, Pallas kernels: 23 us -> 26.2 us  [move(): pl.pallas_call(move_kernel, in_specs=[whole] * 9, out_specs=[whole, whole...]
    pallas_call x1, Pallas kernels: 15.6 us -> 17.9 us  [deposit(): pl.pallas_call(deposit_kernel, grid=(radii // part,), in_specs=[whole, wh...]
  transfers between devices with their start and end apart: 4 -> 4, of which waited for: 3 -> 3; matrix products, arithmetic and copies ran while one was open for 0% -> 0% of each run, Pallas kernels for 33% -> 43%
where the time goes in v5:
time: 104 us
  Pallas kernels  53.8 us (52%)
  waiting for transfers between devices  30.5 us (29%)
  starting transfers between devices  15 us (14%)
  local copies, waits for them, and re-layouts  3.58 us (3%)
    pallas_call x1, Pallas kernels, move(): pl.pallas_call(move_kernel, in_specs=[whole] * 9, out_specs=[whole, whole...  26.2 us
    pallas_call x1, Pallas kernels, deposit(): pl.pallas_call(deposit_kernel, grid=(radii // part,), in_specs=[whole, wh...  17.9 us
    ppermute x1, waiting for transfers between devices, from_neighbours(): low = lax.ppermute(high_edge, 'rad', forward)  15.6 us
    all_to_all x1, waiting for transfers between devices, per_device(): smooth = lax.all_to_all(solved, 'az', 0, 0, tiled=True)  9.95 us
    pallas_call x1, Pallas kernels, solve(): pl.pallas_call(solve_kernel, grid=(rows // part,), in_specs=[smem, smem,...  7.87 us
    all_to_all x1, starting transfers between devices, per_device(): gathered = lax.all_to_all(pieces, 'az', 0, 0, tiled=True)  5.31 us
    ppermute x1, waiting for transfers between devices, from_neighbours(): high = lax.ppermute(low_edge, 'rad', backward)  5.01 us
    ppermute x1, starting transfers between devices, from_neighbours(): low = lax.ppermute(high_edge, 'rad', forward)  4.38 us
  transfers between devices with their start and end apart: 4, of which 3 were waited for; matrix products, arithmetic and copies ran while one was open for 0% of the time, Pallas kernels for 43%

profile of v5, /device:TPU:0, one launch (start us, length us, event | category | flops | bytes accessed | tf_op | source)
XLA Modules:
  0.0 103.6 jit_solution(4023632548802551552)
XLA Ops:
  0.6 0.0 copy-start.2
  0.6 0.0 copy-start.4
  0.6 5.3 %all-to-all-start = ((f32[8,12,64,128]{3,2,1,0:T(8,128)}), f32[8,12,64,128]{3,2,1,0:T(8,128)S(1)}, u32[]{:S(2)}, u32[]{:S(2)}) async-start(f32[8,12,64,128]{3,2,1,0:T(8,128)} %bitcast.7), calls=%async_computation | async-start | bytes 6291456 | tf_op jit(solution)/shard_map/all_to_all | solution.py:390
  6.0 0.0 copy-done.2
  6.0 0.0 copy-done.4
  6.0 0.0 copy-start.7
  6.0 17.9 %deposit.1 = (f32[3,32,64,128]{3,2,1,0:T(8,128)}, f32[2,3,4,64,128]{4,3,2,1,0:T(8,128)}, f32[2,3,4,64,128]{4,3,2,1,0:T(8,128)}) custom-call(s32[2,1,1,4096]{3,2,1,0:T(1,128)S(1)} %copy-done.4, f32[3,1,1,4096]{3,2,1,0:T(1,128)S(1)} %copy-done.2, f32[3,32,64,128]{3,2,1,0:T(8,128)} %velocity_ref.1, f32[3,32,64,128]{3,2,1,0:T(8,128)} %velocity_ref.1), custom_call_target="tpu_custom_call" | custom-call | flops 12884901888 | bytes 3145728 | tf_op jit(solution)/shard_map/deposit/pallas_call | solution.py:100
  23.9 4.4 %collective-permute-start = (f32[2,3,4,64,128]{4,3,2,1,0:T(8,128)}, f32[2,3,4,64,128]{4,3,2,1,0:T(8,128)}, u32[]{:S(2)}, u32[]{:S(2)}) collective-permute-start(f32[2,3,4,64,128]{4,3,2,1,0:T(8,128)} %get-tuple-element.7), channel_id=1, source_target_pairs={{0,1},{1,2},{2,3},{4,5},{5,6},{6,7},{8,9},{9,10},{10,11},{12,13},{... | collective-permute-start | bytes 2359304 | tf_op jit(solution)/shard_map/ppermute | solution.py:380
  28.3 1.3 %collective-permute-start.1 = (f32[2,3,4,64,128]{4,3,2,1,0:T(8,128)}, f32[2,3,4,64,128]{4,3,2,1,0:T(8,128)}, u32[]{:S(2)}, u32[]{:S(2)}) collective-permute-start(f32[2,3,4,64,128]{4,3,2,1,0:T(8,128)} %get-tuple-element.9), channel_id=1, source_target_pairs={{1,0},{2,1},{3,2},{5,4},{6,5},{7,6},{9,8},{10,9},{11,10},{13,12},{... | collective-permute-start | bytes 2359304 | tf_op jit(solution)/shard_map/ppermute | solution.py:381
  29.6 15.6 %collective-permute-done.low_ref = f32[2,3,4,64,128]{4,3,2,1,0:T(8,128)} collective-permute-done((f32[2,3,4,64,128]{4,3,2,1,0:T(8,128)}, f32[2,3,4,64,128]{4,3,2,1,0:T(8,128)}, u32[]{:S(2)}, u32[]{:S(2)}) %collective-permute-start) | collective-permute-done | bytes 786464 | tf_op jit(solution)/shard_map/ppermute | solution.py:380
  45.1 5.0 %collective-permute-done.1.high_ref = f32[2,3,4,64,128]{4,3,2,1,0:T(8,128)} collective-permute-done((f32[2,3,4,64,128]{4,3,2,1,0:T(8,128)}, f32[2,3,4,64,128]{4,3,2,1,0:T(8,128)}, u32[]{:S(2)}, u32[]{:S(2)}) %collective-permute-start.1) | collective-permute-done | bytes 786464 | tf_op jit(solution)/shard_map/ppermute | solution.py:381
  50.2 0.0 all-to-all-done.in_ref
  50.2 0.0 copy-done.7
  50.2 7.9 %solve.1 = f32[8,12,64,128]{3,2,1,0:T(8,128)} custom-call(f32[32]{0:T(128)S(1)} %copy-done.7, s32[1]{0:T(128)} %bitcast.1.first_ref, f32[4,256,256]{2,1,0:T(8,128)} %constant.10.clone.float_ref, f32[2,3,4,64,128]{4,3,2,1,0:T(8,128)} %collective-permute-done.low_ref, f32[2,3,4,64,128]{4,3,2,1,0:T(8,128)} %collective-permute-done.1.high_ref, ...), custom_call_target="tpu_custom_call" | custom-call | flops 4831838208 | bytes 6291456 | tf_op jit(solution)/shard_map/solve/pallas_call | solution.py:327
  58.0 0.0 copy-start.3
  58.0 0.0 copy-start.5
  58.0 0.0 copy-start.6
  58.0 4.0 %all-to-all-start.1 = ((f32[8,12,64,128]{3,2,1,0:T(8,128)}), f32[8,12,64,128]{3,2,1,0:T(8,128)S(1)}, u32[]{:S(2)}, u32[]{:S(2)}) async-start(f32[8,12,64,128]{3,2,1,0:T(8,128)} %solve.1), calls=%async_computation.1 | async-start | bytes 6291456 | tf_op jit(solution)/shard_map/all_to_all | solution.py:395
  62.0 0.0 copy-done.3
  62.0 0.0 copy-done.5
  62.0 0.0 copy-done.6
  62.0 26.2 %move.1 = (f32[3,1,1,4096]{3,2,1,0:T(1,128)}, f32[3,32,64,128]{3,2,1,0:T(8,128)S(1)}) custom-call(f32[9,32]{1,0:T(8,128)S(1)} %copy-done.6, f32[32,32]{1,0:T(8,128)S(1)} %copy-done.5, f32[2,3,4,64,128]{4,3,2,1,0:T(8,128)} %collective-permute-done.low_ref, f32[3,32,64,128]{3,2,1,0:T(8,128)} %velocity_ref.1, f32[3,32,64,128]{3,2,1,0:T(8,128)} %get-tuple-element.8.stress_ref, ...), custom_call_target="tpu_custom_call" | custom-call | flops 15032385536 | bytes 10485760 | tf_op jit(solution)/shard_map/move/pallas_call | solution.py:229
  88.3 0.0 copy-start
  88.3 1.7 %copy-done = f32[3,32,64,128]{3,2,1,0:T(8,128)} copy-done((f32[3,32,64,128]{3,2,1,0:T(8,128)}, f32[3,32,64,128]{3,2,1,0:T(8,128)S(1)}, u32[]{:S(2)}) %copy-start) | copy-done | bytes 3145752
  89.9 10.0 %all-to-all-done.1 = f32[8,12,64,128]{3,2,1,0:T(8,128)S(1)} async-done(((f32[8,12,64,128]{3,2,1,0:T(8,128)}), f32[8,12,64,128]{3,2,1,0:T(8,128)S(1)}, u32[]{:S(2)}, u32[]{:S(2)}) %all-to-all-start.1) | async-done | bytes 3145760 | tf_op jit(solution)/shard_map/all_to_all | solution.py:395
  99.9 0.0 copy-start.1
  99.9 1.9 %copy-done.1 = f32[3,32,64,128]{3,2,1,0:T(8,128)S(1)} copy-done((f32[3,32,64,128]{3,2,1,0:T(8,128)S(1)}, f32[3,32,64,128]{3,2,1,0:T(8,128)}, u32[]{:S(2)}) %copy-start.1) | copy-done | bytes 3145752
  101.8 1.8 %join.1 = f32[96,64,128]{2,1,0:T(8,128)} custom-call(f32[96,64,128]{2,1,0:T(8,128)S(1)} %bitcast.6, f32[96,64,128]{2,1,0:T(8,128)S(1)} %bitcast.5), custom_call_target="tpu_custom_call" | custom-call | flops 786432 | bytes 9437184 | tf_op jit(solution)/shard_map/join/pallas_call | solution.py:359
Async XLA Ops:
  0.6 5.3 %copy-start.2 = (f32[3,1,1,4096]{3,2,1,0:T(1,128)S(1)}, f32[3,1,1,4096]{3,2,1,0:T(1,128)}, u32[]{:S(2)}) copy-start(f32[3,1,1,4096]{3,2,1,0:T(1,128)} %spring_ref.3) | copy-start | bytes 147460
  0.6 5.3 %copy-start.4 = (s32[2,1,1,4096]{3,2,1,0:T(1,128)S(1)}, s32[2,1,1,4096]{3,2,1,0:T(1,128)}, u32[]{:S(2)}) copy-start(s32[2,1,1,4096]{3,2,1,0:T(1,128)} %ids_ref.3) | copy-start | bytes 98308
  0.6 49.5 %all-to-all-start = ((f32[8,12,64,128]{3,2,1,0:T(8,128)}), f32[8,12,64,128]{3,2,1,0:T(8,128)S(1)}, u32[]{:S(2)}, u32[]{:S(2)}) async-start(f32[8,12,64,128]{3,2,1,0:T(8,128)} %bitcast.7), calls=%async_computation | async-start | bytes 6291456 | tf_op jit(solution)/shard_map/all_to_all | solution.py:390
  6.0 44.2 %copy-start.7 = (f32[32]{0:T(128)S(1)}, f32[32]{0:T(128)}, u32[]{:S(2)}) copy-start(f32[32]{0:T(128)} %coef_ref.1) | copy-start | bytes 388
  23.9 21.2 %collective-permute-start = (f32[2,3,4,64,128]{4,3,2,1,0:T(8,128)}, f32[2,3,4,64,128]{4,3,2,1,0:T(8,128)}, u32[]{:S(2)}, u32[]{:S(2)}) collective-permute-start(f32[2,3,4,64,128]{4,3,2,1,0:T(8,128)} %get-tuple-element.7), channel_id=1, source_target_pairs={{0,1},{1,2},{2,3},{4,5},{5,6},{6,7},{8,9},{9,10},{10,11},{12,13},{... | collective-permute-start | bytes 2359304 | tf_op jit(solution)/shard_map/ppermute | solution.py:380
  28.3 21.9 %collective-permute-start.1 = (f32[2,3,4,64,128]{4,3,2,1,0:T(8,128)}, f32[2,3,4,64,128]{4,3,2,1,0:T(8,128)}, u32[]{:S(2)}, u32[]{:S(2)}) collective-permute-start(f32[2,3,4,64,128]{4,3,2,1,0:T(8,128)} %get-tuple-element.9), channel_id=1, source_target_pairs={{1,0},{2,1},{3,2},{5,4},{6,5},{7,6},{9,8},{10,9},{11,10},{13,12},{... | collective-permute-start | bytes 2359304 | tf_op jit(solution)/shard_map/ppermute | solution.py:381
  58.0 4.0 %copy-start.3 = (f32[3,1,1,4096]{3,2,1,0:T(1,128)S(1)}, f32[3,1,1,4096]{3,2,1,0:T(1,128)}, u32[]{:S(2)}) copy-start(f32[3,1,1,4096]{3,2,1,0:T(1,128)} %noise_ref.1) | copy-start | bytes 147460
  58.0 4.0 %copy-start.5 = (f32[32,32]{1,0:T(8,128)S(1)}, f32[32,32]{1,0:T(8,128)}, u32[]{:S(2)}) copy-start(f32[32,32]{1,0:T(8,128)} %inverse_ref.1) | copy-start | bytes 12292
  58.0 4.0 %copy-start.6 = (f32[9,32]{1,0:T(8,128)S(1)}, f32[9,32]{1,0:T(8,128)}, u32[]{:S(2)}) copy-start(f32[9,32]{1,0:T(8,128)} %stencil_ref.1) | copy-start | bytes 3460
  58.0 41.9 %all-to-all-start.1 = ((f32[8,12,64,128]{3,2,1,0:T(8,128)}), f32[8,12,64,128]{3,2,1,0:T(8,128)S(1)}, u32[]{:S(2)}, u32[]{:S(2)}) async-start(f32[8,12,64,128]{3,2,1,0:T(8,128)} %solve.1), calls=%async_computation.1 | async-start | bytes 6291456 | tf_op jit(solution)/shard_map/all_to_all | solution.py:395
  88.3 1.7 %copy-start = (f32[3,32,64,128]{3,2,1,0:T(8,128)}, f32[3,32,64,128]{3,2,1,0:T(8,128)S(1)}, u32[]{:S(2)}) copy-start(f32[3,32,64,128]{3,2,1,0:T(8,128)S(1)} %get-tuple-element.10) | copy-start | bytes 9437188
  99.9 1.9 %copy-start.1 = (f32[3,32,64,128]{3,2,1,0:T(8,128)S(1)}, f32[3,32,64,128]{3,2,1,0:T(8,128)}, u32[]{:S(2)}) copy-start(f32[3,32,64,128]{3,2,1,0:T(8,128)} %copy-done) | copy-start | bytes 9437188

commit v6 on v5

--- a/solution.py
+++ b/solution.py
@@ -1,3 +1,4 @@
+import functools
 import functools
 import math
 
@@ -46,85 +47,111 @@
     return lax.broadcasted_iota(jnp.int32, shape, dim)
 
 
-def deposit_kernel(
-    ids_ref, spring_ref, first_ref, last_ref, stress_ref, low_ref, high_ref, weight_ref
-):
+def weigh(ids_ref, spring_ref, weight_ref):
+    axial = weight_ref.shape[0] // 6
+    count = weight_ref.shape[1]
+    q = [spring_ref[c, 0] for c in range(3)]
+    stretch_sq = q[0] * q[0] + q[1] * q[1] + q[2] * q[2]
+    factor = 1.0 / (1.0 - stretch_sq / MAX_STRETCH)
+    here = iota((axial, count), 0) == ids_ref[1, 0]
+    for c in range(3):
+        weight = STRESS_SCALE * factor * q[0] * q[c]
+        high = weight.astype(BF16).astype(F32)
+        weight_ref[c * axial : (c + 1) * axial, :] = jnp.where(here, high, 0.0).astype(BF16)
+        weight_ref[(3 + c) * axial : (4 + c) * axial, :] = jnp.where(
+            here, weight - high, 0.0
+        ).astype(BF16)
+
+
+def gather_rows(ids_ref, weight_ref, first_row, rows):
+    axial = weight_ref.shape[0] // 6
+    count = weight_ref.shape[1]
+    hot = jnp.where(iota((rows, count), 0) + first_row == ids_ref[0, 0], 1.0, 0.0).astype(BF16)
+    both = lax.dot_general(
+        hot, weight_ref[...], (((1,), (1,)), ((), ())), preferred_element_type=F32
+    )
+    return [
+        both[:, c * axial : (c + 1) * axial] + both[:, (3 + c) * axial : (4 + c) * axial]
+        for c in range(3)
+    ]
+
+
+def edge_kernel(ids_ref, spring_ref, first_ref, last_ref, low_ref, high_ref, weight_ref, *, radii):
+    _, _, _, angles, axial = low_ref.shape
+    weigh(ids_ref, spring_ref, weight_ref)
+    for field_ref, out_ref, radius in (
+        (first_ref, low_ref, 0),
+        (last_ref, high_ref, radii - HALO),
+    ):
+        out_ref[0] = field_ref[...]
+        values = gather_rows(ids_ref, weight_ref, radius * angles, HALO * angles)
+        for c in range(3):
+            out_ref[1, c] = values[c].reshape(HALO, angles, axial)
+
+
+def middle_kernel(ids_ref, spring_ref, stress_ref, weight_ref):
     step = pl.program_id(0)
-    count = spring_ref.shape[3]
-    axial = stress_ref.shape[3]
+    _, radii, angles, axial = stress_ref.shape
 
     @pl.when(step == 0)
     def _():
-        low_ref[0] = first_ref[...]
-        high_ref[0] = last_ref[...]
-        q = [spring_ref[c, 0] for c in range(3)]
-        stretch_sq = q[0] * q[0] + q[1] * q[1] + q[2] * q[2]
-        factor = 1.0 / (1.0 - stretch_sq / MAX_STRETCH)
-        here = iota((axial, count), 0) == ids_ref[1, 0]
-        for c in range(3):
-            weight = STRESS_SCALE * factor * q[0] * q[c]
-            high = weight.astype(BF16).astype(F32)
-            weight_ref[c * axial : (c + 1) * axial, :] = jnp.where(here, high, 0.0).astype(BF16)
-            weight_ref[(3 + c) * axial : (4 + c) * axial, :] = jnp.where(
-                here, weight - high, 0.0
-            ).astype(BF16)
-
-    radii, angles = stress_ref.shape[1], stress_ref.shape[2]
+        weigh(ids_ref, spring_ref, weight_ref)
+
     rows = radii * angles
-    hot = jnp.where(iota((rows, count), 0) + step * rows == ids_ref[0, 0], 1.0, 0.0).astype(BF16)
-    both = lax.dot_general(
-        hot, weight_ref[...], (((1,), (1,)), ((), ())), preferred_element_type=F32
-    )
+    values = gather_rows(ids_ref, weight_ref, HALO * angles + step * rows, rows)
     for c in range(3):
-        total = (
-            both[:, c * axial : (c + 1) * axial] + both[:, (3 + c) * axial : (4 + c) * axial]
-        )
-        stress_ref[c] = total.reshape(radii, angles, axial)
-
-    @pl.when(step == 0)
-    def _():
-        low_ref[1] = stress_ref[:, :HALO]
-
-    @pl.when(step == pl.num_programs(0) - 1)
-    def _():
-        high_ref[1] = stress_ref[:, radii - HALO :]
-
-
-def deposit(ids, spring, velocity):
+        stress_ref[c] = values[c].reshape(radii, angles, axial)
+
+
+def deposit_edges(ids, spring, velocity):
     _, radii, angles, axial = velocity.shape
     count = ids.shape[3]
-    part = max(HALO, min(radii, 512 // angles))
     edge = (2, 3, HALO, angles, axial)
     edge_block = (3, HALO, angles, axial)
     whole = pl.BlockSpec(memory_space=pltpu.VMEM)
     return pl.pallas_call(
-        deposit_kernel,
-        grid=(radii // part,),
+        functools.partial(edge_kernel, radii=radii),
+        grid=(1,),
         in_specs=[
             whole,
             whole,
             pl.BlockSpec(edge_block, lambda i: (0, 0, 0, 0)),
             pl.BlockSpec(edge_block, lambda i: (0, radii // HALO - 1, 0, 0)),
         ],
-        out_specs=[
-            pl.BlockSpec((3, part, angles, axial), lambda i: (0, i, 0, 0)),
-            pl.BlockSpec(edge, lambda i: (0, 0, 0, 0, 0)),
-            pl.BlockSpec(edge, lambda i: (0, 0, 0, 0, 0)),
-        ],
-        out_shape=[
-            pltpu.HBM(velocity.shape, F32),
-            pltpu.HBM(edge, F32),
-            pltpu.HBM(edge, F32),
-        ],
+        out_specs=[pl.BlockSpec(edge, lambda i: (0, 0, 0, 0, 0))] * 2,
+        out_shape=[pltpu.HBM(edge, F32)] * 2,
         scratch_shapes=[pltpu.VMEM((6 * axial, count), BF16)],
-        compiler_params=pltpu.CompilerParams(vmem_limit_bytes=24 * MIB),
+        compiler_params=pltpu.CompilerParams(vmem_limit_bytes=28 * MIB),
         cost_estimate=pl.CostEstimate(
-            flops=12 * radii * angles * count * axial,
-            bytes_accessed=12 * radii * angles * axial,
+            flops=24 * HALO * angles * count * axial,
+            bytes_accessed=96 * HALO * angles * axial,
             transcendentals=0,
         ),
-        name="deposit",
+        name="deposit_edges",
     )(ids, spring, in_hbm(velocity), in_hbm(velocity))
+
+
+def deposit_middle(ids, spring, low_edge, shape):
+    _, radii, angles, axial = shape
+    count = ids.shape[3]
+    inner = radii - 2 * HALO
+    part = math.gcd(inner, max(1, 512 // angles))
+    whole = pl.BlockSpec(memory_space=pltpu.VMEM)
+    return pl.pallas_call(
+        lambda ids_ref, spring_ref, _, *refs: middle_kernel(ids_ref, spring_ref, *refs),
+        grid=(inner // part,),
+        in_specs=[whole, whole, pl.BlockSpec(memory_space=pl.ANY)],
+        out_specs=pl.BlockSpec((3, part, angles, axial), lambda i: (0, i, 0, 0)),
+        out_shape=pltpu.HBM((3, inner, angles, axial), F32),
+        scratch_shapes=[pltpu.VMEM((6 * axial, count), BF16)],
+        compiler_params=pltpu.CompilerParams(vmem_limit_bytes=28 * MIB),
+        cost_estimate=pl.CostEstimate(
+            flops=12 * inner * angles * count * axial,
+            bytes_accessed=12 * inner * angles * axial,
+            transcendentals=0,
+        ),
+        name="deposit_middle",
+    )(ids, spring, in_hbm(low_edge))
 
 
 def derivative_matrix(stencil_ref, inverse_ref):
@@ -157,7 +184,9 @@
     inverse_ref,
     low_ref,
     velocity_ref,
-    stress_ref,
+    low_edge_ref,
+    middle_ref,
+    high_edge_ref,
     high_ref,
     ids_ref,
     spring_ref,
@@ -174,12 +203,14 @@
     def derive(i, carry):
         at = pl.ds(pl.multiple_of(i * SUB, SUB), SUB)
         columns = []
-        for f, own_ref in enumerate((velocity_ref, stress_ref)):
+        own = [
+            [velocity_ref],
+            [low_edge_ref.at[1], middle_ref, high_edge_ref.at[1]],
+        ]
+        for f in range(2):
+            refs = [low_ref.at[f]] + own[f] + [high_ref.at[f]]
             for c in range(3):
-                value = jnp.concatenate(
-                    [low_ref[f, c, :, at, :], own_ref[c, :, at, :], high_ref[f, c, :, at, :]],
-                    axis=0,
-                )
+                value = jnp.concatenate([ref[c, :, at, :] for ref in refs], axis=0)
                 columns.append(value.reshape((radii + 2 * HALO) * SUB, axial))
         field_high, field_low = split(jnp.concatenate(columns, axis=1))
         result = dot3(matrix_ref[...], field_high, field_low)
@@ -224,15 +255,16 @@
 
 
 def move(stencil, inverse, low, velocity, stress, high, ids, spring, noise):
+    low_edge, middle, high_edge = stress
     radii, angles, axial = velocity.shape[1:]
     whole = pl.BlockSpec(memory_space=pltpu.VMEM)
     return pl.pallas_call(
         move_kernel,
-        in_specs=[whole] * 9,
+        in_specs=[whole] * 11,
         out_specs=[whole, whole],
         out_shape=[
             jax.ShapeDtypeStruct(spring.shape, F32),
-            pltpu.VMEM(velocity.shape, F32),
+            pltpu.HBM(velocity.shape, F32),
         ],
         scratch_shapes=[
             pltpu.VMEM((6 * axial, radii * angles), BF16),
@@ -250,7 +282,9 @@
         inverse,
         in_vmem(low),
         in_hbm(velocity),
-        in_hbm(stress),
+        in_hbm(low_edge),
+        in_hbm(middle),
+        in_hbm(high_edge),
         in_vmem(high),
         ids,
         spring,
@@ -274,22 +308,23 @@
         table = np.where(even[:, None], np.cos(angle), np.sin(angle))
         weight = np.where((wave == 0) | (wave == half), 1.0, 2.0) / all_angles
         for value in (table, table.T * weight[None, :]):
-            tables.append(value.astype(np.float32))
+            value = value.astype(np.float32)
+            high = value.astype(BF16)
+            low = (value - high.astype(np.float32)).astype(BF16)
+            tables.append(np.concatenate([high, low, high], axis=1))
     return np.stack(tables)
 
 
-def solve_kernel(coef_ref, first_ref, float_ref, low_ref, high_ref, in_ref, out_ref, table_ref):
+def product(table, value):
+    high, low = split(value)
+    return dot(table, jnp.concatenate([high, high, low], axis=0))
+
+
+def solve_kernel(coef_ref, first_ref, table_ref, *refs):
+    in_ref, out_ref = refs[-2:]
     blocks, rows, angles, axial = in_ref.shape
     half = blocks * angles // 2
     quarter = half // 2
-
-    @pl.when(pl.program_id(0) == 0)
-    def _():
-        for i in range(4):
-            high, low = split(float_ref[i])
-            table_ref[i, :half] = high
-            table_ref[i, half:] = low
-
     row = iota((half, axial), 0)
     waves = [
         jnp.where(row <= quarter, 2 * row, 2 * (row - quarter)),
@@ -304,22 +339,21 @@
         field = jnp.concatenate(
             [a - b if odd else a + b for a, b in zip(near, far)], axis=1
         )
-        spectrum = dot3(table_ref[2 * odd], *split(field))
+        spectrum = product(table_ref[2 * odd], field)
         square = (waves[odd] * waves[odd]).astype(F32)
         damped = spectrum / (1.0 + jnp.concatenate([s * square for s in scale], axis=1))
-        results.append(dot3(table_ref[2 * odd + 1], *split(damped)))
+        results.append(product(table_ref[2 * odd + 1], damped))
     for q in range(rows):
         even, odd = [value[:, q * axial : (q + 1) * axial] for value in results]
         out_ref[: blocks // 2, q] = (even + odd).reshape(blocks // 2, angles, axial)
         out_ref[blocks // 2 :, q] = (even - odd).reshape(blocks // 2, angles, axial)
 
 
-def solve(coef, first, field, low, high):
+def solve(coef, first, field, after):
     blocks, rows, angles, axial = field.shape
     all_angles = blocks * angles
     tables = fourier_tables(all_angles)
-    half = all_angles // 2
-    part = 2 if rows % 2 == 0 else 1
+    part = math.gcd(rows, 4)
     field_spec = pl.BlockSpec((blocks, part, angles, axial), lambda i: (0, i, 0, 0))
     smem = pl.BlockSpec(memory_space=pltpu.SMEM)
     whole = pl.BlockSpec(memory_space=pltpu.VMEM)
@@ -327,30 +361,44 @@
     return pl.pallas_call(
         solve_kernel,
         grid=(rows // part,),
-        in_specs=[smem, smem, whole, unread, unread, field_spec],
+        in_specs=[smem, smem, whole] + [unread] * len(after) + [field_spec],
         out_specs=field_spec,
         out_shape=pltpu.HBM(field.shape, F32),
-        scratch_shapes=[pltpu.VMEM((4, 2 * half, half), BF16)],
-        compiler_params=pltpu.CompilerParams(vmem_limit_bytes=14 * MIB),
+        compiler_params=pltpu.CompilerParams(vmem_limit_bytes=24 * MIB),
         cost_estimate=pl.CostEstimate(
             flops=12 * all_angles * all_angles * rows * axial,
             bytes_accessed=8 * all_angles * rows * axial,
             transcendentals=0,
         ),
         name="solve",
-    )(coef, first, in_hbm(jnp.asarray(tables)), in_vmem(low), in_vmem(high), in_vmem(field))
-
-
-def join_kernel(force_ref, smooth_ref, out_ref, sum_ref, sems):
-    parts = sems.shape[0]
-    part = force_ref.shape[0] // parts
-    copies = []
-    for i in range(parts):
-        at = pl.ds(i * part, part)
-        sum_ref[at] = force_ref[at] + smooth_ref[at]
-        copies.append(pltpu.make_async_copy(sum_ref.at[at], out_ref.at[at], sems.at[i]))
-        copies[-1].start()
-    for copy in copies:
+    )(
+        coef,
+        first,
+        in_hbm(jnp.asarray(tables)),
+        *after,
+        in_vmem(field),
+    )
+
+
+def join_kernel(force_ref, smooth_ref, out_ref, sum_ref, in_sems, out_sems):
+    parts = in_sems.shape[0]
+    part = sum_ref.shape[0] // parts
+    spans = [pl.ds(i * part, part) for i in range(parts)]
+    reads = [
+        pltpu.make_async_copy(force_ref.at[at], sum_ref.at[at], in_sems.at[i])
+        for i, at in enumerate(spans)
+    ]
+    writes = [
+        pltpu.make_async_copy(sum_ref.at[at], out_ref.at[at], out_sems.at[i])
+        for i, at in enumerate(spans)
+    ]
+    for copy in reads:
+        copy.start()
+    for i, at in enumerate(spans):
+        reads[i].wait()
+        sum_ref[at] = sum_ref[at] + smooth_ref[at]
+        writes[i].start()
+    for copy in writes:
         copy.wait()
 
 
@@ -358,11 +406,12 @@
     whole = pl.BlockSpec(memory_space=pltpu.VMEM)
     return pl.pallas_call(
         join_kernel,
-        in_specs=[whole, whole],
+        in_specs=[pl.BlockSpec(memory_space=pl.ANY), whole],
         out_specs=pl.BlockSpec(memory_space=pl.ANY),
         out_shape=pltpu.HBM(force.shape, F32),
         scratch_shapes=[
             pltpu.VMEM(force.shape, F32),
+            pltpu.SemaphoreType.DMA((math.gcd(force.shape[0], 8),)),
             pltpu.SemaphoreType.DMA((math.gcd(force.shape[0], 8),)),
         ],
         compiler_params=pltpu.CompilerParams(vmem_limit_bytes=14 * MIB),
@@ -370,7 +419,7 @@
             flops=force.size, bytes_accessed=12 * force.size, transcendentals=0
         ),
         name="join",
-    )(in_vmem(force), in_vmem(smooth))
+    )(in_hbm(force), in_vmem(smooth))
 
 
 def from_neighbours(low_edge, high_edge):
@@ -388,10 +437,12 @@
     rows = 3 * radii // az
     pieces = velocity.reshape(az, rows, angles, axial)
     gathered = lax.all_to_all(pieces, "az", 0, 0, tiled=True)
-    stress, low_edge, high_edge = deposit(cell_ids, dumbbells, velocity)
+    low_edge, high_edge = deposit_edges(cell_ids, dumbbells, velocity)
     low, high = from_neighbours(low_edge, high_edge)
+    middle = deposit_middle(cell_ids, dumbbells, low_edge, velocity.shape)
+    stress = (low_edge, middle, high_edge)
     first = (lax.axis_index("az") * rows).astype(jnp.int32).reshape(1)
-    solved = solve(azim_coef, first, gathered, low, high)
+    solved = solve(azim_coef, first, gathered, (in_vmem(low), in_vmem(high), in_hbm(middle)))
     smooth = lax.all_to_all(solved, "az", 0, 0, tiled=True)
     moved, force = move(
         stencil_coef, block_inverse, low, velocity, stress, high, cell_ids, dumbbells, brownian

time: 104 us -> 95.3 us (0.916)
  waiting for transfers between devices: 30.5 us -> 25.2 us
  local copies, waits for them, and re-layouts: 3.58 us -> 0.03 us
    ppermute x1, waiting for transfers between devices: 15.6 us -> 2.97 us  [from_neighbours(): low = lax.ppermute(high_edge, 'rad', forward)]
    all_to_all x1, waiting for transfers between devices: 0.01 us -> 5.91 us  [per_device(): gathered = lax.all_to_all(pieces, 'az', 0, 0, tiled=True)]
    unnamed x16 -> x12, local copies, waits for them, and re-layouts: 3.58 us -> 0.03 us
    pallas_call x3 -> x4, Pallas kernels: 45.9 us -> 47.6 us  [the longest x1 26.5 us: move(): pl.pallas_call(move_kernel, in_specs=[whole] * 11, out_specs=[whole, whol...]
    all_to_all x1, waiting for transfers between devices: 9.95 us -> 11.3 us  [per_device(): smooth = lax.all_to_all(solved, 'az', 0, 0, tiled=True)]
    pallas_call x1, Pallas kernels: 7.87 us -> 6.52 us  [solve(): pl.pallas_call(solve_kernel, grid=(rows // part,), in_specs=[smem, smem,...]
  transfers between devices with their start and end apart: 4 -> 4, of which waited for: 3 -> 4; matrix products, arithmetic and copies ran while one was open for 0% -> 0% of each run, Pallas kernels for 43% -> 47%
where the time goes in v6:
time: 95.3 us; the launch traced here: 94.8 us
  Pallas kernels  54.2 us (57%)
  waiting for transfers between devices  25.2 us (26%)
  starting transfers between devices  14.7 us (15%)
    pallas_call x1, Pallas kernels, move(): pl.pallas_call(move_kernel, in_specs=[whole] * 11, out_specs=[whole, whol...  26.5 us
    pallas_call x1, Pallas kernels, deposit_middle(): pl.pallas_call(lambda ids_ref, spring_ref, _, *refs: middle_kernel(ids_re...  12.6 us
    all_to_all x1, waiting for transfers between devices, per_device(): smooth = lax.all_to_all(solved, 'az', 0, 0, tiled=True)  11.3 us
    pallas_call x1, Pallas kernels, solve(): pl.pallas_call(solve_kernel, grid=(rows // part,), in_specs=[smem, smem,...  6.52 us
    all_to_all x1, waiting for transfers between devices, per_device(): gathered = lax.all_to_all(pieces, 'az', 0, 0, tiled=True)  5.91 us
    pallas_call x1, Pallas kernels, deposit_edges(): pl.pallas_call(functools.partial(edge_kernel, radii=radii), grid=(1,), in...  5.73 us
    all_to_all x1, starting transfers between devices, per_device(): gathered = lax.all_to_all(pieces, 'az', 0, 0, tiled=True)  5.31 us
    ppermute x1, waiting for transfers between devices, from_neighbours(): high = lax.ppermute(low_edge, 'rad', backward)  4.98 us
  transfers between devices with their start and end apart: 4, of which 4 were waited for; matrix products, arithmetic and copies ran while one was open for 0% of the time, Pallas kernels for 47%

profile of v6, /device:TPU:0, one launch (start us, length us, event | category | flops | bytes accessed | tf_op | source)
XLA Modules:
  0.0 94.8 jit_solution(16315362816978662501)
XLA Ops:
  0.6 0.0 copy-start
  0.6 0.0 copy-start.2
  0.6 5.3 %all-to-all-start = ((f32[8,12,64,128]{3,2,1,0:T(8,128)}), f32[8,12,64,128]{3,2,1,0:T(8,128)S(1)}, u32[]{:S(2)}, u32[]{:S(2)}) async-start(f32[8,12,64,128]{3,2,1,0:T(8,128)} %bitcast.6), calls=%async_computation | async-start | bytes 6291456 | tf_op jit(solution)/shard_map/all_to_all | solution.py:439
  6.0 0.0 copy-done
  6.0 0.0 copy-done.2
  6.0 5.7 %deposit_edges.1 = (f32[2,3,4,64,128]{4,3,2,1,0:T(8,128)}, f32[2,3,4,64,128]{4,3,2,1,0:T(8,128)}) custom-call(s32[2,1,1,4096]{3,2,1,0:T(1,128)S(1)} %copy-done.2, f32[3,1,1,4096]{3,2,1,0:T(1,128)S(1)} %copy-done, f32[3,32,64,128]{3,2,1,0:T(8,128)} %velocity_ref.1, f32[3,32,64,128]{3,2,1,0:T(8,128)} %velocity_ref.1), custom_call_target="tpu_custom_call" | custom-call | flops 3221225472 | bytes 3145728 | tf_op jit(solution)/shard_map/deposit_edges/pallas_call | solution.py:112
  11.7 4.4 %collective-permute-start = (f32[2,3,4,64,128]{4,3,2,1,0:T(8,128)}, f32[2,3,4,64,128]{4,3,2,1,0:T(8,128)}, u32[]{:S(2)}, u32[]{:S(2)}) collective-permute-start(f32[2,3,4,64,128]{4,3,2,1,0:T(8,128)} %get-tuple-element.6.high_edge_ref), channel_id=1, source_target_pairs={{0,1},{1,2},{2,3},{4,5},{5,6},{6,7},{8,9},{9,10},{10,11},{12,13},{... | collective-permute-start | bytes 2359304 | tf_op jit(solution)/shard_map/ppermute | solution.py:429
  16.1 1.3 %collective-permute-start.1 = (f32[2,3,4,64,128]{4,3,2,1,0:T(8,128)}, f32[2,3,4,64,128]{4,3,2,1,0:T(8,128)}, u32[]{:S(2)}, u32[]{:S(2)}) collective-permute-start(f32[2,3,4,64,128]{4,3,2,1,0:T(8,128)} %get-tuple-element.7._.low_edge_ref), channel_id=1, source_target_pairs={{1,0},{2,1},{3,2},{5,4},{6,5},{7,6},{9,8},{10,9},{11,10},{13,12},{... | collective-permute-start | bytes 2359304 | tf_op jit(solution)/shard_map/ppermute | solution.py:430
  17.4 0.0 copy-start.5
  17.4 12.6 %deposit_middle.1.middle_ref.refs_2_ = f32[3,24,64,128]{3,2,1,0:T(8,128)} custom-call(s32[2,1,1,4096]{3,2,1,0:T(1,128)S(1)} %copy-done.2, f32[3,1,1,4096]{3,2,1,0:T(1,128)S(1)} %copy-done, f32[2,3,4,64,128]{4,3,2,1,0:T(8,128)} %get-tuple-element.7._.low_edge_ref), custom_call_target="tpu_custom_call" | custom-call | flops 9663676416 | bytes 2359296 | tf_op jit(solution)/shard_map/deposit_middle/pallas_call | solution.py:140
  30.0 3.0 %collective-permute-done.low_ref.refs_0_ = f32[2,3,4,64,128]{4,3,2,1,0:T(8,128)} collective-permute-done((f32[2,3,4,64,128]{4,3,2,1,0:T(8,128)}, f32[2,3,4,64,128]{4,3,2,1,0:T(8,128)}, u32[]{:S(2)}, u32[]{:S(2)}) %collective-permute-start) | collective-permute-done | bytes 786464 | tf_op jit(solution)/shard_map/ppermute | solution.py:429
  33.0 5.0 %collective-permute-done.1.high_ref.refs_1_ = f32[2,3,4,64,128]{4,3,2,1,0:T(8,128)} collective-permute-done((f32[2,3,4,64,128]{4,3,2,1,0:T(8,128)}, f32[2,3,4,64,128]{4,3,2,1,0:T(8,128)}, u32[]{:S(2)}, u32[]{:S(2)}) %collective-permute-start.1) | collective-permute-done | bytes 786464 | tf_op jit(solution)/shard_map/ppermute | solution.py:430
  37.9 5.9 %all-to-all-done.refs_3_ = f32[8,12,64,128]{3,2,1,0:T(8,128)S(1)} async-done(((f32[8,12,64,128]{3,2,1,0:T(8,128)}), f32[8,12,64,128]{3,2,1,0:T(8,128)S(1)}, u32[]{:S(2)}, u32[]{:S(2)}) %all-to-all-start) | async-done | bytes 3145760 | tf_op jit(solution)/shard_map/all_to_all | solution.py:439
  43.8 0.0 copy-done.5
  43.8 6.5 %solve.1 = f32[8,12,64,128]{3,2,1,0:T(8,128)} custom-call(f32[32]{0:T(128)S(1)} %copy-done.5, s32[1]{0:T(128)} %bitcast.1.first_ref, bf16[4,256,768]{2,1,0:T(8,128)(2,1)} %constant.10.clone.table_ref, f32[2,3,4,64,128]{4,3,2,1,0:T(8,128)} %collective-permute-done.low_ref.refs_0_, f32[2,3,4,64,128]{4,3,2,1,0:T(8,128)} %collective-permute-done.1.high_ref.refs_1_, ...), custom_call_target="tpu_custom_call" | custom-call | flops 4831838208 | bytes 6291456 | tf_op jit(solution)/shard_map/solve/pallas_call | solution.py:361
  50.4 0.0 copy-start.1
  50.4 0.0 copy-start.3
  50.4 0.0 copy-start.4
  50.4 3.8 %all-to-all-start.1 = ((f32[8,12,64,128]{3,2,1,0:T(8,128)}), f32[8,12,64,128]{3,2,1,0:T(8,128)S(1)}, u32[]{:S(2)}, u32[]{:S(2)}) async-start(f32[8,12,64,128]{3,2,1,0:T(8,128)} %solve.1), calls=%async_computation.1 | async-start | bytes 6291456 | tf_op jit(solution)/shard_map/all_to_all | solution.py:446
  54.2 0.0 copy-done.1
  54.2 0.0 copy-done.3
  54.2 0.0 copy-done.4
  54.2 26.5 %move.1 = (f32[3,1,1,4096]{3,2,1,0:T(1,128)}, f32[3,32,64,128]{3,2,1,0:T(8,128)}) custom-call(f32[9,32]{1,0:T(8,128)S(1)} %copy-done.4, f32[32,32]{1,0:T(8,128)S(1)} %copy-done.3, f32[2,3,4,64,128]{4,3,2,1,0:T(8,128)} %collective-permute-done.low_ref.refs_0_, f32[3,32,64,128]{3,2,1,0:T(8,128)} %velocity_ref.1, ...), custom_call_target="tpu_custom_call" | custom-call | flops 15032385536 | bytes 10485760 | tf_op jit(solution)/shard_map/move/pallas_call | solution.py:261
  80.7 11.3 %all-to-all-done.1 = f32[8,12,64,128]{3,2,1,0:T(8,128)S(1)} async-done(((f32[8,12,64,128]{3,2,1,0:T(8,128)}), f32[8,12,64,128]{3,2,1,0:T(8,128)S(1)}, u32[]{:S(2)}, u32[]{:S(2)}) %all-to-all-start.1) | async-done | bytes 3145760 | tf_op jit(solution)/shard_map/all_to_all | solution.py:446
  92.0 2.8 %join.1 = f32[96,64,128]{2,1,0:T(8,128)} custom-call(f32[96,64,128]{2,1,0:T(8,128)} %bitcast.7, f32[96,64,128]{2,1,0:T(8,128)S(1)} %bitcast.5), custom_call_target="tpu_custom_call" | custom-call | flops 786432 | bytes 9437184 | tf_op jit(solution)/shard_map/join/pallas_call | solution.py:407
Async XLA Ops:
  0.6 5.3 %copy-start = (f32[3,1,1,4096]{3,2,1,0:T(1,128)S(1)}, f32[3,1,1,4096]{3,2,1,0:T(1,128)}, u32[]{:S(2)}) copy-start(f32[3,1,1,4096]{3,2,1,0:T(1,128)} %spring_ref.5) | copy-start | bytes 147460
  0.6 5.3 %copy-start.2 = (s32[2,1,1,4096]{3,2,1,0:T(1,128)S(1)}, s32[2,1,1,4096]{3,2,1,0:T(1,128)}, u32[]{:S(2)}) copy-start(s32[2,1,1,4096]{3,2,1,0:T(1,128)} %ids_ref.5) | copy-start | bytes 98308
  0.6 43.2 %all-to-all-start = ((f32[8,12,64,128]{3,2,1,0:T(8,128)}), f32[8,12,64,128]{3,2,1,0:T(8,128)S(1)}, u32[]{:S(2)}, u32[]{:S(2)}) async-start(f32[8,12,64,128]{3,2,1,0:T(8,128)} %bitcast.6), calls=%async_computation | async-start | bytes 6291456 | tf_op jit(solution)/shard_map/all_to_all | solution.py:439
  11.7 21.2 %collective-permute-start = (f32[2,3,4,64,128]{4,3,2,1,0:T(8,128)}, f32[2,3,4,64,128]{4,3,2,1,0:T(8,128)}, u32[]{:S(2)}, u32[]{:S(2)}) collective-permute-start(f32[2,3,4,64,128]{4,3,2,1,0:T(8,128)} %get-tuple-element.6.high_edge_ref), channel_id=1, source_target_pairs={{0,1},{1,2},{2,3},{4,5},{5,6},{6,7},{8,9},{9,10},{10,11},{12,13},{... | collective-permute-start | bytes 2359304 | tf_op jit(solution)/shard_map/ppermute | solution.py:429
  16.1 21.9 %collective-permute-start.1 = (f32[2,3,4,64,128]{4,3,2,1,0:T(8,128)}, f32[2,3,4,64,128]{4,3,2,1,0:T(8,128)}, u32[]{:S(2)}, u32[]{:S(2)}) collective-permute-start(f32[2,3,4,64,128]{4,3,2,1,0:T(8,128)} %get-tuple-element.7._.low_edge_ref), channel_id=1, source_target_pairs={{1,0},{2,1},{3,2},{5,4},{6,5},{7,6},{9,8},{10,9},{11,10},{13,12},{... | collective-permute-start | bytes 2359304 | tf_op jit(solution)/shard_map/ppermute | solution.py:430
  17.4 26.5 %copy-start.5 = (f32[32]{0:T(128)S(1)}, f32[32]{0:T(128)}, u32[]{:S(2)}) copy-start(f32[32]{0:T(128)} %coef_ref.1) | copy-start | bytes 388
  50.4 3.8 %copy-start.1 = (f32[3,1,1,4096]{3,2,1,0:T(1,128)S(1)}, f32[3,1,1,4096]{3,2,1,0:T(1,128)}, u32[]{:S(2)}) copy-start(f32[3,1,1,4096]{3,2,1,0:T(1,128)} %noise_ref.1) | copy-start | bytes 147460
  50.4 3.8 %copy-start.3 = (f32[32,32]{1,0:T(8,128)S(1)}, f32[32,32]{1,0:T(8,128)}, u32[]{:S(2)}) copy-start(f32[32,32]{1,0:T(8,128)} %inverse_ref.1) | copy-start | bytes 12292
  50.4 3.8 %copy-start.4 = (f32[9,32]{1,0:T(8,128)S(1)}, f32[9,32]{1,0:T(8,128)}, u32[]{:S(2)}) copy-start(f32[9,32]{1,0:T(8,128)} %stencil_ref.1) | copy-start | bytes 3460
  50.4 41.6 %all-to-all-start.1 = ((f32[8,12,64,128]{3,2,1,0:T(8,128)}), f32[8,12,64,128]{3,2,1,0:T(8,128)S(1)}, u32[]{:S(2)}, u32[]{:S(2)}) async-start(f32[8,12,64,128]{3,2,1,0:T(8,128)} %solve.1), calls=%async_computation.1 | async-start | bytes 6291456 | tf_op jit(solution)/shard_map/all_to_all | solution.py:446

commit v7 on v6

--- a/solution.py
+++ b/solution.py
@@ -320,51 +320,82 @@
     return dot(table, jnp.concatenate([high, high, low], axis=0))
 
 
-def solve_kernel(coef_ref, first_ref, table_ref, *refs):
-    in_ref, out_ref = refs[-2:]
+def solve_kernel(coef_ref, first_ref, tables_ref, *refs):
+    in_ref, out_ref, table_ref, done_ref, table_sems, out_sems = refs[-6:]
     blocks, rows, angles, axial = in_ref.shape
     half = blocks * angles // 2
     quarter = half // 2
+    part = rows // out_sems.shape[0]
+    loads = [
+        pltpu.make_async_copy(tables_ref.at[i], table_ref.at[i], table_sems.at[i])
+        for i in range(4)
+    ]
+    for copy in loads:
+        copy.start()
+
+    base = first_ref[0]
+    lane = iota((1, axial), 1)
+    coef = jnp.zeros((1, axial), F32)
+    for q in range(rows):
+        coef = jnp.where(lane == q, coef_ref[lax.rem(base + q, coef_ref.shape[0])], coef)
     row = iota((half, axial), 0)
     waves = [
         jnp.where(row <= quarter, 2 * row, 2 * (row - quarter)),
         jnp.where(row < quarter, 2 * row + 1, 2 * (row - quarter) + 1),
     ]
-    base = first_ref[0] + pl.program_id(0) * rows
-    scale = [coef_ref[lax.rem(base + q, coef_ref.shape[0])] for q in range(rows)]
-    near = [in_ref[: blocks // 2, q].reshape(half, axial) for q in range(rows)]
-    far = [in_ref[blocks // 2 :, q].reshape(half, axial) for q in range(rows)]
-    results = []
-    for odd in range(2):
-        field = jnp.concatenate(
-            [a - b if odd else a + b for a, b in zip(near, far)], axis=1
+    damping = [1.0 / (1.0 + coef * (wave * wave).astype(F32)) for wave in waves]
+
+    stores = []
+    for g in range(rows // part):
+        chosen = range(g * part, (g + 1) * part)
+        near = [in_ref[: blocks // 2, q].reshape(half, axial) for q in chosen]
+        far = [in_ref[blocks // 2 :, q].reshape(half, axial) for q in chosen]
+        results = []
+        for odd in range(2):
+            field = jnp.concatenate([a - b if odd else a + b for a, b in zip(near, far)], axis=1)
+            if g == 0:
+                loads[2 * odd].wait()
+            spectrum = product(table_ref[2 * odd], field)
+            scale = [
+                jnp.broadcast_to(damping[odd][:, q : q + 1], (half, axial)) for q in chosen
+            ]
+            if g == 0:
+                loads[2 * odd + 1].wait()
+            damped = spectrum * jnp.concatenate(scale, axis=1)
+            results.append(product(table_ref[2 * odd + 1], damped))
+        for i, q in enumerate(chosen):
+            even, odd = [value[:, i * axial : (i + 1) * axial] for value in results]
+            done_ref[: blocks // 2, q] = (even + odd).reshape(blocks // 2, angles, axial)
+            done_ref[blocks // 2 :, q] = (even - odd).reshape(blocks // 2, angles, axial)
+        at = pl.ds(g * part, part)
+        stores.append(
+            pltpu.make_async_copy(done_ref.at[:, at], out_ref.at[:, at], out_sems.at[g])
         )
-        spectrum = product(table_ref[2 * odd], field)
-        square = (waves[odd] * waves[odd]).astype(F32)
-        damped = spectrum / (1.0 + jnp.concatenate([s * square for s in scale], axis=1))
-        results.append(product(table_ref[2 * odd + 1], damped))
-    for q in range(rows):
-        even, odd = [value[:, q * axial : (q + 1) * axial] for value in results]
-        out_ref[: blocks // 2, q] = (even + odd).reshape(blocks // 2, angles, axial)
-        out_ref[blocks // 2 :, q] = (even - odd).reshape(blocks // 2, angles, axial)
+        stores[-1].start()
+    for copy in stores:
+        copy.wait()
 
 
 def solve(coef, first, field, after):
     blocks, rows, angles, axial = field.shape
     all_angles = blocks * angles
     tables = fourier_tables(all_angles)
-    part = math.gcd(rows, 4)
-    field_spec = pl.BlockSpec((blocks, part, angles, axial), lambda i: (0, i, 0, 0))
+    parts = rows // math.gcd(rows, 4)
     smem = pl.BlockSpec(memory_space=pltpu.SMEM)
     whole = pl.BlockSpec(memory_space=pltpu.VMEM)
     unread = pl.BlockSpec(memory_space=pl.ANY)
     return pl.pallas_call(
         solve_kernel,
-        grid=(rows // part,),
-        in_specs=[smem, smem, whole] + [unread] * len(after) + [field_spec],
-        out_specs=field_spec,
+        in_specs=[smem, smem, unread] + [unread] * len(after) + [whole],
+        out_specs=unread,
         out_shape=pltpu.HBM(field.shape, F32),
-        compiler_params=pltpu.CompilerParams(vmem_limit_bytes=24 * MIB),
+        scratch_shapes=[
+            pltpu.VMEM(tables.shape, BF16),
+            pltpu.VMEM(field.shape, F32),
+            pltpu.SemaphoreType.DMA((4,)),
+            pltpu.SemaphoreType.DMA((parts,)),
+        ],
+        compiler_params=pltpu.CompilerParams(vmem_limit_bytes=28 * MIB),
         cost_estimate=pl.CostEstimate(
             flops=12 * all_angles * all_angles * rows * axial,
             bytes_accessed=8 * all_angles * rows * axial,
@@ -380,25 +411,16 @@
     )
 
 
-def join_kernel(force_ref, smooth_ref, out_ref, sum_ref, in_sems, out_sems):
-    parts = in_sems.shape[0]
-    part = sum_ref.shape[0] // parts
-    spans = [pl.ds(i * part, part) for i in range(parts)]
-    reads = [
-        pltpu.make_async_copy(force_ref.at[at], sum_ref.at[at], in_sems.at[i])
-        for i, at in enumerate(spans)
-    ]
-    writes = [
-        pltpu.make_async_copy(sum_ref.at[at], out_ref.at[at], out_sems.at[i])
-        for i, at in enumerate(spans)
-    ]
-    for copy in reads:
-        copy.start()
-    for i, at in enumerate(spans):
-        reads[i].wait()
-        sum_ref[at] = sum_ref[at] + smooth_ref[at]
-        writes[i].start()
-    for copy in writes:
+def join_kernel(force_ref, smooth_ref, out_ref, sum_ref, sems):
+    parts = sems.shape[0]
+    part = force_ref.shape[0] // parts
+    copies = []
+    for i in range(parts):
+        at = pl.ds(i * part, part)
+        sum_ref[at] = force_ref[at] + smooth_ref[at]
+        copies.append(pltpu.make_async_copy(sum_ref.at[at], out_ref.at[at], sems.at[i]))
+        copies[-1].start()
+    for copy in copies:
         copy.wait()
 
 
@@ -406,12 +428,11 @@
     whole = pl.BlockSpec(memory_space=pltpu.VMEM)
     return pl.pallas_call(
         join_kernel,
-        in_specs=[pl.BlockSpec(memory_space=pl.ANY), whole],
+        in_specs=[whole, whole],
         out_specs=pl.BlockSpec(memory_space=pl.ANY),
         out_shape=pltpu.HBM(force.shape, F32),
         scratch_shapes=[
             pltpu.VMEM(force.shape, F32),
-            pltpu.SemaphoreType.DMA((math.gcd(force.shape[0], 8),)),
             pltpu.SemaphoreType.DMA((math.gcd(force.shape[0], 8),)),
         ],
         compiler_params=pltpu.CompilerParams(vmem_limit_bytes=14 * MIB),
@@ -419,7 +440,7 @@
             flops=force.size, bytes_accessed=12 * force.size, transcendentals=0
         ),
         name="join",
-    )(in_hbm(force), in_vmem(smooth))
+    )(in_vmem(force), in_vmem(smooth))
 
 
 def from_neighbours(low_edge, high_edge):

time: 95.3 us -> 96.3 us (1.010)
  local copies, waits for them, and re-layouts: 0.03 us -> 1.92 us
  Pallas kernels: 54.2 us -> 53.1 us
    unnamed x12 -> x14, local copies, waits for them, and re-layouts: 0.03 us -> 1.92 us
    pallas_call x2, Pallas kernels: 9.34 us -> 8.23 us  [the longest x1 6.47 us: solve(): pl.pallas_call(solve_kernel, in_specs=[smem, smem, unread] + [unread] * l...]
where the time goes in v7:
time: 96.3 us; the launch traced here: 95.8 us
  Pallas kernels  53.1 us (55%)
  waiting for transfers between devices  24.9 us (26%)
  starting transfers between devices  14.9 us (15%)
  local copies, waits for them, and re-layouts  1.92 us (2%)
    pallas_call x1, Pallas kernels, move(): pl.pallas_call(move_kernel, in_specs=[whole] * 11, out_specs=[whole, whol...  26.5 us
    pallas_call x1, Pallas kernels, deposit_middle(): pl.pallas_call(lambda ids_ref, spring_ref, _, *refs: middle_kernel(ids_re...  12.6 us
    all_to_all x1, waiting for transfers between devices, per_device(): smooth = lax.all_to_all(solved, 'az', 0, 0, tiled=True)  11.1 us
    pallas_call x1, Pallas kernels, solve(): pl.pallas_call(solve_kernel, in_specs=[smem, smem, unread] + [unread] * l...  6.47 us
    all_to_all x1, waiting for transfers between devices, per_device(): gathered = lax.all_to_all(pieces, 'az', 0, 0, tiled=True)  5.92 us
    pallas_call x1, Pallas kernels, deposit_edges(): pl.pallas_call(functools.partial(edge_kernel, radii=radii), grid=(1,), in...  5.73 us
    all_to_all x1, starting transfers between devices, per_device(): gathered = lax.all_to_all(pieces, 'az', 0, 0, tiled=True)  5.31 us
    ppermute x1, waiting for transfers between devices, from_neighbours(): high = lax.ppermute(low_edge, 'rad', backward)  4.98 us
  transfers between devices with their start and end apart: 4, of which 4 were waited for; matrix products, arithmetic and copies ran while one was open for 0% of the time, Pallas kernels for 47%

profile of v7, /device:TPU:0, one launch (start us, length us, event | category | flops | bytes accessed | tf_op | source)
XLA Modules:
  0.0 95.8 jit_solution(12882220793943546642)
XLA Ops:
  0.6 0.0 copy-start.1
  0.6 0.0 copy-start.3
  0.6 5.3 %all-to-all-start = ((f32[8,12,64,128]{3,2,1,0:T(8,128)}), f32[8,12,64,128]{3,2,1,0:T(8,128)S(1)}, u32[]{:S(2)}, u32[]{:S(2)}) async-start(f32[8,12,64,128]{3,2,1,0:T(8,128)} %bitcast.7), calls=%async_computation | async-start | bytes 6291456 | tf_op jit(solution)/shard_map/all_to_all | solution.py:460
  6.0 0.0 copy-done.1
  6.0 0.0 copy-done.3
  6.0 5.7 %deposit_edges.1 = (f32[2,3,4,64,128]{4,3,2,1,0:T(8,128)}, f32[2,3,4,64,128]{4,3,2,1,0:T(8,128)}) custom-call(s32[2,1,1,4096]{3,2,1,0:T(1,128)S(1)} %copy-done.3, f32[3,1,1,4096]{3,2,1,0:T(1,128)S(1)} %copy-done.1, f32[3,32,64,128]{3,2,1,0:T(8,128)} %velocity_ref.1, f32[3,32,64,128]{3,2,1,0:T(8,128)} %velocity_ref.1), custom_call_target="tpu_custom_call" | custom-call | flops 3221225472 | bytes 3145728 | tf_op jit(solution)/shard_map/deposit_edges/pallas_call | solution.py:112
  11.7 4.4 %collective-permute-start = (f32[2,3,4,64,128]{4,3,2,1,0:T(8,128)}, f32[2,3,4,64,128]{4,3,2,1,0:T(8,128)}, u32[]{:S(2)}, u32[]{:S(2)}) collective-permute-start(f32[2,3,4,64,128]{4,3,2,1,0:T(8,128)} %get-tuple-element.6.high_edge_ref), channel_id=1, source_target_pairs={{0,1},{1,2},{2,3},{4,5},{5,6},{6,7},{8,9},{9,10},{10,11},{12,13},{... | collective-permute-start | bytes 2359304 | tf_op jit(solution)/shard_map/ppermute | solution.py:450
  16.1 1.3 %collective-permute-start.1 = (f32[2,3,4,64,128]{4,3,2,1,0:T(8,128)}, f32[2,3,4,64,128]{4,3,2,1,0:T(8,128)}, u32[]{:S(2)}, u32[]{:S(2)}) collective-permute-start(f32[2,3,4,64,128]{4,3,2,1,0:T(8,128)} %get-tuple-element.7._.low_edge_ref), channel_id=1, source_target_pairs={{1,0},{2,1},{3,2},{5,4},{6,5},{7,6},{9,8},{10,9},{11,10},{13,12},{... | collective-permute-start | bytes 2359304 | tf_op jit(solution)/shard_map/ppermute | solution.py:451
  17.4 0.0 copy-start.6
  17.4 12.6 %deposit_middle.1.middle_ref.refs_2_ = f32[3,24,64,128]{3,2,1,0:T(8,128)} custom-call(s32[2,1,1,4096]{3,2,1,0:T(1,128)S(1)} %copy-done.3, f32[3,1,1,4096]{3,2,1,0:T(1,128)S(1)} %copy-done.1, f32[2,3,4,64,128]{4,3,2,1,0:T(8,128)} %get-tuple-element.7._.low_edge_ref), custom_call_target="tpu_custom_call" | custom-call | flops 9663676416 | bytes 2359296 | tf_op jit(solution)/shard_map/deposit_middle/pallas_call | solution.py:140
  30.0 2.9 %collective-permute-done.low_ref.refs_0_ = f32[2,3,4,64,128]{4,3,2,1,0:T(8,128)} collective-permute-done((f32[2,3,4,64,128]{4,3,2,1,0:T(8,128)}, f32[2,3,4,64,128]{4,3,2,1,0:T(8,128)}, u32[]{:S(2)}, u32[]{:S(2)}) %collective-permute-start) | collective-permute-done | bytes 786464 | tf_op jit(solution)/shard_map/ppermute | solution.py:450
  32.9 5.0 %collective-permute-done.1.high_ref.refs_1_ = f32[2,3,4,64,128]{4,3,2,1,0:T(8,128)} collective-permute-done((f32[2,3,4,64,128]{4,3,2,1,0:T(8,128)}, f32[2,3,4,64,128]{4,3,2,1,0:T(8,128)}, u32[]{:S(2)}, u32[]{:S(2)}) %collective-permute-start.1) | collective-permute-done | bytes 786464 | tf_op jit(solution)/shard_map/ppermute | solution.py:451
  37.9 5.9 %all-to-all-done.refs_3_ = f32[8,12,64,128]{3,2,1,0:T(8,128)S(1)} async-done(((f32[8,12,64,128]{3,2,1,0:T(8,128)}), f32[8,12,64,128]{3,2,1,0:T(8,128)S(1)}, u32[]{:S(2)}, u32[]{:S(2)}) %all-to-all-start) | async-done | bytes 3145760 | tf_op jit(solution)/shard_map/all_to_all | solution.py:460
  43.8 0.0 copy-done.6
  43.8 6.5 %solve.1 = f32[8,12,64,128]{3,2,1,0:T(8,128)} custom-call(f32[32]{0:T(128)S(1)} %copy-done.6, s32[1]{0:T(128)} %bitcast.1.first_ref, bf16[4,256,768]{2,1,0:T(8,128)(2,1)} %constant.10.clone.tables_ref, f32[2,3,4,64,128]{4,3,2,1,0:T(8,128)} %collective-permute-done.low_ref.refs_0_, f32[2,3,4,64,128]{4,3,2,1,0:T(8,128)} %collective-permute-done.1.high_ref.refs_1_, ...), custom_call_target="tpu_custom_call" | custom-call | flops 4831838208 | bytes 6291456 | tf_op jit(solution)/shard_map/solve/pallas_call | solution.py:387
  50.3 0.0 copy-start.2
  50.3 0.0 copy-start.4
  50.4 0.0 copy-start.5
  50.4 4.0 %all-to-all-start.1 = ((f32[8,12,64,128]{3,2,1,0:T(8,128)}), f32[8,12,64,128]{3,2,1,0:T(8,128)S(1)}, u32[]{:S(2)}, u32[]{:S(2)}) async-start(f32[8,12,64,128]{3,2,1,0:T(8,128)} %solve.1), calls=%async_computation.1 | async-start | bytes 6291456 | tf_op jit(solution)/shard_map/all_to_all | solution.py:467
  54.3 0.0 copy-done.2
  54.4 0.0 copy-done.4
  54.4 0.0 copy-done.5
  54.4 26.5 %move.1 = (f32[3,1,1,4096]{3,2,1,0:T(1,128)}, f32[3,32,64,128]{3,2,1,0:T(8,128)}) custom-call(f32[9,32]{1,0:T(8,128)S(1)} %copy-done.5, f32[32,32]{1,0:T(8,128)S(1)} %copy-done.4, f32[2,3,4,64,128]{4,3,2,1,0:T(8,128)} %collective-permute-done.low_ref.refs_0_, f32[3,32,64,128]{3,2,1,0:T(8,128)} %velocity_ref.1, ...), custom_call_target="tpu_custom_call" | custom-call | flops 15032385536 | bytes 10485760 | tf_op jit(solution)/shard_map/move/pallas_call | solution.py:261
  80.9 11.1 %all-to-all-done.1 = f32[8,12,64,128]{3,2,1,0:T(8,128)S(1)} async-done(((f32[8,12,64,128]{3,2,1,0:T(8,128)}), f32[8,12,64,128]{3,2,1,0:T(8,128)S(1)}, u32[]{:S(2)}, u32[]{:S(2)}) %all-to-all-start.1) | async-done | bytes 3145760 | tf_op jit(solution)/shard_map/all_to_all | solution.py:467
  92.0 0.0 copy-start
  92.0 1.9 %copy-done = f32[3,32,64,128]{3,2,1,0:T(8,128)S(1)} copy-done((f32[3,32,64,128]{3,2,1,0:T(8,128)S(1)}, f32[3,32,64,128]{3,2,1,0:T(8,128)}, u32[]{:S(2)}) %copy-start) | copy-done | bytes 3145752
  93.9 1.8 %join.1 = f32[96,64,128]{2,1,0:T(8,128)} custom-call(f32[96,64,128]{2,1,0:T(8,128)S(1)} %bitcast.6, f32[96,64,128]{2,1,0:T(8,128)S(1)} %bitcast.5), custom_call_target="tpu_custom_call" | custom-call | flops 786432 | bytes 9437184 | tf_op jit(solution)/shard_map/join/pallas_call | solution.py:429
Async XLA Ops:
  0.6 5.3 %copy-start.1 = (f32[3,1,1,4096]{3,2,1,0:T(1,128)S(1)}, f32[3,1,1,4096]{3,2,1,0:T(1,128)}, u32[]{:S(2)}) copy-start(f32[3,1,1,4096]{3,2,1,0:T(1,128)} %spring_ref.5) | copy-start | bytes 147460
  0.6 5.3 %copy-start.3 = (s32[2,1,1,4096]{3,2,1,0:T(1,128)S(1)}, s32[2,1,1,4096]{3,2,1,0:T(1,128)}, u32[]{:S(2)}) copy-start(s32[2,1,1,4096]{3,2,1,0:T(1,128)} %ids_ref.5) | copy-start | bytes 98308
  0.6 43.2 %all-to-all-start = ((f32[8,12,64,128]{3,2,1,0:T(8,128)}), f32[8,12,64,128]{3,2,1,0:T(8,128)S(1)}, u32[]{:S(2)}, u32[]{:S(2)}) async-start(f32[8,12,64,128]{3,2,1,0:T(8,128)} %bitcast.7), calls=%async_computation | async-start | bytes 6291456 | tf_op jit(solution)/shard_map/all_to_all | solution.py:460
  11.7 21.2 %collective-permute-start = (f32[2,3,4,64,128]{4,3,2,1,0:T(8,128)}, f32[2,3,4,64,128]{4,3,2,1,0:T(8,128)}, u32[]{:S(2)}, u32[]{:S(2)}) collective-permute-start(f32[2,3,4,64,128]{4,3,2,1,0:T(8,128)} %get-tuple-element.6.high_edge_ref), channel_id=1, source_target_pairs={{0,1},{1,2},{2,3},{4,5},{5,6},{6,7},{8,9},{9,10},{10,11},{12,13},{... | collective-permute-start | bytes 2359304 | tf_op jit(solution)/shard_map/ppermute | solution.py:450
  16.1 21.9 %collective-permute-start.1 = (f32[2,3,4,64,128]{4,3,2,1,0:T(8,128)}, f32[2,3,4,64,128]{4,3,2,1,0:T(8,128)}, u32[]{:S(2)}, u32[]{:S(2)}) collective-permute-start(f32[2,3,4,64,128]{4,3,2,1,0:T(8,128)} %get-tuple-element.7._.low_edge_ref), channel_id=1, source_target_pairs={{1,0},{2,1},{3,2},{5,4},{6,5},{7,6},{9,8},{10,9},{11,10},{13,12},{... | collective-permute-start | bytes 2359304 | tf_op jit(solution)/shard_map/ppermute | solution.py:451
  17.4 26.5 %copy-start.6 = (f32[32]{0:T(128)S(1)}, f32[32]{0:T(128)}, u32[]{:S(2)}) copy-start(f32[32]{0:T(128)} %coef_ref.1) | copy-start | bytes 388
  50.3 4.0 %copy-start.2 = (f32[3,1,1,4096]{3,2,1,0:T(1,128)S(1)}, f32[3,1,1,4096]{3,2,1,0:T(1,128)}, u32[]{:S(2)}) copy-start(f32[3,1,1,4096]{3,2,1,0:T(1,128)} %noise_ref.1) | copy-start | bytes 147460
  50.3 4.0 %copy-start.4 = (f32[32,32]{1,0:T(8,128)S(1)}, f32[32,32]{1,0:T(8,128)}, u32[]{:S(2)}) copy-start(f32[32,32]{1,0:T(8,128)} %inverse_ref.1) | copy-start | bytes 12292
  50.4 4.0 %copy-start.5 = (f32[9,32]{1,0:T(8,128)S(1)}, f32[9,32]{1,0:T(8,128)}, u32[]{:S(2)}) copy-start(f32[9,32]{1,0:T(8,128)} %stencil_ref.1) | copy-start | bytes 3460
  50.4 41.6 %all-to-all-start.1 = ((f32[8,12,64,128]{3,2,1,0:T(8,128)}), f32[8,12,64,128]{3,2,1,0:T(8,128)S(1)}, u32[]{:S(2)}, u32[]{:S(2)}) async-start(f32[8,12,64,128]{3,2,1,0:T(8,128)} %solve.1), calls=%async_computation.1 | async-start | bytes 6291456 | tf_op jit(solution)/shard_map/all_to_all | solution.py:467
  92.0 1.9 %copy-start = (f32[3,32,64,128]{3,2,1,0:T(8,128)S(1)}, f32[3,32,64,128]{3,2,1,0:T(8,128)}, u32[]{:S(2)}) copy-start(f32[3,32,64,128]{3,2,1,0:T(8,128)} %get-tuple-element.8) | copy-start | bytes 9437188

commit v8 on v7

--- a/solution.py
+++ b/solution.py
@@ -311,13 +311,8 @@
             value = value.astype(np.float32)
             high = value.astype(BF16)
             low = (value - high.astype(np.float32)).astype(BF16)
-            tables.append(np.concatenate([high, low, high], axis=1))
+            tables.append(np.concatenate([high, low], axis=0))
     return np.stack(tables)
-
-
-def product(table, value):
-    high, low = split(value)
-    return dot(table, jnp.concatenate([high, high, low], axis=0))
 
 
 def solve_kernel(coef_ref, first_ref, tables_ref, *refs):
@@ -325,7 +320,7 @@
     blocks, rows, angles, axial = in_ref.shape
     half = blocks * angles // 2
     quarter = half // 2
-    part = rows // out_sems.shape[0]
+    part = math.gcd(rows, 4)
     loads = [
         pltpu.make_async_copy(tables_ref.at[i], table_ref.at[i], table_sems.at[i])
         for i in range(4)
@@ -355,23 +350,22 @@
             field = jnp.concatenate([a - b if odd else a + b for a, b in zip(near, far)], axis=1)
             if g == 0:
                 loads[2 * odd].wait()
-            spectrum = product(table_ref[2 * odd], field)
+            spectrum = dot3(table_ref[2 * odd], *split(field))
             scale = [
                 jnp.broadcast_to(damping[odd][:, q : q + 1], (half, axial)) for q in chosen
             ]
             if g == 0:
                 loads[2 * odd + 1].wait()
             damped = spectrum * jnp.concatenate(scale, axis=1)
-            results.append(product(table_ref[2 * odd + 1], damped))
+            results.append(dot3(table_ref[2 * odd + 1], *split(damped)))
         for i, q in enumerate(chosen):
             even, odd = [value[:, i * axial : (i + 1) * axial] for value in results]
             done_ref[: blocks // 2, q] = (even + odd).reshape(blocks // 2, angles, axial)
             done_ref[blocks // 2 :, q] = (even - odd).reshape(blocks // 2, angles, axial)
-        at = pl.ds(g * part, part)
-        stores.append(
-            pltpu.make_async_copy(done_ref.at[:, at], out_ref.at[:, at], out_sems.at[g])
-        )
-        stores[-1].start()
+            stores.append(
+                pltpu.make_async_copy(done_ref.at[:, q], out_ref.at[:, q], out_sems.at[q])
+            )
+            stores[-1].start()
     for copy in stores:
         copy.wait()
 
@@ -380,7 +374,6 @@
     blocks, rows, angles, axial = field.shape
     all_angles = blocks * angles
     tables = fourier_tables(all_angles)
-    parts = rows // math.gcd(rows, 4)
     smem = pl.BlockSpec(memory_space=pltpu.SMEM)
     whole = pl.BlockSpec(memory_space=pltpu.VMEM)
     unread = pl.BlockSpec(memory_space=pl.ANY)
@@ -393,7 +386,7 @@
             pltpu.VMEM(tables.shape, BF16),
             pltpu.VMEM(field.shape, F32),
             pltpu.SemaphoreType.DMA((4,)),
-            pltpu.SemaphoreType.DMA((parts,)),
+            pltpu.SemaphoreType.DMA((rows,)),
         ],
         compiler_params=pltpu.CompilerParams(vmem_limit_bytes=28 * MIB),
         cost_estimate=pl.CostEstimate(
@@ -411,16 +404,25 @@
     )
 
 
-def join_kernel(force_ref, smooth_ref, out_ref, sum_ref, sems):
-    parts = sems.shape[0]
-    part = force_ref.shape[0] // parts
-    copies = []
-    for i in range(parts):
-        at = pl.ds(i * part, part)
-        sum_ref[at] = force_ref[at] + smooth_ref[at]
-        copies.append(pltpu.make_async_copy(sum_ref.at[at], out_ref.at[at], sems.at[i]))
-        copies[-1].start()
-    for copy in copies:
+def join_kernel(force_ref, smooth_ref, out_ref, sum_ref, in_sems, out_sems):
+    parts = in_sems.shape[0]
+    part = sum_ref.shape[0] // parts
+    spans = [pl.ds(i * part, part) for i in range(parts)]
+    reads = [
+        pltpu.make_async_copy(force_ref.at[at], sum_ref.at[at], in_sems.at[i])
+        for i, at in enumerate(spans)
+    ]
+    writes = [
+        pltpu.make_async_copy(sum_ref.at[at], out_ref.at[at], out_sems.at[i])
+        for i, at in enumerate(spans)
+    ]
+    for copy in reads:
+        copy.start()
+    for i, at in enumerate(spans):
+        reads[i].wait()
+        sum_ref[at] = sum_ref[at] + smooth_ref[at]
+        writes[i].start()
+    for copy in writes:
         copy.wait()
 
 
@@ -428,19 +430,20 @@
     whole = pl.BlockSpec(memory_space=pltpu.VMEM)
     return pl.pallas_call(
         join_kernel,
-        in_specs=[whole, whole],
+        in_specs=[pl.BlockSpec(memory_space=pl.ANY), whole],
         out_specs=pl.BlockSpec(memory_space=pl.ANY),
         out_shape=pltpu.HBM(force.shape, F32),
         scratch_shapes=[
             pltpu.VMEM(force.shape, F32),
-            pltpu.SemaphoreType.DMA((math.gcd(force.shape[0], 8),)),
+            pltpu.SemaphoreType.DMA((math.gcd(force.shape[0], 16),)),
+            pltpu.SemaphoreType.DMA((math.gcd(force.shape[0], 16),)),
         ],
         compiler_params=pltpu.CompilerParams(vmem_limit_bytes=14 * MIB),
         cost_estimate=pl.CostEstimate(
             flops=force.size, bytes_accessed=12 * force.size, transcendentals=0
         ),
         name="join",
-    )(in_vmem(force), in_vmem(smooth))
+    )(in_hbm(force), in_vmem(smooth))
 
 
 def from_neighbours(low_edge, high_edge):

time: 96.3 us -> 95.8 us (level)
  local copies, waits for them, and re-layouts: 1.92 us -> 0.03 us
  Pallas kernels: 53.1 us -> 54.5 us
    unnamed x14 -> x12, local copies, waits for them, and re-layouts: 1.92 us -> 0.03 us
    pallas_call x1, Pallas kernels: 1.76 us -> 3.14 us  [join(): pl.pallas_call(join_kernel, in_specs=[pl.BlockSpec(memory_space=pl.ANY),...]
where the time goes in v8:
time: 95.8 us; the launch traced here: 95.4 us
  Pallas kernels  54.5 us (57%)
  waiting for transfers between devices  25 us (26%)
  starting transfers between devices  14.9 us (16%)
    pallas_call x1, Pallas kernels, move(): pl.pallas_call(move_kernel, in_specs=[whole] * 11, out_specs=[whole, whol...  26.5 us
    pallas_call x1, Pallas kernels, deposit_middle(): pl.pallas_call(lambda ids_ref, spring_ref, _, *refs: middle_kernel(ids_re...  12.6 us
    all_to_all x1, waiting for transfers between devices, per_device(): smooth = lax.all_to_all(solved, 'az', 0, 0, tiled=True)  11.1 us
    pallas_call x1, Pallas kernels, solve(): pl.pallas_call(solve_kernel, in_specs=[smem, smem, unread] + [unread] * l...  6.55 us
    all_to_all x1, waiting for transfers between devices, per_device(): gathered = lax.all_to_all(pieces, 'az', 0, 0, tiled=True)  5.91 us
    pallas_call x1, Pallas kernels, deposit_edges(): pl.pallas_call(functools.partial(edge_kernel, radii=radii), grid=(1,), in...  5.73 us
    all_to_all x1, starting transfers between devices, per_device(): gathered = lax.all_to_all(pieces, 'az', 0, 0, tiled=True)  5.31 us
    ppermute x1, waiting for transfers between devices, from_neighbours(): high = lax.ppermute(low_edge, 'rad', backward)  4.98 us
  transfers between devices with their start and end apart: 4, of which 4 were waited for; matrix products, arithmetic and copies ran while one was open for 0% of the time, Pallas kernels for 47%

profile of v8, /device:TPU:0, one launch (start us, length us, event | category | flops | bytes accessed | tf_op | source)
XLA Modules:
  0.0 95.4 jit_solution(16737696667941842585)
XLA Ops:
  0.6 0.0 copy-start
  0.6 0.0 copy-start.2
  0.6 5.3 %all-to-all-start = ((f32[8,12,64,128]{3,2,1,0:T(8,128)}), f32[8,12,64,128]{3,2,1,0:T(8,128)S(1)}, u32[]{:S(2)}, u32[]{:S(2)}) async-start(f32[8,12,64,128]{3,2,1,0:T(8,128)} %bitcast.6), calls=%async_computation | async-start | bytes 6291456 | tf_op jit(solution)/shard_map/all_to_all | solution.py:463
  6.0 0.0 copy-done
  6.0 0.0 copy-done.2
  6.0 5.7 %deposit_edges.1 = (f32[2,3,4,64,128]{4,3,2,1,0:T(8,128)}, f32[2,3,4,64,128]{4,3,2,1,0:T(8,128)}) custom-call(s32[2,1,1,4096]{3,2,1,0:T(1,128)S(1)} %copy-done.2, f32[3,1,1,4096]{3,2,1,0:T(1,128)S(1)} %copy-done, f32[3,32,64,128]{3,2,1,0:T(8,128)} %velocity_ref.1, f32[3,32,64,128]{3,2,1,0:T(8,128)} %velocity_ref.1), custom_call_target="tpu_custom_call" | custom-call | flops 3221225472 | bytes 3145728 | tf_op jit(solution)/shard_map/deposit_edges/pallas_call | solution.py:112
  11.7 4.4 %collective-permute-start = (f32[2,3,4,64,128]{4,3,2,1,0:T(8,128)}, f32[2,3,4,64,128]{4,3,2,1,0:T(8,128)}, u32[]{:S(2)}, u32[]{:S(2)}) collective-permute-start(f32[2,3,4,64,128]{4,3,2,1,0:T(8,128)} %get-tuple-element.6.high_edge_ref), channel_id=1, source_target_pairs={{0,1},{1,2},{2,3},{4,5},{5,6},{6,7},{8,9},{9,10},{10,11},{12,13},{... | collective-permute-start | bytes 2359304 | tf_op jit(solution)/shard_map/ppermute | solution.py:453
  16.1 1.3 %collective-permute-start.1 = (f32[2,3,4,64,128]{4,3,2,1,0:T(8,128)}, f32[2,3,4,64,128]{4,3,2,1,0:T(8,128)}, u32[]{:S(2)}, u32[]{:S(2)}) collective-permute-start(f32[2,3,4,64,128]{4,3,2,1,0:T(8,128)} %get-tuple-element.7._.low_edge_ref), channel_id=1, source_target_pairs={{1,0},{2,1},{3,2},{5,4},{6,5},{7,6},{9,8},{10,9},{11,10},{13,12},{... | collective-permute-start | bytes 2359304 | tf_op jit(solution)/shard_map/ppermute | solution.py:454
  17.4 0.0 copy-start.5
  17.4 12.6 %deposit_middle.1.middle_ref.refs_2_ = f32[3,24,64,128]{3,2,1,0:T(8,128)} custom-call(s32[2,1,1,4096]{3,2,1,0:T(1,128)S(1)} %copy-done.2, f32[3,1,1,4096]{3,2,1,0:T(1,128)S(1)} %copy-done, f32[2,3,4,64,128]{4,3,2,1,0:T(8,128)} %get-tuple-element.7._.low_edge_ref), custom_call_target="tpu_custom_call" | custom-call | flops 9663676416 | bytes 2359296 | tf_op jit(solution)/shard_map/deposit_middle/pallas_call | solution.py:140
  30.0 3.0 %collective-permute-done.low_ref.refs_0_ = f32[2,3,4,64,128]{4,3,2,1,0:T(8,128)} collective-permute-done((f32[2,3,4,64,128]{4,3,2,1,0:T(8,128)}, f32[2,3,4,64,128]{4,3,2,1,0:T(8,128)}, u32[]{:S(2)}, u32[]{:S(2)}) %collective-permute-start) | collective-permute-done | bytes 786464 | tf_op jit(solution)/shard_map/ppermute | solution.py:453
  33.0 5.0 %collective-permute-done.1.high_ref.refs_1_ = f32[2,3,4,64,128]{4,3,2,1,0:T(8,128)} collective-permute-done((f32[2,3,4,64,128]{4,3,2,1,0:T(8,128)}, f32[2,3,4,64,128]{4,3,2,1,0:T(8,128)}, u32[]{:S(2)}, u32[]{:S(2)}) %collective-permute-start.1) | collective-permute-done | bytes 786464 | tf_op jit(solution)/shard_map/ppermute | solution.py:454
  37.9 5.9 %all-to-all-done.refs_3_ = f32[8,12,64,128]{3,2,1,0:T(8,128)S(1)} async-done(((f32[8,12,64,128]{3,2,1,0:T(8,128)}), f32[8,12,64,128]{3,2,1,0:T(8,128)S(1)}, u32[]{:S(2)}, u32[]{:S(2)}) %all-to-all-start) | async-done | bytes 3145760 | tf_op jit(solution)/shard_map/all_to_all | solution.py:463
  43.8 0.0 copy-done.5
  43.8 6.6 %solve.1 = f32[8,12,64,128]{3,2,1,0:T(8,128)} custom-call(f32[32]{0:T(128)S(1)} %copy-done.5, s32[1]{0:T(128)} %bitcast.1.first_ref, bf16[4,512,256]{2,1,0:T(8,128)(2,1)} %constant.10.clone.tables_ref, f32[2,3,4,64,128]{4,3,2,1,0:T(8,128)} %collective-permute-done.low_ref.refs_0_, f32[2,3,4,64,128]{4,3,2,1,0:T(8,128)} %collective-permute-done.1.high_ref.refs_1_, ...), custom_call_target="tpu_custom_call" | custom-call | flops 4831838208 | bytes 6291456 | tf_op jit(solution)/shard_map/solve/pallas_call | solution.py:380
  50.4 0.0 copy-start.1
  50.4 0.0 copy-start.3
  50.4 0.0 copy-start.4
  50.4 4.0 %all-to-all-start.1 = ((f32[8,12,64,128]{3,2,1,0:T(8,128)}), f32[8,12,64,128]{3,2,1,0:T(8,128)S(1)}, u32[]{:S(2)}, u32[]{:S(2)}) async-start(f32[8,12,64,128]{3,2,1,0:T(8,128)} %solve.1), calls=%async_computation.1 | async-start | bytes 6291456 | tf_op jit(solution)/shard_map/all_to_all | solution.py:470
  54.4 0.0 copy-done.1
  54.4 0.0 copy-done.3
  54.4 0.0 copy-done.4
  54.5 26.5 %move.1 = (f32[3,1,1,4096]{3,2,1,0:T(1,128)}, f32[3,32,64,128]{3,2,1,0:T(8,128)}) custom-call(f32[9,32]{1,0:T(8,128)S(1)} %copy-done.4, f32[32,32]{1,0:T(8,128)S(1)} %copy-done.3, f32[2,3,4,64,128]{4,3,2,1,0:T(8,128)} %collective-permute-done.low_ref.refs_0_, f32[3,32,64,128]{3,2,1,0:T(8,128)} %velocity_ref.1, ...), custom_call_target="tpu_custom_call" | custom-call | flops 15032385536 | bytes 10485760 | tf_op jit(solution)/shard_map/move/pallas_call | solution.py:261
  80.9 11.1 %all-to-all-done.1 = f32[8,12,64,128]{3,2,1,0:T(8,128)S(1)} async-done(((f32[8,12,64,128]{3,2,1,0:T(8,128)}), f32[8,12,64,128]{3,2,1,0:T(8,128)S(1)}, u32[]{:S(2)}, u32[]{:S(2)}) %all-to-all-start.1) | async-done | bytes 3145760 | tf_op jit(solution)/shard_map/all_to_all | solution.py:470
  92.1 3.1 %join.1 = f32[96,64,128]{2,1,0:T(8,128)} custom-call(f32[96,64,128]{2,1,0:T(8,128)} %bitcast.7, f32[96,64,128]{2,1,0:T(8,128)S(1)} %bitcast.5), custom_call_target="tpu_custom_call" | custom-call | flops 786432 | bytes 9437184 | tf_op jit(solution)/shard_map/join/pallas_call | solution.py:431
Async XLA Ops:
  0.6 5.3 %copy-start = (f32[3,1,1,4096]{3,2,1,0:T(1,128)S(1)}, f32[3,1,1,4096]{3,2,1,0:T(1,128)}, u32[]{:S(2)}) copy-start(f32[3,1,1,4096]{3,2,1,0:T(1,128)} %spring_ref.5) | copy-start | bytes 147460
  0.6 5.3 %copy-start.2 = (s32[2,1,1,4096]{3,2,1,0:T(1,128)S(1)}, s32[2,1,1,4096]{3,2,1,0:T(1,128)}, u32[]{:S(2)}) copy-start(s32[2,1,1,4096]{3,2,1,0:T(1,128)} %ids_ref.5) | copy-start | bytes 98308
  0.6 43.2 %all-to-all-start = ((f32[8,12,64,128]{3,2,1,0:T(8,128)}), f32[8,12,64,128]{3,2,1,0:T(8,128)S(1)}, u32[]{:S(2)}, u32[]{:S(2)}) async-start(f32[8,12,64,128]{3,2,1,0:T(8,128)} %bitcast.6), calls=%async_computation | async-start | bytes 6291456 | tf_op jit(solution)/shard_map/all_to_all | solution.py:463
  11.7 21.2 %collective-permute-start = (f32[2,3,4,64,128]{4,3,2,1,0:T(8,128)}, f32[2,3,4,64,128]{4,3,2,1,0:T(8,128)}, u32[]{:S(2)}, u32[]{:S(2)}) collective-permute-start(f32[2,3,4,64,128]{4,3,2,1,0:T(8,128)} %get-tuple-element.6.high_edge_ref), channel_id=1, source_target_pairs={{0,1},{1,2},{2,3},{4,5},{5,6},{6,7},{8,9},{9,10},{10,11},{12,13},{... | collective-permute-start | bytes 2359304 | tf_op jit(solution)/shard_map/ppermute | solution.py:453
  16.1 21.9 %collective-permute-start.1 = (f32[2,3,4,64,128]{4,3,2,1,0:T(8,128)}, f32[2,3,4,64,128]{4,3,2,1,0:T(8,128)}, u32[]{:S(2)}, u32[]{:S(2)}) collective-permute-start(f32[2,3,4,64,128]{4,3,2,1,0:T(8,128)} %get-tuple-element.7._.low_edge_ref), channel_id=1, source_target_pairs={{1,0},{2,1},{3,2},{5,4},{6,5},{7,6},{9,8},{10,9},{11,10},{13,12},{... | collective-permute-start | bytes 2359304 | tf_op jit(solution)/shard_map/ppermute | solution.py:454
  17.4 26.5 %copy-start.5 = (f32[32]{0:T(128)S(1)}, f32[32]{0:T(128)}, u32[]{:S(2)}) copy-start(f32[32]{0:T(128)} %coef_ref.1) | copy-start | bytes 388
  50.4 4.0 %copy-start.1 = (f32[3,1,1,4096]{3,2,1,0:T(1,128)S(1)}, f32[3,1,1,4096]{3,2,1,0:T(1,128)}, u32[]{:S(2)}) copy-start(f32[3,1,1,4096]{3,2,1,0:T(1,128)} %noise_ref.1) | copy-start | bytes 147460
  50.4 4.0 %copy-start.3 = (f32[32,32]{1,0:T(8,128)S(1)}, f32[32,32]{1,0:T(8,128)}, u32[]{:S(2)}) copy-start(f32[32,32]{1,0:T(8,128)} %inverse_ref.1) | copy-start | bytes 12292
  50.4 4.0 %copy-start.4 = (f32[9,32]{1,0:T(8,128)S(1)}, f32[9,32]{1,0:T(8,128)}, u32[]{:S(2)}) copy-start(f32[9,32]{1,0:T(8,128)} %stencil_ref.1) | copy-start | bytes 3460
  50.4 41.6 %all-to-all-start.1 = ((f32[8,12,64,128]{3,2,1,0:T(8,128)}), f32[8,12,64,128]{3,2,1,0:T(8,128)S(1)}, u32[]{:S(2)}, u32[]{:S(2)}) async-start(f32[8,12,64,128]{3,2,1,0:T(8,128)} %solve.1), calls=%async_computation.1 | async-start | bytes 6291456 | tf_op jit(solution)/shard_map/all_to_all | solution.py:470

commit v9 on v8

--- a/solution.py
+++ b/solution.py
@@ -315,9 +315,11 @@
     return np.stack(tables)
 
 
-def solve_kernel(coef_ref, first_ref, tables_ref, *refs):
-    in_ref, out_ref, table_ref, done_ref, table_sems, out_sems = refs[-6:]
+def solve_kernel(coef_ref, me_ref, tables_ref, *refs, extra):
+    in_ref, refs = refs[extra], refs[extra + 1 :]
     blocks, rows, angles, axial = in_ref.shape
+    out_refs = refs[:blocks]
+    table_ref, done_ref, table_sems, out_sems = refs[blocks:]
     half = blocks * angles // 2
     quarter = half // 2
     part = math.gcd(rows, 4)
@@ -328,7 +330,7 @@
     for copy in loads:
         copy.start()
 
-    base = first_ref[0]
+    base = me_ref[0] * rows
     lane = iota((1, axial), 1)
     coef = jnp.zeros((1, axial), F32)
     for q in range(rows):
@@ -362,15 +364,19 @@
             even, odd = [value[:, i * axial : (i + 1) * axial] for value in results]
             done_ref[: blocks // 2, q] = (even + odd).reshape(blocks // 2, angles, axial)
             done_ref[blocks // 2 :, q] = (even - odd).reshape(blocks // 2, angles, axial)
+        at = pl.ds(g * part, part)
+        for s in range(blocks):
             stores.append(
-                pltpu.make_async_copy(done_ref.at[:, q], out_ref.at[:, q], out_sems.at[q])
+                pltpu.make_async_copy(
+                    done_ref.at[me_ref[0] ^ s, at], out_refs[s].at[at], out_sems.at[g, s]
+                )
             )
             stores[-1].start()
     for copy in stores:
         copy.wait()
 
 
-def solve(coef, first, field, after):
+def solve(coef, me, field, after):
     blocks, rows, angles, axial = field.shape
     all_angles = blocks * angles
     tables = fourier_tables(all_angles)
@@ -378,15 +384,15 @@
     whole = pl.BlockSpec(memory_space=pltpu.VMEM)
     unread = pl.BlockSpec(memory_space=pl.ANY)
     return pl.pallas_call(
-        solve_kernel,
+        functools.partial(solve_kernel, extra=len(after)),
         in_specs=[smem, smem, unread] + [unread] * len(after) + [whole],
-        out_specs=unread,
-        out_shape=pltpu.HBM(field.shape, F32),
+        out_specs=[unread] * blocks,
+        out_shape=[pltpu.HBM(field.shape[1:], F32)] * blocks,
         scratch_shapes=[
             pltpu.VMEM(tables.shape, BF16),
             pltpu.VMEM(field.shape, F32),
             pltpu.SemaphoreType.DMA((4,)),
-            pltpu.SemaphoreType.DMA((rows,)),
+            pltpu.SemaphoreType.DMA((rows // math.gcd(rows, 4), blocks)),
         ],
         compiler_params=pltpu.CompilerParams(vmem_limit_bytes=28 * MIB),
         cost_estimate=pl.CostEstimate(
@@ -397,53 +403,71 @@
         name="solve",
     )(
         coef,
-        first,
+        me,
         in_hbm(jnp.asarray(tables)),
         *after,
         in_vmem(field),
     )
 
 
-def join_kernel(force_ref, smooth_ref, out_ref, sum_ref, in_sems, out_sems):
-    parts = in_sems.shape[0]
-    part = sum_ref.shape[0] // parts
-    spans = [pl.ds(i * part, part) for i in range(parts)]
-    reads = [
-        pltpu.make_async_copy(force_ref.at[at], sum_ref.at[at], in_sems.at[i])
-        for i, at in enumerate(spans)
-    ]
-    writes = [
-        pltpu.make_async_copy(sum_ref.at[at], out_ref.at[at], out_sems.at[i])
-        for i, at in enumerate(spans)
-    ]
+def join_kernel(me_ref, force_ref, own_ref, *refs):
+    count = len(refs) - 4
+    piece_refs, (out_ref, sum_ref, in_sems, out_sems) = refs[:count], refs[count:]
+    blocks, rows = sum_ref.shape[0] - 1, sum_ref.shape[1]
+    me = me_ref[0]
+    reads, writes = [], []
+    for s in range(blocks):
+        at = pl.ds((me ^ s) * rows, rows)
+        reads.append(
+            pltpu.make_async_copy(force_ref.at[at], sum_ref.at[s], in_sems.at[s])
+        )
+        writes.append(
+            pltpu.make_async_copy(sum_ref.at[s], out_ref.at[at], out_sems.at[s])
+        )
+    own = pltpu.make_async_copy(own_ref, sum_ref.at[blocks], in_sems.at[blocks])
+    own.start()
     for copy in reads:
         copy.start()
-    for i, at in enumerate(spans):
-        reads[i].wait()
-        sum_ref[at] = sum_ref[at] + smooth_ref[at]
-        writes[i].start()
+    own.wait()
+    for s in range(blocks):
+        reads[s].wait()
+        piece = sum_ref[blocks] if s == 0 else piece_refs[s - 1][...]
+        sum_ref[s] = sum_ref[s] + piece
+        writes[s].start()
     for copy in writes:
         copy.wait()
 
 
-def join(force, smooth):
+def join(me, force, pieces):
+    rows, angles, axial = pieces[0].shape
+    blocks = len(pieces)
     whole = pl.BlockSpec(memory_space=pltpu.VMEM)
+    away = pl.BlockSpec(memory_space=pl.ANY)
     return pl.pallas_call(
         join_kernel,
-        in_specs=[pl.BlockSpec(memory_space=pl.ANY), whole],
-        out_specs=pl.BlockSpec(memory_space=pl.ANY),
+        in_specs=[pl.BlockSpec(memory_space=pltpu.SMEM), away, away] + [whole] * (blocks - 1),
+        out_specs=away,
         out_shape=pltpu.HBM(force.shape, F32),
         scratch_shapes=[
-            pltpu.VMEM(force.shape, F32),
-            pltpu.SemaphoreType.DMA((math.gcd(force.shape[0], 16),)),
-            pltpu.SemaphoreType.DMA((math.gcd(force.shape[0], 16),)),
+            pltpu.VMEM((blocks + 1, rows, angles, axial), F32),
+            pltpu.SemaphoreType.DMA((blocks + 1,)),
+            pltpu.SemaphoreType.DMA((blocks,)),
         ],
         compiler_params=pltpu.CompilerParams(vmem_limit_bytes=14 * MIB),
         cost_estimate=pl.CostEstimate(
             flops=force.size, bytes_accessed=12 * force.size, transcendentals=0
         ),
         name="join",
-    )(in_hbm(force), in_vmem(smooth))
+    )(me, in_hbm(force), in_hbm(pieces[0]), *[in_vmem(piece) for piece in pieces[1:]])
+
+
+def exchange(pieces):
+    count = len(pieces)
+    received = [pieces[0]] + [None] * (count - 1)
+    order = list(range(2, count, 2)) + list(range(3, count, 2)) + [1]
+    for s in order:
+        received[s] = lax.ppermute(pieces[s], "az", [(i, i ^ s) for i in range(count)])
+    return received
 
 
 def from_neighbours(low_edge, high_edge):
@@ -465,14 +489,14 @@
     low, high = from_neighbours(low_edge, high_edge)
     middle = deposit_middle(cell_ids, dumbbells, low_edge, velocity.shape)
     stress = (low_edge, middle, high_edge)
-    first = (lax.axis_index("az") * rows).astype(jnp.int32).reshape(1)
-    solved = solve(azim_coef, first, gathered, (in_vmem(low), in_vmem(high), in_hbm(middle)))
-    smooth = lax.all_to_all(solved, "az", 0, 0, tiled=True)
+    me = lax.axis_index("az").astype(jnp.int32).reshape(1)
+    solved = solve(azim_coef, me, gathered, (in_vmem(low), in_vmem(high), in_hbm(middle)))
+    pieces = exchange(solved)
     moved, force = move(
         stencil_coef, block_inverse, low, velocity, stress, high, cell_ids, dumbbells, brownian
     )
     lines = (3 * radii, angles, axial)
-    result = join(force.reshape(lines), smooth.reshape(lines))
+    result = join(me, force.reshape(lines), pieces)
     return result.reshape(velocity.shape), moved
 
 

time: 95.8 us -> 92.9 us (0.970)
  waiting for transfers between devices: 25 us -> 20.9 us
  starting transfers between devices: 14.9 us -> 16.3 us
    all_to_all x1 -> x0, waiting for transfers between devices: 11.1 us -> none  [per_device(): smooth = lax.all_to_all(solved, 'az', 0, 0, tiled=True)]
    ppermute x0 -> x7, waiting for transfers between devices: none -> 8.05 us  [exchange(): lax.ppermute(pieces[s], 'az', [(i, i ^ s) for i in range(count)])]
    ppermute x0 -> x7, starting transfers between devices: none -> 4.23 us  [exchange(): lax.ppermute(pieces[s], 'az', [(i, i ^ s) for i in range(count)])]
    all_to_all x1 -> x0, starting transfers between devices: 3.97 us -> none  [per_device(): smooth = lax.all_to_all(solved, 'az', 0, 0, tiled=True)]
    all_to_all x1, waiting for transfers between devices: 5.91 us -> 8.83 us  [per_device(): gathered = lax.all_to_all(pieces, 'az', 0, 0, tiled=True)]
    ppermute x1, waiting for transfers between devices: 4.98 us -> 2.83 us  [from_neighbours(): high = lax.ppermute(low_edge, 'rad', backward)]
    ppermute x1, waiting for transfers between devices: 2.97 us -> 1.18 us  [from_neighbours(): low = lax.ppermute(high_edge, 'rad', forward)]
    ppermute x1, starting transfers between devices: 4.36 us -> 5.46 us  [from_neighbours(): low = lax.ppermute(high_edge, 'rad', forward)]
  transfers between devices with their start and end apart: 4 -> 10, of which waited for: 4 -> 4; matrix products, arithmetic and copies ran while one was open for 0% -> 0% of each run, Pallas kernels for 47% -> 48%
where the time goes in v9:
time: 92.9 us; the launch traced here: 92.4 us
  Pallas kernels  54.3 us (58%)
  waiting for transfers between devices  20.9 us (22%)
  starting transfers between devices  16.3 us (18%)
    pallas_call x1, Pallas kernels, move(): pl.pallas_call(move_kernel, in_specs=[whole] * 11, out_specs=[whole, whol...  26.5 us
    pallas_call x1, Pallas kernels, deposit_middle(): pl.pallas_call(lambda ids_ref, spring_ref, _, *refs: middle_kernel(ids_re...  12.6 us
    all_to_all x1, waiting for transfers between devices, per_device(): gathered = lax.all_to_all(pieces, 'az', 0, 0, tiled=True)  8.83 us
    ppermute x7, waiting for transfers between devices, exchange(): lax.ppermute(pieces[s], 'az', [(i, i ^ s) for i in range(count)])  8.05 us
    pallas_call x1, Pallas kernels, solve(): pl.pallas_call(functools.partial(solve_kernel, extra=len(after)), in_spec...  6.56 us
    pallas_call x1, Pallas kernels, deposit_edges(): pl.pallas_call(functools.partial(edge_kernel, radii=radii), grid=(1,), in...  5.71 us
    ppermute x1, starting transfers between devices, from_neighbours(): low = lax.ppermute(high_edge, 'rad', forward)  5.46 us
    all_to_all x1, starting transfers between devices, per_device(): gathered = lax.all_to_all(pieces, 'az', 0, 0, tiled=True)  5.31 us
  transfers between devices with their start and end apart: 10, of which 4 were waited for; matrix products, arithmetic and copies ran while one was open for 0% of the time, Pallas kernels for 48%

profile of v9, /device:TPU:0, one launch (start us, length us, event | category | flops | bytes accessed | tf_op | source)
XLA Modules:
  0.0 92.4 jit_solution(16179934048222308679)
XLA Ops:
  0.6 0.0 copy-start
  0.6 0.0 copy-start.2
  0.6 5.3 %all-to-all-start = ((f32[8,12,64,128]{3,2,1,0:T(8,128)}), f32[8,12,64,128]{3,2,1,0:T(8,128)S(1)}, u32[]{:S(2)}, u32[]{:S(2)}) async-start(f32[8,12,64,128]{3,2,1,0:T(8,128)} %bitcast.4), calls=%async_computation | async-start | bytes 6291456 | tf_op jit(solution)/shard_map/all_to_all | solution.py:487
  6.0 0.0 copy-done
  6.0 0.0 copy-done.2
  6.0 5.7 %deposit_edges.1 = (f32[2,3,4,64,128]{4,3,2,1,0:T(8,128)}, f32[2,3,4,64,128]{4,3,2,1,0:T(8,128)}) custom-call(s32[2,1,1,4096]{3,2,1,0:T(1,128)S(1)} %copy-done.2, f32[3,1,1,4096]{3,2,1,0:T(1,128)S(1)} %copy-done, f32[3,32,64,128]{3,2,1,0:T(8,128)} %velocity_ref.1, f32[3,32,64,128]{3,2,1,0:T(8,128)} %velocity_ref.1), custom_call_target="tpu_custom_call" | custom-call | flops 3221225472 | bytes 3145728 | tf_op jit(solution)/shard_map/deposit_edges/pallas_call | solution.py:112
  11.7 1.3 %collective-permute-start.1 = (f32[2,3,4,64,128]{4,3,2,1,0:T(8,128)}, f32[2,3,4,64,128]{4,3,2,1,0:T(8,128)}, u32[]{:S(2)}, u32[]{:S(2)}) collective-permute-start(f32[2,3,4,64,128]{4,3,2,1,0:T(8,128)} %get-tuple-element.15._.low_edge_ref), channel_id=1, source_target_pairs={{1,0},{2,1},{3,2},{5,4},{6,5},{7,6},{9,8},{10,9},{11,10},{13,12},{... | collective-permute-start | bytes 2359304 | tf_op jit(solution)/shard_map/ppermute | solution.py:478
  13.0 5.5 %collective-permute-start = (f32[2,3,4,64,128]{4,3,2,1,0:T(8,128)}, f32[2,3,4,64,128]{4,3,2,1,0:T(8,128)}, u32[]{:S(2)}, u32[]{:S(2)}) collective-permute-start(f32[2,3,4,64,128]{4,3,2,1,0:T(8,128)} %get-tuple-element.14.high_edge_ref), channel_id=1, source_target_pairs={{0,1},{1,2},{2,3},{4,5},{5,6},{6,7},{8,9},{9,10},{10,11},{12,13},{... | collective-permute-start | bytes 2359304 | tf_op jit(solution)/shard_map/ppermute | solution.py:477
  18.4 12.6 %deposit_middle.1.middle_ref.refs_2_ = f32[3,24,64,128]{3,2,1,0:T(8,128)} custom-call(s32[2,1,1,4096]{3,2,1,0:T(1,128)S(1)} %copy-done.2, f32[3,1,1,4096]{3,2,1,0:T(1,128)S(1)} %copy-done, f32[2,3,4,64,128]{4,3,2,1,0:T(8,128)} %get-tuple-element.15._.low_edge_ref), custom_call_target="tpu_custom_call" | custom-call | flops 9663676416 | bytes 2359296 | tf_op jit(solution)/shard_map/deposit_middle/pallas_call | solution.py:140
  31.0 2.8 %collective-permute-done.1.high_ref.refs_1_ = f32[2,3,4,64,128]{4,3,2,1,0:T(8,128)} collective-permute-done((f32[2,3,4,64,128]{4,3,2,1,0:T(8,128)}, f32[2,3,4,64,128]{4,3,2,1,0:T(8,128)}, u32[]{:S(2)}, u32[]{:S(2)}) %collective-permute-start.1) | collective-permute-done | bytes 786464 | tf_op jit(solution)/shard_map/ppermute | solution.py:478
  33.8 1.2 %collective-permute-done.low_ref.refs_0_ = f32[2,3,4,64,128]{4,3,2,1,0:T(8,128)} collective-permute-done((f32[2,3,4,64,128]{4,3,2,1,0:T(8,128)}, f32[2,3,4,64,128]{4,3,2,1,0:T(8,128)}, u32[]{:S(2)}, u32[]{:S(2)}) %collective-permute-start) | collective-permute-done | bytes 786464 | tf_op jit(solution)/shard_map/ppermute | solution.py:477
  35.0 8.8 %all-to-all-done.refs_3_ = f32[8,12,64,128]{3,2,1,0:T(8,128)S(1)} async-done(((f32[8,12,64,128]{3,2,1,0:T(8,128)}), f32[8,12,64,128]{3,2,1,0:T(8,128)S(1)}, u32[]{:S(2)}, u32[]{:S(2)}) %all-to-all-start) | async-done | bytes 3145760 | tf_op jit(solution)/shard_map/all_to_all | solution.py:487
  43.8 0.0 copy-done.5
  43.9 6.6 %solve.1 = (f32[12,64,128]{2,1,0:T(8,128)}, f32[12,64,128]{2,1,0:T(8,128)}, f32[12,64,128]{2,1,0:T(8,128)}, f32[12,64,128]{2,1,0:T(8,128)}, f32[12,64,128]{2,1,0...) custom-call(f32[32]{0:T(128)S(1)} %copy-done.5, s32[1]{0:T(128)} %bitcast.me_ref, ...), custom_call_target="tpu_custom_call" | custom-call | flops 4831838208 | bytes 6291456 | tf_op jit(solution)/shard_map/solve/pallas_call | solution.py:386
  50.4 0.1 collective-permute-start.2
  50.5 0.6 collective-permute-start.3
  51.1 1.3 %collective-permute-start.4 = (f32[12,64,128]{2,1,0:T(8,128)}, f32[12,64,128]{2,1,0:T(8,128)S(1)}, u32[]{:S(2)}, u32[]{:S(2)}) collective-permute-start(f32[12,64,128]{2,1,0:T(8,128)} %get-tuple-element.20), channel_id=1, source_target_pairs={{0,12},{4,8},{8,4},{12,0},{16,28},{20,24},{24,20},{28,16},{1,13},{... | collective-permute-start | bytes 1179656 | tf_op jit(solution)/shard_map/ppermute | solution.py:469
  52.4 0.6 collective-permute-start.5
  52.9 1.1 %collective-permute-start.6 = (f32[12,64,128]{2,1,0:T(8,128)}, f32[12,64,128]{2,1,0:T(8,128)S(1)}, u32[]{:S(2)}, u32[]{:S(2)}) collective-permute-start(f32[12,64,128]{2,1,0:T(8,128)} %get-tuple-element.22), channel_id=1, source_target_pairs={{0,20},{4,16},{8,28},{12,24},{16,4},{20,0},{24,12},{28,8},{1,21},{... | collective-permute-start | bytes 1179656 | tf_op jit(solution)/shard_map/ppermute | solution.py:469
  54.1 0.0 collective-permute-done.2.refs_0_
  54.1 0.6 collective-permute-start.7
  54.7 8.0 %collective-permute-done.3.refs_1_ = f32[12,64,128]{2,1,0:T(8,128)S(1)} collective-permute-done((f32[12,64,128]{2,1,0:T(8,128)}, f32[12,64,128]{2,1,0:T(8,128)S(1)}, u32[]{:S(2)}, u32[]{:S(2)}) %collective-permute-start.3) | collective-permute-done | bytes 393248 | tf_op jit(solution)/shard_map/ppermute | solution.py:469
  62.7 0.0 collective-permute-start.8
  62.7 0.0 copy-done.1
  62.7 0.0 copy-done.3
  62.7 26.5 %move.1 = (f32[3,1,1,4096]{3,2,1,0:T(1,128)}, f32[3,32,64,128]{3,2,1,0:T(8,128)}) custom-call(f32[9,32]{1,0:T(8,128)S(1)} %copy-done.4, f32[32,32]{1,0:T(8,128)S(1)} %copy-done.3, f32[2,3,4,64,128]{4,3,2,1,0:T(8,128)} %collective-permute-done.low_ref.refs_0_, f32[3,32,64,128]{3,2,1,0:T(8,128)} %velocity_ref.1, ...), custom_call_target="tpu_custom_call" | custom-call | flops 15032385536 | bytes 10485760 | tf_op jit(solution)/shard_map/move/pallas_call | solution.py:261
  89.2 0.0 collective-permute-done.4.refs_2_
  89.2 0.0 collective-permute-done.5.refs_3_
  89.2 0.0 collective-permute-done.6.refs_4_
  89.2 0.0 collective-permute-done.7.refs_5_
  89.2 0.0 collective-permute-done.8.refs_6_
  89.2 3.0 %join.1 = f32[96,64,128]{2,1,0:T(8,128)} custom-call(s32[1]{0:T(128)} %bitcast.me_ref, f32[96,64,128]{2,1,0:T(8,128)} %bitcast.5, f32[12,64,128]{2,1,0:T(8,128)} %get-tuple-element.17.own_ref, f32[12,64,128]{2,1,0:T(8,128)S(1)} %collective-permute-done.2.refs_0_, f32[12,64,128]{2,1,0:T(8,128)S(1)} %collective-permute-done.3.refs_1_, ...), custom_call_target="tpu_custom_call" | custom-call | flops 786432 | bytes 9437184 | tf_op jit(solution)/shard_map/join/pallas_call | solution.py:446
  (5 shorter events, 0.0 us)
Async XLA Ops:
  0.6 5.3 %copy-start = (f32[3,1,1,4096]{3,2,1,0:T(1,128)S(1)}, f32[3,1,1,4096]{3,2,1,0:T(1,128)}, u32[]{:S(2)}) copy-start(f32[3,1,1,4096]{3,2,1,0:T(1,128)} %spring_ref.5) | copy-start | bytes 147460
  0.6 5.3 %copy-start.2 = (s32[2,1,1,4096]{3,2,1,0:T(1,128)S(1)}, s32[2,1,1,4096]{3,2,1,0:T(1,128)}, u32[]{:S(2)}) copy-start(s32[2,1,1,4096]{3,2,1,0:T(1,128)} %ids_ref.5) | copy-start | bytes 98308
  0.6 43.2 %all-to-all-start = ((f32[8,12,64,128]{3,2,1,0:T(8,128)}), f32[8,12,64,128]{3,2,1,0:T(8,128)S(1)}, u32[]{:S(2)}, u32[]{:S(2)}) async-start(f32[8,12,64,128]{3,2,1,0:T(8,128)} %bitcast.4), calls=%async_computation | async-start | bytes 6291456 | tf_op jit(solution)/shard_map/all_to_all | solution.py:487
  11.7 22.1 %collective-permute-start.1 = (f32[2,3,4,64,128]{4,3,2,1,0:T(8,128)}, f32[2,3,4,64,128]{4,3,2,1,0:T(8,128)}, u32[]{:S(2)}, u32[]{:S(2)}) collective-permute-start(f32[2,3,4,64,128]{4,3,2,1,0:T(8,128)} %get-tuple-element.15._.low_edge_ref), channel_id=1, source_target_pairs={{1,0},{2,1},{3,2},{5,4},{6,5},{7,6},{9,8},{10,9},{11,10},{13,12},{... | collective-permute-start | bytes 2359304 | tf_op jit(solution)/shard_map/ppermute | solution.py:478
  13.0 22.0 %collective-permute-start = (f32[2,3,4,64,128]{4,3,2,1,0:T(8,128)}, f32[2,3,4,64,128]{4,3,2,1,0:T(8,128)}, u32[]{:S(2)}, u32[]{:S(2)}) collective-permute-start(f32[2,3,4,64,128]{4,3,2,1,0:T(8,128)} %get-tuple-element.14.high_edge_ref), channel_id=1, source_target_pairs={{0,1},{1,2},{2,3},{4,5},{5,6},{6,7},{8,9},{9,10},{10,11},{12,13},{... | collective-permute-start | bytes 2359304 | tf_op jit(solution)/shard_map/ppermute | solution.py:477
  18.4 25.4 %copy-start.5 = (f32[32]{0:T(128)S(1)}, f32[32]{0:T(128)}, u32[]{:S(2)}) copy-start(f32[32]{0:T(128)} %coef_ref.1) | copy-start | bytes 388
  43.8 18.9 %copy-start.1 = (f32[3,1,1,4096]{3,2,1,0:T(1,128)S(1)}, f32[3,1,1,4096]{3,2,1,0:T(1,128)}, u32[]{:S(2)}) copy-start(f32[3,1,1,4096]{3,2,1,0:T(1,128)} %noise_ref.1) | copy-start | bytes 147460
  43.9 18.9 %copy-start.3 = (f32[32,32]{1,0:T(8,128)S(1)}, f32[32,32]{1,0:T(8,128)}, u32[]{:S(2)}) copy-start(f32[32,32]{1,0:T(8,128)} %inverse_ref.1) | copy-start | bytes 12292
  43.9 18.9 %copy-start.4 = (f32[9,32]{1,0:T(8,128)S(1)}, f32[9,32]{1,0:T(8,128)}, u32[]{:S(2)}) copy-start(f32[9,32]{1,0:T(8,128)} %stencil_ref.1) | copy-start | bytes 3460
  50.4 3.6 %collective-permute-start.2 = (f32[12,64,128]{2,1,0:T(8,128)}, f32[12,64,128]{2,1,0:T(8,128)S(1)}, u32[]{:S(2)}, u32[]{:S(2)}) collective-permute-start(f32[12,64,128]{2,1,0:T(8,128)} %get-tuple-element.18), channel_id=1, source_target_pairs={{0,4},{4,0},{8,12},{12,8},{16,20},{20,16},{24,28},{28,24},{1,5},{5... | collective-permute-start | bytes 1179656 | tf_op jit(solution)/shard_map/ppermute | solution.py:469
  50.5 12.2 %collective-permute-start.3 = (f32[12,64,128]{2,1,0:T(8,128)}, f32[12,64,128]{2,1,0:T(8,128)S(1)}, u32[]{:S(2)}, u32[]{:S(2)}) collective-permute-start(f32[12,64,128]{2,1,0:T(8,128)} %get-tuple-element.19), channel_id=1, source_target_pairs={{0,8},{4,12},{8,0},{12,4},{16,24},{20,28},{24,16},{28,20},{1,9},{5... | collective-permute-start | bytes 1179656 | tf_op jit(solution)/shard_map/ppermute | solution.py:469
  51.1 38.1 %collective-permute-start.4 = (f32[12,64,128]{2,1,0:T(8,128)}, f32[12,64,128]{2,1,0:T(8,128)S(1)}, u32[]{:S(2)}, u32[]{:S(2)}) collective-permute-start(f32[12,64,128]{2,1,0:T(8,128)} %get-tuple-element.20), channel_id=1, source_target_pairs={{0,12},{4,8},{8,4},{12,0},{16,28},{20,24},{24,20},{28,16},{1,13},{... | collective-permute-start | bytes 1179656 | tf_op jit(solution)/shard_map/ppermute | solution.py:469
  52.4 36.8 %collective-permute-start.5 = (f32[12,64,128]{2,1,0:T(8,128)}, f32[12,64,128]{2,1,0:T(8,128)S(1)}, u32[]{:S(2)}, u32[]{:S(2)}) collective-permute-start(f32[12,64,128]{2,1,0:T(8,128)} %get-tuple-element.21), channel_id=1, source_target_pairs={{0,16},{4,20},{8,24},{12,28},{16,0},{20,4},{24,8},{28,12},{1,17},{... | collective-permute-start | bytes 1179656 | tf_op jit(solution)/shard_map/ppermute | solution.py:469
  52.9 36.3 %collective-permute-start.6 = (f32[12,64,128]{2,1,0:T(8,128)}, f32[12,64,128]{2,1,0:T(8,128)S(1)}, u32[]{:S(2)}, u32[]{:S(2)}) collective-permute-start(f32[12,64,128]{2,1,0:T(8,128)} %get-tuple-element.22), channel_id=1, source_target_pairs={{0,20},{4,16},{8,28},{12,24},{16,4},{20,0},{24,12},{28,8},{1,21},{... | collective-permute-start | bytes 1179656 | tf_op jit(solution)/shard_map/ppermute | solution.py:469
  54.1 35.1 %collective-permute-start.7 = (f32[12,64,128]{2,1,0:T(8,128)}, f32[12,64,128]{2,1,0:T(8,128)S(1)}, u32[]{:S(2)}, u32[]{:S(2)}) collective-permute-start(f32[12,64,128]{2,1,0:T(8,128)} %get-tuple-element.23), channel_id=1, source_target_pairs={{0,24},{4,28},{8,16},{12,20},{16,8},{20,12},{24,0},{28,4},{1,25},{... | collective-permute-start | bytes 1179656 | tf_op jit(solution)/shard_map/ppermute | solution.py:469
  62.7 26.5 %collective-permute-start.8 = (f32[12,64,128]{2,1,0:T(8,128)}, f32[12,64,128]{2,1,0:T(8,128)S(1)}, u32[]{:S(2)}, u32[]{:S(2)}) collective-permute-start(f32[12,64,128]{2,1,0:T(8,128)} %get-tuple-element.24), channel_id=1, source_target_pairs={{0,28},{4,24},{8,20},{12,16},{16,12},{20,8},{24,4},{28,0},{1,29},{... | collective-permute-start | bytes 1179656 | tf_op jit(solution)/shard_map/ppermute | solution.py:469

commit v10 on v9

--- a/solution.py
+++ b/solution.py
@@ -179,7 +179,7 @@
     return jnp.concatenate(parts, axis=0)
 
 
-def move_kernel(
+def derive_kernel(
     stencil_ref,
     inverse_ref,
     low_ref,
@@ -188,12 +188,8 @@
     middle_ref,
     high_edge_ref,
     high_ref,
-    ids_ref,
-    spring_ref,
-    noise_ref,
-    moved_ref,
+    grad_ref,
     force_ref,
-    grad_ref,
     matrix_ref,
 ):
     radii, angles, axial = velocity_ref.shape[1:]
@@ -225,6 +221,43 @@
 
     lax.fori_loop(0, angles // SUB, derive, 0)
 
+
+def derive(stencil, inverse, low, velocity, stress, high):
+    low_edge, middle, high_edge = stress
+    radii, angles, axial = velocity.shape[1:]
+    whole = pl.BlockSpec(memory_space=pltpu.VMEM)
+    return pl.pallas_call(
+        derive_kernel,
+        in_specs=[whole] * 8,
+        out_specs=[whole, whole],
+        out_shape=[
+            pltpu.HBM((6 * axial, radii * angles), BF16),
+            pltpu.HBM(velocity.shape, F32),
+        ],
+        scratch_shapes=[pltpu.VMEM((2 * radii * SUB, (radii + 2 * HALO) * SUB), BF16)],
+        compiler_params=pltpu.CompilerParams(vmem_limit_bytes=28 * MIB),
+        cost_estimate=pl.CostEstimate(
+            flops=3600 * radii * radii * angles * axial // 8,
+            bytes_accessed=40 * radii * angles * axial,
+            transcendentals=0,
+        ),
+        name="derive",
+    )(
+        stencil,
+        inverse,
+        in_vmem(low),
+        in_hbm(velocity),
+        in_hbm(low_edge),
+        in_hbm(middle),
+        in_hbm(high_edge),
+        in_vmem(high),
+    )
+
+
+def move_kernel(grad_ref, ids_ref, spring_ref, noise_ref, moved_ref, *, angles):
+    axial, cells = grad_ref.shape[0] // 6, grad_ref.shape[1]
+    group = cells // angles * SUB
+
     count = spring_ref.shape[3]
     part = min(count, 512)
 
@@ -233,7 +266,7 @@
         plane = ids_ref[0, 0, :, at]
         radius, angle = plane // angles, plane % angles
         column = (angle // SUB) * group + radius * SUB + angle % SUB
-        hot = jnp.where(iota((radii * angles, part), 0) == column, 1.0, 0.0).astype(BF16)
+        hot = jnp.where(iota((cells, part), 0) == column, 1.0, 0.0).astype(BF16)
         picked = dot(grad_ref[...], hot)
         here = iota((axial, part), 0) == ids_ref[1, 0, :, at]
         q = [spring_ref[c, 0, :, at] for c in range(3)]
@@ -254,42 +287,22 @@
     lax.fori_loop(0, count // part, read, 0)
 
 
-def move(stencil, inverse, low, velocity, stress, high, ids, spring, noise):
-    low_edge, middle, high_edge = stress
-    radii, angles, axial = velocity.shape[1:]
+def move(grad, ids, spring, noise, angles):
+    cells = grad.shape[1]
     whole = pl.BlockSpec(memory_space=pltpu.VMEM)
     return pl.pallas_call(
-        move_kernel,
-        in_specs=[whole] * 11,
-        out_specs=[whole, whole],
-        out_shape=[
-            jax.ShapeDtypeStruct(spring.shape, F32),
-            pltpu.HBM(velocity.shape, F32),
-        ],
-        scratch_shapes=[
-            pltpu.VMEM((6 * axial, radii * angles), BF16),
-            pltpu.VMEM((2 * radii * SUB, (radii + 2 * HALO) * SUB), BF16),
-        ],
-        compiler_params=pltpu.CompilerParams(vmem_limit_bytes=28 * MIB),
+        functools.partial(move_kernel, angles=angles),
+        in_specs=[whole] * 4,
+        out_specs=whole,
+        out_shape=jax.ShapeDtypeStruct(spring.shape, F32),
+        compiler_params=pltpu.CompilerParams(vmem_limit_bytes=24 * MIB),
         cost_estimate=pl.CostEstimate(
-            flops=14 * radii * angles * spring.shape[3] * axial,
-            bytes_accessed=40 * radii * angles * axial,
+            flops=2 * grad.size * spring.shape[3],
+            bytes_accessed=2 * grad.size,
             transcendentals=0,
         ),
         name="move",
-    )(
-        stencil,
-        inverse,
-        in_vmem(low),
-        in_hbm(velocity),
-        in_hbm(low_edge),
-        in_hbm(middle),
-        in_hbm(high_edge),
-        in_vmem(high),
-        ids,
-        spring,
-        noise,
-    )
+    )(in_hbm(grad), ids, spring, noise)
 
 
 def fourier_tables(all_angles):
@@ -489,12 +502,11 @@
     low, high = from_neighbours(low_edge, high_edge)
     middle = deposit_middle(cell_ids, dumbbells, low_edge, velocity.shape)
     stress = (low_edge, middle, high_edge)
+    grad, force = derive(stencil_coef, block_inverse, low, velocity, stress, high)
     me = lax.axis_index("az").astype(jnp.int32).reshape(1)
-    solved = solve(azim_coef, me, gathered, (in_vmem(low), in_vmem(high), in_hbm(middle)))
+    solved = solve(azim_coef, me, gathered, (in_hbm(force),))
     pieces = exchange(solved)
-    moved, force = move(
-        stencil_coef, block_inverse, low, velocity, stress, high, cell_ids, dumbbells, brownian
-    )
+    moved = move(grad, cell_ids, dumbbells, brownian, angles)
     lines = (3 * radii, angles, axial)
     result = join(me, force.reshape(lines), pieces)
     return result.reshape(velocity.shape), moved

time: 92.9 us -> 98.3 us (1.058); the launches traced: 92.4 us -> 96.7 us
  Pallas kernels: 54.3 us -> 58.8 us
  waiting for transfers between devices: 20.9 us -> 17.3 us
  starting transfers between devices: 16.3 us -> 19.6 us
    all_to_all x1, waiting for transfers between devices: 8.83 us -> 0.01 us  [per_device(): gathered = lax.all_to_all(pieces, 'az', 0, 0, tiled=True)]
    ppermute x7, waiting for transfers between devices: 8.05 us -> 13.4 us  [exchange(): lax.ppermute(pieces[s], 'az', [(i, i ^ s) for i in range(count)])]
    pallas_call x1 -> x2, Pallas kernels: 26.5 us -> 30.9 us  [the longest x1 17.1 us: move(): pl.pallas_call(functools.partial(move_kernel, angles=angles), in_specs=[w...]
    ppermute x7, starting transfers between devices: 4.23 us -> 7.57 us  [exchange(): lax.ppermute(pieces[s], 'az', [(i, i ^ s) for i in range(count)])]
  transfers between devices with their start and end apart: 10 -> 10, of which waited for: 4 -> 4; matrix products, arithmetic and copies ran while one was open for 0% -> 0% of each run, Pallas kernels for 48% -> 51%
where the time goes in v10:
time: 98.3 us; the launch traced here: 96.7 us
  Pallas kernels  58.8 us (60%)
  starting transfers between devices  19.6 us (20%)
  waiting for transfers between devices  17.3 us (18%)
    pallas_call x1, Pallas kernels, move(): pl.pallas_call(functools.partial(move_kernel, angles=angles), in_specs=[w...  17.1 us
    pallas_call x1, Pallas kernels, derive(): pl.pallas_call(derive_kernel, in_specs=[whole] * 8, out_specs=[whole, who...  13.8 us
    ppermute x7, waiting for transfers between devices, exchange(): lax.ppermute(pieces[s], 'az', [(i, i ^ s) for i in range(count)])  13.4 us
    pallas_call x1, Pallas kernels, deposit_middle(): pl.pallas_call(lambda ids_ref, spring_ref, _, *refs: middle_kernel(ids_re...  12.6 us
    ppermute x7, starting transfers between devices, exchange(): lax.ppermute(pieces[s], 'az', [(i, i ^ s) for i in range(count)])  7.57 us
    pallas_call x1, Pallas kernels, solve(): pl.pallas_call(functools.partial(solve_kernel, extra=len(after)), in_spec...  6.56 us
    pallas_call x1, Pallas kernels, deposit_edges(): pl.pallas_call(functools.partial(edge_kernel, radii=radii), grid=(1,), in...  5.73 us
    ppermute x1, starting transfers between devices, from_neighbours(): low = lax.ppermute(high_edge, 'rad', forward)  5.44 us
  transfers between devices with their start and end apart: 10, of which 4 were waited for; matrix products, arithmetic and copies ran while one was open for 0% of the time, Pallas kernels for 51%

profile of v10, /device:TPU:0, one launch (start us, length us, event | category | flops | bytes accessed | tf_op | source)
XLA Modules:
  0.0 96.7 jit_solution(17346140440793209288)
XLA Ops:
  0.6 0.0 copy-start
  0.6 0.0 copy-start.2
  0.6 5.3 %all-to-all-start = ((f32[8,12,64,128]{3,2,1,0:T(8,128)}), f32[8,12,64,128]{3,2,1,0:T(8,128)S(1)}, u32[]{:S(2)}, u32[]{:S(2)}) async-start(f32[8,12,64,128]{3,2,1,0:T(8,128)} %bitcast.4), calls=%async_computation | async-start | bytes 6291456 | tf_op jit(solution)/shard_map/all_to_all | solution.py:500
  6.0 0.0 copy-done
  6.0 0.0 copy-done.2
  6.0 5.7 %deposit_edges.1 = (f32[2,3,4,64,128]{4,3,2,1,0:T(8,128)}, f32[2,3,4,64,128]{4,3,2,1,0:T(8,128)}) custom-call(s32[2,1,1,4096]{3,2,1,0:T(1,128)S(1)} %copy-done.2, f32[3,1,1,4096]{3,2,1,0:T(1,128)S(1)} %copy-done, f32[3,32,64,128]{3,2,1,0:T(8,128)} %velocity_ref.1, f32[3,32,64,128]{3,2,1,0:T(8,128)} %velocity_ref.1), custom_call_target="tpu_custom_call" | custom-call | flops 3221225472 | bytes 3145728 | tf_op jit(solution)/shard_map/deposit_edges/pallas_call | solution.py:112
  11.7 1.3 %collective-permute-start.1 = (f32[2,3,4,64,128]{4,3,2,1,0:T(8,128)}, f32[2,3,4,64,128]{4,3,2,1,0:T(8,128)}, u32[]{:S(2)}, u32[]{:S(2)}) collective-permute-start(f32[2,3,4,64,128]{4,3,2,1,0:T(8,128)} %get-tuple-element.15._.low_edge_ref), channel_id=1, source_target_pairs={{1,0},{2,1},{3,2},{5,4},{6,5},{7,6},{9,8},{10,9},{11,10},{13,12},{... | collective-permute-start | bytes 2359304 | tf_op jit(solution)/shard_map/ppermute | solution.py:491
  13.0 5.4 %collective-permute-start = (f32[2,3,4,64,128]{4,3,2,1,0:T(8,128)}, f32[2,3,4,64,128]{4,3,2,1,0:T(8,128)}, u32[]{:S(2)}, u32[]{:S(2)}) collective-permute-start(f32[2,3,4,64,128]{4,3,2,1,0:T(8,128)} %get-tuple-element.14.high_edge_ref), channel_id=1, source_target_pairs={{0,1},{1,2},{2,3},{4,5},{5,6},{6,7},{8,9},{9,10},{10,11},{12,13},{... | collective-permute-start | bytes 2359304 | tf_op jit(solution)/shard_map/ppermute | solution.py:490
  18.4 12.6 %deposit_middle.1.middle_ref = f32[3,24,64,128]{3,2,1,0:T(8,128)} custom-call(s32[2,1,1,4096]{3,2,1,0:T(1,128)S(1)} %copy-done.2, f32[3,1,1,4096]{3,2,1,0:T(1,128)S(1)} %copy-done, f32[2,3,4,64,128]{4,3,2,1,0:T(8,128)} %get-tuple-element.15._.low_edge_ref), custom_call_target="tpu_custom_call" | custom-call | flops 9663676416 | bytes 2359296 | tf_op jit(solution)/shard_map/deposit_middle/pallas_call | solution.py:140
  31.1 2.8 %collective-permute-done.1.high_ref = f32[2,3,4,64,128]{4,3,2,1,0:T(8,128)} collective-permute-done((f32[2,3,4,64,128]{4,3,2,1,0:T(8,128)}, f32[2,3,4,64,128]{4,3,2,1,0:T(8,128)}, u32[]{:S(2)}, u32[]{:S(2)}) %collective-permute-start.1) | collective-permute-done | bytes 786464 | tf_op jit(solution)/shard_map/ppermute | solution.py:491
  33.9 1.2 %collective-permute-done.low_ref = f32[2,3,4,64,128]{4,3,2,1,0:T(8,128)} collective-permute-done((f32[2,3,4,64,128]{4,3,2,1,0:T(8,128)}, f32[2,3,4,64,128]{4,3,2,1,0:T(8,128)}, u32[]{:S(2)}, u32[]{:S(2)}) %collective-permute-start) | collective-permute-done | bytes 786464 | tf_op jit(solution)/shard_map/ppermute | solution.py:490
  35.0 13.8 %derive.1 = (bf16[768,2048]{1,0:T(8,128)(2,1)}, f32[3,32,64,128]{3,2,1,0:T(8,128)}) custom-call(f32[9,32]{1,0:T(8,128)S(1)} %copy-done.4, f32[32,32]{1,0:T(8,128)S(1)} %copy-done.3, f32[2,3,4,64,128]{4,3,2,1,0:T(8,128)} %collective-permute-done.low_ref, f32[3,32,64,128]{3,2,1,0:T(8,128)} %velocity_ref.1, ...), custom_call_target="tpu_custom_call" | custom-call | flops 3774873600 | bytes 10485760 | tf_op jit(solution)/shard_map/derive/pallas_call | solution.py:229
  48.9 0.0 all-to-all-done.refs_1_
  48.9 0.0 copy-done.5
  48.9 0.0 copy-start.1
  48.9 6.6 %solve.1 = (f32[12,64,128]{2,1,0:T(8,128)}, f32[12,64,128]{2,1,0:T(8,128)}, f32[12,64,128]{2,1,0:T(8,128)}, f32[12,64,128]{2,1,0:T(8,128)}, f32[12,64,128]{2,1,0...) custom-call(f32[32]{0:T(128)S(1)} %copy-done.5, s32[1]{0:T(128)} %bitcast.me_ref, ...), custom_call_target="tpu_custom_call" | custom-call | flops 4831838208 | bytes 6291456 | tf_op jit(solution)/shard_map/solve/pallas_call | solution.py:399
  55.5 0.1 collective-permute-start.2
  55.5 1.7 %collective-permute-start.3 = (f32[12,64,128]{2,1,0:T(8,128)}, f32[12,64,128]{2,1,0:T(8,128)S(1)}, u32[]{:S(2)}, u32[]{:S(2)}) collective-permute-start(f32[12,64,128]{2,1,0:T(8,128)} %get-tuple-element.19), channel_id=1, source_target_pairs={{0,8},{4,12},{8,0},{12,4},{16,24},{20,28},{24,16},{28,20},{1,9},{5... | collective-permute-start | bytes 1179656 | tf_op jit(solution)/shard_map/ppermute | solution.py:482
  57.3 0.1 collective-permute-start.4
  57.4 1.7 %collective-permute-start.5 = (f32[12,64,128]{2,1,0:T(8,128)}, f32[12,64,128]{2,1,0:T(8,128)S(1)}, u32[]{:S(2)}, u32[]{:S(2)}) collective-permute-start(f32[12,64,128]{2,1,0:T(8,128)} %get-tuple-element.21), channel_id=1, source_target_pairs={{0,16},{4,20},{8,24},{12,28},{16,0},{20,4},{24,8},{28,12},{1,17},{... | collective-permute-start | bytes 1179656 | tf_op jit(solution)/shard_map/ppermute | solution.py:482
  59.1 0.0 collective-permute-start.6
  59.1 0.0 collective-permute-done.2.refs_0_
  59.1 2.5 %collective-permute-start.7 = (f32[12,64,128]{2,1,0:T(8,128)}, f32[12,64,128]{2,1,0:T(8,128)S(1)}, u32[]{:S(2)}, u32[]{:S(2)}) collective-permute-start(f32[12,64,128]{2,1,0:T(8,128)} %get-tuple-element.23), channel_id=1, source_target_pairs={{0,24},{4,28},{8,16},{12,20},{16,8},{20,12},{24,0},{28,4},{1,25},{... | collective-permute-start | bytes 1179656 | tf_op jit(solution)/shard_map/ppermute | solution.py:482
  61.7 6.1 %collective-permute-done.3.refs_1_ = f32[12,64,128]{2,1,0:T(8,128)S(1)} collective-permute-done((f32[12,64,128]{2,1,0:T(8,128)}, f32[12,64,128]{2,1,0:T(8,128)S(1)}, u32[]{:S(2)}, u32[]{:S(2)}) %collective-permute-start.3) | collective-permute-done | bytes 393248 | tf_op jit(solution)/shard_map/ppermute | solution.py:482
  67.7 1.4 %collective-permute-start.8 = (f32[12,64,128]{2,1,0:T(8,128)}, f32[12,64,128]{2,1,0:T(8,128)S(1)}, u32[]{:S(2)}, u32[]{:S(2)}) collective-permute-start(f32[12,64,128]{2,1,0:T(8,128)} %get-tuple-element.24), channel_id=1, source_target_pairs={{0,28},{4,24},{8,20},{12,16},{16,12},{20,8},{24,4},{28,0},{1,29},{... | collective-permute-start | bytes 1179656 | tf_op jit(solution)/shard_map/ppermute | solution.py:482
  69.1 17.1 %move.1 = f32[3,1,1,4096]{3,2,1,0:T(1,128)} custom-call(bf16[768,2048]{1,0:T(8,128)(2,1)} %get-tuple-element.25.grad_ref, s32[2,1,1,4096]{3,2,1,0:T(1,128)S(1)} %copy-done.2, f32[3,1,1,4096]{3,2,1,0:T(1,128)S(1)} %copy-done, f32[3,1,1,4096]{3,2,1,0:T(1,128)S(1)} %copy-done.1), custom_call_target="tpu_custom_call" | custom-call | flops 12884901888 | bytes 3145728 | tf_op jit(solution)/shard_map/move/pallas_call | solution.py:293
  86.2 0.0 collective-permute-done.4.refs_2_
  86.2 0.0 collective-permute-done.5.refs_3_
  86.2 7.3 %collective-permute-done.6.refs_4_ = f32[12,64,128]{2,1,0:T(8,128)S(1)} collective-permute-done((f32[12,64,128]{2,1,0:T(8,128)}, f32[12,64,128]{2,1,0:T(8,128)S(1)}, u32[]{:S(2)}, u32[]{:S(2)}) %collective-permute-start.6) | collective-permute-done | bytes 393248 | tf_op jit(solution)/shard_map/ppermute | solution.py:482
  93.5 0.0 collective-permute-done.7.refs_5_
  93.6 0.0 collective-permute-done.8.refs_6_
  93.6 3.0 %join.1 = f32[96,64,128]{2,1,0:T(8,128)} custom-call(s32[1]{0:T(128)} %bitcast.me_ref, f32[96,64,128]{2,1,0:T(8,128)} %bitcast.5, f32[12,64,128]{2,1,0:T(8,128)} %get-tuple-element.17.own_ref, f32[12,64,128]{2,1,0:T(8,128)S(1)} %collective-permute-done.2.refs_0_, f32[12,64,128]{2,1,0:T(8,128)S(1)} %collective-permute-done.3.refs_1_, ...), custom_call_target="tpu_custom_call" | custom-call | flops 786432 | bytes 9437184 | tf_op jit(solution)/shard_map/join/pallas_call | solution.py:459
  (6 shorter events, 0.0 us)
Async XLA Ops:
  0.6 5.3 %copy-start = (f32[3,1,1,4096]{3,2,1,0:T(1,128)S(1)}, f32[3,1,1,4096]{3,2,1,0:T(1,128)}, u32[]{:S(2)}) copy-start(f32[3,1,1,4096]{3,2,1,0:T(1,128)} %spring_ref.5) | copy-start | bytes 147460
  0.6 5.3 %copy-start.2 = (s32[2,1,1,4096]{3,2,1,0:T(1,128)S(1)}, s32[2,1,1,4096]{3,2,1,0:T(1,128)}, u32[]{:S(2)}) copy-start(s32[2,1,1,4096]{3,2,1,0:T(1,128)} %ids_ref.5) | copy-start | bytes 98308
  0.6 48.2 %all-to-all-start = ((f32[8,12,64,128]{3,2,1,0:T(8,128)}), f32[8,12,64,128]{3,2,1,0:T(8,128)S(1)}, u32[]{:S(2)}, u32[]{:S(2)}) async-start(f32[8,12,64,128]{3,2,1,0:T(8,128)} %bitcast.4), calls=%async_computation | async-start | bytes 6291456 | tf_op jit(solution)/shard_map/all_to_all | solution.py:500
  11.7 22.1 %collective-permute-start.1 = (f32[2,3,4,64,128]{4,3,2,1,0:T(8,128)}, f32[2,3,4,64,128]{4,3,2,1,0:T(8,128)}, u32[]{:S(2)}, u32[]{:S(2)}) collective-permute-start(f32[2,3,4,64,128]{4,3,2,1,0:T(8,128)} %get-tuple-element.15._.low_edge_ref), channel_id=1, source_target_pairs={{1,0},{2,1},{3,2},{5,4},{6,5},{7,6},{9,8},{10,9},{11,10},{13,12},{... | collective-permute-start | bytes 2359304 | tf_op jit(solution)/shard_map/ppermute | solution.py:491
  13.0 22.0 %collective-permute-start = (f32[2,3,4,64,128]{4,3,2,1,0:T(8,128)}, f32[2,3,4,64,128]{4,3,2,1,0:T(8,128)}, u32[]{:S(2)}, u32[]{:S(2)}) collective-permute-start(f32[2,3,4,64,128]{4,3,2,1,0:T(8,128)} %get-tuple-element.14.high_edge_ref), channel_id=1, source_target_pairs={{0,1},{1,2},{2,3},{4,5},{5,6},{6,7},{8,9},{9,10},{10,11},{12,13},{... | collective-permute-start | bytes 2359304 | tf_op jit(solution)/shard_map/ppermute | solution.py:490
  18.4 16.6 %copy-start.3 = (f32[32,32]{1,0:T(8,128)S(1)}, f32[32,32]{1,0:T(8,128)}, u32[]{:S(2)}) copy-start(f32[32,32]{1,0:T(8,128)} %inverse_ref.1) | copy-start | bytes 12292
  18.4 16.6 %copy-start.4 = (f32[9,32]{1,0:T(8,128)S(1)}, f32[9,32]{1,0:T(8,128)}, u32[]{:S(2)}) copy-start(f32[9,32]{1,0:T(8,128)} %stencil_ref.1) | copy-start | bytes 3460
  31.1 17.8 %copy-start.5 = (f32[32]{0:T(128)S(1)}, f32[32]{0:T(128)}, u32[]{:S(2)}) copy-start(f32[32]{0:T(128)} %coef_ref.1) | copy-start | bytes 388
  48.9 20.2 %copy-start.1 = (f32[3,1,1,4096]{3,2,1,0:T(1,128)S(1)}, f32[3,1,1,4096]{3,2,1,0:T(1,128)}, u32[]{:S(2)}) copy-start(f32[3,1,1,4096]{3,2,1,0:T(1,128)} %noise_ref.1) | copy-start | bytes 147460
  55.5 3.7 %collective-permute-start.2 = (f32[12,64,128]{2,1,0:T(8,128)}, f32[12,64,128]{2,1,0:T(8,128)S(1)}, u32[]{:S(2)}, u32[]{:S(2)}) collective-permute-start(f32[12,64,128]{2,1,0:T(8,128)} %get-tuple-element.18), channel_id=1, source_target_pairs={{0,4},{4,0},{8,12},{12,8},{16,20},{20,16},{24,28},{28,24},{1,5},{5... | collective-permute-start | bytes 1179656 | tf_op jit(solution)/shard_map/ppermute | solution.py:482
  55.5 12.2 %collective-permute-start.3 = (f32[12,64,128]{2,1,0:T(8,128)}, f32[12,64,128]{2,1,0:T(8,128)S(1)}, u32[]{:S(2)}, u32[]{:S(2)}) collective-permute-start(f32[12,64,128]{2,1,0:T(8,128)} %get-tuple-element.19), channel_id=1, source_target_pairs={{0,8},{4,12},{8,0},{12,4},{16,24},{20,28},{24,16},{28,20},{1,9},{5... | collective-permute-start | bytes 1179656 | tf_op jit(solution)/shard_map/ppermute | solution.py:482
  57.3 29.0 %collective-permute-start.4 = (f32[12,64,128]{2,1,0:T(8,128)}, f32[12,64,128]{2,1,0:T(8,128)S(1)}, u32[]{:S(2)}, u32[]{:S(2)}) collective-permute-start(f32[12,64,128]{2,1,0:T(8,128)} %get-tuple-element.20), channel_id=1, source_target_pairs={{0,12},{4,8},{8,4},{12,0},{16,28},{20,24},{24,20},{28,16},{1,13},{... | collective-permute-start | bytes 1179656 | tf_op jit(solution)/shard_map/ppermute | solution.py:482
  57.4 28.8 %collective-permute-start.5 = (f32[12,64,128]{2,1,0:T(8,128)}, f32[12,64,128]{2,1,0:T(8,128)S(1)}, u32[]{:S(2)}, u32[]{:S(2)}) collective-permute-start(f32[12,64,128]{2,1,0:T(8,128)} %get-tuple-element.21), channel_id=1, source_target_pairs={{0,16},{4,20},{8,24},{12,28},{16,0},{20,4},{24,8},{28,12},{1,17},{... | collective-permute-start | bytes 1179656 | tf_op jit(solution)/shard_map/ppermute | solution.py:482
  59.1 34.5 %collective-permute-start.6 = (f32[12,64,128]{2,1,0:T(8,128)}, f32[12,64,128]{2,1,0:T(8,128)S(1)}, u32[]{:S(2)}, u32[]{:S(2)}) collective-permute-start(f32[12,64,128]{2,1,0:T(8,128)} %get-tuple-element.22), channel_id=1, source_target_pairs={{0,20},{4,16},{8,28},{12,24},{16,4},{20,0},{24,12},{28,8},{1,21},{... | collective-permute-start | bytes 1179656 | tf_op jit(solution)/shard_map/ppermute | solution.py:482
  59.1 34.4 %collective-permute-start.7 = (f32[12,64,128]{2,1,0:T(8,128)}, f32[12,64,128]{2,1,0:T(8,128)S(1)}, u32[]{:S(2)}, u32[]{:S(2)}) collective-permute-start(f32[12,64,128]{2,1,0:T(8,128)} %get-tuple-element.23), channel_id=1, source_target_pairs={{0,24},{4,28},{8,16},{12,20},{16,8},{20,12},{24,0},{28,4},{1,25},{... | collective-permute-start | bytes 1179656 | tf_op jit(solution)/shard_map/ppermute | solution.py:482
  67.7 25.8 %collective-permute-start.8 = (f32[12,64,128]{2,1,0:T(8,128)}, f32[12,64,128]{2,1,0:T(8,128)S(1)}, u32[]{:S(2)}, u32[]{:S(2)}) collective-permute-start(f32[12,64,128]{2,1,0:T(8,128)} %get-tuple-element.24), channel_id=1, source_target_pairs={{0,28},{4,24},{8,20},{12,16},{16,12},{20,8},{24,4},{28,0},{1,29},{... | collective-permute-start | bytes 1179656 | tf_op jit(solution)/shard_map/ppermute | solution.py:482

commit v11 on v10

--- a/solution.py
+++ b/solution.py
@@ -193,15 +193,19 @@
     matrix_ref,
 ):
     radii, angles, axial = velocity_ref.shape[1:]
-    matrix_ref[...] = derivative_matrix(stencil_ref, inverse_ref)
+
+    @pl.when(pl.program_id(0) == 0)
+    def _():
+        matrix_ref[...] = derivative_matrix(stencil_ref, inverse_ref)
+
     group = radii * SUB
 
-    def derive(i, carry):
-        at = pl.ds(pl.multiple_of(i * SUB, SUB), SUB)
+    for i in range(angles // SUB):
+        at = pl.ds(i * SUB, SUB)
         columns = []
         own = [
             [velocity_ref],
-            [low_edge_ref.at[1], middle_ref, high_edge_ref.at[1]],
+            [low_edge_ref.at[0], middle_ref, high_edge_ref.at[0]],
         ]
         for f in range(2):
             refs = [low_ref.at[f]] + own[f] + [high_ref.at[f]]
@@ -214,22 +218,38 @@
             force = TIME_STEP * result[:, (3 + c) * axial : (4 + c) * axial]
             force_ref[c, :, at, :] = force.reshape(radii, SUB, axial)
         turned_high, turned_low = split(result[:, : 3 * axial].T)
-        cols = pl.ds(pl.multiple_of(i * group, group), group)
+        cols = pl.ds(i * group, group)
         grad_ref[: 3 * axial, cols] = turned_high
         grad_ref[3 * axial :, cols] = turned_low
-        return carry
-
-    lax.fori_loop(0, angles // SUB, derive, 0)
 
 
 def derive(stencil, inverse, low, velocity, stress, high):
     low_edge, middle, high_edge = stress
     radii, angles, axial = velocity.shape[1:]
-    whole = pl.BlockSpec(memory_space=pltpu.VMEM)
+    part = 2 * SUB
+
+    def block(count, first=None):
+        if first is None:
+            return pl.BlockSpec((3, count, part, axial), lambda i: (0, 0, i, 0))
+        return pl.BlockSpec((2 - first, 3, count, part, axial), lambda i: (first, 0, 0, i, 0))
+
     return pl.pallas_call(
         derive_kernel,
-        in_specs=[whole] * 8,
-        out_specs=[whole, whole],
+        grid=(angles // part,),
+        in_specs=[
+            pl.BlockSpec(stencil.shape, lambda i: (0, 0)),
+            pl.BlockSpec(inverse.shape, lambda i: (0, 0)),
+            block(HALO, 0),
+            block(radii),
+            block(HALO, 1),
+            block(radii - 2 * HALO),
+            block(HALO, 1),
+            block(HALO, 0),
+        ],
+        out_specs=[
+            pl.BlockSpec((6 * axial, radii * part), lambda i: (0, i)),
+            block(radii),
+        ],
         out_shape=[
             pltpu.HBM((6 * axial, radii * angles), BF16),
             pltpu.HBM(velocity.shape, F32),
@@ -335,7 +355,7 @@
     table_ref, done_ref, table_sems, out_sems = refs[blocks:]
     half = blocks * angles // 2
     quarter = half // 2
-    part = math.gcd(rows, 4)
+    part = math.gcd(rows, 2)
     loads = [
         pltpu.make_async_copy(tables_ref.at[i], table_ref.at[i], table_sems.at[i])
         for i in range(4)
@@ -405,7 +425,7 @@
             pltpu.VMEM(tables.shape, BF16),
             pltpu.VMEM(field.shape, F32),
             pltpu.SemaphoreType.DMA((4,)),
-            pltpu.SemaphoreType.DMA((rows // math.gcd(rows, 4), blocks)),
+            pltpu.SemaphoreType.DMA((rows // math.gcd(rows, 2), blocks)),
         ],
         compiler_params=pltpu.CompilerParams(vmem_limit_bytes=28 * MIB),
         cost_estimate=pl.CostEstimate(

time: 98.3 us -> 94.5 us (0.961)
  Pallas kernels: 58.8 us -> 54.9 us
    pallas_call x1, Pallas kernels: 13.8 us -> 10 us  [derive(): pl.pallas_call(derive_kernel, grid=(angles // part,), in_specs=[pl.BlockS...]
  transfers between devices with their start and end apart: 10 -> 10, of which waited for: 4 -> 4; matrix products, arithmetic and copies ran while one was open for 0% -> 0% of each run, Pallas kernels for 51% -> 49%
where the time goes in v11:
time: 94.5 us; the launch traced here: 92.8 us
  Pallas kernels  54.9 us (58%)
  starting transfers between devices  19.6 us (21%)
  waiting for transfers between devices  17.3 us (18%)
    pallas_call x1, Pallas kernels, move(): pl.pallas_call(functools.partial(move_kernel, angles=angles), in_specs=[w...  17.1 us
    ppermute x7, waiting for transfers between devices, exchange(): lax.ppermute(pieces[s], 'az', [(i, i ^ s) for i in range(count)])  13.4 us
    pallas_call x1, Pallas kernels, deposit_middle(): pl.pallas_call(lambda ids_ref, spring_ref, _, *refs: middle_kernel(ids_re...  12.6 us
    pallas_call x1, Pallas kernels, derive(): pl.pallas_call(derive_kernel, grid=(angles // part,), in_specs=[pl.BlockS...  10 us
    ppermute x7, starting transfers between devices, exchange(): lax.ppermute(pieces[s], 'az', [(i, i ^ s) for i in range(count)])  7.58 us
    pallas_call x1, Pallas kernels, solve(): pl.pallas_call(functools.partial(solve_kernel, extra=len(after)), in_spec...  6.44 us
    pallas_call x1, Pallas kernels, deposit_edges(): pl.pallas_call(functools.partial(edge_kernel, radii=radii), grid=(1,), in...  5.73 us
    ppermute x1, starting transfers between devices, from_neighbours(): low = lax.ppermute(high_edge, 'rad', forward)  5.44 us
  transfers between devices with their start and end apart: 10, of which 4 were waited for; matrix products, arithmetic and copies ran while one was open for 0% of the time, Pallas kernels for 49%

profile of v11, /device:TPU:0, one launch (start us, length us, event | category | flops | bytes accessed | tf_op | source)
XLA Modules:
  0.0 92.8 jit_solution(14280970296729771159)
XLA Ops:
  0.6 0.0 copy-start
  0.6 0.0 copy-start.2
  0.6 5.3 %all-to-all-start = ((f32[8,12,64,128]{3,2,1,0:T(8,128)}), f32[8,12,64,128]{3,2,1,0:T(8,128)S(1)}, u32[]{:S(2)}, u32[]{:S(2)}) async-start(f32[8,12,64,128]{3,2,1,0:T(8,128)} %bitcast.4), calls=%async_computation | async-start | bytes 6291456 | tf_op jit(solution)/shard_map/all_to_all | solution.py:520
  6.0 0.0 copy-done
  6.0 0.0 copy-done.2
  6.0 5.7 %deposit_edges.1 = (f32[2,3,4,64,128]{4,3,2,1,0:T(8,128)}, f32[2,3,4,64,128]{4,3,2,1,0:T(8,128)}) custom-call(s32[2,1,1,4096]{3,2,1,0:T(1,128)S(1)} %copy-done.2, f32[3,1,1,4096]{3,2,1,0:T(1,128)S(1)} %copy-done, f32[3,32,64,128]{3,2,1,0:T(8,128)} %velocity_ref.1, f32[3,32,64,128]{3,2,1,0:T(8,128)} %velocity_ref.1), custom_call_target="tpu_custom_call" | custom-call | flops 3221225472 | bytes 3145728 | tf_op jit(solution)/shard_map/deposit_edges/pallas_call | solution.py:112
  11.7 1.3 %collective-permute-start.1 = (f32[2,3,4,64,128]{4,3,2,1,0:T(8,128)}, f32[2,3,4,64,128]{4,3,2,1,0:T(8,128)}, u32[]{:S(2)}, u32[]{:S(2)}) collective-permute-start(f32[2,3,4,64,128]{4,3,2,1,0:T(8,128)} %get-tuple-element.15._.low_edge_ref), channel_id=1, source_target_pairs={{1,0},{2,1},{3,2},{5,4},{6,5},{7,6},{9,8},{10,9},{11,10},{13,12},{... | collective-permute-start | bytes 2359304 | tf_op jit(solution)/shard_map/ppermute | solution.py:511
  13.0 5.4 %collective-permute-start = (f32[2,3,4,64,128]{4,3,2,1,0:T(8,128)}, f32[2,3,4,64,128]{4,3,2,1,0:T(8,128)}, u32[]{:S(2)}, u32[]{:S(2)}) collective-permute-start(f32[2,3,4,64,128]{4,3,2,1,0:T(8,128)} %get-tuple-element.14.high_edge_ref), channel_id=1, source_target_pairs={{0,1},{1,2},{2,3},{4,5},{5,6},{6,7},{8,9},{9,10},{10,11},{12,13},{... | collective-permute-start | bytes 2359304 | tf_op jit(solution)/shard_map/ppermute | solution.py:510
  18.4 12.6 %deposit_middle.1.middle_ref = f32[3,24,64,128]{3,2,1,0:T(8,128)} custom-call(s32[2,1,1,4096]{3,2,1,0:T(1,128)S(1)} %copy-done.2, f32[3,1,1,4096]{3,2,1,0:T(1,128)S(1)} %copy-done, f32[2,3,4,64,128]{4,3,2,1,0:T(8,128)} %get-tuple-element.15._.low_edge_ref), custom_call_target="tpu_custom_call" | custom-call | flops 9663676416 | bytes 2359296 | tf_op jit(solution)/shard_map/deposit_middle/pallas_call | solution.py:140
  31.1 2.8 %collective-permute-done.1.high_ref = f32[2,3,4,64,128]{4,3,2,1,0:T(8,128)} collective-permute-done((f32[2,3,4,64,128]{4,3,2,1,0:T(8,128)}, f32[2,3,4,64,128]{4,3,2,1,0:T(8,128)}, u32[]{:S(2)}, u32[]{:S(2)}) %collective-permute-start.1) | collective-permute-done | bytes 786464 | tf_op jit(solution)/shard_map/ppermute | solution.py:511
  33.9 1.2 %collective-permute-done.low_ref = f32[2,3,4,64,128]{4,3,2,1,0:T(8,128)} collective-permute-done((f32[2,3,4,64,128]{4,3,2,1,0:T(8,128)}, f32[2,3,4,64,128]{4,3,2,1,0:T(8,128)}, u32[]{:S(2)}, u32[]{:S(2)}) %collective-permute-start) | collective-permute-done | bytes 786464 | tf_op jit(solution)/shard_map/ppermute | solution.py:510
  35.0 0.0 copy-done.3
  35.0 10.0 %derive.1 = (bf16[768,2048]{1,0:T(8,128)(2,1)}, f32[3,32,64,128]{3,2,1,0:T(8,128)}) custom-call(f32[9,32]{1,0:T(8,128)S(1)} %copy-done.4, f32[32,32]{1,0:T(8,128)S(1)} %copy-done.3, f32[2,3,4,64,128]{4,3,2,1,0:T(8,128)} %collective-permute-done.low_ref, f32[3,32,64,128]{3,2,1,0:T(8,128)} %velocity_ref.1, ...), custom_call_target="tpu_custom_call" | custom-call | flops 3774873600 | bytes 10485760 | tf_op jit(solution)/shard_map/derive/pallas_call | solution.py:236
  45.1 0.0 all-to-all-done.refs_1_
  45.1 0.0 copy-start.1
  45.1 6.4 %solve.1 = (f32[12,64,128]{2,1,0:T(8,128)}, f32[12,64,128]{2,1,0:T(8,128)}, f32[12,64,128]{2,1,0:T(8,128)}, f32[12,64,128]{2,1,0:T(8,128)}, f32[12,64,128]{2,1,0...) custom-call(f32[32]{0:T(128)S(1)} %copy-done.5, s32[1]{0:T(128)} %bitcast.me_ref, ...), custom_call_target="tpu_custom_call" | custom-call | flops 4831838208 | bytes 6291456 | tf_op jit(solution)/shard_map/solve/pallas_call | solution.py:419
  51.6 0.1 collective-permute-start.2
  51.6 1.7 %collective-permute-start.3 = (f32[12,64,128]{2,1,0:T(8,128)}, f32[12,64,128]{2,1,0:T(8,128)S(1)}, u32[]{:S(2)}, u32[]{:S(2)}) collective-permute-start(f32[12,64,128]{2,1,0:T(8,128)} %get-tuple-element.19), channel_id=1, source_target_pairs={{0,8},{4,12},{8,0},{12,4},{16,24},{20,28},{24,16},{28,20},{1,9},{5... | collective-permute-start | bytes 1179656 | tf_op jit(solution)/shard_map/ppermute | solution.py:502
  53.4 0.1 collective-permute-start.4
  53.5 1.7 %collective-permute-start.5 = (f32[12,64,128]{2,1,0:T(8,128)}, f32[12,64,128]{2,1,0:T(8,128)S(1)}, u32[]{:S(2)}, u32[]{:S(2)}) collective-permute-start(f32[12,64,128]{2,1,0:T(8,128)} %get-tuple-element.21), channel_id=1, source_target_pairs={{0,16},{4,20},{8,24},{12,28},{16,0},{20,4},{24,8},{28,12},{1,17},{... | collective-permute-start | bytes 1179656 | tf_op jit(solution)/shard_map/ppermute | solution.py:502
  55.2 0.0 collective-permute-start.6
  55.2 0.0 collective-permute-done.2.refs_0_
  55.2 2.6 %collective-permute-start.7 = (f32[12,64,128]{2,1,0:T(8,128)}, f32[12,64,128]{2,1,0:T(8,128)S(1)}, u32[]{:S(2)}, u32[]{:S(2)}) collective-permute-start(f32[12,64,128]{2,1,0:T(8,128)} %get-tuple-element.23), channel_id=1, source_target_pairs={{0,24},{4,28},{8,16},{12,20},{16,8},{20,12},{24,0},{28,4},{1,25},{... | collective-permute-start | bytes 1179656 | tf_op jit(solution)/shard_map/ppermute | solution.py:502
  57.8 6.1 %collective-permute-done.3.refs_1_ = f32[12,64,128]{2,1,0:T(8,128)S(1)} collective-permute-done((f32[12,64,128]{2,1,0:T(8,128)}, f32[12,64,128]{2,1,0:T(8,128)S(1)}, u32[]{:S(2)}, u32[]{:S(2)}) %collective-permute-start.3) | collective-permute-done | bytes 393248 | tf_op jit(solution)/shard_map/ppermute | solution.py:502
  63.8 1.4 %collective-permute-start.8 = (f32[12,64,128]{2,1,0:T(8,128)}, f32[12,64,128]{2,1,0:T(8,128)S(1)}, u32[]{:S(2)}, u32[]{:S(2)}) collective-permute-start(f32[12,64,128]{2,1,0:T(8,128)} %get-tuple-element.24), channel_id=1, source_target_pairs={{0,28},{4,24},{8,20},{12,16},{16,12},{20,8},{24,4},{28,0},{1,29},{... | collective-permute-start | bytes 1179656 | tf_op jit(solution)/shard_map/ppermute | solution.py:502
  65.2 17.1 %move.1 = f32[3,1,1,4096]{3,2,1,0:T(1,128)} custom-call(bf16[768,2048]{1,0:T(8,128)(2,1)} %get-tuple-element.25.grad_ref, s32[2,1,1,4096]{3,2,1,0:T(1,128)S(1)} %copy-done.2, f32[3,1,1,4096]{3,2,1,0:T(1,128)S(1)} %copy-done, f32[3,1,1,4096]{3,2,1,0:T(1,128)S(1)} %copy-done.1), custom_call_target="tpu_custom_call" | custom-call | flops 12884901888 | bytes 3145728 | tf_op jit(solution)/shard_map/move/pallas_call | solution.py:313
  82.3 0.0 collective-permute-done.4.refs_2_
  82.3 0.0 collective-permute-done.5.refs_3_
  82.3 7.3 %collective-permute-done.6.refs_4_ = f32[12,64,128]{2,1,0:T(8,128)S(1)} collective-permute-done((f32[12,64,128]{2,1,0:T(8,128)}, f32[12,64,128]{2,1,0:T(8,128)S(1)}, u32[]{:S(2)}, u32[]{:S(2)}) %collective-permute-start.6) | collective-permute-done | bytes 393248 | tf_op jit(solution)/shard_map/ppermute | solution.py:502
  89.7 0.0 collective-permute-done.7.refs_5_
  89.7 0.0 collective-permute-done.8.refs_6_
  89.7 3.0 %join.1 = f32[96,64,128]{2,1,0:T(8,128)} custom-call(s32[1]{0:T(128)} %bitcast.me_ref, f32[96,64,128]{2,1,0:T(8,128)} %bitcast.5, f32[12,64,128]{2,1,0:T(8,128)} %get-tuple-element.17.own_ref, f32[12,64,128]{2,1,0:T(8,128)S(1)} %collective-permute-done.2.refs_0_, f32[12,64,128]{2,1,0:T(8,128)S(1)} %collective-permute-done.3.refs_1_, ...), custom_call_target="tpu_custom_call" | custom-call | flops 786432 | bytes 9437184 | tf_op jit(solution)/shard_map/join/pallas_call | solution.py:479
  (6 shorter events, 0.0 us)
Async XLA Ops:
  0.6 5.3 %copy-start = (f32[3,1,1,4096]{3,2,1,0:T(1,128)S(1)}, f32[3,1,1,4096]{3,2,1,0:T(1,128)}, u32[]{:S(2)}) copy-start(f32[3,1,1,4096]{3,2,1,0:T(1,128)} %spring_ref.5) | copy-start | bytes 147460
  0.6 5.3 %copy-start.2 = (s32[2,1,1,4096]{3,2,1,0:T(1,128)S(1)}, s32[2,1,1,4096]{3,2,1,0:T(1,128)}, u32[]{:S(2)}) copy-start(s32[2,1,1,4096]{3,2,1,0:T(1,128)} %ids_ref.5) | copy-start | bytes 98308
  0.6 44.4 %all-to-all-start = ((f32[8,12,64,128]{3,2,1,0:T(8,128)}), f32[8,12,64,128]{3,2,1,0:T(8,128)S(1)}, u32[]{:S(2)}, u32[]{:S(2)}) async-start(f32[8,12,64,128]{3,2,1,0:T(8,128)} %bitcast.4), calls=%async_computation | async-start | bytes 6291456 | tf_op jit(solution)/shard_map/all_to_all | solution.py:520
  11.7 22.1 %collective-permute-start.1 = (f32[2,3,4,64,128]{4,3,2,1,0:T(8,128)}, f32[2,3,4,64,128]{4,3,2,1,0:T(8,128)}, u32[]{:S(2)}, u32[]{:S(2)}) collective-permute-start(f32[2,3,4,64,128]{4,3,2,1,0:T(8,128)} %get-tuple-element.15._.low_edge_ref), channel_id=1, source_target_pairs={{1,0},{2,1},{3,2},{5,4},{6,5},{7,6},{9,8},{10,9},{11,10},{13,12},{... | collective-permute-start | bytes 2359304 | tf_op jit(solution)/shard_map/ppermute | solution.py:511
  13.0 22.0 %collective-permute-start = (f32[2,3,4,64,128]{4,3,2,1,0:T(8,128)}, f32[2,3,4,64,128]{4,3,2,1,0:T(8,128)}, u32[]{:S(2)}, u32[]{:S(2)}) collective-permute-start(f32[2,3,4,64,128]{4,3,2,1,0:T(8,128)} %get-tuple-element.14.high_edge_ref), channel_id=1, source_target_pairs={{0,1},{1,2},{2,3},{4,5},{5,6},{6,7},{8,9},{9,10},{10,11},{12,13},{... | collective-permute-start | bytes 2359304 | tf_op jit(solution)/shard_map/ppermute | solution.py:510
  18.4 16.6 %copy-start.3 = (f32[32,32]{1,0:T(8,128)S(1)}, f32[32,32]{1,0:T(8,128)}, u32[]{:S(2)}) copy-start(f32[32,32]{1,0:T(8,128)} %inverse_ref.1) | copy-start | bytes 12292
  18.4 16.6 %copy-start.4 = (f32[9,32]{1,0:T(8,128)S(1)}, f32[9,32]{1,0:T(8,128)}, u32[]{:S(2)}) copy-start(f32[9,32]{1,0:T(8,128)} %stencil_ref.1) | copy-start | bytes 3460
  31.1 14.0 %copy-start.5 = (f32[32]{0:T(128)S(1)}, f32[32]{0:T(128)}, u32[]{:S(2)}) copy-start(f32[32]{0:T(128)} %coef_ref.1) | copy-start | bytes 388
  45.1 20.1 %copy-start.1 = (f32[3,1,1,4096]{3,2,1,0:T(1,128)S(1)}, f32[3,1,1,4096]{3,2,1,0:T(1,128)}, u32[]{:S(2)}) copy-start(f32[3,1,1,4096]{3,2,1,0:T(1,128)} %noise_ref.1) | copy-start | bytes 147460
  51.6 3.7 %collective-permute-start.2 = (f32[12,64,128]{2,1,0:T(8,128)}, f32[12,64,128]{2,1,0:T(8,128)S(1)}, u32[]{:S(2)}, u32[]{:S(2)}) collective-permute-start(f32[12,64,128]{2,1,0:T(8,128)} %get-tuple-element.18), channel_id=1, source_target_pairs={{0,4},{4,0},{8,12},{12,8},{16,20},{20,16},{24,28},{28,24},{1,5},{5... | collective-permute-start | bytes 1179656 | tf_op jit(solution)/shard_map/ppermute | solution.py:502
  51.6 12.2 %collective-permute-start.3 = (f32[12,64,128]{2,1,0:T(8,128)}, f32[12,64,128]{2,1,0:T(8,128)S(1)}, u32[]{:S(2)}, u32[]{:S(2)}) collective-permute-start(f32[12,64,128]{2,1,0:T(8,128)} %get-tuple-element.19), channel_id=1, source_target_pairs={{0,8},{4,12},{8,0},{12,4},{16,24},{20,28},{24,16},{28,20},{1,9},{5... | collective-permute-start | bytes 1179656 | tf_op jit(solution)/shard_map/ppermute | solution.py:502
  53.4 29.0 %collective-permute-start.4 = (f32[12,64,128]{2,1,0:T(8,128)}, f32[12,64,128]{2,1,0:T(8,128)S(1)}, u32[]{:S(2)}, u32[]{:S(2)}) collective-permute-start(f32[12,64,128]{2,1,0:T(8,128)} %get-tuple-element.20), channel_id=1, source_target_pairs={{0,12},{4,8},{8,4},{12,0},{16,28},{20,24},{24,20},{28,16},{1,13},{... | collective-permute-start | bytes 1179656 | tf_op jit(solution)/shard_map/ppermute | solution.py:502
  53.5 28.8 %collective-permute-start.5 = (f32[12,64,128]{2,1,0:T(8,128)}, f32[12,64,128]{2,1,0:T(8,128)S(1)}, u32[]{:S(2)}, u32[]{:S(2)}) collective-permute-start(f32[12,64,128]{2,1,0:T(8,128)} %get-tuple-element.21), channel_id=1, source_target_pairs={{0,16},{4,20},{8,24},{12,28},{16,0},{20,4},{24,8},{28,12},{1,17},{... | collective-permute-start | bytes 1179656 | tf_op jit(solution)/shard_map/ppermute | solution.py:502
  55.2 34.5 %collective-permute-start.6 = (f32[12,64,128]{2,1,0:T(8,128)}, f32[12,64,128]{2,1,0:T(8,128)S(1)}, u32[]{:S(2)}, u32[]{:S(2)}) collective-permute-start(f32[12,64,128]{2,1,0:T(8,128)} %get-tuple-element.22), channel_id=1, source_target_pairs={{0,20},{4,16},{8,28},{12,24},{16,4},{20,0},{24,12},{28,8},{1,21},{... | collective-permute-start | bytes 1179656 | tf_op jit(solution)/shard_map/ppermute | solution.py:502
  55.2 34.4 %collective-permute-start.7 = (f32[12,64,128]{2,1,0:T(8,128)}, f32[12,64,128]{2,1,0:T(8,128)S(1)}, u32[]{:S(2)}, u32[]{:S(2)}) collective-permute-start(f32[12,64,128]{2,1,0:T(8,128)} %get-tuple-element.23), channel_id=1, source_target_pairs={{0,24},{4,28},{8,16},{12,20},{16,8},{20,12},{24,0},{28,4},{1,25},{... | collective-permute-start | bytes 1179656 | tf_op jit(solution)/shard_map/ppermute | solution.py:502
  63.8 25.8 %collective-permute-start.8 = (f32[12,64,128]{2,1,0:T(8,128)}, f32[12,64,128]{2,1,0:T(8,128)S(1)}, u32[]{:S(2)}, u32[]{:S(2)}) collective-permute-start(f32[12,64,128]{2,1,0:T(8,128)} %get-tuple-element.24), channel_id=1, source_target_pairs={{0,28},{4,24},{8,20},{12,16},{16,12},{20,8},{24,4},{28,0},{1,29},{... | collective-permute-start | bytes 1179656 | tf_op jit(solution)/shard_map/ppermute | solution.py:502

commit v12 on v11

--- a/solution.py
+++ b/solution.py
@@ -198,8 +198,6 @@
     def _():
         matrix_ref[...] = derivative_matrix(stencil_ref, inverse_ref)
 
-    group = radii * SUB
-
     for i in range(angles // SUB):
         at = pl.ds(i * SUB, SUB)
         columns = []
@@ -217,10 +215,8 @@
         for c in range(3):
             force = TIME_STEP * result[:, (3 + c) * axial : (4 + c) * axial]
             force_ref[c, :, at, :] = force.reshape(radii, SUB, axial)
-        turned_high, turned_low = split(result[:, : 3 * axial].T)
-        cols = pl.ds(i * group, group)
-        grad_ref[: 3 * axial, cols] = turned_high
-        grad_ref[3 * axial :, cols] = turned_low
+            grad = result[:, c * axial : (c + 1) * axial]
+            grad_ref[c, :, at, :] = grad.reshape(radii, SUB, axial)
 
 
 def derive(stencil, inverse, low, velocity, stress, high):
@@ -247,11 +243,11 @@
             block(HALO, 0),
         ],
         out_specs=[
-            pl.BlockSpec((6 * axial, radii * part), lambda i: (0, i)),
+            block(radii),
             block(radii),
         ],
         out_shape=[
-            pltpu.HBM((6 * axial, radii * angles), BF16),
+            pltpu.HBM(velocity.shape, F32),
             pltpu.HBM(velocity.shape, F32),
         ],
         scratch_shapes=[pltpu.VMEM((2 * radii * SUB, (radii + 2 * HALO) * SUB), BF16)],
@@ -274,9 +270,23 @@
     )
 
 
-def move_kernel(grad_ref, ids_ref, spring_ref, noise_ref, moved_ref, *, angles):
-    axial, cells = grad_ref.shape[0] // 6, grad_ref.shape[1]
-    group = cells // angles * SUB
+def move_kernel(grad_ref, ids_ref, spring_ref, noise_ref, moved_ref, turned_ref):
+    _, radii, angles, axial = grad_ref.shape
+    cells = radii * angles
+    group = radii * SUB
+
+    def turn(i, carry):
+        at = pl.ds(pl.multiple_of(i * SUB, SUB), SUB)
+        value = jnp.concatenate(
+            [grad_ref[c, :, at, :].reshape(group, axial) for c in range(3)], axis=1
+        )
+        turned_high, turned_low = split(value.T)
+        cols = pl.ds(pl.multiple_of(i * group, group), group)
+        turned_ref[: 3 * axial, cols] = turned_high
+        turned_ref[3 * axial :, cols] = turned_low
+        return carry
+
+    lax.fori_loop(0, angles // SUB, turn, 0)
 
     count = spring_ref.shape[3]
     part = min(count, 512)
@@ -287,7 +297,7 @@
         radius, angle = plane // angles, plane % angles
         column = (angle // SUB) * group + radius * SUB + angle % SUB
         hot = jnp.where(iota((cells, part), 0) == column, 1.0, 0.0).astype(BF16)
-        picked = dot(grad_ref[...], hot)
+        picked = dot(turned_ref[...], hot)
         here = iota((axial, part), 0) == ids_ref[1, 0, :, at]
         q = [spring_ref[c, 0, :, at] for c in range(3)]
         stretch_sq = q[0] * q[0] + q[1] * q[1] + q[2] * q[2]
@@ -307,18 +317,19 @@
     lax.fori_loop(0, count // part, read, 0)
 
 
-def move(grad, ids, spring, noise, angles):
-    cells = grad.shape[1]
+def move(grad, ids, spring, noise):
+    _, radii, angles, axial = grad.shape
     whole = pl.BlockSpec(memory_space=pltpu.VMEM)
     return pl.pallas_call(
-        functools.partial(move_kernel, angles=angles),
+        move_kernel,
         in_specs=[whole] * 4,
         out_specs=whole,
         out_shape=jax.ShapeDtypeStruct(spring.shape, F32),
-        compiler_params=pltpu.CompilerParams(vmem_limit_bytes=24 * MIB),
+        scratch_shapes=[pltpu.VMEM((6 * axial, radii * angles), BF16)],
+        compiler_params=pltpu.CompilerParams(vmem_limit_bytes=28 * MIB),
         cost_estimate=pl.CostEstimate(
-            flops=2 * grad.size * spring.shape[3],
-            bytes_accessed=2 * grad.size,
+            flops=4 * grad.size * spring.shape[3],
+            bytes_accessed=4 * grad.size,
             transcendentals=0,
         ),
         name="move",
@@ -443,55 +454,53 @@
     )
 
 
-def join_kernel(me_ref, force_ref, own_ref, *refs):
-    count = len(refs) - 4
-    piece_refs, (out_ref, sum_ref, in_sems, out_sems) = refs[:count], refs[count:]
-    blocks, rows = sum_ref.shape[0] - 1, sum_ref.shape[1]
-    me = me_ref[0]
+def join_kernel(me_ref, force_ref, *refs, first, given):
+    count = len(refs) - 4 - given
+    piece_refs, refs = refs[:count], refs[count + given :]
+    out_ref, sum_ref, in_sems, out_sems = refs
+    rows = sum_ref.shape[1]
     reads, writes = [], []
-    for s in range(blocks):
-        at = pl.ds((me ^ s) * rows, rows)
-        reads.append(
-            pltpu.make_async_copy(force_ref.at[at], sum_ref.at[s], in_sems.at[s])
-        )
-        writes.append(
-            pltpu.make_async_copy(sum_ref.at[s], out_ref.at[at], out_sems.at[s])
-        )
-    own = pltpu.make_async_copy(own_ref, sum_ref.at[blocks], in_sems.at[blocks])
-    own.start()
+    for i in range(count):
+        at = pl.ds((me_ref[0] ^ (first + i)) * rows, rows)
+        reads.append(pltpu.make_async_copy(force_ref.at[at], sum_ref.at[i], in_sems.at[i]))
+        writes.append(pltpu.make_async_copy(sum_ref.at[i], out_ref.at[at], out_sems.at[i]))
     for copy in reads:
         copy.start()
-    own.wait()
-    for s in range(blocks):
-        reads[s].wait()
-        piece = sum_ref[blocks] if s == 0 else piece_refs[s - 1][...]
-        sum_ref[s] = sum_ref[s] + piece
-        writes[s].start()
+    for i in range(count):
+        reads[i].wait()
+        sum_ref[i] = sum_ref[i] + piece_refs[i][...]
+        writes[i].start()
     for copy in writes:
         copy.wait()
 
 
-def join(me, force, pieces):
+def join(me, force, pieces, first, result=None):
     rows, angles, axial = pieces[0].shape
-    blocks = len(pieces)
+    count = len(pieces)
+    given = [] if result is None else [in_hbm(result)]
     whole = pl.BlockSpec(memory_space=pltpu.VMEM)
     away = pl.BlockSpec(memory_space=pl.ANY)
     return pl.pallas_call(
-        join_kernel,
-        in_specs=[pl.BlockSpec(memory_space=pltpu.SMEM), away, away] + [whole] * (blocks - 1),
+        functools.partial(join_kernel, first=first, given=len(given)),
+        in_specs=[pl.BlockSpec(memory_space=pltpu.SMEM), away]
+        + [whole] * count
+        + [away] * len(given),
         out_specs=away,
         out_shape=pltpu.HBM(force.shape, F32),
+        input_output_aliases={2 + count: 0} if given else {},
         scratch_shapes=[
-            pltpu.VMEM((blocks + 1, rows, angles, axial), F32),
-            pltpu.SemaphoreType.DMA((blocks + 1,)),
-            pltpu.SemaphoreType.DMA((blocks,)),
+            pltpu.VMEM((count, rows, angles, axial), F32),
+            pltpu.SemaphoreType.DMA((count,)),
+            pltpu.SemaphoreType.DMA((count,)),
         ],
         compiler_params=pltpu.CompilerParams(vmem_limit_bytes=14 * MIB),
         cost_estimate=pl.CostEstimate(
-            flops=force.size, bytes_accessed=12 * force.size, transcendentals=0
+            flops=count * rows * angles * axial,
+            bytes_accessed=12 * count * rows * angles * axial,
+            transcendentals=0,
         ),
         name="join",
-    )(me, in_hbm(force), in_hbm(pieces[0]), *[in_vmem(piece) for piece in pieces[1:]])
+    )(me, in_hbm(force), *pieces, *given)
 
 
 def exchange(pieces):
@@ -526,9 +535,12 @@
     me = lax.axis_index("az").astype(jnp.int32).reshape(1)
     solved = solve(azim_coef, me, gathered, (in_hbm(force),))
     pieces = exchange(solved)
-    moved = move(grad, cell_ids, dumbbells, brownian, angles)
+    moved = move(grad, cell_ids, dumbbells, brownian)
     lines = (3 * radii, angles, axial)
-    result = join(me, force.reshape(lines), pieces)
+    force = force.reshape(lines)
+    early = len(pieces) * 3 // 8
+    result = join(me, force, pieces[:early], 0)
+    result = join(me, force, [in_vmem(piece) for piece in pieces[early:]], early, result)
     return result.reshape(velocity.shape), moved
 
 

time: 94.5 us -> 93.7 us (level)
  waiting for transfers between devices: 17.3 us -> 13.7 us
  Pallas kernels: 54.9 us -> 57.7 us
    ppermute x7, waiting for transfers between devices: 13.4 us -> 9.79 us  [exchange(): lax.ppermute(pieces[s], 'az', [(i, i ^ s) for i in range(count)])]
    pallas_call x2 -> x3, Pallas kernels: 20.1 us -> 23.1 us  [the longest x1 18.6 us: move(): pl.pallas_call(move_kernel, in_specs=[whole] * 4, out_specs=whole, out_sh...]
  transfers between devices with their start and end apart: 10 -> 10, of which waited for: 4 -> 4; matrix products, arithmetic and copies ran while one was open for 0% -> 0% of each run, Pallas kernels for 49% -> 53%
where the time goes in v12:
time: 93.7 us; the launch traced here: 92 us
  Pallas kernels  57.7 us (62%)
  starting transfers between devices  19.6 us (21%)
  waiting for transfers between devices  13.7 us (15%)
    pallas_call x1, Pallas kernels, move(): pl.pallas_call(move_kernel, in_specs=[whole] * 4, out_specs=whole, out_sh...  18.6 us
    pallas_call x1, Pallas kernels, deposit_middle(): pl.pallas_call(lambda ids_ref, spring_ref, _, *refs: middle_kernel(ids_re...  12.6 us
    pallas_call x1, Pallas kernels, derive(): pl.pallas_call(derive_kernel, grid=(angles // part,), in_specs=[pl.BlockS...  9.86 us
    ppermute x7, waiting for transfers between devices, exchange(): lax.ppermute(pieces[s], 'az', [(i, i ^ s) for i in range(count)])  9.79 us
    ppermute x7, starting transfers between devices, exchange(): lax.ppermute(pieces[s], 'az', [(i, i ^ s) for i in range(count)])  7.58 us
    pallas_call x1, Pallas kernels, solve(): pl.pallas_call(functools.partial(solve_kernel, extra=len(after)), in_spec...  6.43 us
    pallas_call x1, Pallas kernels, deposit_edges(): pl.pallas_call(functools.partial(edge_kernel, radii=radii), grid=(1,), in...  5.73 us
    ppermute x1, starting transfers between devices, from_neighbours(): low = lax.ppermute(high_edge, 'rad', forward)  5.45 us
  transfers between devices with their start and end apart: 10, of which 4 were waited for; matrix products, arithmetic and copies ran while one was open for 0% of the time, Pallas kernels for 53%

profile of v12, /device:TPU:0, one launch (start us, length us, event | category | flops | bytes accessed | tf_op | source)
XLA Modules:
  0.0 92.0 jit_solution(13154631884635763063)
XLA Ops:
  0.6 0.0 copy-start.1
  0.6 0.0 copy-start.3
  0.6 5.3 %all-to-all-start = ((f32[8,12,64,128]{3,2,1,0:T(8,128)}), f32[8,12,64,128]{3,2,1,0:T(8,128)S(1)}, u32[]{:S(2)}, u32[]{:S(2)}) async-start(f32[8,12,64,128]{3,2,1,0:T(8,128)} %bitcast.7), calls=%async_computation | async-start | bytes 6291456 | tf_op jit(solution)/shard_map/all_to_all | solution.py:529
  6.0 5.7 %deposit_edges.1 = (f32[2,3,4,64,128]{4,3,2,1,0:T(8,128)}, f32[2,3,4,64,128]{4,3,2,1,0:T(8,128)}) custom-call(s32[2,1,1,4096]{3,2,1,0:T(1,128)S(1)} %copy-done.3, f32[3,1,1,4096]{3,2,1,0:T(1,128)S(1)} %copy-done.1, f32[3,32,64,128]{3,2,1,0:T(8,128)} %velocity_ref.1, f32[3,32,64,128]{3,2,1,0:T(8,128)} %velocity_ref.1), custom_call_target="tpu_custom_call" | custom-call | flops 3221225472 | bytes 3145728 | tf_op jit(solution)/shard_map/deposit_edges/pallas_call | solution.py:112
  11.7 1.3 %collective-permute-start.1 = (f32[2,3,4,64,128]{4,3,2,1,0:T(8,128)}, f32[2,3,4,64,128]{4,3,2,1,0:T(8,128)}, u32[]{:S(2)}, u32[]{:S(2)}) collective-permute-start(f32[2,3,4,64,128]{4,3,2,1,0:T(8,128)} %get-tuple-element.15._.low_edge_ref), channel_id=1, source_target_pairs={{1,0},{2,1},{3,2},{5,4},{6,5},{7,6},{9,8},{10,9},{11,10},{13,12},{... | collective-permute-start | bytes 2359304 | tf_op jit(solution)/shard_map/ppermute | solution.py:520
  13.0 5.5 %collective-permute-start = (f32[2,3,4,64,128]{4,3,2,1,0:T(8,128)}, f32[2,3,4,64,128]{4,3,2,1,0:T(8,128)}, u32[]{:S(2)}, u32[]{:S(2)}) collective-permute-start(f32[2,3,4,64,128]{4,3,2,1,0:T(8,128)} %get-tuple-element.14.high_edge_ref), channel_id=1, source_target_pairs={{0,1},{1,2},{2,3},{4,5},{5,6},{6,7},{8,9},{9,10},{10,11},{12,13},{... | collective-permute-start | bytes 2359304 | tf_op jit(solution)/shard_map/ppermute | solution.py:519
  18.5 12.6 %deposit_middle.1.middle_ref = f32[3,24,64,128]{3,2,1,0:T(8,128)} custom-call(s32[2,1,1,4096]{3,2,1,0:T(1,128)S(1)} %copy-done.3, f32[3,1,1,4096]{3,2,1,0:T(1,128)S(1)} %copy-done.1, f32[2,3,4,64,128]{4,3,2,1,0:T(8,128)} %get-tuple-element.15._.low_edge_ref), custom_call_target="tpu_custom_call" | custom-call | flops 9663676416 | bytes 2359296 | tf_op jit(solution)/shard_map/deposit_middle/pallas_call | solution.py:140
  31.1 2.8 %collective-permute-done.1.high_ref = f32[2,3,4,64,128]{4,3,2,1,0:T(8,128)} collective-permute-done((f32[2,3,4,64,128]{4,3,2,1,0:T(8,128)}, f32[2,3,4,64,128]{4,3,2,1,0:T(8,128)}, u32[]{:S(2)}, u32[]{:S(2)}) %collective-permute-start.1) | collective-permute-done | bytes 786464 | tf_op jit(solution)/shard_map/ppermute | solution.py:520
  33.9 1.2 %collective-permute-done.low_ref = f32[2,3,4,64,128]{4,3,2,1,0:T(8,128)} collective-permute-done((f32[2,3,4,64,128]{4,3,2,1,0:T(8,128)}, f32[2,3,4,64,128]{4,3,2,1,0:T(8,128)}, u32[]{:S(2)}, u32[]{:S(2)}) %collective-permute-start) | collective-permute-done | bytes 786464 | tf_op jit(solution)/shard_map/ppermute | solution.py:519
  35.0 9.9 %derive.1 = (f32[3,32,64,128]{3,2,1,0:T(8,128)}, f32[3,32,64,128]{3,2,1,0:T(8,128)}) custom-call(f32[9,32]{1,0:T(8,128)S(1)} %copy-done.5, f32[32,32]{1,0:T(8,128)S(1)} %copy-done.4, f32[2,3,4,64,128]{4,3,2,1,0:T(8,128)} %collective-permute-done.low_ref, f32[3,32,64,128]{3,2,1,0:T(8,128)} %velocity_ref.1, ...), custom_call_target="tpu_custom_call" | custom-call | flops 3774873600 | bytes 10485760 | tf_op jit(solution)/shard_map/derive/pallas_call | solution.py:232
  44.9 0.0 all-to-all-done.refs_1_
  44.9 0.0 copy-done.6
  44.9 0.0 copy-start.2
  44.9 6.4 %solve.1 = (f32[12,64,128]{2,1,0:T(8,128)}, f32[12,64,128]{2,1,0:T(8,128)}, f32[12,64,128]{2,1,0:T(8,128)}, f32[12,64,128]{2,1,0:T(8,128)}, f32[12,64,128]{2,1,0...) custom-call(f32[32]{0:T(128)S(1)} %copy-done.6, s32[1]{0:T(128)} %bitcast.me_ref, ...), custom_call_target="tpu_custom_call" | custom-call | flops 4831838208 | bytes 6291456 | tf_op jit(solution)/shard_map/solve/pallas_call | solution.py:430
  51.4 0.1 collective-permute-start.7
  51.5 1.7 %collective-permute-start.8 = (f32[12,64,128]{2,1,0:T(8,128)}, f32[12,64,128]{2,1,0:T(8,128)S(1)}, u32[]{:S(2)}, u32[]{:S(2)}) collective-permute-start(f32[12,64,128]{2,1,0:T(8,128)} %get-tuple-element.24), channel_id=1, source_target_pairs={{0,8},{4,12},{8,0},{12,4},{16,24},{20,28},{24,16},{28,20},{1,9},{5... | collective-permute-start | bytes 1179656 | tf_op jit(solution)/shard_map/ppermute | solution.py:511
  53.2 0.1 collective-permute-start.2
  53.3 1.7 %collective-permute-start.3 = (f32[12,64,128]{2,1,0:T(8,128)}, f32[12,64,128]{2,1,0:T(8,128)S(1)}, u32[]{:S(2)}, u32[]{:S(2)}) collective-permute-start(f32[12,64,128]{2,1,0:T(8,128)} %get-tuple-element.18), channel_id=1, source_target_pairs={{0,16},{4,20},{8,24},{12,28},{16,0},{20,4},{24,8},{28,12},{1,17},{... | collective-permute-start | bytes 1179656 | tf_op jit(solution)/shard_map/ppermute | solution.py:511
  55.0 0.0 collective-permute-start.4
  55.0 0.0 collective-permute-done.7.refs_1_
  55.0 2.6 %collective-permute-start.5 = (f32[12,64,128]{2,1,0:T(8,128)}, f32[12,64,128]{2,1,0:T(8,128)S(1)}, u32[]{:S(2)}, u32[]{:S(2)}) collective-permute-start(f32[12,64,128]{2,1,0:T(8,128)} %get-tuple-element.20), channel_id=1, source_target_pairs={{0,24},{4,28},{8,16},{12,20},{16,8},{20,12},{24,0},{28,4},{1,25},{... | collective-permute-start | bytes 1179656 | tf_op jit(solution)/shard_map/ppermute | solution.py:511
  57.6 6.1 %collective-permute-done.8.refs_2_ = f32[12,64,128]{2,1,0:T(8,128)S(1)} collective-permute-done((f32[12,64,128]{2,1,0:T(8,128)}, f32[12,64,128]{2,1,0:T(8,128)S(1)}, u32[]{:S(2)}, u32[]{:S(2)}) %collective-permute-start.8) | collective-permute-done | bytes 393248 | tf_op jit(solution)/shard_map/ppermute | solution.py:511
  63.6 1.4 %collective-permute-start.6 = (f32[12,64,128]{2,1,0:T(8,128)}, f32[12,64,128]{2,1,0:T(8,128)S(1)}, u32[]{:S(2)}, u32[]{:S(2)}) collective-permute-start(f32[12,64,128]{2,1,0:T(8,128)} %get-tuple-element.21), channel_id=1, source_target_pairs={{0,28},{4,24},{8,20},{12,16},{16,12},{20,8},{24,4},{28,0},{1,29},{... | collective-permute-start | bytes 1179656 | tf_op jit(solution)/shard_map/ppermute | solution.py:511
  65.0 18.6 %move.1 = f32[3,1,1,4096]{3,2,1,0:T(1,128)} custom-call(f32[3,32,64,128]{3,2,1,0:T(8,128)} %get-tuple-element.25.grad_ref, s32[2,1,1,4096]{3,2,1,0:T(1,128)S(1)} %copy-done.3, f32[3,1,1,4096]{3,2,1,0:T(1,128)S(1)} %copy-done.1, f32[3,1,1,4096]{3,2,1,0:T(1,128)S(1)} %copy-done.2), custom_call_target="tpu_custom_call" | custom-call | flops 12884901888 | bytes 3145728 | tf_op jit(solution)/shard_map/move/pallas_call | solution.py:323
  83.6 0.0 copy-done
  83.6 2.1 %join.2.refs_5_ = f32[96,64,128]{2,1,0:T(8,128)} custom-call(s32[1]{0:T(128)} %bitcast.me_ref, f32[96,64,128]{2,1,0:T(8,128)} %bitcast.4, f32[12,64,128]{2,1,0:T(8,128)S(1)} %copy-done, f32[12,64,128]{2,1,0:T(8,128)S(1)} %collective-permute-done.7.refs_1_, f32[12,64,128]{2,1,0:T(8,128)S(1)} %collective-permute-done.8.refs_2_), custom_call_target="tpu_custom_call" | custom-call | flops 294912 | bytes 3538944 | tf_op jit(solution)/shard_map/join/pallas_call | solution.py:483
  85.7 0.0 collective-permute-done.2.refs_0_
  85.7 0.0 collective-permute-done.3.refs_1_
  85.7 3.7 %collective-permute-done.4.refs_2_ = f32[12,64,128]{2,1,0:T(8,128)S(1)} collective-permute-done((f32[12,64,128]{2,1,0:T(8,128)}, f32[12,64,128]{2,1,0:T(8,128)S(1)}, u32[]{:S(2)}, u32[]{:S(2)}) %collective-permute-start.4) | collective-permute-done | bytes 393248 | tf_op jit(solution)/shard_map/ppermute | solution.py:511
  89.5 0.0 collective-permute-done.5.refs_3_
  89.5 0.0 collective-permute-done.6.refs_4_
  89.5 2.4 %join.3 = f32[96,64,128]{2,1,0:T(8,128)} custom-call(s32[1]{0:T(128)} %bitcast.me_ref, f32[96,64,128]{2,1,0:T(8,128)} %bitcast.5, f32[12,64,128]{2,1,0:T(8,128)S(1)} %collective-permute-done.2.refs_0_, f32[12,64,128]{2,1,0:T(8,128)S(1)} %collective-permute-done.3.refs_1_, ...), custom_call_target="tpu_custom_call", output_to_operand_aliasing={{}: (7, {})} | custom-call | flops 491520 | bytes 5898240 | tf_op jit(solution)/shard_map/join/pallas_call | solution.py:483
  (9 shorter events, 0.0 us)
Async XLA Ops:
  0.6 5.3 %copy-start.1 = (f32[3,1,1,4096]{3,2,1,0:T(1,128)S(1)}, f32[3,1,1,4096]{3,2,1,0:T(1,128)}, u32[]{:S(2)}) copy-start(f32[3,1,1,4096]{3,2,1,0:T(1,128)} %spring_ref.5) | copy-start | bytes 147460
  0.6 5.3 %copy-start.3 = (s32[2,1,1,4096]{3,2,1,0:T(1,128)S(1)}, s32[2,1,1,4096]{3,2,1,0:T(1,128)}, u32[]{:S(2)}) copy-start(s32[2,1,1,4096]{3,2,1,0:T(1,128)} %ids_ref.5) | copy-start | bytes 98308
  0.6 44.3 %all-to-all-start = ((f32[8,12,64,128]{3,2,1,0:T(8,128)}), f32[8,12,64,128]{3,2,1,0:T(8,128)S(1)}, u32[]{:S(2)}, u32[]{:S(2)}) async-start(f32[8,12,64,128]{3,2,1,0:T(8,128)} %bitcast.7), calls=%async_computation | async-start | bytes 6291456 | tf_op jit(solution)/shard_map/all_to_all | solution.py:529
  11.7 22.1 %collective-permute-start.1 = (f32[2,3,4,64,128]{4,3,2,1,0:T(8,128)}, f32[2,3,4,64,128]{4,3,2,1,0:T(8,128)}, u32[]{:S(2)}, u32[]{:S(2)}) collective-permute-start(f32[2,3,4,64,128]{4,3,2,1,0:T(8,128)} %get-tuple-element.15._.low_edge_ref), channel_id=1, source_target_pairs={{1,0},{2,1},{3,2},{5,4},{6,5},{7,6},{9,8},{10,9},{11,10},{13,12},{... | collective-permute-start | bytes 2359304 | tf_op jit(solution)/shard_map/ppermute | solution.py:520
  13.0 22.0 %collective-permute-start = (f32[2,3,4,64,128]{4,3,2,1,0:T(8,128)}, f32[2,3,4,64,128]{4,3,2,1,0:T(8,128)}, u32[]{:S(2)}, u32[]{:S(2)}) collective-permute-start(f32[2,3,4,64,128]{4,3,2,1,0:T(8,128)} %get-tuple-element.14.high_edge_ref), channel_id=1, source_target_pairs={{0,1},{1,2},{2,3},{4,5},{5,6},{6,7},{8,9},{9,10},{10,11},{12,13},{... | collective-permute-start | bytes 2359304 | tf_op jit(solution)/shard_map/ppermute | solution.py:519
  18.5 16.6 %copy-start.4 = (f32[32,32]{1,0:T(8,128)S(1)}, f32[32,32]{1,0:T(8,128)}, u32[]{:S(2)}) copy-start(f32[32,32]{1,0:T(8,128)} %inverse_ref.1) | copy-start | bytes 12292
  18.5 16.6 %copy-start.5 = (f32[9,32]{1,0:T(8,128)S(1)}, f32[9,32]{1,0:T(8,128)}, u32[]{:S(2)}) copy-start(f32[9,32]{1,0:T(8,128)} %stencil_ref.1) | copy-start | bytes 3460
  31.1 13.8 %copy-start.6 = (f32[32]{0:T(128)S(1)}, f32[32]{0:T(128)}, u32[]{:S(2)}) copy-start(f32[32]{0:T(128)} %coef_ref.1) | copy-start | bytes 388
  44.9 20.1 %copy-start.2 = (f32[3,1,1,4096]{3,2,1,0:T(1,128)S(1)}, f32[3,1,1,4096]{3,2,1,0:T(1,128)}, u32[]{:S(2)}) copy-start(f32[3,1,1,4096]{3,2,1,0:T(1,128)} %noise_ref.1) | copy-start | bytes 147460
  51.4 3.7 %collective-permute-start.7 = (f32[12,64,128]{2,1,0:T(8,128)}, f32[12,64,128]{2,1,0:T(8,128)S(1)}, u32[]{:S(2)}, u32[]{:S(2)}) collective-permute-start(f32[12,64,128]{2,1,0:T(8,128)} %get-tuple-element.23), channel_id=1, source_target_pairs={{0,4},{4,0},{8,12},{12,8},{16,20},{20,16},{24,28},{28,24},{1,5},{5... | collective-permute-start | bytes 1179656 | tf_op jit(solution)/shard_map/ppermute | solution.py:511
  51.5 12.2 %collective-permute-start.8 = (f32[12,64,128]{2,1,0:T(8,128)}, f32[12,64,128]{2,1,0:T(8,128)S(1)}, u32[]{:S(2)}, u32[]{:S(2)}) collective-permute-start(f32[12,64,128]{2,1,0:T(8,128)} %get-tuple-element.24), channel_id=1, source_target_pairs={{0,8},{4,12},{8,0},{12,4},{16,24},{20,28},{24,16},{28,20},{1,9},{5... | collective-permute-start | bytes 1179656 | tf_op jit(solution)/shard_map/ppermute | solution.py:511
  53.2 32.5 %collective-permute-start.2 = (f32[12,64,128]{2,1,0:T(8,128)}, f32[12,64,128]{2,1,0:T(8,128)S(1)}, u32[]{:S(2)}, u32[]{:S(2)}) collective-permute-start(f32[12,64,128]{2,1,0:T(8,128)} %get-tuple-element.17), channel_id=1, source_target_pairs={{0,12},{4,8},{8,4},{12,0},{16,28},{20,24},{24,20},{28,16},{1,13},{... | collective-permute-start | bytes 1179656 | tf_op jit(solution)/shard_map/ppermute | solution.py:511
  53.3 32.4 %collective-permute-start.3 = (f32[12,64,128]{2,1,0:T(8,128)}, f32[12,64,128]{2,1,0:T(8,128)S(1)}, u32[]{:S(2)}, u32[]{:S(2)}) collective-permute-start(f32[12,64,128]{2,1,0:T(8,128)} %get-tuple-element.18), channel_id=1, source_target_pairs={{0,16},{4,20},{8,24},{12,28},{16,0},{20,4},{24,8},{28,12},{1,17},{... | collective-permute-start | bytes 1179656 | tf_op jit(solution)/shard_map/ppermute | solution.py:511
  55.0 34.5 %collective-permute-start.4 = (f32[12,64,128]{2,1,0:T(8,128)}, f32[12,64,128]{2,1,0:T(8,128)S(1)}, u32[]{:S(2)}, u32[]{:S(2)}) collective-permute-start(f32[12,64,128]{2,1,0:T(8,128)} %get-tuple-element.19), channel_id=1, source_target_pairs={{0,20},{4,16},{8,28},{12,24},{16,4},{20,0},{24,12},{28,8},{1,21},{... | collective-permute-start | bytes 1179656 | tf_op jit(solution)/shard_map/ppermute | solution.py:511
  55.0 34.4 %collective-permute-start.5 = (f32[12,64,128]{2,1,0:T(8,128)}, f32[12,64,128]{2,1,0:T(8,128)S(1)}, u32[]{:S(2)}, u32[]{:S(2)}) collective-permute-start(f32[12,64,128]{2,1,0:T(8,128)} %get-tuple-element.20), channel_id=1, source_target_pairs={{0,24},{4,28},{8,16},{12,20},{16,8},{20,12},{24,0},{28,4},{1,25},{... | collective-permute-start | bytes 1179656 | tf_op jit(solution)/shard_map/ppermute | solution.py:511
  63.6 25.8 %collective-permute-start.6 = (f32[12,64,128]{2,1,0:T(8,128)}, f32[12,64,128]{2,1,0:T(8,128)S(1)}, u32[]{:S(2)}, u32[]{:S(2)}) collective-permute-start(f32[12,64,128]{2,1,0:T(8,128)} %get-tuple-element.21), channel_id=1, source_target_pairs={{0,28},{4,24},{8,20},{12,16},{16,12},{20,8},{24,4},{28,0},{1,29},{... | collective-permute-start | bytes 1179656 | tf_op jit(solution)/shard_map/ppermute | solution.py:511
  65.0 18.6 %copy-start = (f32[12,64,128]{2,1,0:T(8,128)S(1)}, f32[12,64,128]{2,1,0:T(8,128)}, u32[]{:S(2)}) copy-start(f32[12,64,128]{2,1,0:T(8,128)} %get-tuple-element.22.refs_0_) | copy-start | bytes 1179652

commit v13 on v12

--- a/solution.py
+++ b/solution.py
@@ -188,15 +188,23 @@
     middle_ref,
     high_edge_ref,
     high_ref,
+    piece_ref,
     grad_ref,
     force_ref,
+    passed_ref,
     matrix_ref,
+    sem,
 ):
     radii, angles, axial = velocity_ref.shape[1:]
 
+    passing = pltpu.make_async_copy(piece_ref, passed_ref, sem.at[0])
+
     @pl.when(pl.program_id(0) == 0)
     def _():
+        passing.start()
         matrix_ref[...] = derivative_matrix(stencil_ref, inverse_ref)
+
+    group = radii * SUB
 
     for i in range(angles // SUB):
         at = pl.ds(i * SUB, SUB)
@@ -215,11 +223,17 @@
         for c in range(3):
             force = TIME_STEP * result[:, (3 + c) * axial : (4 + c) * axial]
             force_ref[c, :, at, :] = force.reshape(radii, SUB, axial)
-            grad = result[:, c * axial : (c + 1) * axial]
-            grad_ref[c, :, at, :] = grad.reshape(radii, SUB, axial)
-
-
-def derive(stencil, inverse, low, velocity, stress, high):
+        turned_high, turned_low = split(result[:, : 3 * axial].T)
+        cols = pl.ds(i * group, group)
+        grad_ref[: 3 * axial, cols] = turned_high
+        grad_ref[3 * axial :, cols] = turned_low
+
+    @pl.when(pl.program_id(0) == pl.num_programs(0) - 1)
+    def _():
+        passing.wait()
+
+
+def derive(stencil, inverse, low, velocity, stress, high, piece):
     low_edge, middle, high_edge = stress
     radii, angles, axial = velocity.shape[1:]
     part = 2 * SUB
@@ -241,16 +255,22 @@
             block(radii - 2 * HALO),
             block(HALO, 1),
             block(HALO, 0),
+            pl.BlockSpec(memory_space=pl.ANY),
         ],
         out_specs=[
+            pl.BlockSpec((6 * axial, radii * part), lambda i: (0, i)),
             block(radii),
-            block(radii),
+            pl.BlockSpec(memory_space=pl.ANY),
         ],
         out_shape=[
+            pltpu.HBM((6 * axial, radii * angles), BF16),
             pltpu.HBM(velocity.shape, F32),
-            pltpu.HBM(velocity.shape, F32),
-        ],
-        scratch_shapes=[pltpu.VMEM((2 * radii * SUB, (radii + 2 * HALO) * SUB), BF16)],
+            pltpu.HBM(piece.shape, F32),
+        ],
+        scratch_shapes=[
+            pltpu.VMEM((2 * radii * SUB, (radii + 2 * HALO) * SUB), BF16),
+            pltpu.SemaphoreType.DMA((1,)),
+        ],
         compiler_params=pltpu.CompilerParams(vmem_limit_bytes=28 * MIB),
         cost_estimate=pl.CostEstimate(
             flops=3600 * radii * radii * angles * axial // 8,
@@ -267,26 +287,13 @@
         in_hbm(middle),
         in_hbm(high_edge),
         in_vmem(high),
-    )
-
-
-def move_kernel(grad_ref, ids_ref, spring_ref, noise_ref, moved_ref, turned_ref):
-    _, radii, angles, axial = grad_ref.shape
-    cells = radii * angles
-    group = radii * SUB
-
-    def turn(i, carry):
-        at = pl.ds(pl.multiple_of(i * SUB, SUB), SUB)
-        value = jnp.concatenate(
-            [grad_ref[c, :, at, :].reshape(group, axial) for c in range(3)], axis=1
-        )
-        turned_high, turned_low = split(value.T)
-        cols = pl.ds(pl.multiple_of(i * group, group), group)
-        turned_ref[: 3 * axial, cols] = turned_high
-        turned_ref[3 * axial :, cols] = turned_low
-        return carry
-
-    lax.fori_loop(0, angles // SUB, turn, 0)
+        in_hbm(piece),
+    )
+
+
+def move_kernel(grad_ref, ids_ref, spring_ref, noise_ref, moved_ref, *, angles):
+    axial, cells = grad_ref.shape[0] // 6, grad_ref.shape[1]
+    group = cells // angles * SUB
 
     count = spring_ref.shape[3]
     part = min(count, 512)
@@ -297,7 +304,7 @@
         radius, angle = plane // angles, plane % angles
         column = (angle // SUB) * group + radius * SUB + angle % SUB
         hot = jnp.where(iota((cells, part), 0) == column, 1.0, 0.0).astype(BF16)
-        picked = dot(turned_ref[...], hot)
+        picked = dot(grad_ref[...], hot)
         here = iota((axial, part), 0) == ids_ref[1, 0, :, at]
         q = [spring_ref[c, 0, :, at] for c in range(3)]
         stretch_sq = q[0] * q[0] + q[1] * q[1] + q[2] * q[2]
@@ -317,19 +324,18 @@
     lax.fori_loop(0, count // part, read, 0)
 
 
-def move(grad, ids, spring, noise):
-    _, radii, angles, axial = grad.shape
+def move(grad, ids, spring, noise, angles):
+    cells = grad.shape[1]
     whole = pl.BlockSpec(memory_space=pltpu.VMEM)
     return pl.pallas_call(
-        move_kernel,
+        functools.partial(move_kernel, angles=angles),
         in_specs=[whole] * 4,
         out_specs=whole,
         out_shape=jax.ShapeDtypeStruct(spring.shape, F32),
-        scratch_shapes=[pltpu.VMEM((6 * axial, radii * angles), BF16)],
-        compiler_params=pltpu.CompilerParams(vmem_limit_bytes=28 * MIB),
+        compiler_params=pltpu.CompilerParams(vmem_limit_bytes=24 * MIB),
         cost_estimate=pl.CostEstimate(
-            flops=4 * grad.size * spring.shape[3],
-            bytes_accessed=4 * grad.size,
+            flops=2 * grad.size * spring.shape[3],
+            bytes_accessed=2 * grad.size,
             transcendentals=0,
         ),
         name="move",
@@ -531,11 +537,13 @@
     low, high = from_neighbours(low_edge, high_edge)
     middle = deposit_middle(cell_ids, dumbbells, low_edge, velocity.shape)
     stress = (low_edge, middle, high_edge)
-    grad, force = derive(stencil_coef, block_inverse, low, velocity, stress, high)
     me = lax.axis_index("az").astype(jnp.int32).reshape(1)
-    solved = solve(azim_coef, me, gathered, (in_hbm(force),))
-    pieces = exchange(solved)
-    moved = move(grad, cell_ids, dumbbells, brownian)
+    solved = solve(azim_coef, me, gathered, (in_vmem(low), in_vmem(high), in_hbm(middle)))
+    grad, force, passed = derive(
+        stencil_coef, block_inverse, low, velocity, stress, high, solved[-1]
+    )
+    pieces = exchange(list(solved[:-1]) + [passed])
+    moved = move(grad, cell_ids, dumbbells, brownian, angles)
     lines = (3 * radii, angles, axial)
     force = force.reshape(lines)
     early = len(pieces) * 3 // 8

time: 93.7 us -> 94.8 us (1.012); the launches traced: 92 us -> 94.4 us
  Pallas kernels: 57.7 us -> 62.2 us
  starting transfers between devices: 19.6 us -> 17.5 us
    ppermute x7, waiting for transfers between devices: 9.79 us -> 0.02 us  [exchange(): lax.ppermute(pieces[s], 'az', [(i, i ^ s) for i in range(count)])]
    pallas_call x1, Pallas kernels: 9.86 us -> 15.8 us  [derive(): pl.pallas_call(derive_kernel, grid=(angles // part,), in_specs=[pl.BlockS...]
    all_to_all x1, waiting for transfers between devices: 0.01 us -> 5.9 us  [per_device(): gathered = lax.all_to_all(pieces, 'az', 0, 0, tiled=True)]
    ppermute x1, waiting for transfers between devices: 2.77 us -> 4.99 us  [from_neighbours(): high = lax.ppermute(low_edge, 'rad', backward)]
    ppermute x1, waiting for transfers between devices: 1.18 us -> 2.73 us  [from_neighbours(): low = lax.ppermute(high_edge, 'rad', forward)]
    pallas_call x1, Pallas kernels: 18.6 us -> 17.2 us  [move(): pl.pallas_call(functools.partial(move_kernel, angles=angles), in_specs=[w...]
    ppermute x7, starting transfers between devices: 7.58 us -> 6.39 us  [exchange(): lax.ppermute(pieces[s], 'az', [(i, i ^ s) for i in range(count)])]
    ppermute x1, starting transfers between devices: 5.45 us -> 4.37 us  [from_neighbours(): low = lax.ppermute(high_edge, 'rad', forward)]
  transfers between devices with their start and end apart: 10 -> 10, of which waited for: 4 -> 3; matrix products, arithmetic and copies ran while one was open for 0% -> 0% of each run, Pallas kernels for 53% -> 57%
where the time goes in v13:
time: 94.8 us; the launch traced here: 94.4 us
  Pallas kernels  62.2 us (66%)
  starting transfers between devices  17.5 us (18%)
  waiting for transfers between devices  13.6 us (14%)
    pallas_call x1, Pallas kernels, move(): pl.pallas_call(functools.partial(move_kernel, angles=angles), in_specs=[w...  17.2 us
    pallas_call x1, Pallas kernels, derive(): pl.pallas_call(derive_kernel, grid=(angles // part,), in_specs=[pl.BlockS...  15.8 us
    pallas_call x1, Pallas kernels, deposit_middle(): pl.pallas_call(lambda ids_ref, spring_ref, _, *refs: middle_kernel(ids_re...  12.7 us
    ppermute x7, starting transfers between devices, exchange(): lax.ppermute(pieces[s], 'az', [(i, i ^ s) for i in range(count)])  6.39 us
    pallas_call x1, Pallas kernels, solve(): pl.pallas_call(functools.partial(solve_kernel, extra=len(after)), in_spec...  6.38 us
    all_to_all x1, waiting for transfers between devices, per_device(): gathered = lax.all_to_all(pieces, 'az', 0, 0, tiled=True)  5.9 us
    pallas_call x1, Pallas kernels, deposit_edges(): pl.pallas_call(functools.partial(edge_kernel, radii=radii), grid=(1,), in...  5.73 us
    all_to_all x1, starting transfers between devices, per_device(): gathered = lax.all_to_all(pieces, 'az', 0, 0, tiled=True)  5.31 us
  transfers between devices with their start and end apart: 10, of which 3 were waited for; matrix products, arithmetic and copies ran while one was open for 0% of the time, Pallas kernels for 57%

profile of v13, /device:TPU:0, one launch (start us, length us, event | category | flops | bytes accessed | tf_op | source)
XLA Modules:
  0.0 94.4 jit_solution(12040822542760221753)
XLA Ops:
  0.6 0.0 copy-start.1
  0.6 0.0 copy-start.3
  0.6 5.3 %all-to-all-start = ((f32[8,12,64,128]{3,2,1,0:T(8,128)}), f32[8,12,64,128]{3,2,1,0:T(8,128)S(1)}, u32[]{:S(2)}, u32[]{:S(2)}) async-start(f32[8,12,64,128]{3,2,1,0:T(8,128)} %bitcast.7), calls=%async_computation | async-start | bytes 6291456 | tf_op jit(solution)/shard_map/all_to_all | solution.py:535
  6.0 5.7 %deposit_edges.1 = (f32[2,3,4,64,128]{4,3,2,1,0:T(8,128)}, f32[2,3,4,64,128]{4,3,2,1,0:T(8,128)}) custom-call(s32[2,1,1,4096]{3,2,1,0:T(1,128)S(1)} %copy-done.3, f32[3,1,1,4096]{3,2,1,0:T(1,128)S(1)} %copy-done.1, f32[3,32,64,128]{3,2,1,0:T(8,128)} %velocity_ref.1, f32[3,32,64,128]{3,2,1,0:T(8,128)} %velocity_ref.1), custom_call_target="tpu_custom_call" | custom-call | flops 3221225472 | bytes 3145728 | tf_op jit(solution)/shard_map/deposit_edges/pallas_call | solution.py:112
  11.7 4.4 %collective-permute-start = (f32[2,3,4,64,128]{4,3,2,1,0:T(8,128)}, f32[2,3,4,64,128]{4,3,2,1,0:T(8,128)}, u32[]{:S(2)}, u32[]{:S(2)}) collective-permute-start(f32[2,3,4,64,128]{4,3,2,1,0:T(8,128)} %get-tuple-element.15.high_edge_ref), channel_id=1, source_target_pairs={{0,1},{1,2},{2,3},{4,5},{5,6},{6,7},{8,9},{9,10},{10,11},{12,13},{... | collective-permute-start | bytes 2359304 | tf_op jit(solution)/shard_map/ppermute | solution.py:525
  16.1 1.5 %collective-permute-start.1 = (f32[2,3,4,64,128]{4,3,2,1,0:T(8,128)}, f32[2,3,4,64,128]{4,3,2,1,0:T(8,128)}, u32[]{:S(2)}, u32[]{:S(2)}) collective-permute-start(f32[2,3,4,64,128]{4,3,2,1,0:T(8,128)} %get-tuple-element.16._.low_edge_ref), channel_id=1, source_target_pairs={{1,0},{2,1},{3,2},{5,4},{6,5},{7,6},{9,8},{10,9},{11,10},{13,12},{... | collective-permute-start | bytes 2359304 | tf_op jit(solution)/shard_map/ppermute | solution.py:526
  17.6 0.0 copy-start.6
  17.6 12.7 %deposit_middle.1.refs_2_.middle_ref = f32[3,24,64,128]{3,2,1,0:T(8,128)} custom-call(s32[2,1,1,4096]{3,2,1,0:T(1,128)S(1)} %copy-done.3, f32[3,1,1,4096]{3,2,1,0:T(1,128)S(1)} %copy-done.1, f32[2,3,4,64,128]{4,3,2,1,0:T(8,128)} %get-tuple-element.16._.low_edge_ref), custom_call_target="tpu_custom_call" | custom-call | flops 9663676416 | bytes 2359296 | tf_op jit(solution)/shard_map/deposit_middle/pallas_call | solution.py:140
  30.2 2.7 %collective-permute-done.refs_0_.low_ref = f32[2,3,4,64,128]{4,3,2,1,0:T(8,128)} collective-permute-done((f32[2,3,4,64,128]{4,3,2,1,0:T(8,128)}, f32[2,3,4,64,128]{4,3,2,1,0:T(8,128)}, u32[]{:S(2)}, u32[]{:S(2)}) %collective-permute-start) | collective-permute-done | bytes 786464 | tf_op jit(solution)/shard_map/ppermute | solution.py:525
  32.9 5.0 %collective-permute-done.1.refs_1_.high_ref = f32[2,3,4,64,128]{4,3,2,1,0:T(8,128)} collective-permute-done((f32[2,3,4,64,128]{4,3,2,1,0:T(8,128)}, f32[2,3,4,64,128]{4,3,2,1,0:T(8,128)}, u32[]{:S(2)}, u32[]{:S(2)}) %collective-permute-start.1) | collective-permute-done | bytes 786464 | tf_op jit(solution)/shard_map/ppermute | solution.py:526
  37.9 5.9 %all-to-all-done.refs_3_ = f32[8,12,64,128]{3,2,1,0:T(8,128)S(1)} async-done(((f32[8,12,64,128]{3,2,1,0:T(8,128)}), f32[8,12,64,128]{3,2,1,0:T(8,128)S(1)}, u32[]{:S(2)}, u32[]{:S(2)}) %all-to-all-start) | async-done | bytes 3145760 | tf_op jit(solution)/shard_map/all_to_all | solution.py:535
  43.9 6.4 %solve.1 = (f32[12,64,128]{2,1,0:T(8,128)}, f32[12,64,128]{2,1,0:T(8,128)}, f32[12,64,128]{2,1,0:T(8,128)}, f32[12,64,128]{2,1,0:T(8,128)}, f32[12,64,128]{2,1,0...) custom-call(f32[32]{0:T(128)S(1)} %copy-done.6, s32[1]{0:T(128)} %bitcast.me_ref, ...), custom_call_target="tpu_custom_call" | custom-call | flops 4831838208 | bytes 6291456 | tf_op jit(solution)/shard_map/solve/pallas_call | solution.py:436
  50.2 0.1 collective-permute-start.7
  50.3 0.6 collective-permute-start.8
  50.9 1.3 %collective-permute-start.2 = (f32[12,64,128]{2,1,0:T(8,128)}, f32[12,64,128]{2,1,0:T(8,128)S(1)}, u32[]{:S(2)}, u32[]{:S(2)}) collective-permute-start(f32[12,64,128]{2,1,0:T(8,128)} %get-tuple-element.19), channel_id=1, source_target_pairs={{0,12},{4,8},{8,4},{12,0},{16,28},{20,24},{24,20},{28,16},{1,13},{... | collective-permute-start | bytes 1179656 | tf_op jit(solution)/shard_map/ppermute | solution.py:517
  52.2 0.6 collective-permute-start.3
  52.7 1.1 %collective-permute-start.4 = (f32[12,64,128]{2,1,0:T(8,128)}, f32[12,64,128]{2,1,0:T(8,128)S(1)}, u32[]{:S(2)}, u32[]{:S(2)}) collective-permute-start(f32[12,64,128]{2,1,0:T(8,128)} %get-tuple-element.21), channel_id=1, source_target_pairs={{0,20},{4,16},{8,28},{12,24},{16,4},{20,0},{24,12},{28,8},{1,21},{... | collective-permute-start | bytes 1179656 | tf_op jit(solution)/shard_map/ppermute | solution.py:517
  53.9 0.0 copy-done.5
  53.9 15.8 %derive.1 = (bf16[768,2048]{1,0:T(8,128)(2,1)}, f32[3,32,64,128]{3,2,1,0:T(8,128)}, f32[12,64,128]{2,1,0:T(8,128)}) custom-call(f32[9,32]{1,0:T(8,128)S(1)} %copy-done.5, f32[32,32]{1,0:T(8,128)S(1)} %copy-done.4, f32[2,3,4,64,128]{4,3,2,1,0:T(8,128)} %collective-permute-done.refs_0_.low_ref, f32[3,32,64,128]{3,2,1,0:T(8,128)} %velocity_ref.1, ...), custom_call_target="tpu_custom_call" | custom-call | flops 3774873600 | bytes 10485760 | tf_op jit(solution)/shard_map/derive/pallas_call | solution.py:246
  69.7 0.0 collective-permute-done.7.refs_1_
  69.7 0.0 copy-done.7
  69.7 0.7 collective-permute-start.5
  70.4 0.0 collective-permute-done.8.refs_2_
  70.4 2.1 %collective-permute-start.6 = (f32[12,64,128]{2,1,0:T(8,128)}, f32[12,64,128]{2,1,0:T(8,128)S(1)}, u32[]{:S(2)}, u32[]{:S(2)}) collective-permute-start(f32[12,64,128]{2,1,0:T(8,128)} %get-tuple-element.23), channel_id=1, source_target_pairs={{0,28},{4,24},{8,20},{12,16},{16,12},{20,8},{24,4},{28,0},{1,29},{... | collective-permute-start | bytes 1179656 | tf_op jit(solution)/shard_map/ppermute | solution.py:517
  72.5 17.2 %move.1 = f32[3,1,1,4096]{3,2,1,0:T(1,128)} custom-call(bf16[768,2048]{1,0:T(8,128)(2,1)} %get-tuple-element.27.grad_ref, s32[2,1,1,4096]{3,2,1,0:T(1,128)S(1)} %copy-done.3, f32[3,1,1,4096]{3,2,1,0:T(1,128)S(1)} %copy-done.1, f32[3,1,1,4096]{3,2,1,0:T(1,128)S(1)} %copy-done.2), custom_call_target="tpu_custom_call" | custom-call | flops 12884901888 | bytes 3145728 | tf_op jit(solution)/shard_map/move/pallas_call | solution.py:330
  89.7 2.1 %join.2.refs_5_ = f32[96,64,128]{2,1,0:T(8,128)} custom-call(s32[1]{0:T(128)} %bitcast.me_ref, f32[96,64,128]{2,1,0:T(8,128)} %bitcast.4, f32[12,64,128]{2,1,0:T(8,128)S(1)} %copy-done, f32[12,64,128]{2,1,0:T(8,128)S(1)} %collective-permute-done.7.refs_1_, f32[12,64,128]{2,1,0:T(8,128)S(1)} %collective-permute-done.8.refs_2_), custom_call_target="tpu_custom_call" | custom-call | flops 294912 | bytes 3538944 | tf_op jit(solution)/shard_map/join/pallas_call | solution.py:489
  91.8 0.0 collective-permute-done.2.refs_0_
  91.8 0.0 collective-permute-done.3.refs_1_
  91.8 0.0 collective-permute-done.4.refs_2_
  91.8 0.0 collective-permute-done.5.refs_3_
  91.8 0.0 collective-permute-done.6.refs_4_
  91.8 2.4 %join.3 = f32[96,64,128]{2,1,0:T(8,128)} custom-call(s32[1]{0:T(128)} %bitcast.me_ref, f32[96,64,128]{2,1,0:T(8,128)} %bitcast.5, f32[12,64,128]{2,1,0:T(8,128)S(1)} %collective-permute-done.2.refs_0_, f32[12,64,128]{2,1,0:T(8,128)S(1)} %collective-permute-done.3.refs_1_, ...), custom_call_target="tpu_custom_call", output_to_operand_aliasing={{}: (7, {})} | custom-call | flops 491520 | bytes 5898240 | tf_op jit(solution)/shard_map/join/pallas_call | solution.py:489
  (11 shorter events, 0.0 us)
Async XLA Ops:
  0.6 5.3 %copy-start.1 = (f32[3,1,1,4096]{3,2,1,0:T(1,128)S(1)}, f32[3,1,1,4096]{3,2,1,0:T(1,128)}, u32[]{:S(2)}) copy-start(f32[3,1,1,4096]{3,2,1,0:T(1,128)} %spring_ref.5) | copy-start | bytes 147460
  0.6 5.3 %copy-start.3 = (s32[2,1,1,4096]{3,2,1,0:T(1,128)S(1)}, s32[2,1,1,4096]{3,2,1,0:T(1,128)}, u32[]{:S(2)}) copy-start(s32[2,1,1,4096]{3,2,1,0:T(1,128)} %ids_ref.5) | copy-start | bytes 98308
  0.6 43.2 %all-to-all-start = ((f32[8,12,64,128]{3,2,1,0:T(8,128)}), f32[8,12,64,128]{3,2,1,0:T(8,128)S(1)}, u32[]{:S(2)}, u32[]{:S(2)}) async-start(f32[8,12,64,128]{3,2,1,0:T(8,128)} %bitcast.7), calls=%async_computation | async-start | bytes 6291456 | tf_op jit(solution)/shard_map/all_to_all | solution.py:535
  11.7 21.2 %collective-permute-start = (f32[2,3,4,64,128]{4,3,2,1,0:T(8,128)}, f32[2,3,4,64,128]{4,3,2,1,0:T(8,128)}, u32[]{:S(2)}, u32[]{:S(2)}) collective-permute-start(f32[2,3,4,64,128]{4,3,2,1,0:T(8,128)} %get-tuple-element.15.high_edge_ref), channel_id=1, source_target_pairs={{0,1},{1,2},{2,3},{4,5},{5,6},{6,7},{8,9},{9,10},{10,11},{12,13},{... | collective-permute-start | bytes 2359304 | tf_op jit(solution)/shard_map/ppermute | solution.py:525
  16.1 21.9 %collective-permute-start.1 = (f32[2,3,4,64,128]{4,3,2,1,0:T(8,128)}, f32[2,3,4,64,128]{4,3,2,1,0:T(8,128)}, u32[]{:S(2)}, u32[]{:S(2)}) collective-permute-start(f32[2,3,4,64,128]{4,3,2,1,0:T(8,128)} %get-tuple-element.16._.low_edge_ref), channel_id=1, source_target_pairs={{1,0},{2,1},{3,2},{5,4},{6,5},{7,6},{9,8},{10,9},{11,10},{13,12},{... | collective-permute-start | bytes 2359304 | tf_op jit(solution)/shard_map/ppermute | solution.py:526
  17.6 26.3 %copy-start.6 = (f32[32]{0:T(128)S(1)}, f32[32]{0:T(128)}, u32[]{:S(2)}) copy-start(f32[32]{0:T(128)} %coef_ref.1) | copy-start | bytes 388
  43.8 10.0 %copy-start.4 = (f32[32,32]{1,0:T(8,128)S(1)}, f32[32,32]{1,0:T(8,128)}, u32[]{:S(2)}) copy-start(f32[32,32]{1,0:T(8,128)} %inverse_ref.1) | copy-start | bytes 12292
  43.9 10.0 %copy-start.5 = (f32[9,32]{1,0:T(8,128)S(1)}, f32[9,32]{1,0:T(8,128)}, u32[]{:S(2)}) copy-start(f32[9,32]{1,0:T(8,128)} %stencil_ref.1) | copy-start | bytes 3460
  50.2 19.5 %collective-permute-start.7 = (f32[12,64,128]{2,1,0:T(8,128)}, f32[12,64,128]{2,1,0:T(8,128)S(1)}, u32[]{:S(2)}, u32[]{:S(2)}) collective-permute-start(f32[12,64,128]{2,1,0:T(8,128)} %get-tuple-element.25), channel_id=1, source_target_pairs={{0,4},{4,0},{8,12},{12,8},{16,20},{20,16},{24,28},{28,24},{1,5},{5... | collective-permute-start | bytes 1179656 | tf_op jit(solution)/shard_map/ppermute | solution.py:517
  50.3 20.1 %collective-permute-start.8 = (f32[12,64,128]{2,1,0:T(8,128)}, f32[12,64,128]{2,1,0:T(8,128)S(1)}, u32[]{:S(2)}, u32[]{:S(2)}) collective-permute-start(f32[12,64,128]{2,1,0:T(8,128)} %get-tuple-element.26), channel_id=1, source_target_pairs={{0,8},{4,12},{8,0},{12,4},{16,24},{20,28},{24,16},{28,20},{1,9},{5... | collective-permute-start | bytes 1179656 | tf_op jit(solution)/shard_map/ppermute | solution.py:517
  50.9 40.9 %collective-permute-start.2 = (f32[12,64,128]{2,1,0:T(8,128)}, f32[12,64,128]{2,1,0:T(8,128)S(1)}, u32[]{:S(2)}, u32[]{:S(2)}) collective-permute-start(f32[12,64,128]{2,1,0:T(8,128)} %get-tuple-element.19), channel_id=1, source_target_pairs={{0,12},{4,8},{8,4},{12,0},{16,28},{20,24},{24,20},{28,16},{1,13},{... | collective-permute-start | bytes 1179656 | tf_op jit(solution)/shard_map/ppermute | solution.py:517
  52.2 39.6 %collective-permute-start.3 = (f32[12,64,128]{2,1,0:T(8,128)}, f32[12,64,128]{2,1,0:T(8,128)S(1)}, u32[]{:S(2)}, u32[]{:S(2)}) collective-permute-start(f32[12,64,128]{2,1,0:T(8,128)} %get-tuple-element.20), channel_id=1, source_target_pairs={{0,16},{4,20},{8,24},{12,28},{16,0},{20,4},{24,8},{28,12},{1,17},{... | collective-permute-start | bytes 1179656 | tf_op jit(solution)/shard_map/ppermute | solution.py:517
  52.7 39.0 %collective-permute-start.4 = (f32[12,64,128]{2,1,0:T(8,128)}, f32[12,64,128]{2,1,0:T(8,128)S(1)}, u32[]{:S(2)}, u32[]{:S(2)}) collective-permute-start(f32[12,64,128]{2,1,0:T(8,128)} %get-tuple-element.21), channel_id=1, source_target_pairs={{0,20},{4,16},{8,28},{12,24},{16,4},{20,0},{24,12},{28,8},{1,21},{... | collective-permute-start | bytes 1179656 | tf_op jit(solution)/shard_map/ppermute | solution.py:517
  53.9 15.8 %copy-start.7 = (f32[12,64,128]{2,1,0:T(8,128)S(1)}, f32[12,64,128]{2,1,0:T(8,128)}, u32[]{:S(2)}) copy-start(f32[12,64,128]{2,1,0:T(8,128)} %get-tuple-element.22) | copy-start | bytes 1179652
  53.9 18.6 %copy-start.2 = (f32[3,1,1,4096]{3,2,1,0:T(1,128)S(1)}, f32[3,1,1,4096]{3,2,1,0:T(1,128)}, u32[]{:S(2)}) copy-start(f32[3,1,1,4096]{3,2,1,0:T(1,128)} %noise_ref.1) | copy-start | bytes 147460
  69.7 22.1 %collective-permute-start.5 = (f32[12,64,128]{2,1,0:T(8,128)S(1)}, f32[12,64,128]{2,1,0:T(8,128)S(1)}, u32[]{:S(2)}, u32[]{:S(2)}) collective-permute-start(f32[12,64,128]{2,1,0:T(8,128)S(1)} %copy-done.7), channel_id=1, source_target_pairs={{0,24},{4,28},{8,16},{12,20},{16,8},{20,12},{24,0},{28,4},{1,25},{... | collective-permute-start | bytes 1179656 | tf_op jit(solution)/shard_map/ppermute | solution.py:517
  70.4 21.4 %collective-permute-start.6 = (f32[12,64,128]{2,1,0:T(8,128)}, f32[12,64,128]{2,1,0:T(8,128)S(1)}, u32[]{:S(2)}, u32[]{:S(2)}) collective-permute-start(f32[12,64,128]{2,1,0:T(8,128)} %get-tuple-element.23), channel_id=1, source_target_pairs={{0,28},{4,24},{8,20},{12,16},{16,12},{20,8},{24,4},{28,0},{1,29},{... | collective-permute-start | bytes 1179656 | tf_op jit(solution)/shard_map/ppermute | solution.py:517
  72.5 17.2 %copy-start = (f32[12,64,128]{2,1,0:T(8,128)S(1)}, f32[12,64,128]{2,1,0:T(8,128)}, u32[]{:S(2)}) copy-start(f32[12,64,128]{2,1,0:T(8,128)} %get-tuple-element.24.refs_0_) | copy-start | bytes 1179652

commit v14 on v13

--- a/solution.py
+++ b/solution.py
@@ -193,15 +193,13 @@
     force_ref,
     passed_ref,
     matrix_ref,
-    sem,
 ):
     radii, angles, axial = velocity_ref.shape[1:]
 
-    passing = pltpu.make_async_copy(piece_ref, passed_ref, sem.at[0])
+    passed_ref[...] = piece_ref[...]
 
     @pl.when(pl.program_id(0) == 0)
     def _():
-        passing.start()
         matrix_ref[...] = derivative_matrix(stencil_ref, inverse_ref)
 
     group = radii * SUB
@@ -228,15 +226,13 @@
         grad_ref[: 3 * axial, cols] = turned_high
         grad_ref[3 * axial :, cols] = turned_low
 
-    @pl.when(pl.program_id(0) == pl.num_programs(0) - 1)
-    def _():
-        passing.wait()
-
-
 def derive(stencil, inverse, low, velocity, stress, high, piece):
     low_edge, middle, high_edge = stress
     radii, angles, axial = velocity.shape[1:]
     part = 2 * SUB
+    steps = angles // part
+    assert piece.shape[0] % steps == 0
+    piece_block = pl.BlockSpec((piece.shape[0] // steps, angles, axial), lambda i: (i, 0, 0))
 
     def block(count, first=None):
         if first is None:
@@ -245,7 +241,7 @@
 
     return pl.pallas_call(
         derive_kernel,
-        grid=(angles // part,),
+        grid=(steps,),
         in_specs=[
             pl.BlockSpec(stencil.shape, lambda i: (0, 0)),
             pl.BlockSpec(inverse.shape, lambda i: (0, 0)),
@@ -255,12 +251,12 @@
             block(radii - 2 * HALO),
             block(HALO, 1),
             block(HALO, 0),
-            pl.BlockSpec(memory_space=pl.ANY),
+            piece_block,
         ],
         out_specs=[
             pl.BlockSpec((6 * axial, radii * part), lambda i: (0, i)),
             block(radii),
-            pl.BlockSpec(memory_space=pl.ANY),
+            piece_block,
         ],
         out_shape=[
             pltpu.HBM((6 * axial, radii * angles), BF16),
@@ -269,7 +265,6 @@
         ],
         scratch_shapes=[
             pltpu.VMEM((2 * radii * SUB, (radii + 2 * HALO) * SUB), BF16),
-            pltpu.SemaphoreType.DMA((1,)),
         ],
         compiler_params=pltpu.CompilerParams(vmem_limit_bytes=28 * MIB),
         cost_estimate=pl.CostEstimate(

time: 94.8 us -> 91.5 us (0.965)
  Pallas kernels: 62.2 us -> 56.6 us
  waiting for transfers between devices: 13.6 us -> 15.9 us
    pallas_call x1, Pallas kernels: 15.8 us -> 10.2 us  [derive(): pl.pallas_call(derive_kernel, grid=(steps,), in_specs=[pl.BlockSpec(stenc...]
    ppermute x7, waiting for transfers between devices: 0.02 us -> 2.3 us  [exchange(): lax.ppermute(pieces[s], 'az', [(i, i ^ s) for i in range(count)])]
  transfers between devices with their start and end apart: 10 -> 10, of which waited for: 3 -> 4; matrix products, arithmetic and copies ran while one was open for 0% -> 0% of each run, Pallas kernels for 57% -> 53%
where the time goes in v14:
time: 91.5 us; the launch traced here: 91 us
  Pallas kernels  56.6 us (62%)
  starting transfers between devices  17.5 us (19%)
  waiting for transfers between devices  15.9 us (17%)
    pallas_call x1, Pallas kernels, move(): pl.pallas_call(functools.partial(move_kernel, angles=angles), in_specs=[w...  17.2 us
    pallas_call x1, Pallas kernels, deposit_middle(): pl.pallas_call(lambda ids_ref, spring_ref, _, *refs: middle_kernel(ids_re...  12.7 us
    pallas_call x1, Pallas kernels, derive(): pl.pallas_call(derive_kernel, grid=(steps,), in_specs=[pl.BlockSpec(stenc...  10.2 us
    ppermute x7, starting transfers between devices, exchange(): lax.ppermute(pieces[s], 'az', [(i, i ^ s) for i in range(count)])  6.39 us
    pallas_call x1, Pallas kernels, solve(): pl.pallas_call(functools.partial(solve_kernel, extra=len(after)), in_spec...  6.38 us
    all_to_all x1, waiting for transfers between devices, per_device(): gathered = lax.all_to_all(pieces, 'az', 0, 0, tiled=True)  5.9 us
    pallas_call x1, Pallas kernels, deposit_edges(): pl.pallas_call(functools.partial(edge_kernel, radii=radii), grid=(1,), in...  5.73 us
    all_to_all x1, starting transfers between devices, per_device(): gathered = lax.all_to_all(pieces, 'az', 0, 0, tiled=True)  5.31 us
  transfers between devices with their start and end apart: 10, of which 4 were waited for; matrix products, arithmetic and copies ran while one was open for 0% of the time, Pallas kernels for 53%

profile of v14, /device:TPU:0, one launch (start us, length us, event | category | flops | bytes accessed | tf_op | source)
XLA Modules:
  0.0 91.0 jit_solution(16660171085331566620)
XLA Ops:
  0.6 0.0 copy-start.1
  0.6 0.0 copy-start.3
  0.6 5.3 %all-to-all-start = ((f32[8,12,64,128]{3,2,1,0:T(8,128)}), f32[8,12,64,128]{3,2,1,0:T(8,128)S(1)}, u32[]{:S(2)}, u32[]{:S(2)}) async-start(f32[8,12,64,128]{3,2,1,0:T(8,128)} %bitcast.7), calls=%async_computation | async-start | bytes 6291456 | tf_op jit(solution)/shard_map/all_to_all | solution.py:530
  6.0 0.0 copy-done.1
  6.0 0.0 copy-done.3
  6.0 5.7 %deposit_edges.1 = (f32[2,3,4,64,128]{4,3,2,1,0:T(8,128)}, f32[2,3,4,64,128]{4,3,2,1,0:T(8,128)}) custom-call(s32[2,1,1,4096]{3,2,1,0:T(1,128)S(1)} %copy-done.3, f32[3,1,1,4096]{3,2,1,0:T(1,128)S(1)} %copy-done.1, f32[3,32,64,128]{3,2,1,0:T(8,128)} %velocity_ref.1, f32[3,32,64,128]{3,2,1,0:T(8,128)} %velocity_ref.1), custom_call_target="tpu_custom_call" | custom-call | flops 3221225472 | bytes 3145728 | tf_op jit(solution)/shard_map/deposit_edges/pallas_call | solution.py:112
  11.7 4.4 %collective-permute-start = (f32[2,3,4,64,128]{4,3,2,1,0:T(8,128)}, f32[2,3,4,64,128]{4,3,2,1,0:T(8,128)}, u32[]{:S(2)}, u32[]{:S(2)}) collective-permute-start(f32[2,3,4,64,128]{4,3,2,1,0:T(8,128)} %get-tuple-element.15.high_edge_ref), channel_id=1, source_target_pairs={{0,1},{1,2},{2,3},{4,5},{5,6},{6,7},{8,9},{9,10},{10,11},{12,13},{... | collective-permute-start | bytes 2359304 | tf_op jit(solution)/shard_map/ppermute | solution.py:520
  16.1 1.5 %collective-permute-start.1 = (f32[2,3,4,64,128]{4,3,2,1,0:T(8,128)}, f32[2,3,4,64,128]{4,3,2,1,0:T(8,128)}, u32[]{:S(2)}, u32[]{:S(2)}) collective-permute-start(f32[2,3,4,64,128]{4,3,2,1,0:T(8,128)} %get-tuple-element.16._.low_edge_ref), channel_id=1, source_target_pairs={{1,0},{2,1},{3,2},{5,4},{6,5},{7,6},{9,8},{10,9},{11,10},{13,12},{... | collective-permute-start | bytes 2359304 | tf_op jit(solution)/shard_map/ppermute | solution.py:521
  17.6 0.0 copy-start.6
  17.6 12.7 %deposit_middle.1.refs_2_.middle_ref = f32[3,24,64,128]{3,2,1,0:T(8,128)} custom-call(s32[2,1,1,4096]{3,2,1,0:T(1,128)S(1)} %copy-done.3, f32[3,1,1,4096]{3,2,1,0:T(1,128)S(1)} %copy-done.1, f32[2,3,4,64,128]{4,3,2,1,0:T(8,128)} %get-tuple-element.16._.low_edge_ref), custom_call_target="tpu_custom_call" | custom-call | flops 9663676416 | bytes 2359296 | tf_op jit(solution)/shard_map/deposit_middle/pallas_call | solution.py:140
  30.2 2.7 %collective-permute-done.refs_0_.low_ref = f32[2,3,4,64,128]{4,3,2,1,0:T(8,128)} collective-permute-done((f32[2,3,4,64,128]{4,3,2,1,0:T(8,128)}, f32[2,3,4,64,128]{4,3,2,1,0:T(8,128)}, u32[]{:S(2)}, u32[]{:S(2)}) %collective-permute-start) | collective-permute-done | bytes 786464 | tf_op jit(solution)/shard_map/ppermute | solution.py:520
  32.9 5.0 %collective-permute-done.1.refs_1_.high_ref = f32[2,3,4,64,128]{4,3,2,1,0:T(8,128)} collective-permute-done((f32[2,3,4,64,128]{4,3,2,1,0:T(8,128)}, f32[2,3,4,64,128]{4,3,2,1,0:T(8,128)}, u32[]{:S(2)}, u32[]{:S(2)}) %collective-permute-start.1) | collective-permute-done | bytes 786464 | tf_op jit(solution)/shard_map/ppermute | solution.py:521
  37.9 5.9 %all-to-all-done.refs_3_ = f32[8,12,64,128]{3,2,1,0:T(8,128)S(1)} async-done(((f32[8,12,64,128]{3,2,1,0:T(8,128)}), f32[8,12,64,128]{3,2,1,0:T(8,128)S(1)}, u32[]{:S(2)}, u32[]{:S(2)}) %all-to-all-start) | async-done | bytes 3145760 | tf_op jit(solution)/shard_map/all_to_all | solution.py:530
  43.9 6.4 %solve.1 = (f32[12,64,128]{2,1,0:T(8,128)}, f32[12,64,128]{2,1,0:T(8,128)}, f32[12,64,128]{2,1,0:T(8,128)}, f32[12,64,128]{2,1,0:T(8,128)}, f32[12,64,128]{2,1,0...) custom-call(f32[32]{0:T(128)S(1)} %copy-done.6, s32[1]{0:T(128)} %bitcast.me_ref, ...), custom_call_target="tpu_custom_call" | custom-call | flops 4831838208 | bytes 6291456 | tf_op jit(solution)/shard_map/solve/pallas_call | solution.py:431
  50.2 0.1 collective-permute-start.7
  50.3 0.6 collective-permute-start.8
  50.9 1.3 %collective-permute-start.2 = (f32[12,64,128]{2,1,0:T(8,128)}, f32[12,64,128]{2,1,0:T(8,128)S(1)}, u32[]{:S(2)}, u32[]{:S(2)}) collective-permute-start(f32[12,64,128]{2,1,0:T(8,128)} %get-tuple-element.19), channel_id=1, source_target_pairs={{0,12},{4,8},{8,4},{12,0},{16,28},{20,24},{24,20},{28,16},{1,13},{... | collective-permute-start | bytes 1179656 | tf_op jit(solution)/shard_map/ppermute | solution.py:512
  52.2 0.6 collective-permute-start.3
  52.7 1.1 %collective-permute-start.4 = (f32[12,64,128]{2,1,0:T(8,128)}, f32[12,64,128]{2,1,0:T(8,128)S(1)}, u32[]{:S(2)}, u32[]{:S(2)}) collective-permute-start(f32[12,64,128]{2,1,0:T(8,128)} %get-tuple-element.21), channel_id=1, source_target_pairs={{0,20},{4,16},{8,28},{12,24},{16,4},{20,0},{24,12},{28,8},{1,21},{... | collective-permute-start | bytes 1179656 | tf_op jit(solution)/shard_map/ppermute | solution.py:512
  53.9 10.2 %derive.1 = (bf16[768,2048]{1,0:T(8,128)(2,1)}, f32[3,32,64,128]{3,2,1,0:T(8,128)}, f32[12,64,128]{2,1,0:T(8,128)}) custom-call(f32[9,32]{1,0:T(8,128)S(1)} %copy-done.5, f32[32,32]{1,0:T(8,128)S(1)} %copy-done.4, f32[2,3,4,64,128]{4,3,2,1,0:T(8,128)} %collective-permute-done.refs_0_.low_ref, f32[3,32,64,128]{3,2,1,0:T(8,128)} %velocity_ref.1, ...), custom_call_target="tpu_custom_call" | custom-call | flops 3774873600 | bytes 10485760 | tf_op jit(solution)/shard_map/derive/pallas_call | solution.py:242
  64.1 0.0 collective-permute-done.7.refs_1_
  64.1 0.7 collective-permute-start.5
  64.8 0.0 collective-permute-done.8.refs_2_
  64.8 2.1 %collective-permute-start.6 = (f32[12,64,128]{2,1,0:T(8,128)}, f32[12,64,128]{2,1,0:T(8,128)S(1)}, u32[]{:S(2)}, u32[]{:S(2)}) collective-permute-start(f32[12,64,128]{2,1,0:T(8,128)} %get-tuple-element.23), channel_id=1, source_target_pairs={{0,28},{4,24},{8,20},{12,16},{16,12},{20,8},{24,4},{28,0},{1,29},{... | collective-permute-start | bytes 1179656 | tf_op jit(solution)/shard_map/ppermute | solution.py:512
  66.9 17.2 %move.1 = f32[3,1,1,4096]{3,2,1,0:T(1,128)} custom-call(bf16[768,2048]{1,0:T(8,128)(2,1)} %get-tuple-element.27.grad_ref, s32[2,1,1,4096]{3,2,1,0:T(1,128)S(1)} %copy-done.3, f32[3,1,1,4096]{3,2,1,0:T(1,128)S(1)} %copy-done.1, f32[3,1,1,4096]{3,2,1,0:T(1,128)S(1)} %copy-done.2), custom_call_target="tpu_custom_call" | custom-call | flops 12884901888 | bytes 3145728 | tf_op jit(solution)/shard_map/move/pallas_call | solution.py:325
  84.1 2.1 %join.2.refs_5_ = f32[96,64,128]{2,1,0:T(8,128)} custom-call(s32[1]{0:T(128)} %bitcast.me_ref, f32[96,64,128]{2,1,0:T(8,128)} %bitcast.4, f32[12,64,128]{2,1,0:T(8,128)S(1)} %copy-done, f32[12,64,128]{2,1,0:T(8,128)S(1)} %collective-permute-done.7.refs_1_, f32[12,64,128]{2,1,0:T(8,128)S(1)} %collective-permute-done.8.refs_2_), custom_call_target="tpu_custom_call" | custom-call | flops 294912 | bytes 3538944 | tf_op jit(solution)/shard_map/join/pallas_call | solution.py:484
  86.2 0.0 collective-permute-done.2.refs_0_
  86.2 0.0 collective-permute-done.3.refs_1_
  86.2 2.3 %collective-permute-done.4.refs_2_ = f32[12,64,128]{2,1,0:T(8,128)S(1)} collective-permute-done((f32[12,64,128]{2,1,0:T(8,128)}, f32[12,64,128]{2,1,0:T(8,128)S(1)}, u32[]{:S(2)}, u32[]{:S(2)}) %collective-permute-start.4) | collective-permute-done | bytes 393248 | tf_op jit(solution)/shard_map/ppermute | solution.py:512
  88.5 0.0 collective-permute-done.5.refs_3_
  88.5 0.0 collective-permute-done.6.refs_4_
  88.5 2.4 %join.3 = f32[96,64,128]{2,1,0:T(8,128)} custom-call(s32[1]{0:T(128)} %bitcast.me_ref, f32[96,64,128]{2,1,0:T(8,128)} %bitcast.5, f32[12,64,128]{2,1,0:T(8,128)S(1)} %collective-permute-done.2.refs_0_, f32[12,64,128]{2,1,0:T(8,128)S(1)} %collective-permute-done.3.refs_1_, ...), custom_call_target="tpu_custom_call", output_to_operand_aliasing={{}: (7, {})} | custom-call | flops 491520 | bytes 5898240 | tf_op jit(solution)/shard_map/join/pallas_call | solution.py:484
  (11 shorter events, 0.0 us)
Async XLA Ops:
  0.6 5.3 %copy-start.1 = (f32[3,1,1,4096]{3,2,1,0:T(1,128)S(1)}, f32[3,1,1,4096]{3,2,1,0:T(1,128)}, u32[]{:S(2)}) copy-start(f32[3,1,1,4096]{3,2,1,0:T(1,128)} %spring_ref.5) | copy-start | bytes 147460
  0.6 5.3 %copy-start.3 = (s32[2,1,1,4096]{3,2,1,0:T(1,128)S(1)}, s32[2,1,1,4096]{3,2,1,0:T(1,128)}, u32[]{:S(2)}) copy-start(s32[2,1,1,4096]{3,2,1,0:T(1,128)} %ids_ref.5) | copy-start | bytes 98308
  0.6 43.2 %all-to-all-start = ((f32[8,12,64,128]{3,2,1,0:T(8,128)}), f32[8,12,64,128]{3,2,1,0:T(8,128)S(1)}, u32[]{:S(2)}, u32[]{:S(2)}) async-start(f32[8,12,64,128]{3,2,1,0:T(8,128)} %bitcast.7), calls=%async_computation | async-start | bytes 6291456 | tf_op jit(solution)/shard_map/all_to_all | solution.py:530
  11.7 21.2 %collective-permute-start = (f32[2,3,4,64,128]{4,3,2,1,0:T(8,128)}, f32[2,3,4,64,128]{4,3,2,1,0:T(8,128)}, u32[]{:S(2)}, u32[]{:S(2)}) collective-permute-start(f32[2,3,4,64,128]{4,3,2,1,0:T(8,128)} %get-tuple-element.15.high_edge_ref), channel_id=1, source_target_pairs={{0,1},{1,2},{2,3},{4,5},{5,6},{6,7},{8,9},{9,10},{10,11},{12,13},{... | collective-permute-start | bytes 2359304 | tf_op jit(solution)/shard_map/ppermute | solution.py:520
  16.1 21.9 %collective-permute-start.1 = (f32[2,3,4,64,128]{4,3,2,1,0:T(8,128)}, f32[2,3,4,64,128]{4,3,2,1,0:T(8,128)}, u32[]{:S(2)}, u32[]{:S(2)}) collective-permute-start(f32[2,3,4,64,128]{4,3,2,1,0:T(8,128)} %get-tuple-element.16._.low_edge_ref), channel_id=1, source_target_pairs={{1,0},{2,1},{3,2},{5,4},{6,5},{7,6},{9,8},{10,9},{11,10},{13,12},{... | collective-permute-start | bytes 2359304 | tf_op jit(solution)/shard_map/ppermute | solution.py:521
  17.6 26.3 %copy-start.6 = (f32[32]{0:T(128)S(1)}, f32[32]{0:T(128)}, u32[]{:S(2)}) copy-start(f32[32]{0:T(128)} %coef_ref.1) | copy-start | bytes 388
  43.8 10.0 %copy-start.4 = (f32[32,32]{1,0:T(8,128)S(1)}, f32[32,32]{1,0:T(8,128)}, u32[]{:S(2)}) copy-start(f32[32,32]{1,0:T(8,128)} %inverse_ref.1) | copy-start | bytes 12292
  43.9 10.0 %copy-start.5 = (f32[9,32]{1,0:T(8,128)S(1)}, f32[9,32]{1,0:T(8,128)}, u32[]{:S(2)}) copy-start(f32[9,32]{1,0:T(8,128)} %stencil_ref.1) | copy-start | bytes 3460
  50.2 13.9 %collective-permute-start.7 = (f32[12,64,128]{2,1,0:T(8,128)}, f32[12,64,128]{2,1,0:T(8,128)S(1)}, u32[]{:S(2)}, u32[]{:S(2)}) collective-permute-start(f32[12,64,128]{2,1,0:T(8,128)} %get-tuple-element.25), channel_id=1, source_target_pairs={{0,4},{4,0},{8,12},{12,8},{16,20},{20,16},{24,28},{28,24},{1,5},{5... | collective-permute-start | bytes 1179656 | tf_op jit(solution)/shard_map/ppermute | solution.py:512
  50.3 14.5 %collective-permute-start.8 = (f32[12,64,128]{2,1,0:T(8,128)}, f32[12,64,128]{2,1,0:T(8,128)S(1)}, u32[]{:S(2)}, u32[]{:S(2)}) collective-permute-start(f32[12,64,128]{2,1,0:T(8,128)} %get-tuple-element.26), channel_id=1, source_target_pairs={{0,8},{4,12},{8,0},{12,4},{16,24},{20,28},{24,16},{28,20},{1,9},{5... | collective-permute-start | bytes 1179656 | tf_op jit(solution)/shard_map/ppermute | solution.py:512
  50.9 35.3 %collective-permute-start.2 = (f32[12,64,128]{2,1,0:T(8,128)}, f32[12,64,128]{2,1,0:T(8,128)S(1)}, u32[]{:S(2)}, u32[]{:S(2)}) collective-permute-start(f32[12,64,128]{2,1,0:T(8,128)} %get-tuple-element.19), channel_id=1, source_target_pairs={{0,12},{4,8},{8,4},{12,0},{16,28},{20,24},{24,20},{28,16},{1,13},{... | collective-permute-start | bytes 1179656 | tf_op jit(solution)/shard_map/ppermute | solution.py:512
  52.2 34.0 %collective-permute-start.3 = (f32[12,64,128]{2,1,0:T(8,128)}, f32[12,64,128]{2,1,0:T(8,128)S(1)}, u32[]{:S(2)}, u32[]{:S(2)}) collective-permute-start(f32[12,64,128]{2,1,0:T(8,128)} %get-tuple-element.20), channel_id=1, source_target_pairs={{0,16},{4,20},{8,24},{12,28},{16,0},{20,4},{24,8},{28,12},{1,17},{... | collective-permute-start | bytes 1179656 | tf_op jit(solution)/shard_map/ppermute | solution.py:512
  52.7 35.7 %collective-permute-start.4 = (f32[12,64,128]{2,1,0:T(8,128)}, f32[12,64,128]{2,1,0:T(8,128)S(1)}, u32[]{:S(2)}, u32[]{:S(2)}) collective-permute-start(f32[12,64,128]{2,1,0:T(8,128)} %get-tuple-element.21), channel_id=1, source_target_pairs={{0,20},{4,16},{8,28},{12,24},{16,4},{20,0},{24,12},{28,8},{1,21},{... | collective-permute-start | bytes 1179656 | tf_op jit(solution)/shard_map/ppermute | solution.py:512
  53.9 10.2 %copy-start.7 = (f32[12,64,128]{2,1,0:T(8,128)S(1)}, f32[12,64,128]{2,1,0:T(8,128)}, u32[]{:S(2)}) copy-start(f32[12,64,128]{2,1,0:T(8,128)} %get-tuple-element.22) | copy-start | bytes 1179652
  53.9 13.0 %copy-start.2 = (f32[3,1,1,4096]{3,2,1,0:T(1,128)S(1)}, f32[3,1,1,4096]{3,2,1,0:T(1,128)}, u32[]{:S(2)}) copy-start(f32[3,1,1,4096]{3,2,1,0:T(1,128)} %noise_ref.1) | copy-start | bytes 147460
  64.1 24.3 %collective-permute-start.5 = (f32[12,64,128]{2,1,0:T(8,128)S(1)}, f32[12,64,128]{2,1,0:T(8,128)S(1)}, u32[]{:S(2)}, u32[]{:S(2)}) collective-permute-start(f32[12,64,128]{2,1,0:T(8,128)S(1)} %copy-done.7), channel_id=1, source_target_pairs={{0,24},{4,28},{8,16},{12,20},{16,8},{20,12},{24,0},{28,4},{1,25},{... | collective-permute-start | bytes 1179656 | tf_op jit(solution)/shard_map/ppermute | solution.py:512
  64.8 23.7 %collective-permute-start.6 = (f32[12,64,128]{2,1,0:T(8,128)}, f32[12,64,128]{2,1,0:T(8,128)S(1)}, u32[]{:S(2)}, u32[]{:S(2)}) collective-permute-start(f32[12,64,128]{2,1,0:T(8,128)} %get-tuple-element.23), channel_id=1, source_target_pairs={{0,28},{4,24},{8,20},{12,16},{16,12},{20,8},{24,4},{28,0},{1,29},{... | collective-permute-start | bytes 1179656 | tf_op jit(solution)/shard_map/ppermute | solution.py:512
  66.9 17.2 %copy-start = (f32[12,64,128]{2,1,0:T(8,128)S(1)}, f32[12,64,128]{2,1,0:T(8,128)}, u32[]{:S(2)}) copy-start(f32[12,64,128]{2,1,0:T(8,128)} %get-tuple-element.24.refs_0_) | copy-start | bytes 1179652

commit v15 on v14

--- a/solution.py
+++ b/solution.py
@@ -34,6 +34,10 @@
     rows = stacked.shape[0] // 2
     both = dot(stacked, b_high)
     return both[:rows] + both[rows:] + dot(stacked[:rows], b_low)
+
+def partners(count):
+    return [s for s in (0, 1, 2, 4, 6, 5, 7, 3) if s < count] + list(range(8, count))
+
 
 def in_hbm(value):
     return pltpu.with_memory_space_constraint(value, pltpu.HBM)
@@ -410,10 +414,10 @@
             done_ref[: blocks // 2, q] = (even + odd).reshape(blocks // 2, angles, axial)
             done_ref[blocks // 2 :, q] = (even - odd).reshape(blocks // 2, angles, axial)
         at = pl.ds(g * part, part)
-        for s in range(blocks):
+        for s, partner in enumerate(partners(blocks)):
             stores.append(
                 pltpu.make_async_copy(
-                    done_ref.at[me_ref[0] ^ s, at], out_refs[s].at[at], out_sems.at[g, s]
+                    done_ref.at[me_ref[0] ^ partner, at], out_refs[s].at[at], out_sems.at[g, s]
                 )
             )
             stores[-1].start()
@@ -460,9 +464,10 @@
     piece_refs, refs = refs[:count], refs[count + given :]
     out_ref, sum_ref, in_sems, out_sems = refs
     rows = sum_ref.shape[1]
+    order = partners(force_ref.shape[0] // rows)
     reads, writes = [], []
     for i in range(count):
-        at = pl.ds((me_ref[0] ^ (first + i)) * rows, rows)
+        at = pl.ds((me_ref[0] ^ order[first + i]) * rows, rows)
         reads.append(pltpu.make_async_copy(force_ref.at[at], sum_ref.at[i], in_sems.at[i]))
         writes.append(pltpu.make_async_copy(sum_ref.at[i], out_ref.at[at], out_sems.at[i]))
     for copy in reads:
@@ -506,10 +511,9 @@
 
 def exchange(pieces):
     count = len(pieces)
-    received = [pieces[0]] + [None] * (count - 1)
-    order = list(range(2, count, 2)) + list(range(3, count, 2)) + [1]
-    for s in order:
-        received[s] = lax.ppermute(pieces[s], "az", [(i, i ^ s) for i in range(count)])
+    received = [pieces[0]]
+    for piece, partner in list(zip(pieces, partners(count)))[1:]:
+        received.append(lax.ppermute(piece, "az", [(i, i ^ partner) for i in range(count)]))
     return received
 
 

time: 91.5 us -> 89.9 us (0.983)
  waiting for transfers between devices: 15.9 us -> 14.7 us
    ppermute x7, waiting for transfers between devices: 2.3 us -> 1.04 us  [exchange(): lax.ppermute(piece, 'az', [(i, i ^ partner) for i in range(count)])]
  transfers between devices with their start and end apart: 10 -> 10, of which waited for: 4 -> 5; matrix products, arithmetic and copies ran while one was open for 0% -> 0% of each run, Pallas kernels for 53% -> 53%
where the time goes in v15:
time: 89.9 us; the launch traced here: 89.5 us
  Pallas kernels  56.6 us (63%)
  starting transfers between devices  17.2 us (19%)
  waiting for transfers between devices  14.7 us (16%)
  between operations  0.92 us (1%)
    pallas_call x1, Pallas kernels, move(): pl.pallas_call(functools.partial(move_kernel, angles=angles), in_specs=[w...  17.2 us
    pallas_call x1, Pallas kernels, deposit_middle(): pl.pallas_call(lambda ids_ref, spring_ref, _, *refs: middle_kernel(ids_re...  12.7 us
    pallas_call x1, Pallas kernels, derive(): pl.pallas_call(derive_kernel, grid=(steps,), in_specs=[pl.BlockSpec(stenc...  10.2 us
    pallas_call x1, Pallas kernels, solve(): pl.pallas_call(functools.partial(solve_kernel, extra=len(after)), in_spec...  6.38 us
    ppermute x7, starting transfers between devices, exchange(): lax.ppermute(piece, 'az', [(i, i ^ partner) for i in range(count)])  6.1 us
    all_to_all x1, waiting for transfers between devices, per_device(): gathered = lax.all_to_all(pieces, 'az', 0, 0, tiled=True)  5.9 us
    pallas_call x1, Pallas kernels, deposit_edges(): pl.pallas_call(functools.partial(edge_kernel, radii=radii), grid=(1,), in...  5.73 us
    all_to_all x1, starting transfers between devices, per_device(): gathered = lax.all_to_all(pieces, 'az', 0, 0, tiled=True)  5.31 us
  transfers between devices with their start and end apart: 10, of which 5 were waited for; matrix products, arithmetic and copies ran while one was open for 0% of the time, Pallas kernels for 53%

profile of v15, /device:TPU:0, one launch (start us, length us, event | category | flops | bytes accessed | tf_op | source)
XLA Modules:
  0.0 89.5 jit_solution(11949992024750891304)
XLA Ops:
  0.6 5.3 %all-to-all-start = ((f32[8,12,64,128]{3,2,1,0:T(8,128)}), f32[8,12,64,128]{3,2,1,0:T(8,128)S(1)}, u32[]{:S(2)}, u32[]{:S(2)}) async-start(f32[8,12,64,128]{3,2,1,0:T(8,128)} %bitcast.7), calls=%async_computation | async-start | bytes 6291456 | tf_op jit(solution)/shard_map/all_to_all | solution.py:534
  6.0 0.0 copy-done.1
  6.0 5.7 %deposit_edges.1 = (f32[2,3,4,64,128]{4,3,2,1,0:T(8,128)}, f32[2,3,4,64,128]{4,3,2,1,0:T(8,128)}) custom-call(s32[2,1,1,4096]{3,2,1,0:T(1,128)S(1)} %copy-done.3, f32[3,1,1,4096]{3,2,1,0:T(1,128)S(1)} %copy-done.1, f32[3,32,64,128]{3,2,1,0:T(8,128)} %velocity_ref.1, f32[3,32,64,128]{3,2,1,0:T(8,128)} %velocity_ref.1), custom_call_target="tpu_custom_call" | custom-call | flops 3221225472 | bytes 3145728 | tf_op jit(solution)/shard_map/deposit_edges/pallas_call | solution.py:116
  11.7 4.4 %collective-permute-start = (f32[2,3,4,64,128]{4,3,2,1,0:T(8,128)}, f32[2,3,4,64,128]{4,3,2,1,0:T(8,128)}, u32[]{:S(2)}, u32[]{:S(2)}) collective-permute-start(f32[2,3,4,64,128]{4,3,2,1,0:T(8,128)} %get-tuple-element.15.high_edge_ref), channel_id=1, source_target_pairs={{0,1},{1,2},{2,3},{4,5},{5,6},{6,7},{8,9},{9,10},{10,11},{12,13},{... | collective-permute-start | bytes 2359304 | tf_op jit(solution)/shard_map/ppermute | solution.py:524
  16.1 1.5 %collective-permute-start.1 = (f32[2,3,4,64,128]{4,3,2,1,0:T(8,128)}, f32[2,3,4,64,128]{4,3,2,1,0:T(8,128)}, u32[]{:S(2)}, u32[]{:S(2)}) collective-permute-start(f32[2,3,4,64,128]{4,3,2,1,0:T(8,128)} %get-tuple-element.16._.low_edge_ref), channel_id=1, source_target_pairs={{1,0},{2,1},{3,2},{5,4},{6,5},{7,6},{9,8},{10,9},{11,10},{13,12},{... | collective-permute-start | bytes 2359304 | tf_op jit(solution)/shard_map/ppermute | solution.py:525
  17.6 0.0 copy-start.6
  17.6 12.7 %deposit_middle.1.refs_2_.middle_ref = f32[3,24,64,128]{3,2,1,0:T(8,128)} custom-call(s32[2,1,1,4096]{3,2,1,0:T(1,128)S(1)} %copy-done.3, f32[3,1,1,4096]{3,2,1,0:T(1,128)S(1)} %copy-done.1, f32[2,3,4,64,128]{4,3,2,1,0:T(8,128)} %get-tuple-element.16._.low_edge_ref), custom_call_target="tpu_custom_call" | custom-call | flops 9663676416 | bytes 2359296 | tf_op jit(solution)/shard_map/deposit_middle/pallas_call | solution.py:144
  30.2 2.7 %collective-permute-done.refs_0_.low_ref = f32[2,3,4,64,128]{4,3,2,1,0:T(8,128)} collective-permute-done((f32[2,3,4,64,128]{4,3,2,1,0:T(8,128)}, f32[2,3,4,64,128]{4,3,2,1,0:T(8,128)}, u32[]{:S(2)}, u32[]{:S(2)}) %collective-permute-start) | collective-permute-done | bytes 786464 | tf_op jit(solution)/shard_map/ppermute | solution.py:524
  32.9 5.0 %collective-permute-done.1.refs_1_.high_ref = f32[2,3,4,64,128]{4,3,2,1,0:T(8,128)} collective-permute-done((f32[2,3,4,64,128]{4,3,2,1,0:T(8,128)}, f32[2,3,4,64,128]{4,3,2,1,0:T(8,128)}, u32[]{:S(2)}, u32[]{:S(2)}) %collective-permute-start.1) | collective-permute-done | bytes 786464 | tf_op jit(solution)/shard_map/ppermute | solution.py:525
  37.9 5.9 %all-to-all-done.refs_3_ = f32[8,12,64,128]{3,2,1,0:T(8,128)S(1)} async-done(((f32[8,12,64,128]{3,2,1,0:T(8,128)}), f32[8,12,64,128]{3,2,1,0:T(8,128)S(1)}, u32[]{:S(2)}, u32[]{:S(2)}) %all-to-all-start) | async-done | bytes 3145760 | tf_op jit(solution)/shard_map/all_to_all | solution.py:534
  43.8 0.0 copy-done.6
  43.9 6.4 %solve.1 = (f32[12,64,128]{2,1,0:T(8,128)}, f32[12,64,128]{2,1,0:T(8,128)}, f32[12,64,128]{2,1,0:T(8,128)}, f32[12,64,128]{2,1,0:T(8,128)}, f32[12,64,128]{2,1,0...) custom-call(f32[32]{0:T(128)S(1)} %copy-done.6, s32[1]{0:T(128)} %bitcast.me_ref, ...), custom_call_target="tpu_custom_call" | custom-call | flops 4831838208 | bytes 6291456 | tf_op jit(solution)/shard_map/solve/pallas_call | solution.py:435
  50.2 0.1 collective-permute-start.7
  50.3 0.6 collective-permute-start.8
  50.9 0.6 collective-permute-start.2
  51.5 2.3 %collective-permute-start.3 = (f32[12,64,128]{2,1,0:T(8,128)}, f32[12,64,128]{2,1,0:T(8,128)S(1)}, u32[]{:S(2)}, u32[]{:S(2)}) collective-permute-start(f32[12,64,128]{2,1,0:T(8,128)} %get-tuple-element.20), channel_id=1, source_target_pairs={{0,24},{4,28},{8,16},{12,20},{16,8},{20,12},{24,0},{28,4},{1,25},{... | collective-permute-start | bytes 1179656 | tf_op jit(solution)/shard_map/ppermute | solution.py:516
  53.9 0.0 collective-permute-start.4
  53.9 0.0 copy-done.5
  53.9 0.0 copy-start.2
  53.9 10.2 %derive.1 = (bf16[768,2048]{1,0:T(8,128)(2,1)}, f32[3,32,64,128]{3,2,1,0:T(8,128)}, f32[12,64,128]{2,1,0:T(8,128)}) custom-call(f32[9,32]{1,0:T(8,128)S(1)} %copy-done.5, f32[32,32]{1,0:T(8,128)S(1)} %copy-done.4, f32[2,3,4,64,128]{4,3,2,1,0:T(8,128)} %collective-permute-done.refs_0_.low_ref, f32[3,32,64,128]{3,2,1,0:T(8,128)} %velocity_ref.1, ...), custom_call_target="tpu_custom_call" | custom-call | flops 3774873600 | bytes 10485760 | tf_op jit(solution)/shard_map/derive/pallas_call | solution.py:246
  64.1 0.0 collective-permute-done.7.refs_1_
  64.1 1.7 %collective-permute-start.5 = (f32[12,64,128]{2,1,0:T(8,128)S(1)}, f32[12,64,128]{2,1,0:T(8,128)S(1)}, u32[]{:S(2)}, u32[]{:S(2)}) collective-permute-start(f32[12,64,128]{2,1,0:T(8,128)S(1)} %copy-done.7), channel_id=1, source_target_pairs={{0,28},{4,24},{8,20},{12,16},{16,12},{20,8},{24,4},{28,0},{1,29},{... | collective-permute-start | bytes 1179656 | tf_op jit(solution)/shard_map/ppermute | solution.py:516
  65.9 0.0 collective-permute-done.8.refs_2_
  65.9 0.7 collective-permute-start.6
  66.6 17.2 %move.1 = f32[3,1,1,4096]{3,2,1,0:T(1,128)} custom-call(bf16[768,2048]{1,0:T(8,128)(2,1)} %get-tuple-element.27.grad_ref, s32[2,1,1,4096]{3,2,1,0:T(1,128)S(1)} %copy-done.3, f32[3,1,1,4096]{3,2,1,0:T(1,128)S(1)} %copy-done.1, f32[3,1,1,4096]{3,2,1,0:T(1,128)S(1)} %copy-done.2), custom_call_target="tpu_custom_call" | custom-call | flops 12884901888 | bytes 3145728 | tf_op jit(solution)/shard_map/move/pallas_call | solution.py:329
  83.8 2.1 %join.2.refs_5_ = f32[96,64,128]{2,1,0:T(8,128)} custom-call(s32[1]{0:T(128)} %bitcast.me_ref, f32[96,64,128]{2,1,0:T(8,128)} %bitcast.4, f32[12,64,128]{2,1,0:T(8,128)S(1)} %copy-done, f32[12,64,128]{2,1,0:T(8,128)S(1)} %collective-permute-done.7.refs_1_, f32[12,64,128]{2,1,0:T(8,128)S(1)} %collective-permute-done.8.refs_2_), custom_call_target="tpu_custom_call" | custom-call | flops 294912 | bytes 3538944 | tf_op jit(solution)/shard_map/join/pallas_call | solution.py:489
  85.9 0.0 collective-permute-done.2.refs_0_
  85.9 0.0 collective-permute-done.3.refs_1_
  85.9 0.9 %collective-permute-done.4.refs_2_ = f32[12,64,128]{2,1,0:T(8,128)S(1)} collective-permute-done((f32[12,64,128]{2,1,0:T(8,128)}, f32[12,64,128]{2,1,0:T(8,128)S(1)}, u32[]{:S(2)}, u32[]{:S(2)}) %collective-permute-start.4) | collective-permute-done | bytes 393248 | tf_op jit(solution)/shard_map/ppermute | solution.py:516
  86.8 0.0 collective-permute-done.5.refs_3_
  86.8 0.1 collective-permute-done.6.refs_4_
  86.9 2.4 %join.3 = f32[96,64,128]{2,1,0:T(8,128)} custom-call(s32[1]{0:T(128)} %bitcast.me_ref, f32[96,64,128]{2,1,0:T(8,128)} %bitcast.5, f32[12,64,128]{2,1,0:T(8,128)S(1)} %collective-permute-done.2.refs_0_, f32[12,64,128]{2,1,0:T(8,128)S(1)} %collective-permute-done.3.refs_1_, ...), custom_call_target="tpu_custom_call", output_to_operand_aliasing={{}: (7, {})} | custom-call | flops 491520 | bytes 5898240 | tf_op jit(solution)/shard_map/join/pallas_call | solution.py:489
  (11 shorter events, 0.0 us)
Async XLA Ops:
  0.6 5.3 %copy-start.1 = (f32[3,1,1,4096]{3,2,1,0:T(1,128)S(1)}, f32[3,1,1,4096]{3,2,1,0:T(1,128)}, u32[]{:S(2)}) copy-start(f32[3,1,1,4096]{3,2,1,0:T(1,128)} %spring_ref.5) | copy-start | bytes 147460
  0.6 5.3 %copy-start.3 = (s32[2,1,1,4096]{3,2,1,0:T(1,128)S(1)}, s32[2,1,1,4096]{3,2,1,0:T(1,128)}, u32[]{:S(2)}) copy-start(s32[2,1,1,4096]{3,2,1,0:T(1,128)} %ids_ref.5) | copy-start | bytes 98308
  0.6 43.2 %all-to-all-start = ((f32[8,12,64,128]{3,2,1,0:T(8,128)}), f32[8,12,64,128]{3,2,1,0:T(8,128)S(1)}, u32[]{:S(2)}, u32[]{:S(2)}) async-start(f32[8,12,64,128]{3,2,1,0:T(8,128)} %bitcast.7), calls=%async_computation | async-start | bytes 6291456 | tf_op jit(solution)/shard_map/all_to_all | solution.py:534
  11.7 21.2 %collective-permute-start = (f32[2,3,4,64,128]{4,3,2,1,0:T(8,128)}, f32[2,3,4,64,128]{4,3,2,1,0:T(8,128)}, u32[]{:S(2)}, u32[]{:S(2)}) collective-permute-start(f32[2,3,4,64,128]{4,3,2,1,0:T(8,128)} %get-tuple-element.15.high_edge_ref), channel_id=1, source_target_pairs={{0,1},{1,2},{2,3},{4,5},{5,6},{6,7},{8,9},{9,10},{10,11},{12,13},{... | collective-permute-start | bytes 2359304 | tf_op jit(solution)/shard_map/ppermute | solution.py:524
  16.1 21.9 %collective-permute-start.1 = (f32[2,3,4,64,128]{4,3,2,1,0:T(8,128)}, f32[2,3,4,64,128]{4,3,2,1,0:T(8,128)}, u32[]{:S(2)}, u32[]{:S(2)}) collective-permute-start(f32[2,3,4,64,128]{4,3,2,1,0:T(8,128)} %get-tuple-element.16._.low_edge_ref), channel_id=1, source_target_pairs={{1,0},{2,1},{3,2},{5,4},{6,5},{7,6},{9,8},{10,9},{11,10},{13,12},{... | collective-permute-start | bytes 2359304 | tf_op jit(solution)/shard_map/ppermute | solution.py:525
  17.6 26.3 %copy-start.6 = (f32[32]{0:T(128)S(1)}, f32[32]{0:T(128)}, u32[]{:S(2)}) copy-start(f32[32]{0:T(128)} %coef_ref.1) | copy-start | bytes 388
  43.8 10.0 %copy-start.4 = (f32[32,32]{1,0:T(8,128)S(1)}, f32[32,32]{1,0:T(8,128)}, u32[]{:S(2)}) copy-start(f32[32,32]{1,0:T(8,128)} %inverse_ref.1) | copy-start | bytes 12292
  43.9 10.0 %copy-start.5 = (f32[9,32]{1,0:T(8,128)S(1)}, f32[9,32]{1,0:T(8,128)}, u32[]{:S(2)}) copy-start(f32[9,32]{1,0:T(8,128)} %stencil_ref.1) | copy-start | bytes 3460
  50.2 13.9 %collective-permute-start.7 = (f32[12,64,128]{2,1,0:T(8,128)}, f32[12,64,128]{2,1,0:T(8,128)S(1)}, u32[]{:S(2)}, u32[]{:S(2)}) collective-permute-start(f32[12,64,128]{2,1,0:T(8,128)} %get-tuple-element.25), channel_id=1, source_target_pairs={{0,4},{4,0},{8,12},{12,8},{16,20},{20,16},{24,28},{28,24},{1,5},{5... | collective-permute-start | bytes 1179656 | tf_op jit(solution)/shard_map/ppermute | solution.py:516
  50.3 15.6 %collective-permute-start.8 = (f32[12,64,128]{2,1,0:T(8,128)}, f32[12,64,128]{2,1,0:T(8,128)S(1)}, u32[]{:S(2)}, u32[]{:S(2)}) collective-permute-start(f32[12,64,128]{2,1,0:T(8,128)} %get-tuple-element.26), channel_id=1, source_target_pairs={{0,8},{4,12},{8,0},{12,4},{16,24},{20,28},{24,16},{28,20},{1,9},{5... | collective-permute-start | bytes 1179656 | tf_op jit(solution)/shard_map/ppermute | solution.py:516
  50.9 35.0 %collective-permute-start.2 = (f32[12,64,128]{2,1,0:T(8,128)}, f32[12,64,128]{2,1,0:T(8,128)S(1)}, u32[]{:S(2)}, u32[]{:S(2)}) collective-permute-start(f32[12,64,128]{2,1,0:T(8,128)} %get-tuple-element.19), channel_id=1, source_target_pairs={{0,16},{4,20},{8,24},{12,28},{16,0},{20,4},{24,8},{28,12},{1,17},{... | collective-permute-start | bytes 1179656 | tf_op jit(solution)/shard_map/ppermute | solution.py:516
  51.5 34.3 %collective-permute-start.3 = (f32[12,64,128]{2,1,0:T(8,128)}, f32[12,64,128]{2,1,0:T(8,128)S(1)}, u32[]{:S(2)}, u32[]{:S(2)}) collective-permute-start(f32[12,64,128]{2,1,0:T(8,128)} %get-tuple-element.20), channel_id=1, source_target_pairs={{0,24},{4,28},{8,16},{12,20},{16,8},{20,12},{24,0},{28,4},{1,25},{... | collective-permute-start | bytes 1179656 | tf_op jit(solution)/shard_map/ppermute | solution.py:516
  53.9 32.9 %collective-permute-start.4 = (f32[12,64,128]{2,1,0:T(8,128)}, f32[12,64,128]{2,1,0:T(8,128)S(1)}, u32[]{:S(2)}, u32[]{:S(2)}) collective-permute-start(f32[12,64,128]{2,1,0:T(8,128)} %get-tuple-element.21), channel_id=1, source_target_pairs={{0,20},{4,16},{8,28},{12,24},{16,4},{20,0},{24,12},{28,8},{1,21},{... | collective-permute-start | bytes 1179656 | tf_op jit(solution)/shard_map/ppermute | solution.py:516
  53.9 10.2 %copy-start.7 = (f32[12,64,128]{2,1,0:T(8,128)S(1)}, f32[12,64,128]{2,1,0:T(8,128)}, u32[]{:S(2)}) copy-start(f32[12,64,128]{2,1,0:T(8,128)} %get-tuple-element.22) | copy-start | bytes 1179652
  53.9 12.7 %copy-start.2 = (f32[3,1,1,4096]{3,2,1,0:T(1,128)S(1)}, f32[3,1,1,4096]{3,2,1,0:T(1,128)}, u32[]{:S(2)}) copy-start(f32[3,1,1,4096]{3,2,1,0:T(1,128)} %noise_ref.1) | copy-start | bytes 147460
  64.1 22.7 %collective-permute-start.5 = (f32[12,64,128]{2,1,0:T(8,128)S(1)}, f32[12,64,128]{2,1,0:T(8,128)S(1)}, u32[]{:S(2)}, u32[]{:S(2)}) collective-permute-start(f32[12,64,128]{2,1,0:T(8,128)S(1)} %copy-done.7), channel_id=1, source_target_pairs={{0,28},{4,24},{8,20},{12,16},{16,12},{20,8},{24,4},{28,0},{1,29},{... | collective-permute-start | bytes 1179656 | tf_op jit(solution)/shard_map/ppermute | solution.py:516
  65.9 21.0 %collective-permute-start.6 = (f32[12,64,128]{2,1,0:T(8,128)}, f32[12,64,128]{2,1,0:T(8,128)S(1)}, u32[]{:S(2)}, u32[]{:S(2)}) collective-permute-start(f32[12,64,128]{2,1,0:T(8,128)} %get-tuple-element.23), channel_id=1, source_target_pairs={{0,12},{4,8},{8,4},{12,0},{16,28},{20,24},{24,20},{28,16},{1,13},{... | collective-permute-start | bytes 1179656 | tf_op jit(solution)/shard_map/ppermute | solution.py:516
  66.6 17.2 %copy-start = (f32[12,64,128]{2,1,0:T(8,128)S(1)}, f32[12,64,128]{2,1,0:T(8,128)}, u32[]{:S(2)}) copy-start(f32[12,64,128]{2,1,0:T(8,128)} %get-tuple-element.24.refs_0_) | copy-start | bytes 1179652

commit v16 on v15

--- a/solution.py
+++ b/solution.py
@@ -295,7 +295,7 @@
     group = cells // angles * SUB
 
     count = spring_ref.shape[3]
-    part = min(count, 512)
+    part = min(count, 1024)
 
     def read(i, carry):
         at = pl.ds(pl.multiple_of(i * part, part), part)

time: 89.9 us -> 89.9 us (level)
  no operation moved by 1% of the time
where the time goes in v16:
time: 89.9 us; the launch traced here: 89.5 us
  Pallas kernels  56 us (62%)
  starting transfers between devices  17.2 us (19%)
  waiting for transfers between devices  15.3 us (17%)
  between operations  0.92 us (1%)
    pallas_call x1, Pallas kernels, move(): pl.pallas_call(functools.partial(move_kernel, angles=angles), in_specs=[w...  16.5 us
    pallas_call x1, Pallas kernels, deposit_middle(): pl.pallas_call(lambda ids_ref, spring_ref, _, *refs: middle_kernel(ids_re...  12.7 us
    pallas_call x1, Pallas kernels, derive(): pl.pallas_call(derive_kernel, grid=(steps,), in_specs=[pl.BlockSpec(stenc...  10.2 us
    pallas_call x1, Pallas kernels, solve(): pl.pallas_call(functools.partial(solve_kernel, extra=len(after)), in_spec...  6.38 us
    ppermute x7, starting transfers between devices, exchange(): lax.ppermute(piece, 'az', [(i, i ^ partner) for i in range(count)])  6.1 us
    all_to_all x1, waiting for transfers between devices, per_device(): gathered = lax.all_to_all(pieces, 'az', 0, 0, tiled=True)  5.9 us
    pallas_call x1, Pallas kernels, deposit_edges(): pl.pallas_call(functools.partial(edge_kernel, radii=radii), grid=(1,), in...  5.73 us
    all_to_all x1, starting transfers between devices, per_device(): gathered = lax.all_to_all(pieces, 'az', 0, 0, tiled=True)  5.31 us
  transfers between devices with their start and end apart: 10, of which 5 were waited for; matrix products, arithmetic and copies ran while one was open for 0% of the time, Pallas kernels for 53%

profile of v16, /device:TPU:0, one launch (start us, length us, event | category | flops | bytes accessed | tf_op | source)
XLA Modules:
  0.0 89.5 jit_solution(17589155418915455328)
XLA Ops:
  0.6 5.3 %all-to-all-start = ((f32[8,12,64,128]{3,2,1,0:T(8,128)}), f32[8,12,64,128]{3,2,1,0:T(8,128)S(1)}, u32[]{:S(2)}, u32[]{:S(2)}) async-start(f32[8,12,64,128]{3,2,1,0:T(8,128)} %bitcast.7), calls=%async_computation | async-start | bytes 6291456 | tf_op jit(solution)/shard_map/all_to_all | solution.py:534
  6.0 0.0 copy-done.1
  6.0 5.7 %deposit_edges.1 = (f32[2,3,4,64,128]{4,3,2,1,0:T(8,128)}, f32[2,3,4,64,128]{4,3,2,1,0:T(8,128)}) custom-call(s32[2,1,1,4096]{3,2,1,0:T(1,128)S(1)} %copy-done.3, f32[3,1,1,4096]{3,2,1,0:T(1,128)S(1)} %copy-done.1, f32[3,32,64,128]{3,2,1,0:T(8,128)} %velocity_ref.1, f32[3,32,64,128]{3,2,1,0:T(8,128)} %velocity_ref.1), custom_call_target="tpu_custom_call" | custom-call | flops 3221225472 | bytes 3145728 | tf_op jit(solution)/shard_map/deposit_edges/pallas_call | solution.py:116
  11.7 4.4 %collective-permute-start = (f32[2,3,4,64,128]{4,3,2,1,0:T(8,128)}, f32[2,3,4,64,128]{4,3,2,1,0:T(8,128)}, u32[]{:S(2)}, u32[]{:S(2)}) collective-permute-start(f32[2,3,4,64,128]{4,3,2,1,0:T(8,128)} %get-tuple-element.15.high_edge_ref), channel_id=1, source_target_pairs={{0,1},{1,2},{2,3},{4,5},{5,6},{6,7},{8,9},{9,10},{10,11},{12,13},{... | collective-permute-start | bytes 2359304 | tf_op jit(solution)/shard_map/ppermute | solution.py:524
  16.1 1.5 %collective-permute-start.1 = (f32[2,3,4,64,128]{4,3,2,1,0:T(8,128)}, f32[2,3,4,64,128]{4,3,2,1,0:T(8,128)}, u32[]{:S(2)}, u32[]{:S(2)}) collective-permute-start(f32[2,3,4,64,128]{4,3,2,1,0:T(8,128)} %get-tuple-element.16._.low_edge_ref), channel_id=1, source_target_pairs={{1,0},{2,1},{3,2},{5,4},{6,5},{7,6},{9,8},{10,9},{11,10},{13,12},{... | collective-permute-start | bytes 2359304 | tf_op jit(solution)/shard_map/ppermute | solution.py:525
  17.6 0.0 copy-start.6
  17.6 12.7 %deposit_middle.1.refs_2_.middle_ref = f32[3,24,64,128]{3,2,1,0:T(8,128)} custom-call(s32[2,1,1,4096]{3,2,1,0:T(1,128)S(1)} %copy-done.3, f32[3,1,1,4096]{3,2,1,0:T(1,128)S(1)} %copy-done.1, f32[2,3,4,64,128]{4,3,2,1,0:T(8,128)} %get-tuple-element.16._.low_edge_ref), custom_call_target="tpu_custom_call" | custom-call | flops 9663676416 | bytes 2359296 | tf_op jit(solution)/shard_map/deposit_middle/pallas_call | solution.py:144
  30.2 2.7 %collective-permute-done.refs_0_.low_ref = f32[2,3,4,64,128]{4,3,2,1,0:T(8,128)} collective-permute-done((f32[2,3,4,64,128]{4,3,2,1,0:T(8,128)}, f32[2,3,4,64,128]{4,3,2,1,0:T(8,128)}, u32[]{:S(2)}, u32[]{:S(2)}) %collective-permute-start) | collective-permute-done | bytes 786464 | tf_op jit(solution)/shard_map/ppermute | solution.py:524
  32.9 5.0 %collective-permute-done.1.refs_1_.high_ref = f32[2,3,4,64,128]{4,3,2,1,0:T(8,128)} collective-permute-done((f32[2,3,4,64,128]{4,3,2,1,0:T(8,128)}, f32[2,3,4,64,128]{4,3,2,1,0:T(8,128)}, u32[]{:S(2)}, u32[]{:S(2)}) %collective-permute-start.1) | collective-permute-done | bytes 786464 | tf_op jit(solution)/shard_map/ppermute | solution.py:525
  37.9 5.9 %all-to-all-done.refs_3_ = f32[8,12,64,128]{3,2,1,0:T(8,128)S(1)} async-done(((f32[8,12,64,128]{3,2,1,0:T(8,128)}), f32[8,12,64,128]{3,2,1,0:T(8,128)S(1)}, u32[]{:S(2)}, u32[]{:S(2)}) %all-to-all-start) | async-done | bytes 3145760 | tf_op jit(solution)/shard_map/all_to_all | solution.py:534
  43.8 0.0 copy-done.6
  43.9 6.4 %solve.1 = (f32[12,64,128]{2,1,0:T(8,128)}, f32[12,64,128]{2,1,0:T(8,128)}, f32[12,64,128]{2,1,0:T(8,128)}, f32[12,64,128]{2,1,0:T(8,128)}, f32[12,64,128]{2,1,0...) custom-call(f32[32]{0:T(128)S(1)} %copy-done.6, s32[1]{0:T(128)} %bitcast.me_ref, ...), custom_call_target="tpu_custom_call" | custom-call | flops 4831838208 | bytes 6291456 | tf_op jit(solution)/shard_map/solve/pallas_call | solution.py:435
  50.2 0.1 collective-permute-start.7
  50.3 0.6 collective-permute-start.8
  50.9 0.6 collective-permute-start.2
  51.5 2.3 %collective-permute-start.3 = (f32[12,64,128]{2,1,0:T(8,128)}, f32[12,64,128]{2,1,0:T(8,128)S(1)}, u32[]{:S(2)}, u32[]{:S(2)}) collective-permute-start(f32[12,64,128]{2,1,0:T(8,128)} %get-tuple-element.20), channel_id=1, source_target_pairs={{0,24},{4,28},{8,16},{12,20},{16,8},{20,12},{24,0},{28,4},{1,25},{... | collective-permute-start | bytes 1179656 | tf_op jit(solution)/shard_map/ppermute | solution.py:516
  53.9 0.0 collective-permute-start.4
  53.9 0.0 copy-done.5
  53.9 0.0 copy-start.2
  53.9 10.2 %derive.1 = (bf16[768,2048]{1,0:T(8,128)(2,1)}, f32[3,32,64,128]{3,2,1,0:T(8,128)}, f32[12,64,128]{2,1,0:T(8,128)}) custom-call(f32[9,32]{1,0:T(8,128)S(1)} %copy-done.5, f32[32,32]{1,0:T(8,128)S(1)} %copy-done.4, f32[2,3,4,64,128]{4,3,2,1,0:T(8,128)} %collective-permute-done.refs_0_.low_ref, f32[3,32,64,128]{3,2,1,0:T(8,128)} %velocity_ref.1, ...), custom_call_target="tpu_custom_call" | custom-call | flops 3774873600 | bytes 10485760 | tf_op jit(solution)/shard_map/derive/pallas_call | solution.py:246
  64.1 0.0 collective-permute-done.7.refs_1_
  64.1 1.7 %collective-permute-start.5 = (f32[12,64,128]{2,1,0:T(8,128)S(1)}, f32[12,64,128]{2,1,0:T(8,128)S(1)}, u32[]{:S(2)}, u32[]{:S(2)}) collective-permute-start(f32[12,64,128]{2,1,0:T(8,128)S(1)} %copy-done.7), channel_id=1, source_target_pairs={{0,28},{4,24},{8,20},{12,16},{16,12},{20,8},{24,4},{28,0},{1,29},{... | collective-permute-start | bytes 1179656 | tf_op jit(solution)/shard_map/ppermute | solution.py:516
  65.9 0.0 collective-permute-done.8.refs_2_
  65.9 0.7 collective-permute-start.6
  66.6 16.5 %move.1 = f32[3,1,1,4096]{3,2,1,0:T(1,128)} custom-call(bf16[768,2048]{1,0:T(8,128)(2,1)} %get-tuple-element.27.grad_ref, s32[2,1,1,4096]{3,2,1,0:T(1,128)S(1)} %copy-done.3, f32[3,1,1,4096]{3,2,1,0:T(1,128)S(1)} %copy-done.1, f32[3,1,1,4096]{3,2,1,0:T(1,128)S(1)} %copy-done.2), custom_call_target="tpu_custom_call" | custom-call | flops 12884901888 | bytes 3145728 | tf_op jit(solution)/shard_map/move/pallas_call | solution.py:329
  83.2 2.1 %join.2.refs_5_ = f32[96,64,128]{2,1,0:T(8,128)} custom-call(s32[1]{0:T(128)} %bitcast.me_ref, f32[96,64,128]{2,1,0:T(8,128)} %bitcast.4, f32[12,64,128]{2,1,0:T(8,128)S(1)} %copy-done, f32[12,64,128]{2,1,0:T(8,128)S(1)} %collective-permute-done.7.refs_1_, f32[12,64,128]{2,1,0:T(8,128)S(1)} %collective-permute-done.8.refs_2_), custom_call_target="tpu_custom_call" | custom-call | flops 294912 | bytes 3538944 | tf_op jit(solution)/shard_map/join/pallas_call | solution.py:489
  85.2 0.0 collective-permute-done.2.refs_0_
  85.3 0.0 collective-permute-done.3.refs_1_
  85.3 1.5 %collective-permute-done.4.refs_2_ = f32[12,64,128]{2,1,0:T(8,128)S(1)} collective-permute-done((f32[12,64,128]{2,1,0:T(8,128)}, f32[12,64,128]{2,1,0:T(8,128)S(1)}, u32[]{:S(2)}, u32[]{:S(2)}) %collective-permute-start.4) | collective-permute-done | bytes 393248 | tf_op jit(solution)/shard_map/ppermute | solution.py:516
  86.8 0.0 collective-permute-done.5.refs_3_
  86.8 0.1 collective-permute-done.6.refs_4_
  86.9 2.4 %join.3 = f32[96,64,128]{2,1,0:T(8,128)} custom-call(s32[1]{0:T(128)} %bitcast.me_ref, f32[96,64,128]{2,1,0:T(8,128)} %bitcast.5, f32[12,64,128]{2,1,0:T(8,128)S(1)} %collective-permute-done.2.refs_0_, f32[12,64,128]{2,1,0:T(8,128)S(1)} %collective-permute-done.3.refs_1_, ...), custom_call_target="tpu_custom_call", output_to_operand_aliasing={{}: (7, {})} | custom-call | flops 491520 | bytes 5898240 | tf_op jit(solution)/shard_map/join/pallas_call | solution.py:489
  (11 shorter events, 0.0 us)
Async XLA Ops:
  0.6 5.3 %copy-start.1 = (f32[3,1,1,4096]{3,2,1,0:T(1,128)S(1)}, f32[3,1,1,4096]{3,2,1,0:T(1,128)}, u32[]{:S(2)}) copy-start(f32[3,1,1,4096]{3,2,1,0:T(1,128)} %spring_ref.5) | copy-start | bytes 147460
  0.6 5.3 %copy-start.3 = (s32[2,1,1,4096]{3,2,1,0:T(1,128)S(1)}, s32[2,1,1,4096]{3,2,1,0:T(1,128)}, u32[]{:S(2)}) copy-start(s32[2,1,1,4096]{3,2,1,0:T(1,128)} %ids_ref.5) | copy-start | bytes 98308
  0.6 43.2 %all-to-all-start = ((f32[8,12,64,128]{3,2,1,0:T(8,128)}), f32[8,12,64,128]{3,2,1,0:T(8,128)S(1)}, u32[]{:S(2)}, u32[]{:S(2)}) async-start(f32[8,12,64,128]{3,2,1,0:T(8,128)} %bitcast.7), calls=%async_computation | async-start | bytes 6291456 | tf_op jit(solution)/shard_map/all_to_all | solution.py:534
  11.7 21.2 %collective-permute-start = (f32[2,3,4,64,128]{4,3,2,1,0:T(8,128)}, f32[2,3,4,64,128]{4,3,2,1,0:T(8,128)}, u32[]{:S(2)}, u32[]{:S(2)}) collective-permute-start(f32[2,3,4,64,128]{4,3,2,1,0:T(8,128)} %get-tuple-element.15.high_edge_ref), channel_id=1, source_target_pairs={{0,1},{1,2},{2,3},{4,5},{5,6},{6,7},{8,9},{9,10},{10,11},{12,13},{... | collective-permute-start | bytes 2359304 | tf_op jit(solution)/shard_map/ppermute | solution.py:524
  16.1 21.9 %collective-permute-start.1 = (f32[2,3,4,64,128]{4,3,2,1,0:T(8,128)}, f32[2,3,4,64,128]{4,3,2,1,0:T(8,128)}, u32[]{:S(2)}, u32[]{:S(2)}) collective-permute-start(f32[2,3,4,64,128]{4,3,2,1,0:T(8,128)} %get-tuple-element.16._.low_edge_ref), channel_id=1, source_target_pairs={{1,0},{2,1},{3,2},{5,4},{6,5},{7,6},{9,8},{10,9},{11,10},{13,12},{... | collective-permute-start | bytes 2359304 | tf_op jit(solution)/shard_map/ppermute | solution.py:525
  17.6 26.3 %copy-start.6 = (f32[32]{0:T(128)S(1)}, f32[32]{0:T(128)}, u32[]{:S(2)}) copy-start(f32[32]{0:T(128)} %coef_ref.1) | copy-start | bytes 388
  43.8 10.0 %copy-start.4 = (f32[32,32]{1,0:T(8,128)S(1)}, f32[32,32]{1,0:T(8,128)}, u32[]{:S(2)}) copy-start(f32[32,32]{1,0:T(8,128)} %inverse_ref.1) | copy-start | bytes 12292
  43.9 10.0 %copy-start.5 = (f32[9,32]{1,0:T(8,128)S(1)}, f32[9,32]{1,0:T(8,128)}, u32[]{:S(2)}) copy-start(f32[9,32]{1,0:T(8,128)} %stencil_ref.1) | copy-start | bytes 3460
  50.2 13.9 %collective-permute-start.7 = (f32[12,64,128]{2,1,0:T(8,128)}, f32[12,64,128]{2,1,0:T(8,128)S(1)}, u32[]{:S(2)}, u32[]{:S(2)}) collective-permute-start(f32[12,64,128]{2,1,0:T(8,128)} %get-tuple-element.25), channel_id=1, source_target_pairs={{0,4},{4,0},{8,12},{12,8},{16,20},{20,16},{24,28},{28,24},{1,5},{5... | collective-permute-start | bytes 1179656 | tf_op jit(solution)/shard_map/ppermute | solution.py:516
  50.3 15.6 %collective-permute-start.8 = (f32[12,64,128]{2,1,0:T(8,128)}, f32[12,64,128]{2,1,0:T(8,128)S(1)}, u32[]{:S(2)}, u32[]{:S(2)}) collective-permute-start(f32[12,64,128]{2,1,0:T(8,128)} %get-tuple-element.26), channel_id=1, source_target_pairs={{0,8},{4,12},{8,0},{12,4},{16,24},{20,28},{24,16},{28,20},{1,9},{5... | collective-permute-start | bytes 1179656 | tf_op jit(solution)/shard_map/ppermute | solution.py:516
  50.9 34.4 %collective-permute-start.2 = (f32[12,64,128]{2,1,0:T(8,128)}, f32[12,64,128]{2,1,0:T(8,128)S(1)}, u32[]{:S(2)}, u32[]{:S(2)}) collective-permute-start(f32[12,64,128]{2,1,0:T(8,128)} %get-tuple-element.19), channel_id=1, source_target_pairs={{0,16},{4,20},{8,24},{12,28},{16,0},{20,4},{24,8},{28,12},{1,17},{... | collective-permute-start | bytes 1179656 | tf_op jit(solution)/shard_map/ppermute | solution.py:516
  51.5 33.7 %collective-permute-start.3 = (f32[12,64,128]{2,1,0:T(8,128)}, f32[12,64,128]{2,1,0:T(8,128)S(1)}, u32[]{:S(2)}, u32[]{:S(2)}) collective-permute-start(f32[12,64,128]{2,1,0:T(8,128)} %get-tuple-element.20), channel_id=1, source_target_pairs={{0,24},{4,28},{8,16},{12,20},{16,8},{20,12},{24,0},{28,4},{1,25},{... | collective-permute-start | bytes 1179656 | tf_op jit(solution)/shard_map/ppermute | solution.py:516
  53.9 32.9 %collective-permute-start.4 = (f32[12,64,128]{2,1,0:T(8,128)}, f32[12,64,128]{2,1,0:T(8,128)S(1)}, u32[]{:S(2)}, u32[]{:S(2)}) collective-permute-start(f32[12,64,128]{2,1,0:T(8,128)} %get-tuple-element.21), channel_id=1, source_target_pairs={{0,20},{4,16},{8,28},{12,24},{16,4},{20,0},{24,12},{28,8},{1,21},{... | collective-permute-start | bytes 1179656 | tf_op jit(solution)/shard_map/ppermute | solution.py:516
  53.9 10.2 %copy-start.7 = (f32[12,64,128]{2,1,0:T(8,128)S(1)}, f32[12,64,128]{2,1,0:T(8,128)}, u32[]{:S(2)}) copy-start(f32[12,64,128]{2,1,0:T(8,128)} %get-tuple-element.22) | copy-start | bytes 1179652
  53.9 12.7 %copy-start.2 = (f32[3,1,1,4096]{3,2,1,0:T(1,128)S(1)}, f32[3,1,1,4096]{3,2,1,0:T(1,128)}, u32[]{:S(2)}) copy-start(f32[3,1,1,4096]{3,2,1,0:T(1,128)} %noise_ref.1) | copy-start | bytes 147460
  64.1 22.7 %collective-permute-start.5 = (f32[12,64,128]{2,1,0:T(8,128)S(1)}, f32[12,64,128]{2,1,0:T(8,128)S(1)}, u32[]{:S(2)}, u32[]{:S(2)}) collective-permute-start(f32[12,64,128]{2,1,0:T(8,128)S(1)} %copy-done.7), channel_id=1, source_target_pairs={{0,28},{4,24},{8,20},{12,16},{16,12},{20,8},{24,4},{28,0},{1,29},{... | collective-permute-start | bytes 1179656 | tf_op jit(solution)/shard_map/ppermute | solution.py:516
  65.9 21.0 %collective-permute-start.6 = (f32[12,64,128]{2,1,0:T(8,128)}, f32[12,64,128]{2,1,0:T(8,128)S(1)}, u32[]{:S(2)}, u32[]{:S(2)}) collective-permute-start(f32[12,64,128]{2,1,0:T(8,128)} %get-tuple-element.23), channel_id=1, source_target_pairs={{0,12},{4,8},{8,4},{12,0},{16,28},{20,24},{24,20},{28,16},{1,13},{... | collective-permute-start | bytes 1179656 | tf_op jit(solution)/shard_map/ppermute | solution.py:516
  66.6 16.5 %copy-start = (f32[12,64,128]{2,1,0:T(8,128)S(1)}, f32[12,64,128]{2,1,0:T(8,128)}, u32[]{:S(2)}) copy-start(f32[12,64,128]{2,1,0:T(8,128)} %get-tuple-element.24.refs_0_) | copy-start | bytes 1179652
